TPU v7x, 32 devices: a whole 2x2x4 slice. The times are simulated.
32 devices in a mesh: tm: 4 (over y, x), space: 8 (over z, core).
Axes of the slice: x: 2, y: 2, z: 4, core: 2. Of those that a mesh axis runs over, the one named last changes fastest.
Arguments:
- wave_field: bfloat16 [8, 2048, 256], P('tm', 'space'), may hold values from -600 to 600
- cotangent: bfloat16 [8, 2048, 256], P('tm', 'space'), may hold values from -6 to 6
- block_lists: int32 [8, 16, 4], P('tm', 'space'), may hold values from 0 to 15, as said below
- project_weights: bfloat16 [2, 256, 768], replicated, may hold values from -2 to 2
- combine_weights: bfloat16 [2, 256, 256], replicated, may hold values from -0.375 to 0.375
Outputs:
- mixed_field: bfloat16 [8, 2048, 256], P('tm', 'space')
- field_grad: bfloat16 [8, 2048, 256], P('tm', 'space')
- project_grad: float32 [2, 256, 768], replicated
- combine_grad: float32 [2, 256, 256], replicated
Inputs may be any that keep to these rules, and one draw needn't show every extreme that they name: `block_lists`: for frame f and block b, entry 0 is b itself, entry 1 is b - 2 or b + 2, and every entry lies within 2 blocks of b; entries may repeat.
All inputs are finite; a program needn't handle non-finite values.
Results may differ from a plain program's by a relative error of at most 0.012.
Values may be sent and summed in bfloat16 or wider, within the bound.
No kernel may reach another device: no remote copies, remote signals or barrier semaphores. Data moves between devices by JAX's collectives and lax.ppermute only.
A program may use at most 128 MiB of HBM per device.

v0:
```python
import math

import jax
import jax.numpy as jnp
from jax import lax
from jax.experimental import pallas as pl
from jax.experimental.pallas import tpu as pltpu
from jax.sharding import PartitionSpec as P

HEADS = 8
BLOCK = 128
HREACH = 2
LANES = 128
GROUP_ROWS = 16
VMEM_BYTES = 48 * 1024 * 1024
BF16 = jnp.bfloat16
F32 = jnp.float32


epsilon = 1e-05


def dot_nn(left, right):
    return lax.dot_general(left, right, (((1,), (0,)), ((), ())), preferred_element_type=F32)


def dot_nt(left, right):
    return lax.dot_general(left, right, (((1,), (1,)), ((), ())), preferred_element_type=F32)


def dot_tn(left, right):
    return lax.dot_general(left, right, (((0,), (0,)), ((), ())), preferred_element_type=F32)


def layer_norm(rows):
    widened = rows.astype(F32)
    centered = widened - jnp.mean(widened, axis=-1, keepdims=True)
    inverse = lax.rsqrt(jnp.mean(centered * centered, axis=-1, keepdims=True) + epsilon)
    return (centered * inverse, inverse)


def norm_backward(upstream, normed, inverse):
    mean_grad = jnp.mean(upstream, axis=-1, keepdims=True)
    mean_cross = jnp.mean(upstream * normed, axis=-1, keepdims=True)
    return inverse * (upstream - mean_grad - normed * mean_cross)


def flip(matrix):
    return matrix.astype(F32).T.astype(BF16)


def pair_columns(rows_t, pair, width):
    count = rows_t.shape[1]
    base = (pair * 2 * width) // LANES * LANES
    parts = []
    for head in (2 * pair, 2 * pair + 1):
        start = head * width - base
        pieces = []
        if start:
            pieces.append(jnp.zeros((start, count), rows_t.dtype))
        pieces.append(rows_t[head * width : (head + 1) * width])
        if start + width < LANES:
            pieces.append(jnp.zeros((LANES - start - width, count), rows_t.dtype))
        parts.append(jnp.concatenate(pieces, axis=0))
    return jnp.concatenate(parts, axis=1)


def pair_group(matrix, pair, width):
    base = (pair * 2 * width) // LANES * LANES
    return matrix[:, base : base + LANES]


def pair_diagonal(product, width):
    count = product.shape[1] // 2
    return jnp.concatenate([product[:width, :count], product[width:, count:]], axis=0)


def head_rows(rows, width):
    column = lax.broadcasted_iota(jnp.int32, (1, rows.shape[1]), 1) // width
    return jnp.concatenate(
        [rows * (column == head).astype(F32).astype(BF16) for head in range(HEADS)], axis=0
    )


def head_spread(per_head, width):
    return jnp.concatenate(
        [
            jnp.broadcast_to(per_head[head : head + 1], (width, per_head.shape[1]))
            for head in range(HEADS)
        ],
        axis=0,
    )


def listed_blocks(lists_ref, frame, block):
    own = lists_ref[frame, block, 0]
    return [
        lists_ref[frame, block, entry] - own + (block + HREACH)
        for entry in range(lists_ref.shape[2])
    ]


def space_forward_kernel(
    lists_ref,
    left_ref,
    wave_ref,
    right_ref,
    project_ref,
    combine_ref,
    mixed_ref,
    act_ref,
    kv_ref,
    query_ref,
    probs_ref,
    inverse_sum_ref,
    attended_ref,
    values_t,
):
    frame = pl.program_id(0)
    row_count, features = wave_ref.shape[1:]
    width = features // HEADS
    block_count = row_count // BLOCK
    exponent_scale = math.log2(math.e) / math.sqrt(width)
    rows = jnp.concatenate([left_ref[0], wave_ref[0], right_ref[0]], axis=0)
    normed, _ = layer_norm(rows)
    act = normed.astype(BF16)
    act_ref[0] = act
    keys_values = dot_nn(act, project_ref[0, :, features:]).astype(BF16)
    kv_ref[0] = keys_values
    rim = left_ref.shape[1]
    queries = dot_nn(act[rim : rim + row_count], project_ref[0, :, :features]).astype(BF16)
    query_ref[0] = queries
    for place in range(block_count + 2 * HREACH):
        values_t[place] = flip(keys_values[place * BLOCK : (place + 1) * BLOCK, features:])
    for block in range(block_count):
        places = listed_blocks(lists_ref, frame, block)
        keys = jnp.concatenate(
            [kv_ref[0, pl.ds(place * BLOCK, BLOCK), :features] for place in places], axis=0
        )
        block_values_t = jnp.concatenate([values_t[place] for place in places], axis=1)
        query_t = flip(queries[block * BLOCK : (block + 1) * BLOCK])
        outs = []
        for pair in range(HEADS // 2):
            scores = dot_nn(pair_group(keys, pair, width), pair_columns(query_t, pair, width))
            top = jnp.max(scores, axis=0, keepdims=True)
            exp_scores = jnp.exp2((scores - top) * exponent_scale)
            inverse_sum = 1.0 / jnp.sum(exp_scores, axis=0, keepdims=True)
            probs = exp_scores.astype(BF16)
            probs_ref[0, block, :, pair * 2 * BLOCK : (pair + 1) * 2 * BLOCK] = probs
            inverse_sum_ref[0, block, 2 * pair : 2 * pair + 1] = inverse_sum[:, :BLOCK]
            inverse_sum_ref[0, block, 2 * pair + 1 : 2 * pair + 2] = inverse_sum[:, BLOCK:]
            out = dot_nn(block_values_t[pair * 2 * width : (pair + 1) * 2 * width], probs)
            outs.append(pair_diagonal(out * inverse_sum, width))
        attended_t = jnp.concatenate(outs, axis=0)
        attended_ref[0, block] = attended_t.astype(BF16)
        attended = attended_t.T.astype(BF16)
        mixed = (
            wave_ref[0, block * BLOCK : (block + 1) * BLOCK].astype(F32)
            + dot_nn(attended, combine_ref[0])
        ).astype(BF16)
        sent_rows = mixed_ref.shape[2]
        for part in range(max(1, BLOCK // sent_rows)):
            mixed_ref[(block * BLOCK) // sent_rows + part, 0] = mixed[
                part * sent_rows : (part + 1) * sent_rows
            ]


def time_kernel(
    scale,
    factor,
    history_ref,
    cot_ref,
    project_ref,
    combine_ref,
    both_ref,
    grads_ref,
    proj_s,
    dattn_s,
    attended_s,
    dproj_s,
):
    frames, row_count, features = history_ref.shape
    width = features // HEADS
    tokens = frames * row_count
    exponent_scale = scale * math.log2(math.e)
    rows = history_ref[...].reshape(tokens, features)
    normed, inverse = layer_norm(rows)
    act = normed.astype(BF16)
    proj_s[...] = dot_nn(act, project_ref[0]).astype(BF16).reshape(proj_s.shape)
    cot = cot_ref[...].reshape(tokens, features)
    dattn_s[...] = dot_nt(cot, combine_ref[0]).astype(BF16).reshape(dattn_s.shape)
    count = frames * GROUP_ROWS
    key_row = lax.broadcasted_iota(jnp.int32, (count, 2 * count), 0) % GROUP_ROWS
    query_row = lax.broadcasted_iota(jnp.int32, (count, 2 * count), 1) % GROUP_ROWS
    same_row = key_row == query_row
    for group in range(row_count // GROUP_ROWS):
        span = slice(group * GROUP_ROWS, (group + 1) * GROUP_ROWS)
        queries = proj_s[:, span, :features].reshape(count, features)
        keys = proj_s[:, span, features : 2 * features].reshape(count, features)
        values = proj_s[:, span, 2 * features :].reshape(count, features)
        dattn = dattn_s[:, span].reshape(count, features)
        query_t, keys_t, values_t, dattn_t = flip(queries), flip(keys), flip(values), flip(dattn)
        outs, probs_parts, dscore_parts, dquery_parts = [], [], [], []
        for pair in range(HEADS // 2):
            heads = slice(pair * 2 * width, (pair + 1) * 2 * width)
            scores = dot_nn(pair_group(keys, pair, width), pair_columns(query_t, pair, width))
            scores = jnp.where(same_row, scores, -3e38)
            top = jnp.max(scores, axis=0, keepdims=True)
            exp_scores = jnp.exp2((scores - top) * exponent_scale)
            probs = (exp_scores * (1.0 / jnp.sum(exp_scores, axis=0, keepdims=True))).astype(BF16)
            probs_wide = probs.astype(F32)
            outs.append(pair_diagonal(dot_nn(values_t[heads], probs), width))
            dprobs = dot_nn(pair_group(values, pair, width), pair_columns(dattn_t, pair, width))
            delta = jnp.sum(probs_wide * dprobs, axis=0, keepdims=True)
            dscores = (probs_wide * (dprobs - delta) * scale).astype(BF16)
            dquery_parts.append(pair_diagonal(dot_nn(keys_t[heads], dscores), width))
            probs_parts.append(probs)
            dscore_parts.append(dscores)
        attended_s[:, span] = (
            jnp.concatenate(outs, axis=0).T.astype(BF16).reshape(frames, GROUP_ROWS, features)
        )
        dquery = jnp.concatenate(dquery_parts, axis=0).T
        dkeys = dot_nn(jnp.concatenate(dscore_parts, axis=1), head_rows(queries, width))
        dvalues = dot_nn(jnp.concatenate(probs_parts, axis=1), head_rows(dattn, width))
        dproj = jnp.concatenate([dquery, dkeys, dvalues], axis=1).astype(BF16)
        dproj_s[:, span] = dproj.reshape(frames, GROUP_ROWS, 3 * features)
    attended = attended_s[...].reshape(tokens, features)
    mixed = (rows.astype(F32) + dot_nn(attended, combine_ref[0])).astype(BF16)
    both_ref[:, :, :features] = mixed.reshape(frames, row_count, features)
    dproj = dproj_s[...].reshape(tokens, 3 * features)
    dact = dot_nt(dproj, project_ref[0])
    mixed_grad = (cot.astype(F32) + norm_backward(dact, normed, inverse)).astype(BF16)
    both_ref[:, :, features:] = mixed_grad.reshape(frames, row_count, features)
    grads_ref[:, : 3 * features] = (dot_tn(act, dproj) * factor).astype(BF16)
    grads_ref[:, 3 * features :] = (dot_tn(attended, cot) * factor).astype(BF16)


def space_backward_kernel(
    scale,
    factor,
    lists_ref,
    mixed_in_ref,
    grad_in_ref,
    act_ref,
    kv_ref,
    query_ref,
    probs_ref,
    inverse_sum_ref,
    attended_ref,
    project_ref,
    combine_ref,
    mixed_out_ref,
    dact_ref,
    to_left_ref,
    to_right_ref,
    grads_ref,
    keys_t,
    dscores_s,
    dkv_s,
    grads_s,
):
    frame = pl.program_id(0)
    row_count, features = mixed_out_ref.shape[1:]
    width = features // HEADS
    block_count = row_count // BLOCK
    rim = HREACH * BLOCK
    mixed_out_ref[0] = mixed_in_ref[:, 0].reshape(row_count, features)
    mixed_grad = grad_in_ref[:, 0].reshape(row_count, features)
    for place in range(block_count + 2 * HREACH):
        keys_t[place] = flip(kv_ref[0, place * BLOCK : (place + 1) * BLOCK, :features])
    dkv_s[...] = jnp.zeros(dkv_s.shape, F32)

    @pl.when(frame == 0)
    def _():
        grads_s[...] = jnp.zeros(grads_s.shape, F32)

    dquery_blocks = []
    for block in range(block_count):
        span = slice(block * BLOCK, (block + 1) * BLOCK)
        places = listed_blocks(lists_ref, frame, block)
        values = jnp.concatenate(
            [kv_ref[0, pl.ds(place * BLOCK, BLOCK), features:] for place in places], axis=0
        )
        block_keys_t = jnp.concatenate([keys_t[place] for place in places], axis=1)
        block_grad = mixed_grad[span]
        attended_t = attended_ref[0, block]
        grads_s[:, 3 * features :] += dot_nn(attended_t, block_grad)
        dattn_t = dot_nt(combine_ref[0], block_grad).astype(BF16)
        dattn_wide = dattn_t.astype(F32)
        inverse_sum = inverse_sum_ref[0, block]
        scaled_dattn = (dattn_wide * head_spread(inverse_sum, width)).T.astype(BF16)
        delta = jnp.sum(
            (dattn_wide * attended_t.astype(F32)).reshape(HEADS, width, BLOCK), axis=1
        )
        row_scale = inverse_sum * scale
        dquery_parts = []
        for pair in range(HEADS // 2):
            heads = slice(pair * 2 * width, (pair + 1) * 2 * width)
            columns = slice(pair * 2 * BLOCK, (pair + 1) * 2 * BLOCK)
            pair_delta = jnp.concatenate(
                [delta[2 * pair : 2 * pair + 1], delta[2 * pair + 1 : 2 * pair + 2]], axis=1
            )
            pair_scale = jnp.concatenate(
                [row_scale[2 * pair : 2 * pair + 1], row_scale[2 * pair + 1 : 2 * pair + 2]], axis=1
            )
            dprobs = dot_nn(pair_group(values, pair, width), pair_columns(dattn_t, pair, width))
            probs = probs_ref[0, block, :, columns].astype(F32)
            dscores = (probs * ((dprobs - pair_delta) * pair_scale)).astype(BF16)
            dscores_s[:, columns] = dscores
            dquery_parts.append(pair_diagonal(dot_nn(block_keys_t[heads], dscores), width))
        dquery_blocks.append(jnp.concatenate(dquery_parts, axis=0).T.astype(BF16))
        dkeys = dot_nn(dscores_s[...], head_rows(query_ref[0, span], width))
        dvalues = dot_nn(probs_ref[0, block], head_rows(scaled_dattn, width))
        for entry, place in enumerate(places):
            rows = pl.ds(place * BLOCK, BLOCK)
            listed = slice(entry * BLOCK, (entry + 1) * BLOCK)
            dkv_s[rows, :features] += dkeys[listed]
            dkv_s[rows, features:] += dvalues[listed]
    dquery = jnp.concatenate(dquery_blocks, axis=0)
    dkv = dkv_s[...].astype(BF16)
    grads_s[:, :features] += dot_tn(act_ref[0, rim : rim + row_count], dquery)
    grads_s[:, features : 3 * features] += dot_tn(act_ref[0], dkv)
    dact = dot_nt(dkv, project_ref[0, :, features:])
    to_left_ref[0] = dact[:rim].astype(BF16)
    to_right_ref[0] = dact[rim + row_count :].astype(BF16)
    dact_ref[0] = dact[rim : rim + row_count] + dot_nt(dquery, project_ref[0, :, :features])

    @pl.when(frame == pl.num_programs(0) - 1)
    def _():
        for group in range(4 * features // LANES):
            grads_ref[group * features : (group + 1) * features] = (
                grads_s[:, group * LANES : (group + 1) * LANES] * factor
            ).astype(BF16)


def field_kernel(wave_ref, grad_in_ref, dact_ref, from_left_ref, from_right_ref, field_ref):
    row_count, features = wave_ref.shape[1:]
    normed, inverse = layer_norm(wave_ref[0])
    mixed_grad = grad_in_ref[:, 0].reshape(row_count, features).astype(F32)
    dact = dact_ref[0] + from_left_ref[0].astype(F32) + from_right_ref[0].astype(F32)
    field_ref[0] = (mixed_grad + norm_backward(dact, normed, inverse)).astype(BF16)


def grads_kernel(space_ref, time_ref, project_ref, combine_ref):
    features = combine_ref.shape[1]
    for group in range(4 * features // LANES):
        piece = space_ref[group * features : (group + 1) * features].astype(F32)
        start = group * LANES
        if start < 3 * features:
            project_ref[0, :, start : start + LANES] = piece
        else:
            combine_ref[0, :, start - 3 * features : start - 3 * features + LANES] = piece
    project_ref[1] = time_ref[:, : 3 * features].astype(F32)
    combine_ref[1] = time_ref[:, 3 * features :].astype(F32)


def shift(cells, axis, step):
    count = lax.axis_size(axis)
    if step > 0:
        moves = [(i, i + 1) for i in range(count - 1)]
    else:
        moves = [(i + 1, i) for i in range(count - 1)]
    return lax.ppermute(cells, axis, moves)


def swap(parts, axis):
    return lax.all_to_all(parts, axis, split_axis=0, concat_axis=0, tiled=True)


def sum_scattered(cells, axis):
    count = lax.axis_size(axis)
    arrived = swap(cells, axis).reshape(count, cells.shape[0] // count, cells.shape[1])
    return jnp.sum(arrived.astype(F32), axis=0).astype(cells.dtype)


def gathered(cells, axis):
    count = lax.axis_size(axis)
    return swap(jnp.broadcast_to(cells[None], (count, *cells.shape)), axis).reshape(
        count * cells.shape[0], cells.shape[1]
    )


def per_device(wave_field, cotangent, block_lists, project_weights, combine_weights):
    frame_count, row_count, features = wave_field.shape
    width = features // HEADS
    scale = 1.0 / math.sqrt(width)
    block_count = row_count // BLOCK
    list_length = block_lists.shape[-1]
    rim = HREACH * BLOCK
    extended = row_count + 2 * rim
    keys_count = list_length * BLOCK
    time_count = lax.axis_size("tm")
    all_frames = frame_count * time_count
    sent_rows = row_count // time_count
    factor = 1.0 / math.sqrt(frame_count * row_count * time_count * lax.axis_size("space"))
    params = pltpu.CompilerParams(vmem_limit_bytes=VMEM_BYTES)

    def whole(*shape):
        return pl.BlockSpec(shape, lambda f: (0,) * len(shape))

    def framed(*shape):
        return pl.BlockSpec((1, *shape), lambda f: (f,) + (0,) * len(shape))

    def parted(lane_block):
        return pl.BlockSpec((time_count, 1, sent_rows, features), lambda f: (0, f, 0, lane_block))

    lists_spec = pl.BlockSpec(memory_space=pltpu.SMEM)
    project_spec = whole(1, features, 3 * features)
    combine_spec = whole(1, features, features)

    from_left = shift(wave_field[:, row_count - rim :], "space", 1)
    from_right = shift(wave_field[:, :rim], "space", -1)
    history_cot = lax.all_to_all(cotangent, "tm", split_axis=1, concat_axis=0, tiled=True)

    mixed_space, act, keys_values, queries, probs, inverse_sum, attended = pl.pallas_call(
        space_forward_kernel,
        grid=(frame_count,),
        in_specs=[
            lists_spec,
            framed(rim, features),
            framed(row_count, features),
            framed(rim, features),
            project_spec,
            combine_spec,
        ],
        out_specs=[
            parted(0),
            framed(extended, features),
            framed(extended, 2 * features),
            framed(row_count, features),
            framed(block_count, keys_count, HEADS * BLOCK),
            framed(block_count, HEADS, BLOCK),
            framed(block_count, features, BLOCK),
        ],
        out_shape=[
            jax.ShapeDtypeStruct((time_count, frame_count, sent_rows, features), BF16),
            jax.ShapeDtypeStruct((frame_count, extended, features), BF16),
            jax.ShapeDtypeStruct((frame_count, extended, 2 * features), BF16),
            jax.ShapeDtypeStruct((frame_count, row_count, features), BF16),
            jax.ShapeDtypeStruct((frame_count, block_count, keys_count, HEADS * BLOCK), BF16),
            jax.ShapeDtypeStruct((frame_count, block_count, HEADS, BLOCK), F32),
            jax.ShapeDtypeStruct((frame_count, block_count, features, BLOCK), BF16),
        ],
        scratch_shapes=[pltpu.VMEM((block_count + 2 * HREACH, features, BLOCK), BF16)],
        compiler_params=params,
        name="space_forward",
    )(block_lists, from_left, wave_field, from_right, project_weights, combine_weights)

    history = swap(mixed_space, "tm").reshape(all_frames, sent_rows, features)

    def time_body(*refs):
        time_kernel(scale, factor, *refs)

    both, time_grads = pl.pallas_call(
        time_body,
        grid=(1,),
        in_specs=[
            whole(all_frames, sent_rows, features),
            whole(all_frames, sent_rows, features),
            pl.BlockSpec((1, features, 3 * features), lambda f: (1, 0, 0)),
            pl.BlockSpec((1, features, features), lambda f: (1, 0, 0)),
        ],
        out_specs=[whole(all_frames, sent_rows, 2 * features), whole(features, 4 * features)],
        out_shape=[
            jax.ShapeDtypeStruct((all_frames, sent_rows, 2 * features), BF16),
            jax.ShapeDtypeStruct((features, 4 * features), BF16),
        ],
        scratch_shapes=[
            pltpu.VMEM((all_frames, sent_rows, 3 * features), BF16),
            pltpu.VMEM((all_frames, sent_rows, features), BF16),
            pltpu.VMEM((all_frames, sent_rows, features), BF16),
            pltpu.VMEM((all_frames, sent_rows, 3 * features), BF16),
        ],
        compiler_params=params,
        name="time_pair",
    )(history, history_cot, project_weights, combine_weights)

    returned = swap(both.reshape(time_count, frame_count, sent_rows, 2 * features), "tm")
    time_sum = lax.psum(time_grads, ("tm", "space"))

    def backward_body(*refs):
        space_backward_kernel(scale, factor, *refs)

    mixed_field, dact, to_left, to_right, space_grads = pl.pallas_call(
        backward_body,
        grid=(frame_count,),
        in_specs=[
            lists_spec,
            parted(0),
            parted(1),
            framed(extended, features),
            framed(extended, 2 * features),
            framed(row_count, features),
            framed(block_count, keys_count, HEADS * BLOCK),
            framed(block_count, HEADS, BLOCK),
            framed(block_count, features, BLOCK),
            project_spec,
            combine_spec,
        ],
        out_specs=[
            framed(row_count, features),
            framed(row_count, features),
            framed(rim, features),
            framed(rim, features),
            whole(4 * features // LANES * features, LANES),
        ],
        out_shape=[
            jax.ShapeDtypeStruct((frame_count, row_count, features), BF16),
            jax.ShapeDtypeStruct((frame_count, row_count, features), F32),
            jax.ShapeDtypeStruct((frame_count, rim, features), BF16),
            jax.ShapeDtypeStruct((frame_count, rim, features), BF16),
            jax.ShapeDtypeStruct((4 * features // LANES * features, LANES), BF16),
        ],
        scratch_shapes=[
            pltpu.VMEM((block_count + 2 * HREACH, features, BLOCK), BF16),
            pltpu.VMEM((keys_count, HEADS * BLOCK), BF16),
            pltpu.VMEM((extended, 2 * features), F32),
            pltpu.VMEM((features, 4 * features), F32),
        ],
        compiler_params=params,
        name="space_backward",
    )(
        block_lists,
        returned,
        returned,
        act,
        keys_values,
        queries,
        probs,
        inverse_sum,
        attended,
        project_weights,
        combine_weights,
    )

    edge_left = shift(to_right, "space", 1)
    edge_right = shift(to_left, "space", -1)
    space_sum = sum_scattered(sum_scattered(space_grads, "tm"), "space")
    space_sum = gathered(gathered(space_sum, "space"), "tm")

    field_grad = pl.pallas_call(
        field_kernel,
        grid=(frame_count,),
        in_specs=[
            framed(row_count, features),
            parted(1),
            framed(row_count, features),
            framed(row_count, features),
            framed(row_count, features),
        ],
        out_specs=framed(row_count, features),
        out_shape=jax.ShapeDtypeStruct((frame_count, row_count, features), BF16),
        compiler_params=params,
        name="field_grad",
    )(wave_field, returned, dact, edge_left, edge_right)

    project_grad, combine_grad = pl.pallas_call(
        grads_kernel,
        out_shape=[
            jax.ShapeDtypeStruct((2, features, 3 * features), F32),
            jax.ShapeDtypeStruct((2, features, features), F32),
        ],
        compiler_params=params,
        name="weight_grads",
    )(space_sum, time_sum)
    return (mixed_field, field_grad, project_grad, combine_grad)


def solution(mesh):
    in_specs = (P("tm", "space", None), P("tm", "space", None), P("tm", "space", None), P(), P())
    out_specs = (P("tm", "space", None), P("tm", "space", None), P(), P())
    return jax.shard_map(
        per_device, mesh=mesh, in_specs=in_specs, out_specs=out_specs, check_vma=False
    )
```

profile of v0, /device:TPU:0, one launch (start us, length us, event | category | flops | bytes accessed | tf_op | source)
XLA Modules:
  0.0 256.7 jit_solution(3715242272078998374)
XLA Ops:
  7.2 1.4 collective-permute-start.1
  8.6 3.1 %collective-permute-start = (bf16[2,256,256]{2,1,0:T(8,128)(2,1)}, bf16[2,256,256]{2,1,0:T(8,128)(2,1)S(1)}, u32[]{:S(2)}, u32[]{:S(2)}) collective-permute-start(bf16[2,256,256]{2,1,0:T(8,128)(2,1)} %wave_ref.3), channel_id=1, source_target_pairs={{0,1},{1,2},{2,3},{3,4},{4,5},{5,6},{6,7},{8,9},{9,10},{10,11},{11... | collective-permute-start | bytes 786440 | tf_op jit(solution)/shard_map/ppermute | solution.py:363
  11.7 1.9 copy.12
  13.6 5.3 %all-to-all-start.1 = ((bf16[2,256,256]{2,0,1:T(2,128)(2,1)}), bf16[2,256,256]{2,0,1:T(2,128)(2,1)}, u32[]{:S(2)}, u32[]{:S(2)}) async-start(bf16[2,256,256]{2,0,1:T(2,128)(2,1)} %copy.12), calls=%async_computation.1 | async-start | bytes 524288 | tf_op jit(solution)/shard_map/all_to_all | solution.py:413
  18.9 0.9 copy-done.1
  19.9 0.9 copy-done.3
  21.5 11.2 %space_forward.1 = (bf16[4,2,64,256]{3,2,1,0:T(8,128)(2,1)}, bf16[2,768,256]{2,1,0:T(8,128)(2,1)S(1)}, bf16[2,768,512]{2,1,0:T(8,128)(2,1)S(1)}, bf16[2,256,256]...) custom-call(s32[2,2,4]{2,1,0:T(2,128)S(1)} %copy-done.12, ...), custom_call_target="tpu_custom_call" | custom-call | tf_op jit(solution)/shard_map/space_forward/pallas_call | solution.py:415
  34.2 4.2 %all-to-all-start = ((bf16[4,2,64,256]{3,2,1,0:T(8,128)(2,1)}), bf16[4,2,64,256]{3,2,1,0:T(8,128)(2,1)S(1)}, u32[]{:S(2)}, u32[]{:S(2)}) async-start(bf16[4,2,64,256]{3,2,1,0:T(8,128)(2,1)} %get-tuple-element.20), calls=%async_computation | async-start | bytes 524288 | tf_op jit(solution)/shard_map/all_to_all | solution.py:367
  38.4 1.0 copy.13
  39.4 5.5 %all-to-all-done = bf16[4,2,64,256]{3,2,1,0:T(8,128)(2,1)S(1)} async-done(((bf16[4,2,64,256]{3,2,1,0:T(8,128)(2,1)}), bf16[4,2,64,256]{3,2,1,0:T(8,128)(2,1)S(1)}, u32[]{:S(2)}, u32[]{:S(2)}) %all-to-all-start) | async-done | bytes 262176 | tf_op jit(solution)/shard_map/all_to_all | solution.py:367
  45.0 9.2 %time_pair.1 = (bf16[8,64,512]{2,1,0:T(8,128)(2,1)S(1)}, bf16[256,1024]{1,0:T(8,128)(2,1)}) custom-call(bf16[8,64,256]{2,1,0:T(8,128)(2,1)S(1)} %bitcast.11, bf16[8,64,256]{2,1,0:T(8,128)(2,1)S(1)} %bitcast.12, bf16[2,256,768]{2,1,0:T(8,128)(2,1)S(1)} %copy-done, bf16[2,256,256]{2,1,0:T(8,128)(2,1)S(1)} %copy-done.2), custom_call_target="tpu_custom_call" | custom-call | tf_op jit(solution)/shard_map/time_pair/pallas_call | solution.py:454
  54.2 11.4 %all_to_all.56.refs_1_.refs_2_.grad_in_ref = bf16[4,2,64,512]{3,2,1,0:T(8,128)(2,1)S(1)} all-to-all(bf16[4,2,64,512]{3,2,1,0:T(8,128)(2,1)S(1)} %bitcast.14), channel_id=1, replica_groups=mesh['tm'=4,'space'=8] {'tm'}, dimensions={0} | all-to-all | bytes 1048576 | tf_op jit(solution)/shard_map/all_to_all | solution.py:367
  65.6 11.7 %space_backward.1 = (bf16[2,256,256]{2,1,0:T(8,128)(2,1)}, f32[2,256,256]{2,1,0:T(8,128)S(1)}, bf16[2,256,256]{2,1,0:T(8,128)(2,1)S(1)}, bf16[2,256,256]{2,1,0:T(8,128)(2,1)S(1)}, bf16[2048,128]{1,0:T(8,128)(2,1)S(1)}) custom-call(s32[2,2,4]{2,1,0:T(2,128)S(1)} %copy-done.13, bf16[4,2,64,512]{3,2,1,0:T(8,128)(2,1)S(1)} %all_to_all.56.refs_1_.refs_2_.grad_in_ref, ...), custom_call_target="tpu_custom_call" | custom-call | tf_op jit(solution)/shard_map/space_backward/pallas_call | solution.py:484
  79.5 9.9 %all_to_all.57 = bf16[4,512,128]{2,1,0:T(8,128)(2,1)S(1)} all-to-all(bf16[4,512,128]{2,1,0:T(8,128)(2,1)S(1)} %bitcast.13), channel_id=1, replica_groups=mesh['tm'=4,'space'=8] {'tm'}, dimensions={0} | all-to-all | bytes 1048576 | tf_op jit(solution)/shard_map/all_to_all | solution.py:367
  89.4 10.3 %all_to_all.58 = bf16[8,64,128]{2,1,0:T(8,128)(2,1)S(1)} all-to-all(bf16[8,64,128]{2,1,0:T(8,128)(2,1)S(1)} %bitcast.16), channel_id=1, replica_groups=mesh['tm'=4,'space'=8] {'space'}, dimensions={0} | all-to-all | bytes 262144 | tf_op jit(solution)/shard_map/all_to_all | solution.py:367
  99.8 9.3 %all_to_all.59 = bf16[8,64,128]{2,1,0:T(8,128)(2,1)S(1)} all-to-all(bf16[8,64,128]{2,1,0:T(8,128)(2,1)S(1)} %broadcast_in_dim.6), channel_id=1, replica_groups=mesh['tm'=4,'space'=8] {'space'}, dimensions={0} | all-to-all | bytes 262144 | tf_op jit(solution)/shard_map/all_to_all | solution.py:367
  109.9 3.5 %all-to-all-start.6 = ((bf16[4,512,128]{2,1,0:T(8,128)(2,1)}), bf16[4,512,128]{2,1,0:T(8,128)(2,1)S(1)}, u32[]{:S(2)}, u32[]{:S(2)}) async-start(bf16[4,512,128]{2,1,0:T(8,128)(2,1)} %broadcast_in_dim.15), calls=%async_computation.6 | async-start | bytes 1048576 | tf_op jit(solution)/shard_map/all_to_all | solution.py:367
  113.4 1.5 collective-permute-start.2
  114.9 1.3 collective-permute-start.3
  116.2 3.1 %collective-permute-done.3.from_right_ref = bf16[2,256,256]{2,1,0:T(8,128)(2,1)S(1)} collective-permute-done((bf16[2,256,256]{2,1,0:T(8,128)(2,1)S(1)}, bf16[2,256,256]{2,1,0:T(8,128)(2,1)S(1)}, u32[]{:S(2)}, u32[]{:S(2)}) %collective-permute-start.3) | collective-permute-done | bytes 262176 | tf_op jit(solution)/shard_map/ppermute | solution.py:363
  119.3 1.3 field_grad.1
  120.6 126.8 %all-reduce.2.cloned.1.call-done.time_ref = bf16[256,1024]{1,0:T(8,128)(2,1)} async-done(((bf16[256,1024]{1,0:T(8,128)(2,1)}), bf16[256,1024]{1,0:T(8,128)(2,1)}) %all-reduce.2.cloned.1.call-update) | async-done | bytes 524304 | tf_op jit(solution)/shard_map/psum | solution.py:479
  247.4 1.0 copy-done.7
  248.5 1.4 weight_grads.1
  (44 shorter events, 5.6 us)
Async XLA Ops:
  7.2 11.7 %copy-start = (bf16[2,256,768]{2,1,0:T(8,128)(2,1)S(1)}, bf16[2,256,768]{2,1,0:T(8,128)(2,1)}, u32[]{:S(2)}) copy-start(bf16[2,256,768]{2,1,0:T(8,128)(2,1)} %refs_9_.1) | copy-start | bytes 2359300
  7.2 11.7 %collective-permute-start.1 = (bf16[2,256,256]{2,1,0:T(8,128)(2,1)}, bf16[2,256,256]{2,1,0:T(8,128)(2,1)S(1)}, u32[]{:S(2)}, u32[]{:S(2)}) collective-permute-start(bf16[2,256,256]{2,1,0:T(8,128)(2,1)} %wave_ref.3), channel_id=1, source_target_pairs={{1,0},{2,1},{3,2},{4,3},{5,4},{6,5},{7,6},{9,8},{10,9},{11,10},{12... | collective-permute-start | bytes 786440 | tf_op jit(solution)/shard_map/ppermute | solution.py:363
  8.6 10.3 %collective-permute-start = (bf16[2,256,256]{2,1,0:T(8,128)(2,1)}, bf16[2,256,256]{2,1,0:T(8,128)(2,1)S(1)}, u32[]{:S(2)}, u32[]{:S(2)}) collective-permute-start(bf16[2,256,256]{2,1,0:T(8,128)(2,1)} %wave_ref.3), channel_id=1, source_target_pairs={{0,1},{1,2},{2,3},{3,4},{4,5},{5,6},{6,7},{8,9},{9,10},{10,11},{11... | collective-permute-start | bytes 786440 | tf_op jit(solution)/shard_map/ppermute | solution.py:363
  13.6 31.4 %copy-start.2 = (bf16[2,256,256]{2,1,0:T(8,128)(2,1)S(1)}, bf16[2,256,256]{2,1,0:T(8,128)(2,1)}, u32[]{:S(2)}) copy-start(bf16[2,256,256]{2,1,0:T(8,128)(2,1)} %refs_10_.1) | copy-start | bytes 786436
  13.6 20.7 %all-to-all-start.1 = ((bf16[2,256,256]{2,0,1:T(2,128)(2,1)}), bf16[2,256,256]{2,0,1:T(2,128)(2,1)}, u32[]{:S(2)}, u32[]{:S(2)}) async-start(bf16[2,256,256]{2,0,1:T(2,128)(2,1)} %copy.12), calls=%async_computation.1 | async-start | bytes 524288 | tf_op jit(solution)/shard_map/all_to_all | solution.py:413
  18.9 1.0 copy-start.1
  19.9 0.9 copy-start.3
  32.7 0.9 copy-start.5
  33.5 0.7 copy-start.10
  34.2 10.7 %all-to-all-start = ((bf16[4,2,64,256]{3,2,1,0:T(8,128)(2,1)}), bf16[4,2,64,256]{3,2,1,0:T(8,128)(2,1)S(1)}, u32[]{:S(2)}, u32[]{:S(2)}) async-start(bf16[4,2,64,256]{3,2,1,0:T(8,128)(2,1)} %get-tuple-element.20), calls=%async_computation | async-start | bytes 524288 | tf_op jit(solution)/shard_map/all_to_all | solution.py:367
  38.4 27.2 %copy-start.13 = (s32[2,2,4]{2,1,0:T(2,128)S(1)}, s32[2,2,4]{2,1,0:T(2,128)}, u32[]{:S(2)}) copy-start(s32[2,2,4]{2,1,0:T(2,128)} %refs_0_.1) | copy-start | bytes 196
  45.0 20.6 %copy-start.6 = (bf16[2,768,256]{2,1,0:T(8,128)(2,1)S(1)}, bf16[2,768,256]{2,1,0:T(8,128)(2,1)}, u32[]{:S(2)}) copy-start(bf16[2,768,256]{2,1,0:T(8,128)(2,1)} %copy-done.5) | copy-start | bytes 2359300
  45.0 20.6 %copy-start.11 = (bf16[2,2,256,128]{3,2,1,0:T(8,128)(2,1)S(1)}, bf16[2,2,256,128]{3,2,1,0:T(8,128)(2,1)}, u32[]{:S(2)}) copy-start(bf16[2,2,256,128]{3,2,1,0:T(8,128)(2,1)} %copy-done.10) | copy-start | bytes 786436
  77.3 0.8 copy-start.8
  78.8 0.7 copy-start.16
  89.3 24.1 %copy-start.17 = (bf16[2,256,256]{2,1,0:T(8,128)(2,1)S(1)}, bf16[2,256,256]{2,1,0:T(8,128)(2,1)}, u32[]{:S(2)}) copy-start(bf16[2,256,256]{2,1,0:T(8,128)(2,1)} %copy-done.16) | copy-start | bytes 786436
  89.3 25.6 %copy-start.15 = (bf16[2,256,256]{2,1,0:T(8,128)(2,1)S(1)}, bf16[2,256,256]{2,1,0:T(8,128)(2,1)}, u32[]{:S(2)}) copy-start(bf16[2,256,256]{2,1,0:T(8,128)(2,1)} %copy-done.14) | copy-start | bytes 786436
  89.4 29.9 %copy-start.4 = (bf16[2,256,256]{2,1,0:T(8,128)(2,1)S(1)}, bf16[2,256,256]{2,1,0:T(8,128)(2,1)}, u32[]{:S(2)}) copy-start(bf16[2,256,256]{2,1,0:T(8,128)(2,1)} %wave_ref.3) | copy-start | bytes 786436
  89.4 29.9 %copy-start.9 = (f32[2,256,256]{2,1,0:T(8,128)S(1)}, f32[2,256,256]{2,1,0:T(8,128)}, u32[]{:S(2)}) copy-start(f32[2,256,256]{2,1,0:T(8,128)} %copy-done.8) | copy-start | bytes 1572868
  109.9 137.5 %all-to-all-start.6 = ((bf16[4,512,128]{2,1,0:T(8,128)(2,1)}), bf16[4,512,128]{2,1,0:T(8,128)(2,1)S(1)}, u32[]{:S(2)}, u32[]{:S(2)}) async-start(bf16[4,512,128]{2,1,0:T(8,128)(2,1)} %broadcast_in_dim.15), calls=%async_computation.6 | async-start | bytes 1048576 | tf_op jit(solution)/shard_map/all_to_all | solution.py:367
  113.4 134.1 %all-reduce.2.cloned.1.call-start = ((), (), s32[]{:S(2)}) async-start(), calls=%async_computation.7 | async-start | bytes 1048576 | tf_op jit(solution)/shard_map/psum | solution.py:479
  113.4 2.8 %collective-permute-start.2 = (bf16[2,256,256]{2,1,0:T(8,128)(2,1)S(1)}, bf16[2,256,256]{2,1,0:T(8,128)(2,1)S(1)}, u32[]{:S(2)}, u32[]{:S(2)}) collective-permute-start(bf16[2,256,256]{2,1,0:T(8,128)(2,1)S(1)} %copy-done.17), channel_id=1, source_target_pairs={{0,1},{1,2},{2,3},{3,4},{4,5},{5,6},{6,7},{8,9},{9,10},{10,11},{11... | collective-permute-start | bytes 786440 | tf_op jit(solution)/shard_map/ppermute | solution.py:363
  114.9 4.4 %collective-permute-start.3 = (bf16[2,256,256]{2,1,0:T(8,128)(2,1)S(1)}, bf16[2,256,256]{2,1,0:T(8,128)(2,1)S(1)}, u32[]{:S(2)}, u32[]{:S(2)}) collective-permute-start(bf16[2,256,256]{2,1,0:T(8,128)(2,1)S(1)} %copy-done.15), channel_id=1, source_target_pairs={{1,0},{2,1},{3,2},{4,3},{5,4},{6,5},{7,6},{9,8},{10,9},{11,10},{12... | collective-permute-start | bytes 786440 | tf_op jit(solution)/shard_map/ppermute | solution.py:363
  247.4 1.0 copy-start.7
  (2 other events, 1.4 us)
Sparse Core Ops, SparseCore 0:
  120.0 127.3 all-reduce.1
where the time goes:
time: 258 us; the launch traced here: 257 us
  waiting for transfers between devices  135 us (52%)
  blocking collectives  40.8 us (16%)
  Pallas kernels  34.8 us (13%)
  starting transfers between devices  20.2 us (8%)
  between operations  14.2 us (6%)
  local copies, waits for them, and re-layouts  11.2 us (4%)
    psum x1, waiting for transfers between devices, per_device(): time_sum = lax.psum(time_grads, ('tm', 'space'))  127 us
    all_to_all x4, blocking collectives, swap(): return lax.all_to_all(parts, axis, split_axis=0, concat_axis=0, tiled=True)  40.8 us
    pallas_call x1, Pallas kernels, per_device(): pl.pallas_call(backward_body, grid=(frame_count,), in_specs=[lists_spec,...  11.7 us
    pallas_call x1, Pallas kernels, per_device(): pl.pallas_call(space_forward_kernel, grid=(frame_count,), in_specs=[lists...  11.2 us
    unnamed x37, local copies, waits for them, and re-layouts  9.36 us
    pallas_call x1, Pallas kernels, per_device(): pl.pallas_call(time_body, grid=(1,), in_specs=[whole(all_frames, sent_row...  9.19 us
    all_to_all x2, starting transfers between devices, swap(): return lax.all_to_all(parts, axis, split_axis=0, concat_axis=0, tiled=True)  7.65 us
    ppermute x4, starting transfers between devices, shift(): return lax.ppermute(cells, axis, moves)  7.22 us
  transfers between devices with their start and end apart: 8, of which 3 were waited for; matrix products, arithmetic and copies ran while one was open for 1% of the time, Pallas kernels for 5%

commit v1 on v0

--- a/solution.py
+++ b/solution.py
@@ -102,21 +102,24 @@
 
 def space_forward_kernel(
     lists_ref,
+    place_ref,
     left_ref,
     wave_ref,
     right_ref,
+    cot_ref,
     project_ref,
     combine_ref,
-    mixed_ref,
     act_ref,
     kv_ref,
     query_ref,
     probs_ref,
     inverse_sum_ref,
     attended_ref,
-    values_t,
+    *rest,
 ):
+    *sent_refs, values_t, mixed_s = rest
     frame = pl.program_id(0)
+    me = place_ref[0]
     row_count, features = wave_ref.shape[1:]
     width = features // HEADS
     block_count = row_count // BLOCK
@@ -158,36 +161,40 @@
             wave_ref[0, block * BLOCK : (block + 1) * BLOCK].astype(F32)
             + dot_nn(attended, combine_ref[0])
         ).astype(BF16)
-        sent_rows = mixed_ref.shape[2]
-        for part in range(max(1, BLOCK // sent_rows)):
-            mixed_ref[(block * BLOCK) // sent_rows + part, 0] = mixed[
-                part * sent_rows : (part + 1) * sent_rows
-            ]
+        mixed_s[block * BLOCK : (block + 1) * BLOCK] = mixed
+    for distance, sent_ref in enumerate(sent_refs):
+        sent_rows = sent_ref.shape[1]
+        span = pl.ds(pl.multiple_of((me ^ distance) * sent_rows, GROUP_ROWS), sent_rows)
+        sent_ref[0, :, :features] = mixed_s[span]
+        sent_ref[0, :, features:] = cot_ref[0, span]
 
 
 def time_kernel(
     scale,
     factor,
-    history_ref,
-    cot_ref,
-    project_ref,
-    combine_ref,
-    both_ref,
-    grads_ref,
-    proj_s,
-    dattn_s,
-    attended_s,
-    dproj_s,
+    count_in,
+    *refs,
 ):
-    frames, row_count, features = history_ref.shape
+    arrived_refs = refs[:count_in]
+    project_ref, combine_ref = refs[count_in : count_in + 2]
+    returned_refs = refs[count_in + 2 : 2 * count_in + 2]
+    grads_ref, proj_s, dattn_s, attended_s, dproj_s = refs[2 * count_in + 2 :]
+    part_frames, row_count, features = arrived_refs[0].shape
+    features //= 2
+    frames = part_frames * count_in
     width = features // HEADS
     tokens = frames * row_count
     exponent_scale = scale * math.log2(math.e)
-    rows = history_ref[...].reshape(tokens, features)
+    part_tokens = part_frames * row_count
+    rows = jnp.concatenate(
+        [ref[:, :, :features].reshape(part_tokens, features) for ref in arrived_refs], axis=0
+    )
+    cot = jnp.concatenate(
+        [ref[:, :, features:].reshape(part_tokens, features) for ref in arrived_refs], axis=0
+    )
     normed, inverse = layer_norm(rows)
     act = normed.astype(BF16)
     proj_s[...] = dot_nn(act, project_ref[0]).astype(BF16).reshape(proj_s.shape)
-    cot = cot_ref[...].reshape(tokens, features)
     dattn_s[...] = dot_nt(cot, combine_ref[0]).astype(BF16).reshape(dattn_s.shape)
     count = frames * GROUP_ROWS
     key_row = lax.broadcasted_iota(jnp.int32, (count, 2 * count), 0) % GROUP_ROWS
@@ -226,11 +233,13 @@
         dproj_s[:, span] = dproj.reshape(frames, GROUP_ROWS, 3 * features)
     attended = attended_s[...].reshape(tokens, features)
     mixed = (rows.astype(F32) + dot_nn(attended, combine_ref[0])).astype(BF16)
-    both_ref[:, :, :features] = mixed.reshape(frames, row_count, features)
     dproj = dproj_s[...].reshape(tokens, 3 * features)
     dact = dot_nt(dproj, project_ref[0])
     mixed_grad = (cot.astype(F32) + norm_backward(dact, normed, inverse)).astype(BF16)
-    both_ref[:, :, features:] = mixed_grad.reshape(frames, row_count, features)
+    for part, ref in enumerate(returned_refs):
+        span = slice(part * part_tokens, (part + 1) * part_tokens)
+        ref[:, :, :features] = mixed[span].reshape(part_frames, row_count, features)
+        ref[:, :, features:] = mixed_grad[span].reshape(part_frames, row_count, features)
     grads_ref[:, : 3 * features] = (dot_tn(act, dproj) * factor).astype(BF16)
     grads_ref[:, 3 * features :] = (dot_tn(attended, cot) * factor).astype(BF16)
 
@@ -238,34 +247,47 @@
 def space_backward_kernel(
     scale,
     factor,
+    count_in,
     lists_ref,
-    mixed_in_ref,
-    grad_in_ref,
-    act_ref,
-    kv_ref,
-    query_ref,
-    probs_ref,
-    inverse_sum_ref,
-    attended_ref,
-    project_ref,
-    combine_ref,
-    mixed_out_ref,
-    dact_ref,
-    to_left_ref,
-    to_right_ref,
-    grads_ref,
-    keys_t,
-    dscores_s,
-    dkv_s,
-    grads_s,
+    place_ref,
+    *refs,
 ):
+    returned_refs = refs[:count_in]
+    (
+        act_ref,
+        kv_ref,
+        query_ref,
+        probs_ref,
+        inverse_sum_ref,
+        attended_ref,
+        project_ref,
+        combine_ref,
+        mixed_out_ref,
+        mixed_grad_ref,
+        dact_ref,
+        to_left_ref,
+        to_right_ref,
+        kept_ref,
+        sent_ref,
+        keys_t,
+        dscores_s,
+        dkv_s,
+        grads_s,
+        rounded_s,
+    ) = refs[count_in:]
     frame = pl.program_id(0)
+    me = place_ref[0]
+    core = place_ref[1] % 2
     row_count, features = mixed_out_ref.shape[1:]
     width = features // HEADS
     block_count = row_count // BLOCK
     rim = HREACH * BLOCK
-    mixed_out_ref[0] = mixed_in_ref[:, 0].reshape(row_count, features)
-    mixed_grad = grad_in_ref[:, 0].reshape(row_count, features)
+    for distance, ref in enumerate(returned_refs):
+        sent_rows = ref.shape[1]
+        span = pl.ds(pl.multiple_of((me ^ distance) * sent_rows, GROUP_ROWS), sent_rows)
+        mixed_out_ref[0, span] = ref[0, :, :features]
+        mixed_grad_ref[0, span] = ref[0, :, features:]
+    mixed_grad = mixed_grad_ref[0]
     for place in range(block_count + 2 * HREACH):
         keys_t[place] = flip(kv_ref[0, place * BLOCK : (place + 1) * BLOCK, :features])
     dkv_s[...] = jnp.zeros(dkv_s.shape, F32)
@@ -328,23 +350,57 @@
     @pl.when(frame == pl.num_programs(0) - 1)
     def _():
         for group in range(4 * features // LANES):
-            grads_ref[group * features : (group + 1) * features] = (
+            rounded_s[group * features : (group + 1) * features] = (
                 grads_s[:, group * LANES : (group + 1) * LANES] * factor
             ).astype(BF16)
-
-
-def field_kernel(wave_ref, grad_in_ref, dact_ref, from_left_ref, from_right_ref, field_ref):
-    row_count, features = wave_ref.shape[1:]
+        half = kept_ref.shape[0]
+        kept_ref[...] = rounded_s[pl.ds(pl.multiple_of(core * half, GROUP_ROWS), half)]
+        sent_ref[...] = rounded_s[pl.ds(pl.multiple_of((1 - core) * half, GROUP_ROWS), half)]
+
+
+def field_kernel(wave_ref, mixed_grad_ref, dact_ref, from_left_ref, from_right_ref, field_ref):
     normed, inverse = layer_norm(wave_ref[0])
-    mixed_grad = grad_in_ref[:, 0].reshape(row_count, features).astype(F32)
     dact = dact_ref[0] + from_left_ref[0].astype(F32) + from_right_ref[0].astype(F32)
-    field_ref[0] = (mixed_grad + norm_backward(dact, normed, inverse)).astype(BF16)
-
-
-def grads_kernel(space_ref, time_ref, project_ref, combine_ref):
+    field_ref[0] = (
+        mixed_grad_ref[0].astype(F32) + norm_backward(dact, normed, inverse)
+    ).astype(BF16)
+
+
+def split_kernel(place_ref, kept_ref, arrived_ref, *refs):
+    *part_refs, sum_s = refs
+    sum_s[...] = (kept_ref[...].astype(F32) + arrived_ref[...].astype(F32)).astype(BF16)
+    for distance, ref in enumerate(part_refs):
+        rows = ref.shape[0]
+        ref[...] = sum_s[pl.ds(pl.multiple_of((place_ref[0] ^ distance) * rows, GROUP_ROWS), rows)]
+
+
+def sum_kernel(axis, group, place_ref, *refs):
+    *part_refs, total_ref, parts_s = refs
+    me = place_ref[axis] // group
+    for distance, ref in enumerate(part_refs):
+        parts_s[me ^ distance] = ref[...]
+    total = parts_s[0].astype(F32)
+    for part in range(1, len(part_refs)):
+        total = total + parts_s[part].astype(F32)
+    total_ref[...] = total.astype(BF16)
+
+
+def join_kernel(place_ref, *refs):
+    *part_refs, joined_ref = refs
+    for distance, ref in enumerate(part_refs):
+        rows = ref.shape[0]
+        span = pl.ds(pl.multiple_of((place_ref[0] ^ distance) * rows, GROUP_ROWS), rows)
+        joined_ref[span] = ref[...]
+
+
+def grads_kernel(place_ref, own_ref, other_ref, time_ref, project_ref, combine_ref, space_s):
     features = combine_ref.shape[1]
+    core = place_ref[1] % 2
+    half = own_ref.shape[0]
+    space_s[pl.ds(pl.multiple_of(core * half, GROUP_ROWS), half)] = own_ref[...]
+    space_s[pl.ds(pl.multiple_of((1 - core) * half, GROUP_ROWS), half)] = other_ref[...]
     for group in range(4 * features // LANES):
-        piece = space_ref[group * features : (group + 1) * features].astype(F32)
+        piece = space_s[group * features : (group + 1) * features].astype(F32)
         start = group * LANES
         if start < 3 * features:
             project_ref[0, :, start : start + LANES] = piece
@@ -363,21 +419,8 @@
     return lax.ppermute(cells, axis, moves)
 
 
-def swap(parts, axis):
-    return lax.all_to_all(parts, axis, split_axis=0, concat_axis=0, tiled=True)
-
-
-def sum_scattered(cells, axis):
-    count = lax.axis_size(axis)
-    arrived = swap(cells, axis).reshape(count, cells.shape[0] // count, cells.shape[1])
-    return jnp.sum(arrived.astype(F32), axis=0).astype(cells.dtype)
-
-
-def gathered(cells, axis):
-    count = lax.axis_size(axis)
-    return swap(jnp.broadcast_to(cells[None], (count, *cells.shape)), axis).reshape(
-        count * cells.shape[0], cells.shape[1]
-    )
+def exchange(cells, axis, distance):
+    return lax.ppermute(cells, axis, [(i, i ^ distance) for i in range(lax.axis_size(axis))])
 
 
 def per_device(wave_field, cotangent, block_lists, project_weights, combine_weights):
@@ -401,68 +444,81 @@
     def framed(*shape):
         return pl.BlockSpec((1, *shape), lambda f: (f,) + (0,) * len(shape))
 
-    def parted(lane_block):
-        return pl.BlockSpec((time_count, 1, sent_rows, features), lambda f: (0, f, 0, lane_block))
-
     lists_spec = pl.BlockSpec(memory_space=pltpu.SMEM)
     project_spec = whole(1, features, 3 * features)
     combine_spec = whole(1, features, features)
+    part_spec = framed(sent_rows, 2 * features)
+    part_shape = jax.ShapeDtypeStruct((frame_count, sent_rows, 2 * features), BF16)
+    place = jnp.stack([lax.axis_index("tm"), lax.axis_index("space")]).astype(jnp.int32)
 
     from_left = shift(wave_field[:, row_count - rim :], "space", 1)
     from_right = shift(wave_field[:, :rim], "space", -1)
-    history_cot = lax.all_to_all(cotangent, "tm", split_axis=1, concat_axis=0, tiled=True)
-
-    mixed_space, act, keys_values, queries, probs, inverse_sum, attended = pl.pallas_call(
+
+    act, keys_values, queries, probs, inverse_sum, attended, *parts = pl.pallas_call(
         space_forward_kernel,
         grid=(frame_count,),
         in_specs=[
             lists_spec,
+            lists_spec,
             framed(rim, features),
             framed(row_count, features),
             framed(rim, features),
+            framed(row_count, features),
             project_spec,
             combine_spec,
         ],
         out_specs=[
-            parted(0),
             framed(extended, features),
             framed(extended, 2 * features),
             framed(row_count, features),
             framed(block_count, keys_count, HEADS * BLOCK),
             framed(block_count, HEADS, BLOCK),
             framed(block_count, features, BLOCK),
+            *[part_spec] * time_count,
         ],
         out_shape=[
-            jax.ShapeDtypeStruct((time_count, frame_count, sent_rows, features), BF16),
             jax.ShapeDtypeStruct((frame_count, extended, features), BF16),
             jax.ShapeDtypeStruct((frame_count, extended, 2 * features), BF16),
             jax.ShapeDtypeStruct((frame_count, row_count, features), BF16),
             jax.ShapeDtypeStruct((frame_count, block_count, keys_count, HEADS * BLOCK), BF16),
             jax.ShapeDtypeStruct((frame_count, block_count, HEADS, BLOCK), F32),
             jax.ShapeDtypeStruct((frame_count, block_count, features, BLOCK), BF16),
-        ],
-        scratch_shapes=[pltpu.VMEM((block_count + 2 * HREACH, features, BLOCK), BF16)],
+            *[part_shape] * time_count,
+        ],
+        scratch_shapes=[
+            pltpu.VMEM((block_count + 2 * HREACH, features, BLOCK), BF16),
+            pltpu.VMEM((row_count, features), BF16),
+        ],
         compiler_params=params,
         name="space_forward",
-    )(block_lists, from_left, wave_field, from_right, project_weights, combine_weights)
-
-    history = swap(mixed_space, "tm").reshape(all_frames, sent_rows, features)
+    )(
+        block_lists,
+        place,
+        from_left,
+        wave_field,
+        from_right,
+        cotangent,
+        project_weights,
+        combine_weights,
+    )
+
+    arrived = [parts[0]] + [exchange(parts[d], "tm", d) for d in range(1, time_count)]
 
     def time_body(*refs):
-        time_kernel(scale, factor, *refs)
-
-    both, time_grads = pl.pallas_call(
+        time_kernel(scale, factor, time_count, *refs)
+
+    whole_part = whole(frame_count, sent_rows, 2 * features)
+    *parts, time_grads = pl.pallas_call(
         time_body,
         grid=(1,),
         in_specs=[
-            whole(all_frames, sent_rows, features),
-            whole(all_frames, sent_rows, features),
+            *[whole_part] * time_count,
             pl.BlockSpec((1, features, 3 * features), lambda f: (1, 0, 0)),
             pl.BlockSpec((1, features, features), lambda f: (1, 0, 0)),
         ],
-        out_specs=[whole(all_frames, sent_rows, 2 * features), whole(features, 4 * features)],
+        out_specs=[*[whole_part] * time_count, whole(features, 4 * features)],
         out_shape=[
-            jax.ShapeDtypeStruct((all_frames, sent_rows, 2 * features), BF16),
+            *[part_shape] * time_count,
             jax.ShapeDtypeStruct((features, 4 * features), BF16),
         ],
         scratch_shapes=[
@@ -473,21 +529,23 @@
         ],
         compiler_params=params,
         name="time_pair",
-    )(history, history_cot, project_weights, combine_weights)
-
-    returned = swap(both.reshape(time_count, frame_count, sent_rows, 2 * features), "tm")
-    time_sum = lax.psum(time_grads, ("tm", "space"))
+    )(*arrived, project_weights, combine_weights)
+
+    returned = [parts[0]] + [exchange(parts[d], "tm", d) for d in range(1, time_count)]
+    time_sum = lax.psum(lax.psum(time_grads, "tm"), "space")
 
     def backward_body(*refs):
-        space_backward_kernel(scale, factor, *refs)
-
-    mixed_field, dact, to_left, to_right, space_grads = pl.pallas_call(
+        space_backward_kernel(scale, factor, time_count, *refs)
+
+    grad_rows = 4 * features // LANES * features
+    half_shape = jax.ShapeDtypeStruct((grad_rows // 2, LANES), BF16)
+    mixed_field, mixed_grad, dact, to_left, to_right, kept, sent = pl.pallas_call(
         backward_body,
         grid=(frame_count,),
         in_specs=[
             lists_spec,
-            parted(0),
-            parted(1),
+            lists_spec,
+            *[part_spec] * time_count,
             framed(extended, features),
             framed(extended, 2 * features),
             framed(row_count, features),
@@ -500,29 +558,34 @@
         out_specs=[
             framed(row_count, features),
             framed(row_count, features),
+            framed(row_count, features),
             framed(rim, features),
             framed(rim, features),
-            whole(4 * features // LANES * features, LANES),
+            whole(grad_rows // 2, LANES),
+            whole(grad_rows // 2, LANES),
         ],
         out_shape=[
+            jax.ShapeDtypeStruct((frame_count, row_count, features), BF16),
             jax.ShapeDtypeStruct((frame_count, row_count, features), BF16),
             jax.ShapeDtypeStruct((frame_count, row_count, features), F32),
             jax.ShapeDtypeStruct((frame_count, rim, features), BF16),
             jax.ShapeDtypeStruct((frame_count, rim, features), BF16),
-            jax.ShapeDtypeStruct((4 * features // LANES * features, LANES), BF16),
+            half_shape,
+            half_shape,
         ],
         scratch_shapes=[
             pltpu.VMEM((block_count + 2 * HREACH, features, BLOCK), BF16),
             pltpu.VMEM((keys_count, HEADS * BLOCK), BF16),
             pltpu.VMEM((extended, 2 * features), F32),
             pltpu.VMEM((features, 4 * features), F32),
+            pltpu.VMEM((grad_rows, LANES), BF16),
         ],
         compiler_params=params,
         name="space_backward",
     )(
         block_lists,
-        returned,
-        returned,
+        place,
+        *returned,
         act,
         keys_values,
         queries,
@@ -533,36 +596,73 @@
         combine_weights,
     )
 
+    other = exchange(sent, "space", 1)
     edge_left = shift(to_right, "space", 1)
     edge_right = shift(to_left, "space", -1)
-    space_sum = sum_scattered(sum_scattered(space_grads, "tm"), "space")
-    space_sum = gathered(gathered(space_sum, "space"), "tm")
+    vmem_spec = pl.BlockSpec(memory_space=pltpu.VMEM)
+    piece_rows = grad_rows // 2 // time_count
+    piece_shape = jax.ShapeDtypeStruct((piece_rows, LANES), BF16)
+    pieces = pl.pallas_call(
+        split_kernel,
+        in_specs=[lists_spec, vmem_spec, vmem_spec],
+        out_specs=[vmem_spec] * time_count,
+        out_shape=[piece_shape] * time_count,
+        scratch_shapes=[pltpu.VMEM((grad_rows // 2, LANES), BF16)],
+        compiler_params=params,
+        name="add_cores",
+    )(place, kept, other)
+
+    def summed(pieces, axis, group, name):
+        def body(*refs):
+            sum_kernel(axis, group, *refs)
+
+        return pl.pallas_call(
+            body,
+            in_specs=[lists_spec, *[vmem_spec] * len(pieces)],
+            out_specs=vmem_spec,
+            out_shape=piece_shape,
+            scratch_shapes=[pltpu.VMEM((len(pieces), piece_rows, LANES), BF16)],
+            compiler_params=params,
+            name=name,
+        )(place, *pieces)
+
+    pieces = [pieces[0]] + [exchange(pieces[d], "tm", d) for d in range(1, time_count)]
+    piece = summed(pieces, 0, 1, "add_tm")
+    pieces = [piece] + [exchange(piece, "space", d) for d in range(2, lax.axis_size("space"), 2)]
+    piece = summed(pieces, 1, 2, "add_space")
+    pieces = [piece] + [exchange(piece, "tm", d) for d in range(1, time_count)]
+    own_half = pl.pallas_call(
+        join_kernel,
+        in_specs=[lists_spec, *[vmem_spec] * time_count],
+        out_specs=vmem_spec,
+        out_shape=half_shape,
+        compiler_params=params,
+        name="join_tm",
+    )(place, *pieces)
+    other_half = exchange(own_half, "space", 1)
 
     field_grad = pl.pallas_call(
         field_kernel,
         grid=(frame_count,),
-        in_specs=[
-            framed(row_count, features),
-            parted(1),
-            framed(row_count, features),
-            framed(row_count, features),
-            framed(row_count, features),
-        ],
+        in_specs=[framed(row_count, features)] * 5,
         out_specs=framed(row_count, features),
         out_shape=jax.ShapeDtypeStruct((frame_count, row_count, features), BF16),
         compiler_params=params,
         name="field_grad",
-    )(wave_field, returned, dact, edge_left, edge_right)
+    )(wave_field, mixed_grad, dact, edge_left, edge_right)
 
     project_grad, combine_grad = pl.pallas_call(
         grads_kernel,
+        in_specs=[lists_spec, vmem_spec, vmem_spec, vmem_spec],
+        out_specs=[vmem_spec, vmem_spec],
         out_shape=[
             jax.ShapeDtypeStruct((2, features, 3 * features), F32),
             jax.ShapeDtypeStruct((2, features, features), F32),
         ],
+        scratch_shapes=[pltpu.VMEM((grad_rows, LANES), BF16)],
         compiler_params=params,
         name="weight_grads",
-    )(space_sum, time_sum)
+    )(place, own_half, other_half, time_sum)
     return (mixed_field, field_grad, project_grad, combine_grad)
 
 

time: 258 us -> 171 us (0.66)
  waiting for transfers between devices: 135 us -> 80.9 us
  blocking collectives: 40.8 us -> 0 us
  starting transfers between devices: 20.2 us -> 28.8 us
  Pallas kernels: 34.8 us -> 38 us
    psum x1 -> x2, waiting for transfers between devices: 127 us -> 56.9 us  [per_device(): time_sum = lax.psum(lax.psum(time_grads, 'tm'), 'space')]
    all_to_all x4 -> x0, blocking collectives: 40.8 us -> none  [swap(): return lax.all_to_all(parts, axis, split_axis=0, concat_axis=0, tiled=True)]
    ppermute x0 -> x17, waiting for transfers between devices: none -> 22.3 us  [exchange(): lax.ppermute(cells, axis, [(i, i ^ distance) for i in range(lax.axis_size...]
    ppermute x0 -> x17, starting transfers between devices: none -> 21.6 us  [exchange(): lax.ppermute(cells, axis, [(i, i ^ distance) for i in range(lax.axis_size...]
    all_to_all x3 -> x0, starting transfers between devices: 12.9 us -> none  [the longest x2 7.65 us: swap(): return lax.all_to_all(parts, axis, split_axis=0, concat_axis=0, tiled=True)]
    all_to_all x3 -> x0, waiting for transfers between devices: 5.54 us -> none  [the longest x2 5.54 us: swap(): return lax.all_to_all(parts, axis, split_axis=0, concat_axis=0, tiled=True)]
    pallas_call x2 -> x6, Pallas kernels: 10.6 us -> 13.7 us  [the longest x1 9.19 us: per_device(): pl.pallas_call(time_body, grid=(1,), in_specs=[*[whole_part] * time_count...]
    unnamed x37 -> x30, local copies, waits for them, and re-layouts: 9.36 us -> 9.15 us
  transfers between devices with their start and end apart: 8 -> 23, of which waited for: 3 -> 16; matrix products, arithmetic and copies ran while one was open for 1% -> 0% of each run, Pallas kernels for 5% -> 9%
where the time goes in v1:
time: 171 us
  waiting for transfers between devices  80.9 us (47%)
  Pallas kernels  38 us (22%)
  starting transfers between devices  28.8 us (17%)
  between operations  14.2 us (8%)
  local copies, waits for them, and re-layouts  9.15 us (5%)
    psum x2, waiting for transfers between devices, per_device(): time_sum = lax.psum(lax.psum(time_grads, 'tm'), 'space')  56.9 us
    ppermute x17, waiting for transfers between devices, exchange(): lax.ppermute(cells, axis, [(i, i ^ distance) for i in range(lax.axis_size...  22.3 us
    ppermute x17, starting transfers between devices, exchange(): lax.ppermute(cells, axis, [(i, i ^ distance) for i in range(lax.axis_size...  21.6 us
    pallas_call x1, Pallas kernels, per_device(): pl.pallas_call(backward_body, grid=(frame_count,), in_specs=[lists_spec,...  12 us
    pallas_call x1, Pallas kernels, per_device(): pl.pallas_call(space_forward_kernel, grid=(frame_count,), in_specs=[lists...  11 us
    pallas_call x1, Pallas kernels, per_device(): pl.pallas_call(time_body, grid=(1,), in_specs=[*[whole_part] * time_count...  9.19 us
    unnamed x30, local copies, waits for them, and re-layouts  9.15 us
    ppermute x4, starting transfers between devices, shift(): return lax.ppermute(cells, axis, moves)  6.93 us
  transfers between devices with their start and end apart: 23, of which 16 were waited for; matrix products, arithmetic and copies ran while one was open for 0% of the time, Pallas kernels for 9%

profile of v1, /device:TPU:0, one launch (start us, length us, event | category | flops | bytes accessed | tf_op | source)
XLA Modules:
  0.0 171.0 jit_solution(11291500894464423735)
XLA Ops:
  7.2 1.3 collective-permute-start.1
  8.5 3.1 %collective-permute-start = (bf16[2,256,256]{2,1,0:T(8,128)(2,1)}, bf16[2,256,256]{2,1,0:T(8,128)(2,1)S(1)}, u32[]{:S(2)}, u32[]{:S(2)}) collective-permute-start(bf16[2,256,256]{2,1,0:T(8,128)(2,1)} %wave_ref.3), channel_id=1, source_target_pairs={{0,1},{1,2},{2,3},{3,4},{4,5},{5,6},{6,7},{8,9},{9,10},{10,11},{11... | collective-permute-start | bytes 786440 | tf_op jit(solution)/shard_map/ppermute | solution.py:419
  17.6 11.0 %space_forward.1 = (bf16[2,768,256]{2,1,0:T(8,128)(2,1)S(1)}, bf16[2,768,512]{2,1,0:T(8,128)(2,1)S(1)}, bf16[2,256,256]{2,1,0:T(8,128)(2,1)S(1)}, bf16[2,2,512,1...) custom-call(s32[2,2,4]{2,1,0:T(2,128)S(1)} %copy-done.13, ...), custom_call_target="tpu_custom_call" | custom-call | tf_op jit(solution)/shard_map/space_forward/pallas_call | solution.py:457
  29.7 2.9 %collective-permute-start.2 = (bf16[2,64,512]{2,1,0:T(8,128)(2,1)S(1)}, bf16[2,64,512]{2,1,0:T(8,128)(2,1)S(1)}, u32[]{:S(2)}, u32[]{:S(2)}) collective-permute-start(bf16[2,64,512]{2,1,0:T(8,128)(2,1)S(1)} %get-tuple-element.33), channel_id=1, source_target_pairs={{0,8},{8,0},{16,24},{24,16},{1,9},{9,1},{17,25},{25,17},{2,10},{10... | collective-permute-start | bytes 393224 | tf_op jit(solution)/shard_map/ppermute | solution.py:423
  32.7 1.5 collective-permute-start.3
  34.2 1.4 collective-permute-done.2.refs_1_
  35.6 2.0 %collective-permute-done.3.refs_2_ = bf16[2,64,512]{2,1,0:T(8,128)(2,1)S(1)} collective-permute-done((bf16[2,64,512]{2,1,0:T(8,128)(2,1)S(1)}, bf16[2,64,512]{2,1,0:T(8,128)(2,1)S(1)}, u32[]{:S(2)}, u32[]{:S(2)}) %collective-permute-start.3) | collective-permute-done | bytes 131104 | tf_op jit(solution)/shard_map/ppermute | solution.py:423
  37.7 3.8 %collective-permute-done.4.refs_3_ = bf16[2,64,512]{2,1,0:T(8,128)(2,1)S(1)} collective-permute-done((bf16[2,64,512]{2,1,0:T(8,128)(2,1)S(1)}, bf16[2,64,512]{2,1,0:T(8,128)(2,1)S(1)}, u32[]{:S(2)}, u32[]{:S(2)}) %collective-permute-start.4) | collective-permute-done | bytes 131104 | tf_op jit(solution)/shard_map/ppermute | solution.py:423
  41.5 9.2 %time_pair.1 = (bf16[2,64,512]{2,1,0:T(8,128)(2,1)S(1)}, bf16[2,64,512]{2,1,0:T(8,128)(2,1)S(1)}, bf16[2,64,512]{2,1,0:T(8,128)(2,1)S(1)}, bf16[2,64,512]{2,1,0:T(8,128)(2,1)S(1)}, bf16[256,1024]{1,0:T(8,128)(2,1)}) custom-call(bf16[2,64,512]{2,1,0:T(8,128)(2,1)S(1)} %get-tuple-element.32.refs_0_, bf16[2,64,512]{2,1,0:T(8,128)(2,1)S(1)} %collective-permute-done.2.refs_1_, ...), custom_call_target="tpu_custom_call" | custom-call | tf_op jit(solution)/shard_map/time_pair/pallas_call | solution.py:511
  51.2 2.9 %collective-permute-start.7 = (bf16[2,64,512]{2,1,0:T(8,128)(2,1)S(1)}, bf16[2,64,512]{2,1,0:T(8,128)(2,1)S(1)}, u32[]{:S(2)}, u32[]{:S(2)}) collective-permute-start(bf16[2,64,512]{2,1,0:T(8,128)(2,1)S(1)} %get-tuple-element.39), channel_id=1, source_target_pairs={{0,24},{8,16},{16,8},{24,0},{1,25},{9,17},{17,9},{25,1},{2,26},{10... | collective-permute-start | bytes 393224 | tf_op jit(solution)/shard_map/ppermute | solution.py:423
  54.4 2.5 %collective-permute-done.5.refs_3_ = bf16[2,64,512]{2,1,0:T(8,128)(2,1)S(1)} collective-permute-done((bf16[2,64,512]{2,1,0:T(8,128)(2,1)S(1)}, bf16[2,64,512]{2,1,0:T(8,128)(2,1)S(1)}, u32[]{:S(2)}, u32[]{:S(2)}) %collective-permute-start.5) | collective-permute-done | bytes 131104 | tf_op jit(solution)/shard_map/ppermute | solution.py:423
  57.3 2.1 %collective-permute-done.7.refs_5_ = bf16[2,64,512]{2,1,0:T(8,128)(2,1)S(1)} collective-permute-done((bf16[2,64,512]{2,1,0:T(8,128)(2,1)S(1)}, bf16[2,64,512]{2,1,0:T(8,128)(2,1)S(1)}, u32[]{:S(2)}, u32[]{:S(2)}) %collective-permute-start.7) | collective-permute-done | bytes 131104 | tf_op jit(solution)/shard_map/ppermute | solution.py:423
  61.7 12.0 %space_backward.1 = (bf16[2,256,256]{2,1,0:T(8,128)(2,1)}, bf16[2,256,256]{2,1,0:T(8,128)(2,1)S(1)}, f32[2,256,256]{2,1,0:T(8,128)S(1)}, bf16[2,256,256]{2,1,0:T...) custom-call(s32[2,2,4]{2,1,0:T(2,128)S(1)} %copy-done.14, ...), custom_call_target="tpu_custom_call" | custom-call | tf_op jit(solution)/shard_map/space_backward/pallas_call | solution.py:542
  76.0 2.3 %collective-permute-start.11 = (bf16[256,128]{1,0:T(8,128)(2,1)S(1)}, bf16[256,128]{1,0:T(8,128)(2,1)S(1)}, u32[]{:S(2)}, u32[]{:S(2)}) collective-permute-start(bf16[256,128]{1,0:T(8,128)(2,1)S(1)} %get-tuple-element.54), channel_id=1, source_target_pairs={{0,8},{8,0},{16,24},{24,16},{1,9},{9,1},{17,25},{25,17},{2,10},{10... | collective-permute-start | bytes 196616 | tf_op jit(solution)/shard_map/ppermute | solution.py:423
  80.7 2.6 %collective-permute-done.12.refs_3_ = bf16[256,128]{1,0:T(8,128)(2,1)S(1)} collective-permute-done((bf16[256,128]{1,0:T(8,128)(2,1)S(1)}, bf16[256,128]{1,0:T(8,128)(2,1)S(1)}, u32[]{:S(2)}, u32[]{:S(2)}) %collective-permute-start.12) | collective-permute-done | bytes 65568 | tf_op jit(solution)/shard_map/ppermute | solution.py:423
  84.6 4.8 %collective-permute-start.16 = (bf16[256,128]{1,0:T(8,128)(2,1)S(1)}, bf16[256,128]{1,0:T(8,128)(2,1)S(1)}, u32[]{:S(2)}, u32[]{:S(2)}) collective-permute-start(bf16[256,128]{1,0:T(8,128)(2,1)S(1)} %add_tm.1.refs_1_), channel_id=1, source_target_pairs={{0,6},{1,7},{2,4},{3,5},{4,2},{5,3},{6,0},{7,1},{8,14},{9,15},{10,... | collective-permute-start | bytes 196616 | tf_op jit(solution)/shard_map/ppermute | solution.py:423
  90.1 2.0 %collective-permute-done.16.refs_4_ = bf16[256,128]{1,0:T(8,128)(2,1)S(1)} collective-permute-done((bf16[256,128]{1,0:T(8,128)(2,1)S(1)}, bf16[256,128]{1,0:T(8,128)(2,1)S(1)}, u32[]{:S(2)}, u32[]{:S(2)}) %collective-permute-start.16) | collective-permute-done | bytes 65568 | tf_op jit(solution)/shard_map/ppermute | solution.py:423
  92.1 2.7 %collective-permute-done.15.refs_3_ = bf16[256,128]{1,0:T(8,128)(2,1)S(1)} collective-permute-done((bf16[256,128]{1,0:T(8,128)(2,1)S(1)}, bf16[256,128]{1,0:T(8,128)(2,1)S(1)}, u32[]{:S(2)}, u32[]{:S(2)}) %collective-permute-start.15) | collective-permute-done | bytes 65568 | tf_op jit(solution)/shard_map/ppermute | solution.py:423
  97.6 1.4 collective-permute-start.17
  98.9 1.3 collective-permute-start.8
  100.2 1.3 collective-permute-start.9
  101.5 1.5 all-reduce.3.cloned.1.call-done
  105.7 55.3 %all-reduce.5.cloned.1.call-done.time_ref = bf16[256,1024]{1,0:T(8,128)(2,1)} async-done(((bf16[256,1024]{1,0:T(8,128)(2,1)}), bf16[256,1024]{1,0:T(8,128)(2,1)}) %all-reduce.5.cloned.1.call-update) | async-done | bytes 524304 | tf_op jit(solution)/shard_map/psum | solution.py:535
  162.1 2.0 %weight_grads.1 = (f32[2,256,768]{2,1,0:T(8,128)}, f32[2,256,256]{2,1,0:T(8,128)}) custom-call(s32[2]{0:T(128)S(1)} %pad_add_fusion.place_ref.refs_1_.refs_0_, bf16[1024,128]{1,0:T(8,128)(2,1)S(1)} %join_tm.1.own_ref, bf16[1024,128]{1,0:T(8,128)(2,1)S(1)} %collective-permute-done.20.other_ref, bf16[256,1024]{1,0:T(8,128)(2,1)S(1)} %copy-done.7), custom_call_target="tpu_custom_call" | custom-call | tf_op jit(solution)/shard_map/weight_grads/pallas_call | solution.py:654
  (64 shorter events, 23.8 us)
Async XLA Ops:
  7.2 95.9 %all-reduce.3.cloned.1.call-start = ((), (), s32[]{:S(2)}) async-start(), calls=%async_computation | async-start | bytes 1048576 | tf_op jit(solution)/shard_map/psum | solution.py:535
  7.2 4.4 %collective-permute-start.1 = (bf16[2,256,256]{2,1,0:T(8,128)(2,1)}, bf16[2,256,256]{2,1,0:T(8,128)(2,1)S(1)}, u32[]{:S(2)}, u32[]{:S(2)}) collective-permute-start(bf16[2,256,256]{2,1,0:T(8,128)(2,1)} %wave_ref.3), channel_id=1, source_target_pairs={{1,0},{2,1},{3,2},{4,3},{5,4},{6,5},{7,6},{9,8},{10,9},{11,10},{12... | collective-permute-start | bytes 786440 | tf_op jit(solution)/shard_map/ppermute | solution.py:419
  8.5 4.4 %collective-permute-start = (bf16[2,256,256]{2,1,0:T(8,128)(2,1)}, bf16[2,256,256]{2,1,0:T(8,128)(2,1)S(1)}, u32[]{:S(2)}, u32[]{:S(2)}) collective-permute-start(bf16[2,256,256]{2,1,0:T(8,128)(2,1)} %wave_ref.3), channel_id=1, source_target_pairs={{0,1},{1,2},{2,3},{3,4},{4,5},{5,6},{6,7},{8,9},{9,10},{10,11},{11... | collective-permute-start | bytes 786440 | tf_op jit(solution)/shard_map/ppermute | solution.py:419
  29.7 5.9 %collective-permute-start.2 = (bf16[2,64,512]{2,1,0:T(8,128)(2,1)S(1)}, bf16[2,64,512]{2,1,0:T(8,128)(2,1)S(1)}, u32[]{:S(2)}, u32[]{:S(2)}) collective-permute-start(bf16[2,64,512]{2,1,0:T(8,128)(2,1)S(1)} %get-tuple-element.33), channel_id=1, source_target_pairs={{0,8},{8,0},{16,24},{24,16},{1,9},{9,1},{17,25},{25,17},{2,10},{10... | collective-permute-start | bytes 393224 | tf_op jit(solution)/shard_map/ppermute | solution.py:423
  32.7 5.0 %collective-permute-start.3 = (bf16[2,64,512]{2,1,0:T(8,128)(2,1)S(1)}, bf16[2,64,512]{2,1,0:T(8,128)(2,1)S(1)}, u32[]{:S(2)}, u32[]{:S(2)}) collective-permute-start(bf16[2,64,512]{2,1,0:T(8,128)(2,1)S(1)} %get-tuple-element.34), channel_id=1, source_target_pairs={{0,16},{8,24},{16,0},{24,8},{1,17},{9,25},{17,1},{25,9},{2,18},{10... | collective-permute-start | bytes 393224 | tf_op jit(solution)/shard_map/ppermute | solution.py:423
  34.2 7.2 %collective-permute-start.4 = (bf16[2,64,512]{2,1,0:T(8,128)(2,1)S(1)}, bf16[2,64,512]{2,1,0:T(8,128)(2,1)S(1)}, u32[]{:S(2)}, u32[]{:S(2)}) collective-permute-start(bf16[2,64,512]{2,1,0:T(8,128)(2,1)S(1)} %get-tuple-element.35), channel_id=1, source_target_pairs={{0,24},{8,16},{16,8},{24,0},{1,25},{9,17},{17,9},{25,1},{2,26},{10... | collective-permute-start | bytes 393224 | tf_op jit(solution)/shard_map/ppermute | solution.py:423
  50.7 6.3 %collective-permute-start.5 = (bf16[2,64,512]{2,1,0:T(8,128)(2,1)S(1)}, bf16[2,64,512]{2,1,0:T(8,128)(2,1)S(1)}, u32[]{:S(2)}, u32[]{:S(2)}) collective-permute-start(bf16[2,64,512]{2,1,0:T(8,128)(2,1)S(1)} %get-tuple-element.37), channel_id=1, source_target_pairs={{0,8},{8,0},{16,24},{24,16},{1,9},{9,1},{17,25},{25,17},{2,10},{10... | collective-permute-start | bytes 393224 | tf_op jit(solution)/shard_map/ppermute | solution.py:423
  50.8 6.5 %collective-permute-start.6 = (bf16[2,64,512]{2,1,0:T(8,128)(2,1)S(1)}, bf16[2,64,512]{2,1,0:T(8,128)(2,1)S(1)}, u32[]{:S(2)}, u32[]{:S(2)}) collective-permute-start(bf16[2,64,512]{2,1,0:T(8,128)(2,1)S(1)} %get-tuple-element.38), channel_id=1, source_target_pairs={{0,16},{8,24},{16,0},{24,8},{1,17},{9,25},{17,1},{25,9},{2,18},{10... | collective-permute-start | bytes 393224 | tf_op jit(solution)/shard_map/ppermute | solution.py:423
  51.2 8.2 %collective-permute-start.7 = (bf16[2,64,512]{2,1,0:T(8,128)(2,1)S(1)}, bf16[2,64,512]{2,1,0:T(8,128)(2,1)S(1)}, u32[]{:S(2)}, u32[]{:S(2)}) collective-permute-start(bf16[2,64,512]{2,1,0:T(8,128)(2,1)S(1)} %get-tuple-element.39), channel_id=1, source_target_pairs={{0,24},{8,16},{16,8},{24,0},{1,25},{9,17},{17,9},{25,1},{2,26},{10... | collective-permute-start | bytes 393224 | tf_op jit(solution)/shard_map/ppermute | solution.py:423
  54.2 106.9 %all-reduce.5.cloned.1.call-start = ((), (), s32[]{:S(2)}) async-start(), calls=%async_computation.1 | async-start | bytes 1048576 | tf_op jit(solution)/shard_map/psum | solution.py:535
  73.7 30.8 %copy-start.6 = (bf16[2,256,256]{2,1,0:T(8,128)(2,1)S(1)}, bf16[2,256,256]{2,1,0:T(8,128)(2,1)}, u32[]{:S(2)}) copy-start(bf16[2,256,256]{2,1,0:T(8,128)(2,1)} %wave_ref.3) | copy-start | bytes 786436
  73.7 1.6 collective-permute-start.10
  76.0 4.7 %collective-permute-start.11 = (bf16[256,128]{1,0:T(8,128)(2,1)S(1)}, bf16[256,128]{1,0:T(8,128)(2,1)S(1)}, u32[]{:S(2)}, u32[]{:S(2)}) collective-permute-start(bf16[256,128]{1,0:T(8,128)(2,1)S(1)} %get-tuple-element.54), channel_id=1, source_target_pairs={{0,8},{8,0},{16,24},{24,16},{1,9},{9,1},{17,25},{25,17},{2,10},{10... | collective-permute-start | bytes 196616 | tf_op jit(solution)/shard_map/ppermute | solution.py:423
  78.3 5.0 %collective-permute-start.12 = (bf16[256,128]{1,0:T(8,128)(2,1)S(1)}, bf16[256,128]{1,0:T(8,128)(2,1)S(1)}, u32[]{:S(2)}, u32[]{:S(2)}) collective-permute-start(bf16[256,128]{1,0:T(8,128)(2,1)S(1)} %get-tuple-element.55), channel_id=1, source_target_pairs={{0,16},{8,24},{16,0},{24,8},{1,17},{9,25},{17,1},{25,9},{2,18},{10... | collective-permute-start | bytes 196616 | tf_op jit(solution)/shard_map/ppermute | solution.py:423
  78.9 5.2 %collective-permute-start.13 = (bf16[256,128]{1,0:T(8,128)(2,1)S(1)}, bf16[256,128]{1,0:T(8,128)(2,1)S(1)}, u32[]{:S(2)}, u32[]{:S(2)}) collective-permute-start(bf16[256,128]{1,0:T(8,128)(2,1)S(1)} %get-tuple-element.56), channel_id=1, source_target_pairs={{0,24},{8,16},{16,8},{24,0},{1,25},{9,17},{17,9},{25,1},{2,26},{10... | collective-permute-start | bytes 196616 | tf_op jit(solution)/shard_map/ppermute | solution.py:423
  84.6 7.4 %collective-permute-start.16 = (bf16[256,128]{1,0:T(8,128)(2,1)S(1)}, bf16[256,128]{1,0:T(8,128)(2,1)S(1)}, u32[]{:S(2)}, u32[]{:S(2)}) collective-permute-start(bf16[256,128]{1,0:T(8,128)(2,1)S(1)} %add_tm.1.refs_1_), channel_id=1, source_target_pairs={{0,6},{1,7},{2,4},{3,5},{4,2},{5,3},{6,0},{7,1},{8,14},{9,15},{10,... | collective-permute-start | bytes 196616 | tf_op jit(solution)/shard_map/ppermute | solution.py:423
  89.4 5.3 %collective-permute-start.15 = (bf16[256,128]{1,0:T(8,128)(2,1)S(1)}, bf16[256,128]{1,0:T(8,128)(2,1)S(1)}, u32[]{:S(2)}, u32[]{:S(2)}) collective-permute-start(bf16[256,128]{1,0:T(8,128)(2,1)S(1)} %add_tm.1.refs_1_), channel_id=1, source_target_pairs={{0,4},{1,5},{2,6},{3,7},{4,0},{5,1},{6,2},{7,3},{8,12},{9,13},{10,... | collective-permute-start | bytes 196616 | tf_op jit(solution)/shard_map/ppermute | solution.py:423
  89.4 5.3 %collective-permute-start.14 = (bf16[256,128]{1,0:T(8,128)(2,1)S(1)}, bf16[256,128]{1,0:T(8,128)(2,1)S(1)}, u32[]{:S(2)}, u32[]{:S(2)}) collective-permute-start(bf16[256,128]{1,0:T(8,128)(2,1)S(1)} %add_tm.1.refs_1_), channel_id=1, source_target_pairs={{0,2},{1,3},{2,0},{3,1},{4,6},{5,7},{6,4},{7,5},{8,10},{9,11},{10,... | collective-permute-start | bytes 196616 | tf_op jit(solution)/shard_map/ppermute | solution.py:423
  95.4 7.7 %collective-permute-start.19 = (bf16[256,128]{1,0:T(8,128)(2,1)S(1)}, bf16[256,128]{1,0:T(8,128)(2,1)S(1)}, u32[]{:S(2)}, u32[]{:S(2)}) collective-permute-start(bf16[256,128]{1,0:T(8,128)(2,1)S(1)} %add_space.1.refs_0_), channel_id=1, source_target_pairs={{0,24},{8,16},{16,8},{24,0},{1,25},{9,17},{17,9},{25,1},{2,26},{10... | collective-permute-start | bytes 196616 | tf_op jit(solution)/shard_map/ppermute | solution.py:423
  96.3 6.7 %collective-permute-start.18 = (bf16[256,128]{1,0:T(8,128)(2,1)S(1)}, bf16[256,128]{1,0:T(8,128)(2,1)S(1)}, u32[]{:S(2)}, u32[]{:S(2)}) collective-permute-start(bf16[256,128]{1,0:T(8,128)(2,1)S(1)} %add_space.1.refs_0_), channel_id=1, source_target_pairs={{0,16},{8,24},{16,0},{24,8},{1,17},{9,25},{17,1},{25,9},{2,18},{10... | collective-permute-start | bytes 196616 | tf_op jit(solution)/shard_map/ppermute | solution.py:423
  97.6 5.5 %collective-permute-start.17 = (bf16[256,128]{1,0:T(8,128)(2,1)S(1)}, bf16[256,128]{1,0:T(8,128)(2,1)S(1)}, u32[]{:S(2)}, u32[]{:S(2)}) collective-permute-start(bf16[256,128]{1,0:T(8,128)(2,1)S(1)} %add_space.1.refs_0_), channel_id=1, source_target_pairs={{0,8},{8,0},{16,24},{24,16},{1,9},{9,1},{17,25},{25,17},{2,10},{10... | collective-permute-start | bytes 196616 | tf_op jit(solution)/shard_map/ppermute | solution.py:423
  98.9 5.1 %collective-permute-start.8 = (bf16[2,256,256]{2,1,0:T(8,128)(2,1)}, bf16[2,256,256]{2,1,0:T(8,128)(2,1)S(1)}, u32[]{:S(2)}, u32[]{:S(2)}) collective-permute-start(bf16[2,256,256]{2,1,0:T(8,128)(2,1)} %get-tuple-element.49), channel_id=1, source_target_pairs={{0,1},{1,2},{2,3},{3,4},{4,5},{5,6},{6,7},{8,9},{9,10},{10,11},{11... | collective-permute-start | bytes 786440 | tf_op jit(solution)/shard_map/ppermute | solution.py:419
  100.2 4.2 %collective-permute-start.9 = (bf16[2,256,256]{2,1,0:T(8,128)(2,1)}, bf16[2,256,256]{2,1,0:T(8,128)(2,1)S(1)}, u32[]{:S(2)}, u32[]{:S(2)}) collective-permute-start(bf16[2,256,256]{2,1,0:T(8,128)(2,1)} %get-tuple-element.50), channel_id=1, source_target_pairs={{1,0},{2,1},{3,2},{4,3},{5,4},{6,5},{7,6},{9,8},{10,9},{11,10},{12... | collective-permute-start | bytes 786440 | tf_op jit(solution)/shard_map/ppermute | solution.py:419
  103.7 57.4 %collective-permute-start.20 = (bf16[1024,128]{1,0:T(8,128)(2,1)S(1)}, bf16[1024,128]{1,0:T(8,128)(2,1)S(1)}, u32[]{:S(2)}, u32[]{:S(2)}) collective-permute-start(bf16[1024,128]{1,0:T(8,128)(2,1)S(1)} %join_tm.1.own_ref), channel_id=1, source_target_pairs={{0,1},{1,0},{2,3},{3,2},{4,5},{5,4},{6,7},{7,6},{8,9},{9,8},{10,11... | collective-permute-start | bytes 786440 | tf_op jit(solution)/shard_map/ppermute | solution.py:423
  (14 other events, 108.7 us)
Sparse Core Ops, SparseCore 0:
  54.3 48.7 all-reduce.2
  105.4 55.6 all-reduce.4

commit v2 on v1

--- a/solution.py
+++ b/solution.py
@@ -12,7 +12,7 @@
 HREACH = 2
 LANES = 128
 GROUP_ROWS = 16
-VMEM_BYTES = 48 * 1024 * 1024
+VMEM_BYTES = 24 * 1024 * 1024
 BF16 = jnp.bfloat16
 F32 = jnp.float32
 
@@ -173,12 +173,14 @@
     scale,
     factor,
     count_in,
+    place_ref,
     *refs,
 ):
     arrived_refs = refs[:count_in]
     project_ref, combine_ref = refs[count_in : count_in + 2]
-    returned_refs = refs[count_in + 2 : 2 * count_in + 2]
-    grads_ref, proj_s, dattn_s, attended_s, dproj_s = refs[2 * count_in + 2 :]
+    grad_refs = refs[count_in + 2 : 2 * count_in + 2]
+    mixed_refs = refs[2 * count_in + 2 : 3 * count_in + 2]
+    kept_ref, sent_ref, proj_s, dattn_s, attended_s, dproj_s, rounded_s = refs[3 * count_in + 2 :]
     part_frames, row_count, features = arrived_refs[0].shape
     features //= 2
     frames = part_frames * count_in
@@ -236,12 +238,12 @@
     dproj = dproj_s[...].reshape(tokens, 3 * features)
     dact = dot_nt(dproj, project_ref[0])
     mixed_grad = (cot.astype(F32) + norm_backward(dact, normed, inverse)).astype(BF16)
-    for part, ref in enumerate(returned_refs):
+    for part, (grad_ref, mixed_ref) in enumerate(zip(grad_refs, mixed_refs)):
         span = slice(part * part_tokens, (part + 1) * part_tokens)
-        ref[:, :, :features] = mixed[span].reshape(part_frames, row_count, features)
-        ref[:, :, features:] = mixed_grad[span].reshape(part_frames, row_count, features)
-    grads_ref[:, : 3 * features] = (dot_tn(act, dproj) * factor).astype(BF16)
-    grads_ref[:, 3 * features :] = (dot_tn(attended, cot) * factor).astype(BF16)
+        mixed_ref[...] = mixed[span].reshape(part_frames, row_count, features)
+        grad_ref[...] = mixed_grad[span].reshape(part_frames, row_count, features)
+    grads = jnp.concatenate([dot_tn(act, dproj), dot_tn(attended, cot)], axis=1) * factor
+    halve_grads(grads, place_ref[1] % 2, rounded_s, kept_ref, sent_ref)
 
 
 def space_backward_kernel(
@@ -262,7 +264,6 @@
         attended_ref,
         project_ref,
         combine_ref,
-        mixed_out_ref,
         mixed_grad_ref,
         dact_ref,
         to_left_ref,
@@ -278,15 +279,14 @@
     frame = pl.program_id(0)
     me = place_ref[0]
     core = place_ref[1] % 2
-    row_count, features = mixed_out_ref.shape[1:]
+    row_count, features = mixed_grad_ref.shape[1:]
     width = features // HEADS
     block_count = row_count // BLOCK
     rim = HREACH * BLOCK
     for distance, ref in enumerate(returned_refs):
         sent_rows = ref.shape[1]
         span = pl.ds(pl.multiple_of((me ^ distance) * sent_rows, GROUP_ROWS), sent_rows)
-        mixed_out_ref[0, span] = ref[0, :, :features]
-        mixed_grad_ref[0, span] = ref[0, :, features:]
+        mixed_grad_ref[0, span] = ref[0]
     mixed_grad = mixed_grad_ref[0]
     for place in range(block_count + 2 * HREACH):
         keys_t[place] = flip(kv_ref[0, place * BLOCK : (place + 1) * BLOCK, :features])
@@ -349,21 +349,20 @@
 
     @pl.when(frame == pl.num_programs(0) - 1)
     def _():
-        for group in range(4 * features // LANES):
-            rounded_s[group * features : (group + 1) * features] = (
-                grads_s[:, group * LANES : (group + 1) * LANES] * factor
-            ).astype(BF16)
-        half = kept_ref.shape[0]
-        kept_ref[...] = rounded_s[pl.ds(pl.multiple_of(core * half, GROUP_ROWS), half)]
-        sent_ref[...] = rounded_s[pl.ds(pl.multiple_of((1 - core) * half, GROUP_ROWS), half)]
-
-
-def field_kernel(wave_ref, mixed_grad_ref, dact_ref, from_left_ref, from_right_ref, field_ref):
+        halve_grads(grads_s[...] * factor, core, rounded_s, kept_ref, sent_ref)
+
+
+def field_kernel(place_ref, wave_ref, mixed_grad_ref, dact_ref, from_left_ref, from_right_ref, *refs):
+    *mixed_refs, field_ref, mixed_ref = refs
     normed, inverse = layer_norm(wave_ref[0])
     dact = dact_ref[0] + from_left_ref[0].astype(F32) + from_right_ref[0].astype(F32)
     field_ref[0] = (
         mixed_grad_ref[0].astype(F32) + norm_backward(dact, normed, inverse)
     ).astype(BF16)
+    for distance, ref in enumerate(mixed_refs):
+        rows = ref.shape[1]
+        span = pl.ds(pl.multiple_of((place_ref[0] ^ distance) * rows, GROUP_ROWS), rows)
+        mixed_ref[0, span] = ref[0]
 
 
 def split_kernel(place_ref, kept_ref, arrived_ref, *refs):
@@ -393,21 +392,37 @@
         joined_ref[span] = ref[...]
 
 
-def grads_kernel(place_ref, own_ref, other_ref, time_ref, project_ref, combine_ref, space_s):
+def grads_kernel(place_ref, *refs):
+    *half_refs, project_ref, combine_ref, joined_s = refs
     features = combine_ref.shape[1]
     core = place_ref[1] % 2
-    half = own_ref.shape[0]
-    space_s[pl.ds(pl.multiple_of(core * half, GROUP_ROWS), half)] = own_ref[...]
-    space_s[pl.ds(pl.multiple_of((1 - core) * half, GROUP_ROWS), half)] = other_ref[...]
-    for group in range(4 * features // LANES):
-        piece = space_s[group * features : (group + 1) * features].astype(F32)
-        start = group * LANES
-        if start < 3 * features:
-            project_ref[0, :, start : start + LANES] = piece
-        else:
-            combine_ref[0, :, start - 3 * features : start - 3 * features + LANES] = piece
-    project_ref[1] = time_ref[:, : 3 * features].astype(F32)
-    combine_ref[1] = time_ref[:, 3 * features :].astype(F32)
+    half = half_refs[0].shape[0]
+    for layer in range(2):
+        own_ref, other_ref = half_refs[2 * layer : 2 * layer + 2]
+        joined_s[pl.ds(pl.multiple_of(core * half, GROUP_ROWS), half)] = own_ref[...]
+        joined_s[pl.ds(pl.multiple_of((1 - core) * half, GROUP_ROWS), half)] = other_ref[...]
+        for group in range(4 * features // LANES):
+            piece = joined_s[group * features : (group + 1) * features].astype(F32)
+            start = group * LANES
+            if start < 3 * features:
+                project_ref[layer, :, start : start + LANES] = piece
+            else:
+                combine_ref[layer, :, start - 3 * features : start - 3 * features + LANES] = piece
+
+
+def halve_grads(grads, core, rounded_s, kept_ref, sent_ref):
+    features = grads.shape[0]
+    for group in range(grads.shape[1] // LANES):
+        rounded_s[group * features : (group + 1) * features] = grads[
+            :, group * LANES : (group + 1) * LANES
+        ].astype(BF16)
+    half = kept_ref.shape[0]
+    kept_ref[...] = rounded_s[pl.ds(pl.multiple_of(core * half, GROUP_ROWS), half)]
+    sent_ref[...] = rounded_s[pl.ds(pl.multiple_of((1 - core) * half, GROUP_ROWS), half)]
+
+
+def in_hbm(cells):
+    return pltpu.with_memory_space_constraint(cells, pltpu.HBM)
 
 
 def shift(cells, axis, step):
@@ -450,9 +465,18 @@
     part_spec = framed(sent_rows, 2 * features)
     part_shape = jax.ShapeDtypeStruct((frame_count, sent_rows, 2 * features), BF16)
     place = jnp.stack([lax.axis_index("tm"), lax.axis_index("space")]).astype(jnp.int32)
-
-    from_left = shift(wave_field[:, row_count - rim :], "space", 1)
-    from_right = shift(wave_field[:, :rim], "space", -1)
+    wave_field, cotangent, block_lists, project_weights, combine_weights = (
+        in_hbm(cells)
+        for cells in (wave_field, cotangent, block_lists, project_weights, combine_weights)
+    )
+
+    from_left, from_right = (
+        pltpu.with_memory_space_constraint(cells, pltpu.VMEM)
+        for cells in (
+            shift(wave_field[:, row_count - rim :], "space", 1),
+            shift(wave_field[:, :rim], "space", -1),
+        )
+    )
 
     act, keys_values, queries, probs, inverse_sum, attended, *parts = pl.pallas_call(
         space_forward_kernel,
@@ -508,44 +532,51 @@
         time_kernel(scale, factor, time_count, *refs)
 
     whole_part = whole(frame_count, sent_rows, 2 * features)
-    *parts, time_grads = pl.pallas_call(
+    whole_back = whole(frame_count, sent_rows, features)
+    back_shape = jax.ShapeDtypeStruct((frame_count, sent_rows, features), BF16)
+    grad_rows = 4 * features // LANES * features
+    half_shape = jax.ShapeDtypeStruct((grad_rows // 2, LANES), BF16)
+    grad_parts = pl.pallas_call(
         time_body,
         grid=(1,),
         in_specs=[
+            lists_spec,
             *[whole_part] * time_count,
             pl.BlockSpec((1, features, 3 * features), lambda f: (1, 0, 0)),
             pl.BlockSpec((1, features, features), lambda f: (1, 0, 0)),
         ],
-        out_specs=[*[whole_part] * time_count, whole(features, 4 * features)],
-        out_shape=[
-            *[part_shape] * time_count,
-            jax.ShapeDtypeStruct((features, 4 * features), BF16),
-        ],
+        out_specs=[*[whole_back] * (2 * time_count), *[whole(grad_rows // 2, LANES)] * 2],
+        out_shape=[*[back_shape] * (2 * time_count), half_shape, half_shape],
         scratch_shapes=[
             pltpu.VMEM((all_frames, sent_rows, 3 * features), BF16),
             pltpu.VMEM((all_frames, sent_rows, features), BF16),
             pltpu.VMEM((all_frames, sent_rows, features), BF16),
             pltpu.VMEM((all_frames, sent_rows, 3 * features), BF16),
+            pltpu.VMEM((grad_rows, LANES), BF16),
         ],
         compiler_params=params,
         name="time_pair",
-    )(*arrived, project_weights, combine_weights)
-
-    returned = [parts[0]] + [exchange(parts[d], "tm", d) for d in range(1, time_count)]
-    time_sum = lax.psum(lax.psum(time_grads, "tm"), "space")
+    )(place, *arrived, project_weights, combine_weights)
+    *parts, time_kept, time_sent = grad_parts
+
+    def over_tm(pieces):
+        return [pieces[0]] + [exchange(pieces[d], "tm", d) for d in range(1, time_count)]
+
+    returned = over_tm(parts[:time_count])
+    mixed_parts = over_tm(parts[time_count:])
+    time_other = exchange(time_sent, "space", 1)
 
     def backward_body(*refs):
         space_backward_kernel(scale, factor, time_count, *refs)
 
-    grad_rows = 4 * features // LANES * features
-    half_shape = jax.ShapeDtypeStruct((grad_rows // 2, LANES), BF16)
-    mixed_field, mixed_grad, dact, to_left, to_right, kept, sent = pl.pallas_call(
+    back_spec = framed(sent_rows, features)
+    mixed_grad, dact, to_left, to_right, space_kept, space_sent = pl.pallas_call(
         backward_body,
         grid=(frame_count,),
         in_specs=[
             lists_spec,
             lists_spec,
-            *[part_spec] * time_count,
+            *[back_spec] * time_count,
             framed(extended, features),
             framed(extended, 2 * features),
             framed(row_count, features),
@@ -558,14 +589,12 @@
         out_specs=[
             framed(row_count, features),
             framed(row_count, features),
-            framed(row_count, features),
             framed(rim, features),
             framed(rim, features),
             whole(grad_rows // 2, LANES),
             whole(grad_rows // 2, LANES),
         ],
         out_shape=[
-            jax.ShapeDtypeStruct((frame_count, row_count, features), BF16),
             jax.ShapeDtypeStruct((frame_count, row_count, features), BF16),
             jax.ShapeDtypeStruct((frame_count, row_count, features), F32),
             jax.ShapeDtypeStruct((frame_count, rim, features), BF16),
@@ -596,21 +625,20 @@
         combine_weights,
     )
 
-    other = exchange(sent, "space", 1)
-    edge_left = shift(to_right, "space", 1)
-    edge_right = shift(to_left, "space", -1)
     vmem_spec = pl.BlockSpec(memory_space=pltpu.VMEM)
     piece_rows = grad_rows // 2 // time_count
     piece_shape = jax.ShapeDtypeStruct((piece_rows, LANES), BF16)
-    pieces = pl.pallas_call(
-        split_kernel,
-        in_specs=[lists_spec, vmem_spec, vmem_spec],
-        out_specs=[vmem_spec] * time_count,
-        out_shape=[piece_shape] * time_count,
-        scratch_shapes=[pltpu.VMEM((grad_rows // 2, LANES), BF16)],
-        compiler_params=params,
-        name="add_cores",
-    )(place, kept, other)
+
+    def split(kept, other, name):
+        return pl.pallas_call(
+            split_kernel,
+            in_specs=[lists_spec, vmem_spec, vmem_spec],
+            out_specs=[vmem_spec] * time_count,
+            out_shape=[piece_shape] * time_count,
+            scratch_shapes=[pltpu.VMEM((grad_rows // 2, LANES), BF16)],
+            compiler_params=params,
+            name=name,
+        )(place, kept, other)
 
     def summed(pieces, axis, group, name):
         def body(*refs):
@@ -626,34 +654,52 @@
             name=name,
         )(place, *pieces)
 
-    pieces = [pieces[0]] + [exchange(pieces[d], "tm", d) for d in range(1, time_count)]
-    piece = summed(pieces, 0, 1, "add_tm")
-    pieces = [piece] + [exchange(piece, "space", d) for d in range(2, lax.axis_size("space"), 2)]
-    piece = summed(pieces, 1, 2, "add_space")
-    pieces = [piece] + [exchange(piece, "tm", d) for d in range(1, time_count)]
-    own_half = pl.pallas_call(
-        join_kernel,
-        in_specs=[lists_spec, *[vmem_spec] * time_count],
-        out_specs=vmem_spec,
-        out_shape=half_shape,
-        compiler_params=params,
-        name="join_tm",
-    )(place, *pieces)
-    other_half = exchange(own_half, "space", 1)
-
-    field_grad = pl.pallas_call(
+    def over_space(piece):
+        return [piece] + [
+            exchange(piece, "space", d) for d in range(2, lax.axis_size("space"), 2)
+        ]
+
+    def joined(pieces, name):
+        return pl.pallas_call(
+            join_kernel,
+            in_specs=[lists_spec, *[vmem_spec] * time_count],
+            out_specs=vmem_spec,
+            out_shape=half_shape,
+            compiler_params=params,
+            name=name,
+        )(place, *pieces)
+
+    space_sent, *mixed_parts = lax.optimization_barrier((space_sent, *mixed_parts))
+    space_other = exchange(space_sent, "space", 1)
+    edge_left = shift(to_right, "space", 1)
+    edge_right = shift(to_left, "space", -1)
+    time_pieces = over_tm(split(time_kept, time_other, "add_cores_time"))
+    space_pieces = over_tm(split(space_kept, space_other, "add_cores_space"))
+    edge_left, edge_right, *space_pieces = lax.optimization_barrier(
+        (edge_left, edge_right, *space_pieces)
+    )
+    time_pieces = over_space(summed(time_pieces, 0, 1, "add_tm_time"))
+    space_pieces = over_space(summed(space_pieces, 0, 1, "add_tm_space"))
+    time_pieces = over_tm([summed(time_pieces, 1, 2, "add_space_time")] * time_count)
+    space_pieces = over_tm([summed(space_pieces, 1, 2, "add_space_space")] * time_count)
+    time_half = joined(time_pieces, "join_time")
+    time_half_other = exchange(time_half, "space", 1)
+    space_half = joined(space_pieces, "join_space")
+    space_half_other = exchange(space_half, "space", 1)
+
+    field_grad, mixed_field = pl.pallas_call(
         field_kernel,
         grid=(frame_count,),
-        in_specs=[framed(row_count, features)] * 5,
-        out_specs=framed(row_count, features),
-        out_shape=jax.ShapeDtypeStruct((frame_count, row_count, features), BF16),
+        in_specs=[lists_spec, *[framed(row_count, features)] * 5, *[back_spec] * time_count],
+        out_specs=[framed(row_count, features)] * 2,
+        out_shape=[jax.ShapeDtypeStruct((frame_count, row_count, features), BF16)] * 2,
         compiler_params=params,
         name="field_grad",
-    )(wave_field, mixed_grad, dact, edge_left, edge_right)
+    )(place, wave_field, mixed_grad, dact, edge_left, edge_right, *mixed_parts)
 
     project_grad, combine_grad = pl.pallas_call(
         grads_kernel,
-        in_specs=[lists_spec, vmem_spec, vmem_spec, vmem_spec],
+        in_specs=[lists_spec, *[vmem_spec] * 4],
         out_specs=[vmem_spec, vmem_spec],
         out_shape=[
             jax.ShapeDtypeStruct((2, features, 3 * features), F32),
@@ -662,7 +708,7 @@
         scratch_shapes=[pltpu.VMEM((grad_rows, LANES), BF16)],
         compiler_params=params,
         name="weight_grads",
-    )(place, own_half, other_half, time_sum)
+    )(place, space_half, space_half_other, time_half, time_half_other)
     return (mixed_field, field_grad, project_grad, combine_grad)
 
 

time: 171 us -> 103 us (0.60)
  waiting for transfers between devices: 80.9 us -> 14.2 us
  starting transfers between devices: 28.8 us -> 47.6 us
  between operations: 14.2 us -> 0.82 us
  local copies, waits for them, and re-layouts: 9.15 us -> 0 us
  Pallas kernels: 38 us -> 40 us
    psum x2 -> x0, waiting for transfers between devices: 56.9 us -> none  [per_device(): time_sum = lax.psum(lax.psum(time_grads, 'tm'), 'space')]
    ppermute x17 -> x31, starting transfers between devices: 21.6 us -> 39.8 us  [exchange(): lax.ppermute(cells, axis, [(i, i ^ distance) for i in range(lax.axis_size...]
    ppermute x17 -> x31, waiting for transfers between devices: 22.3 us -> 13 us  [exchange(): lax.ppermute(cells, axis, [(i, i ^ distance) for i in range(lax.axis_size...]
    unnamed x30 -> x0, local copies, waits for them, and re-layouts: 9.15 us -> none
    pallas_call x5 -> x7, Pallas kernels: 13.7 us -> 16.3 us  [the longest x1 9.53 us: per_device(): pl.pallas_call(time_body, grid=(1,), in_specs=[lists_spec, *[whole_part]...]
  transfers between devices with their start and end apart: 23 -> 35, of which waited for: 16 -> 11; matrix products, arithmetic and copies ran while one was open for 0% -> 0% of each run, Pallas kernels for 9% -> 17%
where the time goes in v2:
time: 103 us
  starting transfers between devices  47.6 us (46%)
  Pallas kernels  40 us (39%)
  waiting for transfers between devices  14.2 us (14%)
    ppermute x31, starting transfers between devices, exchange(): lax.ppermute(cells, axis, [(i, i ^ distance) for i in range(lax.axis_size...  39.8 us
    ppermute x31, waiting for transfers between devices, exchange(): lax.ppermute(cells, axis, [(i, i ^ distance) for i in range(lax.axis_size...  13 us
    pallas_call x1, Pallas kernels, per_device(): pl.pallas_call(backward_body, grid=(frame_count,), in_specs=[lists_spec,...  10.8 us
    pallas_call x1, Pallas kernels, per_device(): pl.pallas_call(space_forward_kernel, grid=(frame_count,), in_specs=[lists...  10.5 us
    pallas_call x1, Pallas kernels, per_device(): pl.pallas_call(time_body, grid=(1,), in_specs=[lists_spec, *[whole_part]...  9.53 us
    ppermute x4, starting transfers between devices, shift(): return lax.ppermute(cells, axis, moves)  7.77 us
    pallas_call x4, Pallas kernels, summed(): pl.pallas_call(body, in_specs=[lists_spec, *[vmem_spec] * len(pieces)], o...  2.42 us
    pallas_call x1, Pallas kernels, per_device(): pl.pallas_call(field_kernel, grid=(frame_count,), in_specs=[lists_spec, *...  2.23 us
  transfers between devices with their start and end apart: 35, of which 11 were waited for; matrix products, arithmetic and copies ran while one was open for 0% of the time, Pallas kernels for 17%

profile of v2, /device:TPU:0, one launch (start us, length us, event | category | flops | bytes accessed | tf_op | source)
XLA Modules:
  0.0 102.7 jit_solution(5352180091879665268)
XLA Ops:
  1.9 3.1 %collective-permute-start = (bf16[2,256,256]{2,1,0:T(8,128)(2,1)}, bf16[2,256,256]{2,1,0:T(8,128)(2,1)S(1)}, u32[]{:S(2)}, u32[]{:S(2)}) collective-permute-start(bf16[2,256,256]{2,1,0:T(8,128)(2,1)} %wave_ref.3), channel_id=1, source_target_pairs={{0,1},{1,2},{2,3},{3,4},{4,5},{5,6},{6,7},{8,9},{9,10},{10,11},{11... | collective-permute-start | bytes 786440 | tf_op jit(solution)/shard_map/ppermute | solution.py:434
  6.3 10.5 %space_forward.1 = (bf16[2,768,256]{2,1,0:T(8,128)(2,1)S(1)}, bf16[2,768,512]{2,1,0:T(8,128)(2,1)S(1)}, bf16[2,256,256]{2,1,0:T(8,128)(2,1)S(1)}, bf16[2,2,512,1...) custom-call(s32[2,2,4]{2,1,0:T(2,128)} %refs_0_.1, ...), custom_call_target="tpu_custom_call" | custom-call | tf_op jit(solution)/shard_map/space_forward/pallas_call | solution.py:481
  16.8 3.0 %collective-permute-start.2 = (bf16[2,64,512]{2,1,0:T(8,128)(2,1)S(1)}, bf16[2,64,512]{2,1,0:T(8,128)(2,1)S(1)}, u32[]{:S(2)}, u32[]{:S(2)}) collective-permute-start(bf16[2,64,512]{2,1,0:T(8,128)(2,1)S(1)} %get-tuple-element.54), channel_id=1, source_target_pairs={{0,8},{8,0},{16,24},{24,16},{1,9},{9,1},{17,25},{25,17},{2,10},{10... | collective-permute-start | bytes 393224 | tf_op jit(solution)/shard_map/ppermute | solution.py:438
  19.8 1.5 %collective-permute-start.3 = (bf16[2,64,512]{2,1,0:T(8,128)(2,1)S(1)}, bf16[2,64,512]{2,1,0:T(8,128)(2,1)S(1)}, u32[]{:S(2)}, u32[]{:S(2)}) collective-permute-start(bf16[2,64,512]{2,1,0:T(8,128)(2,1)S(1)} %get-tuple-element.55), channel_id=1, source_target_pairs={{0,16},{8,24},{16,0},{24,8},{1,17},{9,25},{17,1},{25,9},{2,18},{10... | collective-permute-start | bytes 393224 | tf_op jit(solution)/shard_map/ppermute | solution.py:438
  21.4 1.4 %collective-permute-done.2.refs_2_ = bf16[2,64,512]{2,1,0:T(8,128)(2,1)S(1)} collective-permute-done((bf16[2,64,512]{2,1,0:T(8,128)(2,1)S(1)}, bf16[2,64,512]{2,1,0:T(8,128)(2,1)S(1)}, u32[]{:S(2)}, u32[]{:S(2)}) %collective-permute-start.2) | collective-permute-done | bytes 131104 | tf_op jit(solution)/shard_map/ppermute | solution.py:438
  22.8 2.0 %collective-permute-done.3.refs_3_ = bf16[2,64,512]{2,1,0:T(8,128)(2,1)S(1)} collective-permute-done((bf16[2,64,512]{2,1,0:T(8,128)(2,1)S(1)}, bf16[2,64,512]{2,1,0:T(8,128)(2,1)S(1)}, u32[]{:S(2)}, u32[]{:S(2)}) %collective-permute-start.3) | collective-permute-done | bytes 131104 | tf_op jit(solution)/shard_map/ppermute | solution.py:438
  24.8 3.8 %collective-permute-done.4.refs_4_ = bf16[2,64,512]{2,1,0:T(8,128)(2,1)S(1)} collective-permute-done((bf16[2,64,512]{2,1,0:T(8,128)(2,1)S(1)}, bf16[2,64,512]{2,1,0:T(8,128)(2,1)S(1)}, u32[]{:S(2)}, u32[]{:S(2)}) %collective-permute-start.4) | collective-permute-done | bytes 131104 | tf_op jit(solution)/shard_map/ppermute | solution.py:438
  28.6 9.5 %time_pair.1 = (bf16[2,64,256]{2,1,0:T(8,128)(2,1)S(1)}, bf16[2,64,256]{2,1,0:T(8,128)(2,1)S(1)}, bf16[2,64,256]{2,1,0:T(8,128)(2,1)S(1)}, bf16[2,64,256]{2,1,0:...) custom-call(s32[2]{0:T(128)S(1)} %pad_add_fusion.place_ref.refs_0_.r, ...), custom_call_target="tpu_custom_call" | custom-call | tf_op jit(solution)/shard_map/time_pair/pallas_call | solution.py:539
  38.8 2.9 %collective-permute-start.7 = (bf16[2,64,256]{2,1,0:T(8,128)(2,1)S(1)}, bf16[2,64,256]{2,1,0:T(8,128)(2,1)S(1)}, u32[]{:S(2)}, u32[]{:S(2)}) collective-permute-start(bf16[2,64,256]{2,1,0:T(8,128)(2,1)S(1)} %get-tuple-element.60), channel_id=1, source_target_pairs={{0,24},{8,16},{16,8},{24,0},{1,25},{9,17},{17,9},{25,1},{2,26},{10... | collective-permute-start | bytes 196616 | tf_op jit(solution)/shard_map/ppermute | solution.py:438
  43.1 2.1 %collective-permute-start.12 = (bf16[2,64,256]{2,1,0:T(8,128)(2,1)S(1)}, bf16[2,64,256]{2,1,0:T(8,128)(2,1)S(1)}, u32[]{:S(2)}, u32[]{:S(2)}) collective-permute-start(bf16[2,64,256]{2,1,0:T(8,128)(2,1)S(1)} %get-tuple-element.76), channel_id=1, source_target_pairs={{0,24},{8,16},{16,8},{24,0},{1,25},{9,17},{17,9},{25,1},{2,26},{10... | collective-permute-start | bytes 196616 | tf_op jit(solution)/shard_map/ppermute | solution.py:438
  45.2 10.8 %space_backward.1 = (bf16[2,256,256]{2,1,0:T(8,128)(2,1)S(1)}, f32[2,256,256]{2,1,0:T(8,128)S(1)}, bf16[2,256,256]{2,1,0:T(8,128)(2,1)S(1)}, bf16[2,256,256]{2,1...) custom-call(s32[2,2,4]{2,1,0:T(2,128)} %refs_0_.1, ...), custom_call_target="tpu_custom_call" | custom-call | tf_op jit(solution)/shard_map/space_backward/pallas_call | solution.py:573
  56.3 2.1 %collective-permute-start.8 = (bf16[2,256,256]{2,1,0:T(8,128)(2,1)S(1)}, bf16[2,256,256]{2,1,0:T(8,128)(2,1)S(1)}, u32[]{:S(2)}, u32[]{:S(2)}) collective-permute-start(bf16[2,256,256]{2,1,0:T(8,128)(2,1)S(1)} %get-tuple-element.69), channel_id=1, source_target_pairs={{0,1},{1,2},{2,3},{3,4},{4,5},{5,6},{6,7},{8,9},{9,10},{10,11},{11... | collective-permute-start | bytes 786440 | tf_op jit(solution)/shard_map/ppermute | solution.py:434
  61.8 1.4 %collective-permute-start.26 = (bf16[256,128]{1,0:T(8,128)(2,1)S(1)}, bf16[256,128]{1,0:T(8,128)(2,1)S(1)}, u32[]{:S(2)}, u32[]{:S(2)}) collective-permute-start(bf16[256,128]{1,0:T(8,128)(2,1)S(1)} %get-tuple-element.98), channel_id=1, source_target_pairs={{0,16},{8,24},{16,0},{24,8},{1,17},{9,25},{17,1},{25,9},{2,18},{10... | collective-permute-start | bytes 196616 | tf_op jit(solution)/shard_map/ppermute | solution.py:438
  66.0 1.4 %collective-permute-start.15 = (bf16[256,128]{1,0:T(8,128)(2,1)S(1)}, bf16[256,128]{1,0:T(8,128)(2,1)S(1)}, u32[]{:S(2)}, u32[]{:S(2)}) collective-permute-start(bf16[256,128]{1,0:T(8,128)(2,1)S(1)} %get-tuple-element.80), channel_id=1, source_target_pairs={{0,16},{8,24},{16,0},{24,8},{1,17},{9,25},{17,1},{25,9},{2,18},{10... | collective-permute-start | bytes 196616 | tf_op jit(solution)/shard_map/ppermute | solution.py:438
  69.8 8.5 %collective-permute-start.30 = (bf16[256,128]{1,0:T(8,128)(2,1)S(1)}, bf16[256,128]{1,0:T(8,128)(2,1)S(1)}, u32[]{:S(2)}, u32[]{:S(2)}) collective-permute-start(bf16[256,128]{1,0:T(8,128)(2,1)S(1)} %add_tm_time.1.refs_1_), channel_id=1, source_target_pairs={{0,6},{1,7},{2,4},{3,5},{4,2},{5,3},{6,0},{7,1},{8,14},{9,15},{10,... | collective-permute-start | bytes 196616 | tf_op jit(solution)/shard_map/ppermute | solution.py:438
  79.6 3.8 %collective-permute-start.19 = (bf16[256,128]{1,0:T(8,128)(2,1)S(1)}, bf16[256,128]{1,0:T(8,128)(2,1)S(1)}, u32[]{:S(2)}, u32[]{:S(2)}) collective-permute-start(bf16[256,128]{1,0:T(8,128)(2,1)S(1)} %add_tm_space.1.refs_1_), channel_id=1, source_target_pairs={{0,6},{1,7},{2,4},{3,5},{4,2},{5,3},{6,0},{7,1},{8,14},{9,15},{10,... | collective-permute-start | bytes 196616 | tf_op jit(solution)/shard_map/ppermute | solution.py:438
  83.4 1.3 %collective-permute-start.17 = (bf16[256,128]{1,0:T(8,128)(2,1)S(1)}, bf16[256,128]{1,0:T(8,128)(2,1)S(1)}, u32[]{:S(2)}, u32[]{:S(2)}) collective-permute-start(bf16[256,128]{1,0:T(8,128)(2,1)S(1)} %add_tm_space.1.refs_1_), channel_id=1, source_target_pairs={{0,2},{1,3},{2,0},{3,1},{4,6},{5,7},{6,4},{7,5},{8,10},{9,11},{10,... | collective-permute-start | bytes 196616 | tf_op jit(solution)/shard_map/ppermute | solution.py:438
  86.2 1.4 %collective-permute-start.33 = (bf16[256,128]{1,0:T(8,128)(2,1)S(1)}, bf16[256,128]{1,0:T(8,128)(2,1)S(1)}, u32[]{:S(2)}, u32[]{:S(2)}) collective-permute-start(bf16[256,128]{1,0:T(8,128)(2,1)S(1)} %add_space_time.1.refs_0_), channel_id=1, source_target_pairs={{0,24},{8,16},{16,8},{24,0},{1,25},{9,17},{17,9},{25,1},{2,26},{10... | collective-permute-start | bytes 196616 | tf_op jit(solution)/shard_map/ppermute | solution.py:438
  87.6 1.7 %collective-permute-start.32 = (bf16[256,128]{1,0:T(8,128)(2,1)S(1)}, bf16[256,128]{1,0:T(8,128)(2,1)S(1)}, u32[]{:S(2)}, u32[]{:S(2)}) collective-permute-start(bf16[256,128]{1,0:T(8,128)(2,1)S(1)} %add_space_time.1.refs_0_), channel_id=1, source_target_pairs={{0,16},{8,24},{16,0},{24,8},{1,17},{9,25},{17,1},{25,9},{2,18},{10... | collective-permute-start | bytes 196616 | tf_op jit(solution)/shard_map/ppermute | solution.py:438
  90.4 1.4 %collective-permute-start.22 = (bf16[256,128]{1,0:T(8,128)(2,1)S(1)}, bf16[256,128]{1,0:T(8,128)(2,1)S(1)}, u32[]{:S(2)}, u32[]{:S(2)}) collective-permute-start(bf16[256,128]{1,0:T(8,128)(2,1)S(1)} %add_space_space.1.refs_0_), channel_id=1, source_target_pairs={{0,24},{8,16},{16,8},{24,0},{1,25},{9,17},{17,9},{25,1},{2,26},{10... | collective-permute-start | bytes 196616 | tf_op jit(solution)/shard_map/ppermute | solution.py:438
  91.8 1.7 %collective-permute-start.21 = (bf16[256,128]{1,0:T(8,128)(2,1)S(1)}, bf16[256,128]{1,0:T(8,128)(2,1)S(1)}, u32[]{:S(2)}, u32[]{:S(2)}) collective-permute-start(bf16[256,128]{1,0:T(8,128)(2,1)S(1)} %add_space_space.1.refs_0_), channel_id=1, source_target_pairs={{0,16},{8,24},{16,0},{24,8},{1,17},{9,25},{17,1},{25,9},{2,18},{10... | collective-permute-start | bytes 196616 | tf_op jit(solution)/shard_map/ppermute | solution.py:438
  96.3 1.4 %collective-permute-done.20.refs_1_ = bf16[256,128]{1,0:T(8,128)(2,1)S(1)} collective-permute-done((bf16[256,128]{1,0:T(8,128)(2,1)S(1)}, bf16[256,128]{1,0:T(8,128)(2,1)S(1)}, u32[]{:S(2)}, u32[]{:S(2)}) %collective-permute-start.20) | collective-permute-done | bytes 65568 | tf_op jit(solution)/shard_map/ppermute | solution.py:438
  98.4 2.2 %field_grad.1 = (bf16[2,256,256]{2,1,0:T(8,128)(2,1)}, bf16[2,256,256]{2,1,0:T(8,128)(2,1)}) custom-call(s32[2]{0:T(128)S(1)} %pad_add_fusion.place_ref.refs_0_.refs_1_, bf16[2,256,256]{2,1,0:T(8,128)(2,1)} %wave_ref.3, bf16[2,256,256]{2,1,0:T(8,128)(2,1)S(1)} %get-tuple-element.67.mixed_grad_ref, f32[2,256,256]{2,1,0:T(8,128)S(1)} %get-tuple-element.68.dact_ref, ...), custom_call_target="tpu_custom_call" | custom-call | tf_op jit(solution)/shard_map/field_grad/pallas_call | solution.py:690
  100.6 2.1 %weight_grads.1 = (f32[2,256,768]{2,1,0:T(8,128)}, f32[2,256,256]{2,1,0:T(8,128)}) custom-call(s32[2]{0:T(128)S(1)} %pad_add_fusion.place_ref.refs_0_.refs_1_, bf16[1024,128]{1,0:T(8,128)(2,1)S(1)} %join_space.1.refs_0_, bf16[1024,128]{1,0:T(8,128)(2,1)S(1)} %collective-permute-done.23.refs_1_, bf16[1024,128]{1,0:T(8,128)(2,1)S(1)} %join_time.1.refs_2_, ...), custom_call_target="tpu_custom_call" | custom-call | tf_op jit(solution)/shard_map/weight_grads/pallas_call | solution.py:700
  (60 shorter events, 20.9 us)
Async XLA Ops:
  16.8 6.0 %collective-permute-start.2 = (bf16[2,64,512]{2,1,0:T(8,128)(2,1)S(1)}, bf16[2,64,512]{2,1,0:T(8,128)(2,1)S(1)}, u32[]{:S(2)}, u32[]{:S(2)}) collective-permute-start(bf16[2,64,512]{2,1,0:T(8,128)(2,1)S(1)} %get-tuple-element.54), channel_id=1, source_target_pairs={{0,8},{8,0},{16,24},{24,16},{1,9},{9,1},{17,25},{25,17},{2,10},{10... | collective-permute-start | bytes 393224 | tf_op jit(solution)/shard_map/ppermute | solution.py:438
  21.3 7.2 %collective-permute-start.4 = (bf16[2,64,512]{2,1,0:T(8,128)(2,1)S(1)}, bf16[2,64,512]{2,1,0:T(8,128)(2,1)S(1)}, u32[]{:S(2)}, u32[]{:S(2)}) collective-permute-start(bf16[2,64,512]{2,1,0:T(8,128)(2,1)S(1)} %get-tuple-element.56), channel_id=1, source_target_pairs={{0,24},{8,16},{16,8},{24,0},{1,25},{9,17},{17,9},{25,1},{2,26},{10... | collective-permute-start | bytes 393224 | tf_op jit(solution)/shard_map/ppermute | solution.py:438
  38.3 6.8 %collective-permute-start.6 = (bf16[2,64,256]{2,1,0:T(8,128)(2,1)S(1)}, bf16[2,64,256]{2,1,0:T(8,128)(2,1)S(1)}, u32[]{:S(2)}, u32[]{:S(2)}) collective-permute-start(bf16[2,64,256]{2,1,0:T(8,128)(2,1)S(1)} %get-tuple-element.59), channel_id=1, source_target_pairs={{0,16},{8,24},{16,0},{24,8},{1,17},{9,25},{17,1},{25,9},{2,18},{10... | collective-permute-start | bytes 196616 | tf_op jit(solution)/shard_map/ppermute | solution.py:438
  38.8 6.4 %collective-permute-start.7 = (bf16[2,64,256]{2,1,0:T(8,128)(2,1)S(1)}, bf16[2,64,256]{2,1,0:T(8,128)(2,1)S(1)}, u32[]{:S(2)}, u32[]{:S(2)}) collective-permute-start(bf16[2,64,256]{2,1,0:T(8,128)(2,1)S(1)} %get-tuple-element.60), channel_id=1, source_target_pairs={{0,24},{8,16},{16,8},{24,0},{1,25},{9,17},{17,9},{25,1},{2,26},{10... | collective-permute-start | bytes 196616 | tf_op jit(solution)/shard_map/ppermute | solution.py:438
  41.7 14.3 %collective-permute-start.10 = (bf16[2,64,256]{2,1,0:T(8,128)(2,1)S(1)}, bf16[2,64,256]{2,1,0:T(8,128)(2,1)S(1)}, u32[]{:S(2)}, u32[]{:S(2)}) collective-permute-start(bf16[2,64,256]{2,1,0:T(8,128)(2,1)S(1)} %get-tuple-element.74), channel_id=1, source_target_pairs={{0,8},{8,0},{16,24},{24,16},{1,9},{9,1},{17,25},{25,17},{2,10},{10... | collective-permute-start | bytes 196616 | tf_op jit(solution)/shard_map/ppermute | solution.py:438
  41.8 14.2 %collective-permute-start.11 = (bf16[2,64,256]{2,1,0:T(8,128)(2,1)S(1)}, bf16[2,64,256]{2,1,0:T(8,128)(2,1)S(1)}, u32[]{:S(2)}, u32[]{:S(2)}) collective-permute-start(bf16[2,64,256]{2,1,0:T(8,128)(2,1)S(1)} %get-tuple-element.75), channel_id=1, source_target_pairs={{0,16},{8,24},{16,0},{24,8},{1,17},{9,25},{17,1},{25,9},{2,18},{10... | collective-permute-start | bytes 196616 | tf_op jit(solution)/shard_map/ppermute | solution.py:438
  43.1 12.9 %collective-permute-start.12 = (bf16[2,64,256]{2,1,0:T(8,128)(2,1)S(1)}, bf16[2,64,256]{2,1,0:T(8,128)(2,1)S(1)}, u32[]{:S(2)}, u32[]{:S(2)}) collective-permute-start(bf16[2,64,256]{2,1,0:T(8,128)(2,1)S(1)} %get-tuple-element.76), channel_id=1, source_target_pairs={{0,24},{8,16},{16,8},{24,0},{1,25},{9,17},{17,9},{25,1},{2,26},{10... | collective-permute-start | bytes 196616 | tf_op jit(solution)/shard_map/ppermute | solution.py:438
  45.2 14.6 %collective-permute-start.24 = (bf16[1024,128]{1,0:T(8,128)(2,1)S(1)}, bf16[1024,128]{1,0:T(8,128)(2,1)S(1)}, u32[]{:S(2)}, u32[]{:S(2)}) collective-permute-start(bf16[1024,128]{1,0:T(8,128)(2,1)S(1)} %get-tuple-element.95), channel_id=1, source_target_pairs={{0,1},{1,0},{2,3},{3,2},{4,5},{5,4},{6,7},{7,6},{8,9},{9,8},{10,11... | collective-permute-start | bytes 786440 | tf_op jit(solution)/shard_map/ppermute | solution.py:438
  56.0 7.2 %collective-permute-start.13 = (bf16[1024,128]{1,0:T(8,128)(2,1)S(1)}, bf16[1024,128]{1,0:T(8,128)(2,1)S(1)}, u32[]{:S(2)}, u32[]{:S(2)}) collective-permute-start(bf16[1024,128]{1,0:T(8,128)(2,1)S(1)} %get-tuple-element.77), channel_id=1, source_target_pairs={{0,1},{1,0},{2,3},{3,2},{4,5},{5,4},{6,7},{7,6},{8,9},{9,8},{10,11... | collective-permute-start | bytes 786440 | tf_op jit(solution)/shard_map/ppermute | solution.py:438
  56.3 13.5 %collective-permute-start.8 = (bf16[2,256,256]{2,1,0:T(8,128)(2,1)S(1)}, bf16[2,256,256]{2,1,0:T(8,128)(2,1)S(1)}, u32[]{:S(2)}, u32[]{:S(2)}) collective-permute-start(bf16[2,256,256]{2,1,0:T(8,128)(2,1)S(1)} %get-tuple-element.69), channel_id=1, source_target_pairs={{0,1},{1,2},{2,3},{3,4},{4,5},{5,6},{6,7},{8,9},{9,10},{10,11},{11... | collective-permute-start | bytes 786440 | tf_op jit(solution)/shard_map/ppermute | solution.py:434
  58.5 19.9 %collective-permute-start.9 = (bf16[2,256,256]{2,1,0:T(8,128)(2,1)S(1)}, bf16[2,256,256]{2,1,0:T(8,128)(2,1)S(1)}, u32[]{:S(2)}, u32[]{:S(2)}) collective-permute-start(bf16[2,256,256]{2,1,0:T(8,128)(2,1)S(1)} %get-tuple-element.70), channel_id=1, source_target_pairs={{1,0},{2,1},{3,2},{4,3},{5,4},{6,5},{7,6},{9,8},{10,9},{11,10},{12... | collective-permute-start | bytes 786440 | tf_op jit(solution)/shard_map/ppermute | solution.py:434
  64.8 13.9 %collective-permute-start.14 = (bf16[256,128]{1,0:T(8,128)(2,1)S(1)}, bf16[256,128]{1,0:T(8,128)(2,1)S(1)}, u32[]{:S(2)}, u32[]{:S(2)}) collective-permute-start(bf16[256,128]{1,0:T(8,128)(2,1)S(1)} %get-tuple-element.79), channel_id=1, source_target_pairs={{0,8},{8,0},{16,24},{24,16},{1,9},{9,1},{17,25},{25,17},{2,10},{10... | collective-permute-start | bytes 196616 | tf_op jit(solution)/shard_map/ppermute | solution.py:438
  66.0 13.0 %collective-permute-start.15 = (bf16[256,128]{1,0:T(8,128)(2,1)S(1)}, bf16[256,128]{1,0:T(8,128)(2,1)S(1)}, u32[]{:S(2)}, u32[]{:S(2)}) collective-permute-start(bf16[256,128]{1,0:T(8,128)(2,1)S(1)} %get-tuple-element.80), channel_id=1, source_target_pairs={{0,16},{8,24},{16,0},{24,8},{1,17},{9,25},{17,1},{25,9},{2,18},{10... | collective-permute-start | bytes 196616 | tf_op jit(solution)/shard_map/ppermute | solution.py:438
  68.3 10.7 %collective-permute-start.16 = (bf16[256,128]{1,0:T(8,128)(2,1)S(1)}, bf16[256,128]{1,0:T(8,128)(2,1)S(1)}, u32[]{:S(2)}, u32[]{:S(2)}) collective-permute-start(bf16[256,128]{1,0:T(8,128)(2,1)S(1)} %get-tuple-element.81), channel_id=1, source_target_pairs={{0,24},{8,16},{16,8},{24,0},{1,25},{9,17},{17,9},{25,1},{2,26},{10... | collective-permute-start | bytes 196616 | tf_op jit(solution)/shard_map/ppermute | solution.py:438
  69.8 13.6 %collective-permute-start.30 = (bf16[256,128]{1,0:T(8,128)(2,1)S(1)}, bf16[256,128]{1,0:T(8,128)(2,1)S(1)}, u32[]{:S(2)}, u32[]{:S(2)}) collective-permute-start(bf16[256,128]{1,0:T(8,128)(2,1)S(1)} %add_tm_time.1.refs_1_), channel_id=1, source_target_pairs={{0,6},{1,7},{2,4},{3,5},{4,2},{5,3},{6,0},{7,1},{8,14},{9,15},{10,... | collective-permute-start | bytes 196616 | tf_op jit(solution)/shard_map/ppermute | solution.py:438
  78.4 7.3 %collective-permute-start.29 = (bf16[256,128]{1,0:T(8,128)(2,1)S(1)}, bf16[256,128]{1,0:T(8,128)(2,1)S(1)}, u32[]{:S(2)}, u32[]{:S(2)}) collective-permute-start(bf16[256,128]{1,0:T(8,128)(2,1)S(1)} %add_tm_time.1.refs_1_), channel_id=1, source_target_pairs={{0,4},{1,5},{2,6},{3,7},{4,0},{5,1},{6,2},{7,3},{8,12},{9,13},{10,... | collective-permute-start | bytes 196616 | tf_op jit(solution)/shard_map/ppermute | solution.py:438
  78.7 6.9 %collective-permute-start.28 = (bf16[256,128]{1,0:T(8,128)(2,1)S(1)}, bf16[256,128]{1,0:T(8,128)(2,1)S(1)}, u32[]{:S(2)}, u32[]{:S(2)}) collective-permute-start(bf16[256,128]{1,0:T(8,128)(2,1)S(1)} %add_tm_time.1.refs_1_), channel_id=1, source_target_pairs={{0,2},{1,3},{2,0},{3,1},{4,6},{5,7},{6,4},{7,5},{8,10},{9,11},{10,... | collective-permute-start | bytes 196616 | tf_op jit(solution)/shard_map/ppermute | solution.py:438
  79.6 9.6 %collective-permute-start.19 = (bf16[256,128]{1,0:T(8,128)(2,1)S(1)}, bf16[256,128]{1,0:T(8,128)(2,1)S(1)}, u32[]{:S(2)}, u32[]{:S(2)}) collective-permute-start(bf16[256,128]{1,0:T(8,128)(2,1)S(1)} %add_tm_space.1.refs_1_), channel_id=1, source_target_pairs={{0,6},{1,7},{2,4},{3,5},{4,2},{5,3},{6,0},{7,1},{8,14},{9,15},{10,... | collective-permute-start | bytes 196616 | tf_op jit(solution)/shard_map/ppermute | solution.py:438
  83.4 6.4 %collective-permute-start.18 = (bf16[256,128]{1,0:T(8,128)(2,1)S(1)}, bf16[256,128]{1,0:T(8,128)(2,1)S(1)}, u32[]{:S(2)}, u32[]{:S(2)}) collective-permute-start(bf16[256,128]{1,0:T(8,128)(2,1)S(1)} %add_tm_space.1.refs_1_), channel_id=1, source_target_pairs={{0,4},{1,5},{2,6},{3,7},{4,0},{5,1},{6,2},{7,3},{8,12},{9,13},{10,... | collective-permute-start | bytes 196616 | tf_op jit(solution)/shard_map/ppermute | solution.py:438
  83.4 6.4 %collective-permute-start.17 = (bf16[256,128]{1,0:T(8,128)(2,1)S(1)}, bf16[256,128]{1,0:T(8,128)(2,1)S(1)}, u32[]{:S(2)}, u32[]{:S(2)}) collective-permute-start(bf16[256,128]{1,0:T(8,128)(2,1)S(1)} %add_tm_space.1.refs_1_), channel_id=1, source_target_pairs={{0,2},{1,3},{2,0},{3,1},{4,6},{5,7},{6,4},{7,5},{8,10},{9,11},{10,... | collective-permute-start | bytes 196616 | tf_op jit(solution)/shard_map/ppermute | solution.py:438
  86.2 7.2 %collective-permute-start.33 = (bf16[256,128]{1,0:T(8,128)(2,1)S(1)}, bf16[256,128]{1,0:T(8,128)(2,1)S(1)}, u32[]{:S(2)}, u32[]{:S(2)}) collective-permute-start(bf16[256,128]{1,0:T(8,128)(2,1)S(1)} %add_space_time.1.refs_0_), channel_id=1, source_target_pairs={{0,24},{8,16},{16,8},{24,0},{1,25},{9,17},{17,9},{25,1},{2,26},{10... | collective-permute-start | bytes 196616 | tf_op jit(solution)/shard_map/ppermute | solution.py:438
  87.6 6.4 %collective-permute-start.32 = (bf16[256,128]{1,0:T(8,128)(2,1)S(1)}, bf16[256,128]{1,0:T(8,128)(2,1)S(1)}, u32[]{:S(2)}, u32[]{:S(2)}) collective-permute-start(bf16[256,128]{1,0:T(8,128)(2,1)S(1)} %add_space_time.1.refs_0_), channel_id=1, source_target_pairs={{0,16},{8,24},{16,0},{24,8},{1,17},{9,25},{17,1},{25,9},{2,18},{10... | collective-permute-start | bytes 196616 | tf_op jit(solution)/shard_map/ppermute | solution.py:438
  90.4 5.3 %collective-permute-start.22 = (bf16[256,128]{1,0:T(8,128)(2,1)S(1)}, bf16[256,128]{1,0:T(8,128)(2,1)S(1)}, u32[]{:S(2)}, u32[]{:S(2)}) collective-permute-start(bf16[256,128]{1,0:T(8,128)(2,1)S(1)} %add_space_space.1.refs_0_), channel_id=1, source_target_pairs={{0,24},{8,16},{16,8},{24,0},{1,25},{9,17},{17,9},{25,1},{2,26},{10... | collective-permute-start | bytes 196616 | tf_op jit(solution)/shard_map/ppermute | solution.py:438
  94.5 6.1 %collective-permute-start.34 = (bf16[1024,128]{1,0:T(8,128)(2,1)S(1)}, bf16[1024,128]{1,0:T(8,128)(2,1)S(1)}, u32[]{:S(2)}, u32[]{:S(2)}) collective-permute-start(bf16[1024,128]{1,0:T(8,128)(2,1)S(1)} %join_time.1.refs_2_), channel_id=1, source_target_pairs={{0,1},{1,0},{2,3},{3,2},{4,5},{5,4},{6,7},{7,6},{8,9},{9,8},{10,11... | collective-permute-start | bytes 786440 | tf_op jit(solution)/shard_map/ppermute | solution.py:438
  (11 other events, 48.4 us)

commit v3 on v2

v3 whole, which is shorter than its diff:
```python
import math

import jax
import jax.numpy as jnp
from jax import lax
from jax.experimental import pallas as pl
from jax.experimental.pallas import tpu as pltpu
from jax.sharding import PartitionSpec as P

HEADS = 8
BLOCK = 128
HREACH = 2
LANES = 128
GROUP_ROWS = 16
VMEM_BYTES = 24 * 1024 * 1024
BF16 = jnp.bfloat16
F32 = jnp.float32


epsilon = 1e-05


def cost(matmuls):
    flops = matmuls * 2 * 1024 * 256 * 512
    return pl.CostEstimate(flops=flops, bytes_accessed=flops // 256, transcendentals=flops // 1024)


def dot_nn(left, right):
    return lax.dot_general(left, right, (((1,), (0,)), ((), ())), preferred_element_type=F32)


def dot_nt(left, right):
    return lax.dot_general(left, right, (((1,), (1,)), ((), ())), preferred_element_type=F32)


def dot_tn(left, right):
    return lax.dot_general(left, right, (((0,), (0,)), ((), ())), preferred_element_type=F32)


def layer_norm(rows):
    widened = rows.astype(F32)
    centered = widened - jnp.mean(widened, axis=-1, keepdims=True)
    inverse = lax.rsqrt(jnp.mean(centered * centered, axis=-1, keepdims=True) + epsilon)
    return (centered * inverse, inverse)


def norm_backward(upstream, normed, inverse):
    mean_grad = jnp.mean(upstream, axis=-1, keepdims=True)
    mean_cross = jnp.mean(upstream * normed, axis=-1, keepdims=True)
    return inverse * (upstream - mean_grad - normed * mean_cross)


def flip(matrix):
    return matrix.astype(BF16).T


def pair_columns(rows_t, pair, width):
    count = rows_t.shape[1]
    base = (pair * 2 * width) // LANES * LANES
    parts = []
    for head in (2 * pair, 2 * pair + 1):
        start = head * width - base
        pieces = []
        if start:
            pieces.append(jnp.zeros((start, count), rows_t.dtype))
        pieces.append(rows_t[head * width : (head + 1) * width])
        if start + width < LANES:
            pieces.append(jnp.zeros((LANES - start - width, count), rows_t.dtype))
        parts.append(jnp.concatenate(pieces, axis=0))
    return jnp.concatenate(parts, axis=1)


def pair_group(matrix, pair, width):
    base = (pair * 2 * width) // LANES * LANES
    return matrix[:, base : base + LANES]


def pair_diagonal(product, width):
    count = product.shape[1] // 2
    return jnp.concatenate([product[:width, :count], product[width:, count:]], axis=0)


def head_rows(rows, width):
    column = lax.broadcasted_iota(jnp.int32, (1, rows.shape[1]), 1) // width
    return jnp.concatenate(
        [rows * (column == head).astype(F32).astype(BF16) for head in range(HEADS)], axis=0
    )


def head_spread(per_head, width):
    return jnp.concatenate(
        [
            jnp.broadcast_to(per_head[head : head + 1], (width, per_head.shape[1]))
            for head in range(HEADS)
        ],
        axis=0,
    )


def listed_blocks(lists_ref, frame, block):
    own = lists_ref[frame, block, 0]
    return [
        lists_ref[frame, block, entry] - own + (block + HREACH)
        for entry in range(lists_ref.shape[2])
    ]


def cut_kernel(place_ref, rows_ref, *sent_refs):
    for distance, ref in enumerate(sent_refs):
        rows = ref.shape[1]
        ref[...] = rows_ref[
            :, pl.ds(pl.multiple_of((place_ref[0] ^ distance) * rows, GROUP_ROWS), rows)
        ]


def space_forward_kernel(
    lists_ref,
    place_ref,
    left_ref,
    wave_ref,
    right_ref,
    project_ref,
    turned_ref,
    combine_ref,
    act_ref,
    kv_ref,
    keys_t_ref,
    query_ref,
    probs_ref,
    inverse_sum_ref,
    attended_ref,
    *rest,
):
    *sent_refs, values_t, mixed_s = rest
    frame = pl.program_id(0)
    me = place_ref[0]
    row_count, features = wave_ref.shape[1:]
    width = features // HEADS
    block_count = row_count // BLOCK
    exponent_scale = math.log2(math.e) / math.sqrt(width)
    rows = jnp.concatenate([left_ref[0], wave_ref[0], right_ref[0]], axis=0)
    normed, _ = layer_norm(rows)
    act = normed.astype(BF16)
    act_ref[0] = act
    keys_values = dot_nn(act, project_ref[0, :, features:]).astype(BF16)
    kv_ref[0] = keys_values
    rim = left_ref.shape[1]
    own_act = act[rim : rim + row_count]
    query_ref[0] = dot_nn(own_act, project_ref[0, :, :features]).astype(BF16)
    queries_t = dot_nt(turned_ref[0, :features], own_act).astype(BF16)
    all_keys_t = dot_nt(turned_ref[0, features : 2 * features], act).astype(BF16)
    all_values_t = dot_nt(turned_ref[0, 2 * features :], act).astype(BF16)
    for place in range(block_count + 2 * HREACH):
        keys_t_ref[0, place] = all_keys_t[:, place * BLOCK : (place + 1) * BLOCK]
        values_t[place] = all_values_t[:, place * BLOCK : (place + 1) * BLOCK]
    for block in range(block_count):
        places = listed_blocks(lists_ref, frame, block)
        keys = jnp.concatenate(
            [kv_ref[0, pl.ds(place * BLOCK, BLOCK), :features] for place in places], axis=0
        )
        block_values_t = jnp.concatenate([values_t[place] for place in places], axis=1)
        query_t = queries_t[:, block * BLOCK : (block + 1) * BLOCK]
        outs = []
        for pair in range(HEADS // 2):
            scores = dot_nn(pair_group(keys, pair, width), pair_columns(query_t, pair, width))
            top = jnp.max(scores, axis=0, keepdims=True)
            exp_scores = jnp.exp2((scores - top) * exponent_scale)
            inverse_sum = 1.0 / jnp.sum(exp_scores, axis=0, keepdims=True)
            probs = exp_scores.astype(BF16)
            probs_ref[0, block, :, pair * 2 * BLOCK : (pair + 1) * 2 * BLOCK] = probs
            inverse_sum_ref[0, block, 2 * pair : 2 * pair + 1] = inverse_sum[:, :BLOCK]
            inverse_sum_ref[0, block, 2 * pair + 1 : 2 * pair + 2] = inverse_sum[:, BLOCK:]
            out = dot_nn(block_values_t[pair * 2 * width : (pair + 1) * 2 * width], probs)
            outs.append(pair_diagonal(out * inverse_sum, width))
        attended_t = jnp.concatenate(outs, axis=0)
        attended_ref[0, block] = attended_t.astype(BF16)
        mixed = (
            wave_ref[0, block * BLOCK : (block + 1) * BLOCK].astype(F32)
            + dot_nn(flip(attended_t), combine_ref[0])
        ).astype(BF16)
        mixed_s[block * BLOCK : (block + 1) * BLOCK] = mixed
    for distance, sent_ref in enumerate(sent_refs):
        sent_rows = sent_ref.shape[1]
        span = pl.ds(pl.multiple_of((me ^ distance) * sent_rows, GROUP_ROWS), sent_rows)
        sent_ref[0] = mixed_s[span]


def time_kernel(
    scale,
    count_in,
    *refs,
):
    arrived_refs, cot_refs = refs[:count_in], refs[count_in : 2 * count_in]
    project_ref, turned_ref, combine_ref = refs[2 * count_in : 2 * count_in + 3]
    grad_refs = refs[2 * count_in + 3 : 3 * count_in + 3]
    act_ref, dproj_ref, attended_t_ref, cot_ref, mixed_ref = refs[3 * count_in + 3 :]
    part_frames, row_count, features = grad_refs[0].shape
    width = features // HEADS
    count = part_frames * count_in * GROUP_ROWS
    groups = row_count // GROUP_ROWS
    exponent_scale = scale * math.log2(math.e)

    def grouped(part_refs):
        return jnp.concatenate(
            [
                ref[:, group * GROUP_ROWS : (group + 1) * GROUP_ROWS].reshape(
                    part_frames * GROUP_ROWS, features
                )
                for group in range(groups)
                for ref in part_refs
            ],
            axis=0,
        )

    rows = grouped(arrived_refs)
    cot = grouped(cot_refs)
    cot_ref[...] = cot
    normed, inverse = layer_norm(rows)
    act = normed.astype(BF16)
    act_ref[...] = act
    projected = dot_nn(act, project_ref[0]).astype(BF16)
    projected_t = dot_nt(turned_ref[0], act).astype(BF16)
    all_dattn = dot_nt(cot, combine_ref[0]).astype(BF16)
    all_dattn_t = dot_nt(combine_ref[0], cot).astype(BF16)
    key_row = lax.broadcasted_iota(jnp.int32, (count, 2 * count), 0) % GROUP_ROWS
    query_row = lax.broadcasted_iota(jnp.int32, (count, 2 * count), 1) % GROUP_ROWS
    same_row = key_row == query_row
    attended_groups, dquery_groups, dkey_groups, dvalue_groups = [], [], [], []
    for group in range(groups):
        span = slice(group * count, (group + 1) * count)
        queries = projected[span, :features]
        keys = projected[span, features : 2 * features]
        values = projected[span, 2 * features :]
        query_t = projected_t[:features, span]
        keys_t = projected_t[features : 2 * features, span]
        values_t = projected_t[2 * features :, span]
        dattn_t = all_dattn_t[:, span]
        outs, probs_parts, dscore_parts, dquery_parts = [], [], [], []
        for pair in range(HEADS // 2):
            heads = slice(pair * 2 * width, (pair + 1) * 2 * width)
            scores = dot_nn(pair_group(keys, pair, width), pair_columns(query_t, pair, width))
            scores = jnp.where(same_row, scores, -3e38)
            top = jnp.max(scores, axis=0, keepdims=True)
            exp_scores = jnp.exp2((scores - top) * exponent_scale)
            probs = (exp_scores * (1.0 / jnp.sum(exp_scores, axis=0, keepdims=True))).astype(BF16)
            probs_wide = probs.astype(F32)
            outs.append(pair_diagonal(dot_nn(values_t[heads], probs), width))
            dprobs = dot_nn(pair_group(values, pair, width), pair_columns(dattn_t, pair, width))
            delta = jnp.sum(probs_wide * dprobs, axis=0, keepdims=True)
            dscores = (probs_wide * (dprobs - delta) * scale).astype(BF16)
            dquery_parts.append(pair_diagonal(dot_nn(keys_t[heads], dscores), width))
            probs_parts.append(probs)
            dscore_parts.append(dscores)
        attended_groups.append(jnp.concatenate(outs, axis=0).astype(BF16))
        dquery_groups.append(flip(jnp.concatenate(dquery_parts, axis=0)))
        dkey_groups.append(
            dot_nn(jnp.concatenate(dscore_parts, axis=1), head_rows(queries, width)).astype(BF16)
        )
        dvalue_groups.append(
            dot_nn(jnp.concatenate(probs_parts, axis=1), head_rows(all_dattn[span], width)).astype(BF16)
        )
    attended = jnp.concatenate([flip(attended_t) for attended_t in attended_groups], axis=0)
    mixed_ref[...] = (rows.astype(F32) + dot_nn(attended, combine_ref[0])).astype(BF16)
    attended_t_ref[...] = jnp.concatenate(attended_groups, axis=1)
    dproj = jnp.concatenate(
        [jnp.concatenate(parts, axis=0) for parts in (dquery_groups, dkey_groups, dvalue_groups)],
        axis=1,
    )
    dproj_ref[...] = dproj
    dact = dot_nt(dproj, project_ref[0])
    mixed_grad = (cot.astype(F32) + norm_backward(dact, normed, inverse)).astype(BF16)
    for part, ref in enumerate(grad_refs):
        for group in range(groups):
            span = slice(group * GROUP_ROWS, (group + 1) * GROUP_ROWS)
            for frame in range(part_frames):
                start = ((group * count_in + part) * part_frames + frame) * GROUP_ROWS
                ref[frame, span] = mixed_grad[start : start + GROUP_ROWS]


def time_grads_kernel(
    factor, part_frames, row_count, place_ref, act_ref, dproj_ref, attended_t_ref, cot_ref, mixed_ref, *refs
):
    *ride_refs, stacked_s = refs
    count_in = len(ride_refs)
    features = act_ref.shape[1]
    groups = row_count // GROUP_ROWS
    grads = jnp.concatenate(
        [dot_tn(act_ref[...], dproj_ref[...]), dot_nn(attended_t_ref[...], cot_ref[...])], axis=1
    )
    stack_grads(grads * factor, stacked_s)
    chunk = stacked_s.shape[0] // count_in
    part_rows = part_frames * row_count
    for part, ref in enumerate(ride_refs):
        for group in range(groups):
            for frame in range(part_frames):
                start = ((group * count_in + part) * part_frames + frame) * GROUP_ROWS
                for lane_group in range(features // LANES):
                    row = chunk + lane_group * part_rows + frame * row_count + group * GROUP_ROWS
                    ref[row : row + GROUP_ROWS] = mixed_ref[
                        start : start + GROUP_ROWS, lane_group * LANES : (lane_group + 1) * LANES
                    ]
        ref[:chunk] = stacked_s[
            pl.ds(pl.multiple_of((place_ref[0] ^ part) * chunk, GROUP_ROWS), chunk)
        ]


def space_backward_kernel(
    scale,
    factor,
    count_in,
    lists_ref,
    place_ref,
    *refs,
):
    returned_refs = refs[:count_in]
    (
        act_ref,
        kv_ref,
        keys_t_ref,
        query_ref,
        probs_ref,
        inverse_sum_ref,
        attended_ref,
        combine_ref,
        mixed_grad_ref,
        dquery_ref,
        dkv_ref,
        stacked_ref,
        dscores_s,
        dkv_s,
        grads_s,
    ) = refs[count_in:]
    frame = pl.program_id(0)
    me = place_ref[0]
    row_count, features = mixed_grad_ref.shape[1:]
    width = features // HEADS
    block_count = row_count // BLOCK
    rim = HREACH * BLOCK
    for distance, ref in enumerate(returned_refs):
        sent_rows = ref.shape[1]
        span = pl.ds(pl.multiple_of((me ^ distance) * sent_rows, GROUP_ROWS), sent_rows)
        mixed_grad_ref[0, span] = ref[0]
    mixed_grad = mixed_grad_ref[0]
    dkv_s[...] = jnp.zeros(dkv_s.shape, F32)

    @pl.when(frame == 0)
    def _():
        grads_s[...] = jnp.zeros(grads_s.shape, F32)

    dquery_blocks = []
    for block in range(block_count):
        span = slice(block * BLOCK, (block + 1) * BLOCK)
        places = listed_blocks(lists_ref, frame, block)
        values = jnp.concatenate(
            [kv_ref[0, pl.ds(place * BLOCK, BLOCK), features:] for place in places], axis=0
        )
        block_keys_t = jnp.concatenate([keys_t_ref[0, place] for place in places], axis=1)
        block_grad = mixed_grad[span]
        attended_t = attended_ref[0, block]
        grads_s[:, 3 * features :] += dot_nn(attended_t, block_grad)
        dattn_t = dot_nt(combine_ref[0], block_grad).astype(BF16)
        dattn_wide = dattn_t.astype(F32)
        inverse_sum = inverse_sum_ref[0, block]
        scaled_dattn = flip(dattn_wide * head_spread(inverse_sum, width))
        delta = jnp.sum(
            (dattn_wide * attended_t.astype(F32)).reshape(HEADS, width, BLOCK), axis=1
        )
        row_scale = inverse_sum * scale
        dquery_parts = []
        for pair in range(HEADS // 2):
            heads = slice(pair * 2 * width, (pair + 1) * 2 * width)
            columns = slice(pair * 2 * BLOCK, (pair + 1) * 2 * BLOCK)
            pair_delta = jnp.concatenate(
                [delta[2 * pair : 2 * pair + 1], delta[2 * pair + 1 : 2 * pair + 2]], axis=1
            )
            pair_scale = jnp.concatenate(
                [row_scale[2 * pair : 2 * pair + 1], row_scale[2 * pair + 1 : 2 * pair + 2]], axis=1
            )
            dprobs = dot_nn(pair_group(values, pair, width), pair_columns(dattn_t, pair, width))
            probs = probs_ref[0, block, :, columns].astype(F32)
            dscores = (probs * ((dprobs - pair_delta) * pair_scale)).astype(BF16)
            dscores_s[:, columns] = dscores
            dquery_parts.append(pair_diagonal(dot_nn(block_keys_t[heads], dscores), width))
        dquery_blocks.append(flip(jnp.concatenate(dquery_parts, axis=0)))
        dkeys = dot_nn(dscores_s[...], head_rows(query_ref[0, span], width))
        dvalues = dot_nn(probs_ref[0, block], head_rows(scaled_dattn, width))
        for entry, place in enumerate(places):
            rows = pl.ds(place * BLOCK, BLOCK)
            listed = slice(entry * BLOCK, (entry + 1) * BLOCK)
            dkv_s[rows, :features] += dkeys[listed]
            dkv_s[rows, features:] += dvalues[listed]
    dquery = jnp.concatenate(dquery_blocks, axis=0)
    dkv = dkv_s[...].astype(BF16)
    dquery_ref[0] = dquery
    dkv_ref[0] = dkv
    grads_s[:, :features] += dot_tn(act_ref[0, rim : rim + row_count], dquery)
    grads_s[:, features : 3 * features] += dot_tn(act_ref[0], dkv)

    @pl.when(frame == pl.num_programs(0) - 1)
    def _():
        stack_grads(grads_s[...] * factor, stacked_ref)


def dact_kernel(dquery_ref, dkv_ref, project_ref, dact_ref, to_left_ref, to_right_ref):
    row_count, features = dquery_ref.shape[1:]
    rim = to_left_ref.shape[1]
    dact = dot_nt(dkv_ref[0], project_ref[0, :, features:])
    to_left_ref[0] = dact[:rim].astype(BF16)
    to_right_ref[0] = dact[rim + row_count :].astype(BF16)
    dact_ref[0] = dact[rim : rim + row_count] + dot_nt(
        dquery_ref[0], project_ref[0, :, :features]
    )


def field_kernel(place_ref, wave_ref, mixed_grad_ref, dact_ref, from_left_ref, from_right_ref, *refs):
    *ride_refs, field_ref, mixed_ref = refs
    frame = pl.program_id(0)
    row_count, features = wave_ref.shape[1:]
    normed, inverse = layer_norm(wave_ref[0])
    dact = dact_ref[0] + from_left_ref[0].astype(F32) + from_right_ref[0].astype(F32)
    field_ref[0] = (
        mixed_grad_ref[0].astype(F32) + norm_backward(dact, normed, inverse)
    ).astype(BF16)
    rows = row_count // len(ride_refs)
    lane_groups = features // LANES
    part_rows = pl.num_programs(0) * rows
    for distance, ref in enumerate(ride_refs):
        span = pl.ds(pl.multiple_of((place_ref[0] ^ distance) * rows, GROUP_ROWS), rows)
        for lane_group in range(lane_groups):
            start = ref.shape[0] - (lane_groups - lane_group) * part_rows + frame * rows
            mixed_ref[0, span, lane_group * LANES : (lane_group + 1) * LANES] = ref[
                pl.ds(pl.multiple_of(start, GROUP_ROWS), rows)
            ]


def ordered_sum(me, refs, parts_s):
    rows = parts_s.shape[1]
    for distance, ref in enumerate(refs):
        parts_s[me ^ distance] = ref[:rows]
    total = parts_s[0].astype(F32)
    for part in range(1, len(refs)):
        total = total + parts_s[part].astype(F32)
    return total.astype(BF16)


def cores_kernel(place_ref, space_ref, *refs):
    *ride_refs, kept_ref, sent_ref, parts_s, time_s = refs
    core = place_ref[1] % 2
    time_s[...] = ordered_sum(place_ref[0], ride_refs, parts_s)
    space_half, time_half = space_ref.shape[0] // 2, time_s.shape[0] // 2
    for half, ref in ((core, kept_ref), (1 - core, sent_ref)):
        ref[:space_half] = space_ref[
            pl.ds(pl.multiple_of(half * space_half, GROUP_ROWS), space_half)
        ]
        ref[space_half:] = time_s[pl.ds(pl.multiple_of(half * time_half, GROUP_ROWS), time_half)]


def split_kernel(place_ref, kept_ref, arrived_ref, *refs):
    *part_refs, time_ref, sum_s = refs
    sum_s[...] = (kept_ref[...].astype(F32) + arrived_ref[...].astype(F32)).astype(BF16)
    rows = part_refs[0].shape[0]
    for distance, ref in enumerate(part_refs):
        ref[...] = sum_s[pl.ds(pl.multiple_of((place_ref[0] ^ distance) * rows, GROUP_ROWS), rows)]
    time_ref[...] = sum_s[rows * len(part_refs) :]


def tm_kernel(count_in, place_ref, *refs):
    part_refs, time_ref, out_refs = refs[:count_in], refs[count_in], refs[count_in + 1 : -2]
    parts_s, both_s = refs[-2:]
    rows = time_ref.shape[0]
    both_s[:rows] = ordered_sum(place_ref[0], part_refs, parts_s)
    both_s[rows:] = time_ref[...]
    rows = out_refs[0].shape[0]
    me = place_ref[1] // 2
    for distance, ref in enumerate(out_refs):
        ref[...] = both_s[pl.ds(pl.multiple_of((me ^ distance) * rows, GROUP_ROWS), rows)]


def space_sum_kernel(place_ref, *refs):
    *part_refs, total_ref, parts_s = refs
    total_ref[...] = ordered_sum(place_ref[1] // 2, part_refs, parts_s)


def join_kernel(axis, group, place_ref, *refs):
    *part_refs, joined_ref = refs
    me = place_ref[axis] // group
    for distance, ref in enumerate(part_refs):
        rows = ref.shape[0]
        joined_ref[pl.ds(pl.multiple_of((me ^ distance) * rows, GROUP_ROWS), rows)] = ref[...]


def grads_kernel(time_count, place_ref, own_ref, other_ref, project_ref, combine_ref, halves_s):
    features = combine_ref.shape[1]
    core = place_ref[1] % 2
    halves_s[core] = own_ref[...]
    halves_s[1 - core] = other_ref[...]
    rows = halves_s.shape[1] // time_count // 2

    def place_rows(layer, row, piece):
        while piece.shape[0]:
            group, inner = divmod(row, features)
            taken = min(piece.shape[0], features - inner)
            start = group * LANES
            target, start = (
                (project_ref, start) if start < 3 * features else (combine_ref, start - 3 * features)
            )
            target[layer, inner : inner + taken, start : start + LANES] = piece[:taken].astype(F32)
            row, piece = row + taken, piece[taken:]

    for half in range(2):
        for part in range(time_count):
            start = 2 * part * rows
            place_rows(0, (half * time_count + part) * rows, halves_s[half, start : start + rows])
            place_rows(1, (2 * part + half) * rows, halves_s[half, start + rows : start + 2 * rows])


def stack_grads(grads, stacked_ref):
    features = grads.shape[0]
    for group in range(grads.shape[1] // LANES):
        stacked_ref[group * features : (group + 1) * features] = grads[
            :, group * LANES : (group + 1) * LANES
        ].astype(BF16)


def in_hbm(cells):
    return pltpu.with_memory_space_constraint(cells, pltpu.HBM)


def shift(cells, axis, step):
    count = lax.axis_size(axis)
    if step > 0:
        moves = [(i, i + 1) for i in range(count - 1)]
    else:
        moves = [(i + 1, i) for i in range(count - 1)]
    return lax.ppermute(cells, axis, moves)


def exchange(cells, axis, distance):
    return lax.ppermute(cells, axis, [(i, i ^ distance) for i in range(lax.axis_size(axis))])


def per_device(wave_field, cotangent, block_lists, project_weights, combine_weights):
    frame_count, row_count, features = wave_field.shape
    width = features // HEADS
    scale = 1.0 / math.sqrt(width)
    block_count = row_count // BLOCK
    list_length = block_lists.shape[-1]
    rim = HREACH * BLOCK
    extended = row_count + 2 * rim
    keys_count = list_length * BLOCK
    time_count = lax.axis_size("tm")
    all_frames = frame_count * time_count
    sent_rows = row_count // time_count
    factor = 1.0 / math.sqrt(frame_count * row_count * time_count * lax.axis_size("space"))
    params = pltpu.CompilerParams(vmem_limit_bytes=VMEM_BYTES)

    def whole(*shape):
        return pl.BlockSpec(shape, lambda f: (0,) * len(shape))

    def framed(*shape):
        return pl.BlockSpec((1, *shape), lambda f: (f,) + (0,) * len(shape))

    lists_spec = pl.BlockSpec(memory_space=pltpu.SMEM)
    project_spec = whole(1, features, 3 * features)
    turned_spec = whole(1, 3 * features, features)
    combine_spec = whole(1, features, features)
    part_spec = framed(sent_rows, features)
    whole_part = whole(frame_count, sent_rows, features)
    part_shape = jax.ShapeDtypeStruct((frame_count, sent_rows, features), BF16)
    place = jnp.stack([lax.axis_index("tm"), lax.axis_index("space")]).astype(jnp.int32)
    turned_weights = jnp.swapaxes(project_weights, 1, 2)
    wave_field, cotangent, block_lists, project_weights, combine_weights = (
        in_hbm(cells)
        for cells in (wave_field, cotangent, block_lists, project_weights, combine_weights)
    )

    from_left, from_right = (
        pltpu.with_memory_space_constraint(cells, pltpu.VMEM)
        for cells in (
            shift(wave_field[:, row_count - rim :], "space", 1),
            shift(wave_field[:, :rim], "space", -1),
        )
    )

    def over_tm(pieces):
        return [pieces[0]] + [exchange(pieces[d], "tm", d) for d in range(1, time_count)]

    vmem_spec = pl.BlockSpec(memory_space=pltpu.VMEM)
    cot_parts = pl.pallas_call(
        cut_kernel,
        grid=(1,),
        in_specs=[lists_spec, whole(frame_count, row_count, features)],
        out_specs=[whole_part] * time_count,
        out_shape=[part_shape] * time_count,
        compiler_params=params,
        name="cut_cotangent",
    )(place, cotangent)
    arrived_cot = over_tm(cot_parts)

    act, keys_values, keys_t, queries, probs, inverse_sum, attended, *parts = pl.pallas_call(
        space_forward_kernel,
        grid=(frame_count,),
        in_specs=[
            lists_spec,
            lists_spec,
            framed(rim, features),
            framed(row_count, features),
            framed(rim, features),
            project_spec,
            turned_spec,
            combine_spec,
        ],
        out_specs=[
            framed(extended, features),
            framed(extended, 2 * features),
            framed(extended // BLOCK, features, BLOCK),
            framed(row_count, features),
            framed(block_count, keys_count, HEADS * BLOCK),
            framed(block_count, HEADS, BLOCK),
            framed(block_count, features, BLOCK),
            *[part_spec] * time_count,
        ],
        out_shape=[
            jax.ShapeDtypeStruct((frame_count, extended, features), BF16),
            jax.ShapeDtypeStruct((frame_count, extended, 2 * features), BF16),
            jax.ShapeDtypeStruct((frame_count, extended // BLOCK, features, BLOCK), BF16),
            jax.ShapeDtypeStruct((frame_count, row_count, features), BF16),
            jax.ShapeDtypeStruct((frame_count, block_count, keys_count, HEADS * BLOCK), BF16),
            jax.ShapeDtypeStruct((frame_count, block_count, HEADS, BLOCK), F32),
            jax.ShapeDtypeStruct((frame_count, block_count, features, BLOCK), BF16),
            *[part_shape] * time_count,
        ],
        scratch_shapes=[
            pltpu.VMEM((block_count + 2 * HREACH, features, BLOCK), BF16),
            pltpu.VMEM((row_count, features), BF16),
        ],
        compiler_params=params,
        cost_estimate=cost(40),
        name="space_forward",
    )(
        block_lists,
        place,
        from_left,
        wave_field,
        from_right,
        project_weights,
        turned_weights,
        combine_weights,
    )

    arrived = over_tm(parts)

    def time_body(*refs):
        time_kernel(scale, time_count, *refs)

    def time_grads_body(*refs):
        time_grads_kernel(factor, frame_count, sent_rows, *refs)

    tokens = all_frames * sent_rows
    grad_rows = 4 * features // LANES * features
    ride_rows = grad_rows // time_count + frame_count * sent_rows * features // LANES
    time_shapes = [
        (tokens, features),
        (tokens, 3 * features),
        (features, tokens),
        (tokens, features),
        (tokens, features),
    ]
    time_outs = pl.pallas_call(
        time_body,
        grid=(1,),
        in_specs=[
            *[whole_part] * (2 * time_count),
            pl.BlockSpec((1, features, 3 * features), lambda f: (1, 0, 0)),
            pl.BlockSpec((1, 3 * features, features), lambda f: (1, 0, 0)),
            pl.BlockSpec((1, features, features), lambda f: (1, 0, 0)),
        ],
        out_specs=[*[whole_part] * time_count, *[whole(*shape) for shape in time_shapes]],
        out_shape=[
            *[part_shape] * time_count,
            *[jax.ShapeDtypeStruct(shape, BF16) for shape in time_shapes],
        ],
        compiler_params=params,
        cost_estimate=cost(36),
        name="time_pair",
    )(*arrived, *arrived_cot, project_weights, turned_weights, combine_weights)
    parts, time_kept = time_outs[:time_count], time_outs[time_count:]
    rides = pl.pallas_call(
        time_grads_body,
        in_specs=[lists_spec] + [vmem_spec] * len(time_kept),
        out_specs=[vmem_spec] * time_count,
        out_shape=[jax.ShapeDtypeStruct((ride_rows, LANES), BF16)] * time_count,
        scratch_shapes=[pltpu.VMEM((grad_rows, LANES), BF16)],
        compiler_params=params,
        cost_estimate=cost(6),
        name="time_grads",
    )(place, *time_kept)

    returned = over_tm(parts)
    rides = over_tm(rides)

    def backward_body(*refs):
        space_backward_kernel(scale, factor, time_count, *refs)

    mixed_grad, dquery, dkv, space_grads = pl.pallas_call(
        backward_body,
        grid=(frame_count,),
        in_specs=[
            lists_spec,
            lists_spec,
            *[part_spec] * time_count,
            framed(extended, features),
            framed(extended, 2 * features),
            framed(extended // BLOCK, features, BLOCK),
            framed(row_count, features),
            framed(block_count, keys_count, HEADS * BLOCK),
            framed(block_count, HEADS, BLOCK),
            framed(block_count, features, BLOCK),
            combine_spec,
        ],
        out_specs=[
            framed(row_count, features),
            framed(row_count, features),
            framed(extended, 2 * features),
            whole(grad_rows, LANES),
        ],
        out_shape=[
            jax.ShapeDtypeStruct((frame_count, row_count, features), BF16),
            jax.ShapeDtypeStruct((frame_count, row_count, features), BF16),
            jax.ShapeDtypeStruct((frame_count, extended, 2 * features), BF16),
            jax.ShapeDtypeStruct((grad_rows, LANES), BF16),
        ],
        scratch_shapes=[
            pltpu.VMEM((keys_count, HEADS * BLOCK), BF16),
            pltpu.VMEM((extended, 2 * features), F32),
            pltpu.VMEM((features, 4 * features), F32),
        ],
        compiler_params=params,
        cost_estimate=cost(44),
        name="space_backward",
    )(
        block_lists,
        place,
        *returned,
        act,
        keys_values,
        keys_t,
        queries,
        probs,
        inverse_sum,
        attended,
        combine_weights,
    )

    space_count = lax.axis_size("space") // 2

    def small(body, out_rows, scratch, name, *operands):
        return pl.pallas_call(
            body,
            in_specs=[lists_spec] + [vmem_spec] * len(operands),
            out_specs=[vmem_spec] * len(out_rows),
            out_shape=[jax.ShapeDtypeStruct((rows, LANES), BF16) for rows in out_rows],
            scratch_shapes=[pltpu.VMEM((*shape, LANES), BF16) for shape in scratch],
            compiler_params=params,
            name=name,
        )(place, *operands)

    def over_space(pieces):
        return [pieces[0]] + [
            exchange(pieces[d], "space", 2 * d) for d in range(1, space_count)
        ]

    def tm_body(*refs):
        tm_kernel(time_count, *refs)

    def join_space(*refs):
        join_kernel(1, 2, *refs)

    def join_tm(*refs):
        join_kernel(0, 1, *refs)

    chunk = grad_rows // time_count
    half_rows = grad_rows // 2 + chunk // 2
    kept, sent = small(
        cores_kernel,
        [half_rows] * 2,
        [(time_count, chunk), (chunk,)],
        "add_tm_time",
        space_grads,
        *rides,
    )
    other = exchange(sent, "space", 1)
    dact, to_left, to_right = pl.pallas_call(
        dact_kernel,
        grid=(frame_count,),
        in_specs=[framed(row_count, features), framed(extended, 2 * features), project_spec],
        out_specs=[framed(row_count, features), framed(rim, features), framed(rim, features)],
        out_shape=[
            jax.ShapeDtypeStruct((frame_count, row_count, features), F32),
            jax.ShapeDtypeStruct((frame_count, rim, features), BF16),
            jax.ShapeDtypeStruct((frame_count, rim, features), BF16),
        ],
        compiler_params=params,
        name="space_dact",
    )(dquery, dkv, project_weights)
    edge_left = shift(to_right, "space", 1)
    edge_right = shift(to_left, "space", -1)
    *pieces, time_piece = small(
        split_kernel, [chunk // 2] * (time_count + 1), [(half_rows,)], "add_cores", kept, other
    )
    edge_left, edge_right, *pieces = lax.optimization_barrier(
        (edge_left, edge_right, *over_tm(pieces))
    )
    pieces = small(
        tm_body,
        [chunk // space_count] * space_count,
        [(time_count, chunk // 2), (chunk,)],
        "add_tm_space",
        *pieces,
        time_piece,
    )
    (piece,) = small(
        space_sum_kernel,
        [chunk // space_count],
        [(space_count, chunk // space_count)],
        "add_space",
        *over_space(pieces),
    )
    (piece,) = small(join_space, [chunk], [], "join_space", *over_space([piece] * space_count))
    (own_half,) = small(join_tm, [grad_rows], [], "join_tm", *over_tm([piece] * time_count))
    other_half = exchange(own_half, "space", 1)

    field_grad, mixed_field = pl.pallas_call(
        field_kernel,
        grid=(frame_count,),
        in_specs=[
            lists_spec,
            *[framed(row_count, features)] * 5,
            *[whole(ride_rows, LANES)] * time_count,
        ],
        out_specs=[framed(row_count, features)] * 2,
        out_shape=[jax.ShapeDtypeStruct((frame_count, row_count, features), BF16)] * 2,
        compiler_params=params,
        name="field_grad",
    )(place, wave_field, mixed_grad, dact, edge_left, edge_right, *rides)

    def grads_body(*refs):
        grads_kernel(time_count, *refs)

    project_grad, combine_grad = pl.pallas_call(
        grads_body,
        in_specs=[lists_spec, vmem_spec, vmem_spec],
        out_specs=[vmem_spec, vmem_spec],
        out_shape=[
            jax.ShapeDtypeStruct((2, features, 3 * features), F32),
            jax.ShapeDtypeStruct((2, features, features), F32),
        ],
        scratch_shapes=[pltpu.VMEM((2, grad_rows, LANES), BF16)],
        compiler_params=params,
        name="weight_grads",
    )(place, own_half, other_half)
    return (mixed_field, field_grad, project_grad, combine_grad)


def solution(mesh):
    in_specs = (P("tm", "space", None), P("tm", "space", None), P("tm", "space", None), P(), P())
    out_specs = (P("tm", "space", None), P("tm", "space", None), P(), P())
    return jax.shard_map(
        per_device, mesh=mesh, in_specs=in_specs, out_specs=out_specs, check_vma=False
    )
```

time: 103 us -> 108 us (1.049)
  waiting for transfers between devices: 14.2 us -> 20.4 us
  starting transfers between devices: 47.6 us -> 43.3 us
  Pallas kernels: 40 us -> 41.8 us
  local copies, waits for them, and re-layouts: 0 us -> 1.4 us
    ppermute x31 -> x26, waiting for transfers between devices: 13 us -> 19.4 us  [exchange(): lax.ppermute(cells, axis, [(i, i ^ distance) for i in range(lax.axis_size...]
    ppermute x31 -> x26, starting transfers between devices: 39.8 us -> 35.9 us  [exchange(): lax.ppermute(cells, axis, [(i, i ^ distance) for i in range(lax.axis_size...]
    pallas_call x10 -> x11, Pallas kernels: 16.5 us -> 19.5 us  [the longest x1 9.74 us: per_device(): pl.pallas_call(time_body, grid=(1,), in_specs=[*[whole_part] * (2 * time_...]
    unnamed x0 -> x1, local copies, waits for them, and re-layouts: none -> 1.4 us
  transfers between devices with their start and end apart: 35 -> 30, of which waited for: 11 -> 14; matrix products, arithmetic and copies ran while one was open for 0% -> 1% of each run, Pallas kernels for 17% -> 25%
where the time goes in v3:
time: 108 us
  starting transfers between devices  43.3 us (40%)
  Pallas kernels  41.8 us (39%)
  waiting for transfers between devices  20.4 us (19%)
  local copies, waits for them, and re-layouts  1.4 us (1%)
    ppermute x26, starting transfers between devices, exchange(): lax.ppermute(cells, axis, [(i, i ^ distance) for i in range(lax.axis_size...  35.9 us
    ppermute x26, waiting for transfers between devices, exchange(): lax.ppermute(cells, axis, [(i, i ^ distance) for i in range(lax.axis_size...  19.4 us
    pallas_call x1, Pallas kernels, per_device(): pl.pallas_call(space_forward_kernel, grid=(frame_count,), in_specs=[lists...  10.2 us
    pallas_call x1, Pallas kernels, per_device(): pl.pallas_call(backward_body, grid=(frame_count,), in_specs=[lists_spec,...  9.88 us
    pallas_call x1, Pallas kernels, per_device(): pl.pallas_call(time_body, grid=(1,), in_specs=[*[whole_part] * (2 * time_...  9.74 us
    ppermute x4, starting transfers between devices, shift(): return lax.ppermute(cells, axis, moves)  7.36 us
    pallas_call x6, Pallas kernels, small(): pl.pallas_call(body, in_specs=[lists_spec] + [vmem_spec] * len(operands),...  3.77 us
    pallas_call x1, Pallas kernels, per_device(): pl.pallas_call(field_kernel, grid=(frame_count,), in_specs=[lists_spec, *...  2.23 us
  transfers between devices with their start and end apart: 30, of which 14 were waited for; matrix products, arithmetic and copies ran while one was open for 1% of the time, Pallas kernels for 25%

profile of v3, /device:TPU:0, one launch (start us, length us, event | category | flops | bytes accessed | tf_op | source)
XLA Modules:
  0.0 107.8 jit_solution(6859893104674035356)
XLA Ops:
  0.6 2.4 %collective-permute-start = (bf16[2,256,256]{2,1,0:T(8,128)(2,1)}, bf16[2,256,256]{2,1,0:T(8,128)(2,1)S(1)}, u32[]{:S(2)}, u32[]{:S(2)}) collective-permute-start(bf16[2,256,256]{2,1,0:T(8,128)(2,1)} %wave_ref.3), channel_id=1, source_target_pairs={{0,1},{1,2},{2,3},{3,4},{4,5},{5,6},{6,7},{8,9},{9,10},{10,11},{11... | collective-permute-start | bytes 786440 | tf_op jit(solution)/shard_map/ppermute | solution.py:535
  5.4 2.4 %collective-permute-start.5 = (bf16[2,64,256]{2,1,0:T(8,128)(2,1)S(1)}, bf16[2,64,256]{2,1,0:T(8,128)(2,1)S(1)}, u32[]{:S(2)}, u32[]{:S(2)}) collective-permute-start(bf16[2,64,256]{2,1,0:T(8,128)(2,1)S(1)} %get-tuple-element.65), channel_id=1, source_target_pairs={{0,8},{8,0},{16,24},{24,16},{1,9},{9,1},{17,25},{25,17},{2,10},{10... | collective-permute-start | bytes 196616 | tf_op jit(solution)/shard_map/ppermute | solution.py:539
  10.7 10.2 %space_forward.1 = (bf16[2,768,256]{2,1,0:T(8,128)(2,1)S(1)}, bf16[2,768,512]{2,1,0:T(8,128)(2,1)S(1)}, bf16[2,6,256,128]{3,2,1,0:T(8,128)(2,1)S(1)}, bf16[2,256...) custom-call(s32[2,2,4]{2,1,0:T(2,128)} %refs_0_.1, ...), custom_call_target="tpu_custom_call" | custom-call | flops 10737418240 | bytes 41943040 | tf_op jit(solution)/shard_map/space_forward/pallas_call | solution.py:600
  21.0 2.0 %collective-permute-start.2 = (bf16[2,64,256]{2,1,0:T(8,128)(2,1)S(1)}, bf16[2,64,256]{2,1,0:T(8,128)(2,1)S(1)}, u32[]{:S(2)}, u32[]{:S(2)}) collective-permute-start(bf16[2,64,256]{2,1,0:T(8,128)(2,1)S(1)} %get-tuple-element.61), channel_id=1, source_target_pairs={{0,8},{8,0},{16,24},{24,16},{1,9},{9,1},{17,25},{25,17},{2,10},{10... | collective-permute-start | bytes 196616 | tf_op jit(solution)/shard_map/ppermute | solution.py:539
  23.0 1.5 %collective-permute-start.3 = (bf16[2,64,256]{2,1,0:T(8,128)(2,1)S(1)}, bf16[2,64,256]{2,1,0:T(8,128)(2,1)S(1)}, u32[]{:S(2)}, u32[]{:S(2)}) collective-permute-start(bf16[2,64,256]{2,1,0:T(8,128)(2,1)S(1)} %get-tuple-element.62), channel_id=1, source_target_pairs={{0,16},{8,24},{16,0},{24,8},{1,17},{9,25},{17,1},{25,9},{2,18},{10... | collective-permute-start | bytes 196616 | tf_op jit(solution)/shard_map/ppermute | solution.py:539
  25.3 1.9 %collective-permute-done.3.refs_2_ = bf16[2,64,256]{2,1,0:T(8,128)(2,1)S(1)} collective-permute-done((bf16[2,64,256]{2,1,0:T(8,128)(2,1)S(1)}, bf16[2,64,256]{2,1,0:T(8,128)(2,1)S(1)}, u32[]{:S(2)}, u32[]{:S(2)}) %collective-permute-start.3) | collective-permute-done | bytes 65568 | tf_op jit(solution)/shard_map/ppermute | solution.py:539
  27.2 2.4 %collective-permute-done.4.refs_3_ = bf16[2,64,256]{2,1,0:T(8,128)(2,1)S(1)} collective-permute-done((bf16[2,64,256]{2,1,0:T(8,128)(2,1)S(1)}, bf16[2,64,256]{2,1,0:T(8,128)(2,1)S(1)}, u32[]{:S(2)}, u32[]{:S(2)}) %collective-permute-start.4) | collective-permute-done | bytes 65568 | tf_op jit(solution)/shard_map/ppermute | solution.py:539
  29.7 9.7 %time_pair.1 = (bf16[2,64,256]{2,1,0:T(8,128)(2,1)S(1)}, bf16[2,64,256]{2,1,0:T(8,128)(2,1)S(1)}, bf16[2,64,256]{2,1,0:T(8,128)(2,1)S(1)}, bf16[2,64,256]{2,1,0:...) custom-call(bf16[2,64,256]{2,1,0:T(8,128)(2,1)S(1)} %get-tuple-eleme, ...), custom_call_target="tpu_custom_call" | custom-call | flops 9663676416 | bytes 37748736 | tf_op jit(solution)/shard_map/time_pair/pallas_call | solution.py:669
  45.3 2.3 %collective-permute-start.15 = (bf16[768,128]{1,0:T(8,128)(2,1)S(1)}, bf16[768,128]{1,0:T(8,128)(2,1)S(1)}, u32[]{:S(2)}, u32[]{:S(2)}) collective-permute-start(bf16[768,128]{1,0:T(8,128)(2,1)S(1)} %get-tuple-element.94), channel_id=1, source_target_pairs={{0,24},{8,16},{16,8},{24,0},{1,25},{9,17},{17,9},{25,1},{2,26},{10... | collective-permute-start | bytes 589832 | tf_op jit(solution)/shard_map/ppermute | solution.py:539
  47.6 9.9 %space_backward.1 = (bf16[2,256,256]{2,1,0:T(8,128)(2,1)S(1)}, bf16[2,256,256]{2,1,0:T(8,128)(2,1)S(1)}, bf16[2,768,512]{2,1,0:T(8,128)(2,1)S(1)}, bf16[2048,128]{1,0:T(8,128)(2,1)S(1)}) custom-call(s32[2,2,4]{2,1,0:T(2,128)} %refs_0_.1, s32[2]{0:T(128)S(1)} %pad_add_fusion.place_ref.refs_1_.refs_0_, bf16[2,64,256]{2,1,0:T(8,128)(2,1)S(1)} %get-tuple-element.68.refs_2_, ...), custom_call_target="tpu_custom_call" | custom-call | flops 11811160064 | bytes 46137344 | tf_op jit(solution)/shard_map/space_backward/pallas_call | solution.py:705
  58.3 1.9 %space_dact.1 = (f32[2,256,256]{2,1,0:T(8,128)S(1)}, bf16[2,256,256]{2,1,0:T(8,128)(2,1)S(1)}, bf16[2,256,256]{2,1,0:T(8,128)(2,1)S(1)}) custom-call(bf16[2,256,256]{2,1,0:T(8,128)(2,1)S(1)} %get-tuple-element.80.dquery_ref, bf16[2,768,512]{2,1,0:T(8,128)(2,1)S(1)} %get-tuple-element.81.dkv_ref, bf16[2,256,768]{2,1,0:T(8,128)(2,1)} %project_ref.3), custom_call_target="tpu_custom_call" | custom-call | tf_op jit(solution)/shard_map/space_dact/pallas_call | solution.py:793
  60.2 2.4 %collective-permute-start.11 = (bf16[2,256,256]{2,1,0:T(8,128)(2,1)S(1)}, bf16[2,256,256]{2,1,0:T(8,128)(2,1)S(1)}, u32[]{:S(2)}, u32[]{:S(2)}) collective-permute-start(bf16[2,256,256]{2,1,0:T(8,128)(2,1)S(1)} %get-tuple-element.83), channel_id=1, source_target_pairs={{0,1},{1,2},{2,3},{3,4},{4,5},{5,6},{6,7},{8,9},{9,10},{10,11},{11... | collective-permute-start | bytes 786440 | tf_op jit(solution)/shard_map/ppermute | solution.py:535
  66.0 2.2 %collective-permute-start.19 = (bf16[256,128]{1,0:T(8,128)(2,1)S(1)}, bf16[256,128]{1,0:T(8,128)(2,1)S(1)}, u32[]{:S(2)}, u32[]{:S(2)}) collective-permute-start(bf16[256,128]{1,0:T(8,128)(2,1)S(1)} %get-tuple-element.100), channel_id=1, source_target_pairs={{0,24},{8,16},{16,8},{24,0},{1,25},{9,17},{17,9},{25,1},{2,26},{10... | collective-permute-start | bytes 196616 | tf_op jit(solution)/shard_map/ppermute | solution.py:539
  71.8 5.9 %collective-permute-start.20 = (bf16[128,128]{1,0:T(8,128)(2,1)S(1)}, bf16[128,128]{1,0:T(8,128)(2,1)S(1)}, u32[]{:S(2)}, u32[]{:S(2)}) collective-permute-start(bf16[128,128]{1,0:T(8,128)(2,1)S(1)} %get-tuple-element.111), channel_id=1, source_target_pairs={{0,2},{1,3},{2,0},{3,1},{4,6},{5,7},{6,4},{7,5},{8,10},{9,11},{10,... | collective-permute-start | bytes 98312 | tf_op jit(solution)/shard_map/ppermute | solution.py:539
  77.6 3.8 %collective-permute-start.21 = (bf16[128,128]{1,0:T(8,128)(2,1)S(1)}, bf16[128,128]{1,0:T(8,128)(2,1)S(1)}, u32[]{:S(2)}, u32[]{:S(2)}) collective-permute-start(bf16[128,128]{1,0:T(8,128)(2,1)S(1)} %get-tuple-element.112), channel_id=1, source_target_pairs={{0,4},{1,5},{2,6},{3,7},{4,0},{5,1},{6,2},{7,3},{8,12},{9,13},{10,... | collective-permute-start | bytes 98312 | tf_op jit(solution)/shard_map/ppermute | solution.py:539
  81.4 2.4 %collective-permute-done.21.refs_2_ = bf16[128,128]{1,0:T(8,128)(2,1)S(1)} collective-permute-done((bf16[128,128]{1,0:T(8,128)(2,1)S(1)}, bf16[128,128]{1,0:T(8,128)(2,1)S(1)}, u32[]{:S(2)}, u32[]{:S(2)}) %collective-permute-start.21) | collective-permute-done | bytes 32800 | tf_op jit(solution)/shard_map/ppermute | solution.py:539
  83.8 3.4 %collective-permute-done.22.refs_3_ = bf16[128,128]{1,0:T(8,128)(2,1)S(1)} collective-permute-done((bf16[128,128]{1,0:T(8,128)(2,1)S(1)}, bf16[128,128]{1,0:T(8,128)(2,1)S(1)}, u32[]{:S(2)}, u32[]{:S(2)}) %collective-permute-start.22) | collective-permute-done | bytes 32800 | tf_op jit(solution)/shard_map/ppermute | solution.py:539
  88.7 3.6 %collective-permute-start.25 = (bf16[128,128]{1,0:T(8,128)(2,1)S(1)}, bf16[128,128]{1,0:T(8,128)(2,1)S(1)}, u32[]{:S(2)}, u32[]{:S(2)}) collective-permute-start(bf16[128,128]{1,0:T(8,128)(2,1)S(1)} %add_space.1.refs_1_), channel_id=1, source_target_pairs={{0,6},{1,7},{2,4},{3,5},{4,2},{5,3},{6,0},{7,1},{8,14},{9,15},{10,... | collective-permute-start | bytes 98312 | tf_op jit(solution)/shard_map/ppermute | solution.py:539
  92.8 1.7 %collective-permute-done.25.refs_4_ = bf16[128,128]{1,0:T(8,128)(2,1)S(1)} collective-permute-done((bf16[128,128]{1,0:T(8,128)(2,1)S(1)}, bf16[128,128]{1,0:T(8,128)(2,1)S(1)}, u32[]{:S(2)}, u32[]{:S(2)}) %collective-permute-start.25) | collective-permute-done | bytes 32800 | tf_op jit(solution)/shard_map/ppermute | solution.py:539
  95.3 1.7 %collective-permute-start.27 = (bf16[512,128]{1,0:T(8,128)(2,1)S(1)}, bf16[512,128]{1,0:T(8,128)(2,1)S(1)}, u32[]{:S(2)}, u32[]{:S(2)}) collective-permute-start(bf16[512,128]{1,0:T(8,128)(2,1)S(1)} %join_space.1.refs_1_), channel_id=1, source_target_pairs={{0,16},{8,24},{16,0},{24,8},{1,17},{9,25},{17,1},{25,9},{2,18},{10... | collective-permute-start | bytes 393224 | tf_op jit(solution)/shard_map/ppermute | solution.py:539
  97.0 1.6 %collective-permute-start.28 = (bf16[512,128]{1,0:T(8,128)(2,1)S(1)}, bf16[512,128]{1,0:T(8,128)(2,1)S(1)}, u32[]{:S(2)}, u32[]{:S(2)}) collective-permute-start(bf16[512,128]{1,0:T(8,128)(2,1)S(1)} %join_space.1.refs_1_), channel_id=1, source_target_pairs={{0,24},{8,16},{16,8},{24,0},{1,25},{9,17},{17,9},{25,1},{2,26},{10... | collective-permute-start | bytes 393224 | tf_op jit(solution)/shard_map/ppermute | solution.py:539
  100.3 2.6 %collective-permute-done.28.refs_4_ = bf16[512,128]{1,0:T(8,128)(2,1)S(1)} collective-permute-done((bf16[512,128]{1,0:T(8,128)(2,1)S(1)}, bf16[512,128]{1,0:T(8,128)(2,1)S(1)}, u32[]{:S(2)}, u32[]{:S(2)}) %collective-permute-start.28) | collective-permute-done | bytes 131104 | tf_op jit(solution)/shard_map/ppermute | solution.py:539
  103.5 2.2 %field_grad.1 = (bf16[2,256,256]{2,1,0:T(8,128)(2,1)}, bf16[2,256,256]{2,1,0:T(8,128)(2,1)}) custom-call(s32[2]{0:T(128)S(1)} %pad_add_fusion.place_ref.refs_1_.refs_0_, bf16[2,256,256]{2,1,0:T(8,128)(2,1)} %wave_ref.3, bf16[2,256,256]{2,1,0:T(8,128)(2,1)S(1)} %get-tuple-element.79.mixed_grad_ref, f32[2,256,256]{2,1,0:T(8,128)S(1)} %get-tuple-element.82.dact_ref, ...), custom_call_target="tpu_custom_call" | custom-call | tf_op jit(solution)/shard_map/field_grad/pallas_call | solution.py:833
  105.8 2.1 %weight_grads.1 = (f32[2,256,768]{2,1,0:T(8,128)}, f32[2,256,256]{2,1,0:T(8,128)}) custom-call(s32[2]{0:T(128)S(1)} %pad_add_fusion.place_ref.refs_1_.refs_0_, bf16[2048,128]{1,0:T(8,128)(2,1)S(1)} %join_tm.1.refs_1_, bf16[2048,128]{1,0:T(8,128)(2,1)S(1)} %collective-permute-done.29.refs_2_), custom_call_target="tpu_custom_call" | custom-call | tf_op jit(solution)/shard_map/weight_grads/pallas_call | solution.py:850
  (52 shorter events, 24.6 us)
Async XLA Ops:
  0.6 10.1 %collective-permute-start = (bf16[2,256,256]{2,1,0:T(8,128)(2,1)}, bf16[2,256,256]{2,1,0:T(8,128)(2,1)S(1)}, u32[]{:S(2)}, u32[]{:S(2)}) collective-permute-start(bf16[2,256,256]{2,1,0:T(8,128)(2,1)} %wave_ref.3), channel_id=1, source_target_pairs={{0,1},{1,2},{2,3},{3,4},{4,5},{5,6},{6,7},{8,9},{9,10},{10,11},{11... | collective-permute-start | bytes 786440 | tf_op jit(solution)/shard_map/ppermute | solution.py:535
  3.0 7.7 %collective-permute-start.1 = (bf16[2,256,256]{2,1,0:T(8,128)(2,1)}, bf16[2,256,256]{2,1,0:T(8,128)(2,1)S(1)}, u32[]{:S(2)}, u32[]{:S(2)}) collective-permute-start(bf16[2,256,256]{2,1,0:T(8,128)(2,1)} %wave_ref.3), channel_id=1, source_target_pairs={{1,0},{2,1},{3,2},{4,3},{5,4},{6,5},{7,6},{9,8},{10,9},{11,10},{12... | collective-permute-start | bytes 786440 | tf_op jit(solution)/shard_map/ppermute | solution.py:535
  5.4 19.1 %collective-permute-start.5 = (bf16[2,64,256]{2,1,0:T(8,128)(2,1)S(1)}, bf16[2,64,256]{2,1,0:T(8,128)(2,1)S(1)}, u32[]{:S(2)}, u32[]{:S(2)}) collective-permute-start(bf16[2,64,256]{2,1,0:T(8,128)(2,1)S(1)} %get-tuple-element.65), channel_id=1, source_target_pairs={{0,8},{8,0},{16,24},{24,16},{1,9},{9,1},{17,25},{25,17},{2,10},{10... | collective-permute-start | bytes 196616 | tf_op jit(solution)/shard_map/ppermute | solution.py:539
  7.8 16.8 %collective-permute-start.6 = (bf16[2,64,256]{2,1,0:T(8,128)(2,1)S(1)}, bf16[2,64,256]{2,1,0:T(8,128)(2,1)S(1)}, u32[]{:S(2)}, u32[]{:S(2)}) collective-permute-start(bf16[2,64,256]{2,1,0:T(8,128)(2,1)S(1)} %get-tuple-element.66), channel_id=1, source_target_pairs={{0,16},{8,24},{16,0},{24,8},{1,17},{9,25},{17,1},{25,9},{2,18},{10... | collective-permute-start | bytes 196616 | tf_op jit(solution)/shard_map/ppermute | solution.py:539
  9.3 15.2 %collective-permute-start.7 = (bf16[2,64,256]{2,1,0:T(8,128)(2,1)S(1)}, bf16[2,64,256]{2,1,0:T(8,128)(2,1)S(1)}, u32[]{:S(2)}, u32[]{:S(2)}) collective-permute-start(bf16[2,64,256]{2,1,0:T(8,128)(2,1)S(1)} %get-tuple-element.67), channel_id=1, source_target_pairs={{0,24},{8,16},{16,8},{24,0},{1,25},{9,17},{17,9},{25,1},{2,26},{10... | collective-permute-start | bytes 196616 | tf_op jit(solution)/shard_map/ppermute | solution.py:539
  24.5 5.2 %collective-permute-start.4 = (bf16[2,64,256]{2,1,0:T(8,128)(2,1)S(1)}, bf16[2,64,256]{2,1,0:T(8,128)(2,1)S(1)}, u32[]{:S(2)}, u32[]{:S(2)}) collective-permute-start(bf16[2,64,256]{2,1,0:T(8,128)(2,1)S(1)} %get-tuple-element.63), channel_id=1, source_target_pairs={{0,24},{8,16},{16,8},{24,0},{1,25},{9,17},{17,9},{25,1},{2,26},{10... | collective-permute-start | bytes 196616 | tf_op jit(solution)/shard_map/ppermute | solution.py:539
  39.4 5.9 %collective-permute-start.10 = (bf16[2,64,256]{2,1,0:T(8,128)(2,1)S(1)}, bf16[2,64,256]{2,1,0:T(8,128)(2,1)S(1)}, u32[]{:S(2)}, u32[]{:S(2)}) collective-permute-start(bf16[2,64,256]{2,1,0:T(8,128)(2,1)S(1)} %get-tuple-element.71), channel_id=1, source_target_pairs={{0,24},{8,16},{16,8},{24,0},{1,25},{9,17},{17,9},{25,1},{2,26},{10... | collective-permute-start | bytes 196616 | tf_op jit(solution)/shard_map/ppermute | solution.py:539
  40.1 7.5 %collective-permute-start.8 = (bf16[2,64,256]{2,1,0:T(8,128)(2,1)S(1)}, bf16[2,64,256]{2,1,0:T(8,128)(2,1)S(1)}, u32[]{:S(2)}, u32[]{:S(2)}) collective-permute-start(bf16[2,64,256]{2,1,0:T(8,128)(2,1)S(1)} %get-tuple-element.69), channel_id=1, source_target_pairs={{0,8},{8,0},{16,24},{24,16},{1,9},{9,1},{17,25},{25,17},{2,10},{10... | collective-permute-start | bytes 196616 | tf_op jit(solution)/shard_map/ppermute | solution.py:539
  41.5 6.1 %collective-permute-start.9 = (bf16[2,64,256]{2,1,0:T(8,128)(2,1)S(1)}, bf16[2,64,256]{2,1,0:T(8,128)(2,1)S(1)}, u32[]{:S(2)}, u32[]{:S(2)}) collective-permute-start(bf16[2,64,256]{2,1,0:T(8,128)(2,1)S(1)} %get-tuple-element.70), channel_id=1, source_target_pairs={{0,16},{8,24},{16,0},{24,8},{1,17},{9,25},{17,1},{25,9},{2,18},{10... | collective-permute-start | bytes 196616 | tf_op jit(solution)/shard_map/ppermute | solution.py:539
  44.0 13.5 %collective-permute-start.13 = (bf16[768,128]{1,0:T(8,128)(2,1)S(1)}, bf16[768,128]{1,0:T(8,128)(2,1)S(1)}, u32[]{:S(2)}, u32[]{:S(2)}) collective-permute-start(bf16[768,128]{1,0:T(8,128)(2,1)S(1)} %get-tuple-element.92), channel_id=1, source_target_pairs={{0,8},{8,0},{16,24},{24,16},{1,9},{9,1},{17,25},{25,17},{2,10},{10... | collective-permute-start | bytes 589832 | tf_op jit(solution)/shard_map/ppermute | solution.py:539
  44.7 12.8 %collective-permute-start.14 = (bf16[768,128]{1,0:T(8,128)(2,1)S(1)}, bf16[768,128]{1,0:T(8,128)(2,1)S(1)}, u32[]{:S(2)}, u32[]{:S(2)}) collective-permute-start(bf16[768,128]{1,0:T(8,128)(2,1)S(1)} %get-tuple-element.93), channel_id=1, source_target_pairs={{0,16},{8,24},{16,0},{24,8},{1,17},{9,25},{17,1},{25,9},{2,18},{10... | collective-permute-start | bytes 589832 | tf_op jit(solution)/shard_map/ppermute | solution.py:539
  45.3 12.2 %collective-permute-start.15 = (bf16[768,128]{1,0:T(8,128)(2,1)S(1)}, bf16[768,128]{1,0:T(8,128)(2,1)S(1)}, u32[]{:S(2)}, u32[]{:S(2)}) collective-permute-start(bf16[768,128]{1,0:T(8,128)(2,1)S(1)} %get-tuple-element.94), channel_id=1, source_target_pairs={{0,24},{8,16},{16,8},{24,0},{1,25},{9,17},{17,9},{25,1},{2,26},{10... | collective-permute-start | bytes 589832 | tf_op jit(solution)/shard_map/ppermute | solution.py:539
  58.3 5.7 %collective-permute-start.16 = (bf16[1280,128]{1,0:T(8,128)(2,1)S(1)}, bf16[1280,128]{1,0:T(8,128)(2,1)S(1)}, u32[]{:S(2)}, u32[]{:S(2)}) collective-permute-start(bf16[1280,128]{1,0:T(8,128)(2,1)S(1)} %get-tuple-element.96), channel_id=1, source_target_pairs={{0,1},{1,0},{2,3},{3,2},{4,5},{5,4},{6,7},{7,6},{8,9},{9,8},{10,11... | collective-permute-start | bytes 983048 | tf_op jit(solution)/shard_map/ppermute | solution.py:539
  60.2 8.0 %collective-permute-start.11 = (bf16[2,256,256]{2,1,0:T(8,128)(2,1)S(1)}, bf16[2,256,256]{2,1,0:T(8,128)(2,1)S(1)}, u32[]{:S(2)}, u32[]{:S(2)}) collective-permute-start(bf16[2,256,256]{2,1,0:T(8,128)(2,1)S(1)} %get-tuple-element.83), channel_id=1, source_target_pairs={{0,1},{1,2},{2,3},{3,4},{4,5},{5,6},{6,7},{8,9},{9,10},{10,11},{11... | collective-permute-start | bytes 786440 | tf_op jit(solution)/shard_map/ppermute | solution.py:535
  62.7 6.6 %collective-permute-start.12 = (bf16[2,256,256]{2,1,0:T(8,128)(2,1)S(1)}, bf16[2,256,256]{2,1,0:T(8,128)(2,1)S(1)}, u32[]{:S(2)}, u32[]{:S(2)}) collective-permute-start(bf16[2,256,256]{2,1,0:T(8,128)(2,1)S(1)} %get-tuple-element.84), channel_id=1, source_target_pairs={{1,0},{2,1},{3,2},{4,3},{5,4},{6,5},{7,6},{9,8},{10,9},{11,10},{12... | collective-permute-start | bytes 786440 | tf_op jit(solution)/shard_map/ppermute | solution.py:535
  66.0 5.2 %collective-permute-start.19 = (bf16[256,128]{1,0:T(8,128)(2,1)S(1)}, bf16[256,128]{1,0:T(8,128)(2,1)S(1)}, u32[]{:S(2)}, u32[]{:S(2)}) collective-permute-start(bf16[256,128]{1,0:T(8,128)(2,1)S(1)} %get-tuple-element.100), channel_id=1, source_target_pairs={{0,24},{8,16},{16,8},{24,0},{1,25},{9,17},{17,9},{25,1},{2,26},{10... | collective-permute-start | bytes 196616 | tf_op jit(solution)/shard_map/ppermute | solution.py:539
  71.8 9.7 %collective-permute-start.20 = (bf16[128,128]{1,0:T(8,128)(2,1)S(1)}, bf16[128,128]{1,0:T(8,128)(2,1)S(1)}, u32[]{:S(2)}, u32[]{:S(2)}) collective-permute-start(bf16[128,128]{1,0:T(8,128)(2,1)S(1)} %get-tuple-element.111), channel_id=1, source_target_pairs={{0,2},{1,3},{2,0},{3,1},{4,6},{5,7},{6,4},{7,5},{8,10},{9,11},{10,... | collective-permute-start | bytes 98312 | tf_op jit(solution)/shard_map/ppermute | solution.py:539
  77.6 6.2 %collective-permute-start.21 = (bf16[128,128]{1,0:T(8,128)(2,1)S(1)}, bf16[128,128]{1,0:T(8,128)(2,1)S(1)}, u32[]{:S(2)}, u32[]{:S(2)}) collective-permute-start(bf16[128,128]{1,0:T(8,128)(2,1)S(1)} %get-tuple-element.112), channel_id=1, source_target_pairs={{0,4},{1,5},{2,6},{3,7},{4,0},{5,1},{6,2},{7,3},{8,12},{9,13},{10,... | collective-permute-start | bytes 98312 | tf_op jit(solution)/shard_map/ppermute | solution.py:539
  81.4 5.8 %collective-permute-start.22 = (bf16[128,128]{1,0:T(8,128)(2,1)S(1)}, bf16[128,128]{1,0:T(8,128)(2,1)S(1)}, u32[]{:S(2)}, u32[]{:S(2)}) collective-permute-start(bf16[128,128]{1,0:T(8,128)(2,1)S(1)} %get-tuple-element.113), channel_id=1, source_target_pairs={{0,6},{1,7},{2,4},{3,5},{4,2},{5,3},{6,0},{7,1},{8,14},{9,15},{10,... | collective-permute-start | bytes 98312 | tf_op jit(solution)/shard_map/ppermute | solution.py:539
  87.9 4.9 %collective-permute-start.24 = (bf16[128,128]{1,0:T(8,128)(2,1)S(1)}, bf16[128,128]{1,0:T(8,128)(2,1)S(1)}, u32[]{:S(2)}, u32[]{:S(2)}) collective-permute-start(bf16[128,128]{1,0:T(8,128)(2,1)S(1)} %add_space.1.refs_1_), channel_id=1, source_target_pairs={{0,4},{1,5},{2,6},{3,7},{4,0},{5,1},{6,2},{7,3},{8,12},{9,13},{10,... | collective-permute-start | bytes 98312 | tf_op jit(solution)/shard_map/ppermute | solution.py:539
  88.7 5.8 %collective-permute-start.25 = (bf16[128,128]{1,0:T(8,128)(2,1)S(1)}, bf16[128,128]{1,0:T(8,128)(2,1)S(1)}, u32[]{:S(2)}, u32[]{:S(2)}) collective-permute-start(bf16[128,128]{1,0:T(8,128)(2,1)S(1)} %add_space.1.refs_1_), channel_id=1, source_target_pairs={{0,6},{1,7},{2,4},{3,5},{4,2},{5,3},{6,0},{7,1},{8,14},{9,15},{10,... | collective-permute-start | bytes 98312 | tf_op jit(solution)/shard_map/ppermute | solution.py:539
  95.1 5.0 %collective-permute-start.26 = (bf16[512,128]{1,0:T(8,128)(2,1)S(1)}, bf16[512,128]{1,0:T(8,128)(2,1)S(1)}, u32[]{:S(2)}, u32[]{:S(2)}) collective-permute-start(bf16[512,128]{1,0:T(8,128)(2,1)S(1)} %join_space.1.refs_1_), channel_id=1, source_target_pairs={{0,8},{8,0},{16,24},{24,16},{1,9},{9,1},{17,25},{25,17},{2,10},{10... | collective-permute-start | bytes 393224 | tf_op jit(solution)/shard_map/ppermute | solution.py:539
  95.3 5.0 %collective-permute-start.27 = (bf16[512,128]{1,0:T(8,128)(2,1)S(1)}, bf16[512,128]{1,0:T(8,128)(2,1)S(1)}, u32[]{:S(2)}, u32[]{:S(2)}) collective-permute-start(bf16[512,128]{1,0:T(8,128)(2,1)S(1)} %join_space.1.refs_1_), channel_id=1, source_target_pairs={{0,16},{8,24},{16,0},{24,8},{1,17},{9,25},{17,1},{25,9},{2,18},{10... | collective-permute-start | bytes 393224 | tf_op jit(solution)/shard_map/ppermute | solution.py:539
  97.0 5.9 %collective-permute-start.28 = (bf16[512,128]{1,0:T(8,128)(2,1)S(1)}, bf16[512,128]{1,0:T(8,128)(2,1)S(1)}, u32[]{:S(2)}, u32[]{:S(2)}) collective-permute-start(bf16[512,128]{1,0:T(8,128)(2,1)S(1)} %join_space.1.refs_1_), channel_id=1, source_target_pairs={{0,24},{8,16},{16,8},{24,0},{1,25},{9,17},{17,9},{25,1},{2,26},{10... | collective-permute-start | bytes 393224 | tf_op jit(solution)/shard_map/ppermute | solution.py:539
  (6 other events, 24.2 us)

commit v4 on v3

v4 whole, which is shorter than its diff:
```python
import math

import jax
import jax.numpy as jnp
from jax import lax
from jax.experimental import pallas as pl
from jax.experimental.pallas import tpu as pltpu
from jax.sharding import PartitionSpec as P

HEADS = 8
BLOCK = 128
HREACH = 2
LANES = 128
GROUP_ROWS = 16
VMEM_BYTES = 24 * 1024 * 1024
BF16 = jnp.bfloat16
F32 = jnp.float32


epsilon = 1e-05


def cost(matmuls):
    flops = matmuls * 2 * 1024 * 256 * 512
    return pl.CostEstimate(flops=flops, bytes_accessed=flops // 256, transcendentals=flops // 1024)


def dot_nn(left, right):
    return lax.dot_general(left, right, (((1,), (0,)), ((), ())), preferred_element_type=F32)


def dot_nt(left, right):
    return lax.dot_general(left, right, (((1,), (1,)), ((), ())), preferred_element_type=F32)


def dot_tn(left, right):
    return lax.dot_general(left, right, (((0,), (0,)), ((), ())), preferred_element_type=F32)


def layer_norm(rows):
    widened = rows.astype(F32)
    centered = widened - jnp.mean(widened, axis=-1, keepdims=True)
    inverse = lax.rsqrt(jnp.mean(centered * centered, axis=-1, keepdims=True) + epsilon)
    return (centered * inverse, inverse)


def norm_backward(upstream, normed, inverse):
    mean_grad = jnp.mean(upstream, axis=-1, keepdims=True)
    mean_cross = jnp.mean(upstream * normed, axis=-1, keepdims=True)
    return inverse * (upstream - mean_grad - normed * mean_cross)


def flip(matrix):
    return matrix.astype(BF16).T


def pair_columns(rows_t, pair, width):
    count = rows_t.shape[1]
    base = (pair * 2 * width) // LANES * LANES
    parts = []
    for head in (2 * pair, 2 * pair + 1):
        start = head * width - base
        pieces = []
        if start:
            pieces.append(jnp.zeros((start, count), rows_t.dtype))
        pieces.append(rows_t[head * width : (head + 1) * width])
        if start + width < LANES:
            pieces.append(jnp.zeros((LANES - start - width, count), rows_t.dtype))
        parts.append(jnp.concatenate(pieces, axis=0))
    return jnp.concatenate(parts, axis=1)


def pair_group(matrix, pair, width):
    base = (pair * 2 * width) // LANES * LANES
    return matrix[:, base : base + LANES]


def pair_diagonal(product, width):
    count = product.shape[1] // 2
    return jnp.concatenate([product[:width, :count], product[width:, count:]], axis=0)


def head_rows(rows, width):
    column = lax.broadcasted_iota(jnp.int32, (1, rows.shape[1]), 1) // width
    return jnp.concatenate(
        [rows * (column == head).astype(F32).astype(BF16) for head in range(HEADS)], axis=0
    )


def head_spread(per_head, width):
    return jnp.concatenate(
        [
            jnp.broadcast_to(per_head[head : head + 1], (width, per_head.shape[1]))
            for head in range(HEADS)
        ],
        axis=0,
    )


def listed_blocks(lists_ref, frame, block):
    own = lists_ref[frame, block, 0]
    return [
        lists_ref[frame, block, entry] - own + (block + HREACH)
        for entry in range(lists_ref.shape[2])
    ]


def prepare_kernel(
    place_ref,
    wave_hbm,
    cot_hbm,
    project_hbm,
    combine_hbm,
    wave_ref,
    project_ref,
    turned_ref,
    combine_ref,
    *rest,
):
    *sent_refs, cot_s, sems = rest
    moves = [
        pltpu.make_async_copy(source, target, sems.at[index])
        for index, (source, target) in enumerate(
            (
                (cot_hbm, cot_s),
                (project_hbm, project_ref),
                (wave_hbm, wave_ref),
                (combine_hbm, combine_ref),
            )
        )
    ]
    for move in moves:
        move.start()
    moves[0].wait()
    for distance, ref in enumerate(sent_refs):
        rows = ref.shape[1]
        ref[...] = cot_s[
            :, pl.ds(pl.multiple_of((place_ref[0] ^ distance) * rows, GROUP_ROWS), rows)
        ]
    moves[1].wait()
    for layer in range(2):
        turned_ref[layer] = flip(project_ref[layer])
    moves[2].wait()
    moves[3].wait()


def halo_start(core, rim, row_count, near):
    after = core == 0 if near else core != 0
    return pl.multiple_of(jnp.where(after, rim + row_count, 0), BLOCK)


def space_forward_kernel(
    lists_ref,
    place_ref,
    near_ref,
    far_ref,
    wave_ref,
    project_ref,
    turned_ref,
    combine_ref,
    act_ref,
    kv_ref,
    keys_t_ref,
    query_ref,
    probs_ref,
    inverse_sum_ref,
    attended_ref,
    *rest,
):
    *sent_refs, values_t, mixed_s, extended_s = rest
    me = place_ref[0]
    core = place_ref[1] % 2
    frame_count, row_count, features = wave_ref.shape
    rim = near_ref.shape[1]
    width = features // HEADS
    block_count = row_count // BLOCK
    exponent_scale = math.log2(math.e) / math.sqrt(width)
    for frame in range(frame_count):
        extended_s[frame, rim : rim + row_count] = wave_ref[frame]
        extended_s[frame, pl.ds(halo_start(core, rim, row_count, True), rim)] = near_ref[frame]
        extended_s[frame, pl.ds(halo_start(core, rim, row_count, False), rim)] = far_ref[frame]
        normed, _ = layer_norm(extended_s[frame])
        act = normed.astype(BF16)
        act_ref[frame] = act
        kv_ref[frame] = dot_nn(act, project_ref[0, :, features:]).astype(BF16)
        own_act = act[rim : rim + row_count]
        query_ref[frame] = dot_nn(own_act, project_ref[0, :, :features]).astype(BF16)
        queries_t = dot_nt(turned_ref[0, :features], own_act).astype(BF16)
        all_keys_t = dot_nt(turned_ref[0, features : 2 * features], act).astype(BF16)
        all_values_t = dot_nt(turned_ref[0, 2 * features :], act).astype(BF16)
        for place in range(block_count + 2 * HREACH):
            keys_t_ref[frame, place] = all_keys_t[:, place * BLOCK : (place + 1) * BLOCK]
            values_t[frame, place] = all_values_t[:, place * BLOCK : (place + 1) * BLOCK]
        for block in range(block_count):
            places = listed_blocks(lists_ref, frame, block)
            keys = jnp.concatenate(
                [kv_ref[frame, pl.ds(place * BLOCK, BLOCK), :features] for place in places], axis=0
            )
            block_values_t = jnp.concatenate([values_t[frame, place] for place in places], axis=1)
            query_t = queries_t[:, block * BLOCK : (block + 1) * BLOCK]
            outs = []
            for pair in range(HEADS // 2):
                scores = dot_nn(pair_group(keys, pair, width), pair_columns(query_t, pair, width))
                top = jnp.max(scores, axis=0, keepdims=True)
                exp_scores = jnp.exp2((scores - top) * exponent_scale)
                inverse_sum = 1.0 / jnp.sum(exp_scores, axis=0, keepdims=True)
                probs = exp_scores.astype(BF16)
                probs_ref[frame, block, :, pair * 2 * BLOCK : (pair + 1) * 2 * BLOCK] = probs
                inverse_sum_ref[frame, block, 2 * pair : 2 * pair + 1] = inverse_sum[:, :BLOCK]
                inverse_sum_ref[frame, block, 2 * pair + 1 : 2 * pair + 2] = inverse_sum[:, BLOCK:]
                out = dot_nn(block_values_t[pair * 2 * width : (pair + 1) * 2 * width], probs)
                outs.append(pair_diagonal(out * inverse_sum, width))
            attended_t = jnp.concatenate(outs, axis=0)
            attended_ref[frame, :, block * BLOCK : (block + 1) * BLOCK] = attended_t.astype(BF16)
            mixed_s[frame, block * BLOCK : (block + 1) * BLOCK] = (
                wave_ref[frame, block * BLOCK : (block + 1) * BLOCK].astype(F32)
                + dot_nn(flip(attended_t), combine_ref[0])
            ).astype(BF16)
    for distance, ref in enumerate(sent_refs):
        rows = ref.shape[1]
        ref[...] = mixed_s[
            :, pl.ds(pl.multiple_of((me ^ distance) * rows, GROUP_ROWS), rows)
        ]


def time_kernel(
    scale,
    count_in,
    *refs,
):
    arrived_refs, cot_refs = refs[:count_in], refs[count_in : 2 * count_in]
    project_ref, turned_ref, combine_ref = refs[2 * count_in : 2 * count_in + 3]
    grad_refs = refs[2 * count_in + 3 : 3 * count_in + 3]
    act_ref, dproj_ref, attended_t_ref, cot_ref, mixed_ref = refs[3 * count_in + 3 :]
    part_frames, row_count, features = grad_refs[0].shape
    width = features // HEADS
    count = part_frames * count_in * GROUP_ROWS
    groups = row_count // GROUP_ROWS
    exponent_scale = scale * math.log2(math.e)

    def grouped(part_refs):
        return jnp.concatenate(
            [
                ref[:, group * GROUP_ROWS : (group + 1) * GROUP_ROWS].reshape(
                    part_frames * GROUP_ROWS, features
                )
                for group in range(groups)
                for ref in part_refs
            ],
            axis=0,
        )

    rows = grouped(arrived_refs)
    cot = grouped(cot_refs)
    cot_ref[...] = cot
    normed, inverse = layer_norm(rows)
    act = normed.astype(BF16)
    act_ref[...] = act
    projected = dot_nn(act, project_ref[1]).astype(BF16)
    projected_t = dot_nt(turned_ref[1], act).astype(BF16)
    all_dattn = dot_nt(cot, combine_ref[1]).astype(BF16)
    all_dattn_t = dot_nt(combine_ref[1], cot).astype(BF16)
    key_row = lax.broadcasted_iota(jnp.int32, (count, 2 * count), 0) % GROUP_ROWS
    query_row = lax.broadcasted_iota(jnp.int32, (count, 2 * count), 1) % GROUP_ROWS
    same_row = key_row == query_row
    attended_groups, dquery_groups, dkey_groups, dvalue_groups = [], [], [], []
    for group in range(groups):
        span = slice(group * count, (group + 1) * count)
        queries = projected[span, :features]
        keys = projected[span, features : 2 * features]
        values = projected[span, 2 * features :]
        query_t = projected_t[:features, span]
        keys_t = projected_t[features : 2 * features, span]
        values_t = projected_t[2 * features :, span]
        dattn_t = all_dattn_t[:, span]
        outs, probs_parts, dscore_parts, dquery_parts = [], [], [], []
        for pair in range(HEADS // 2):
            heads = slice(pair * 2 * width, (pair + 1) * 2 * width)
            scores = dot_nn(pair_group(keys, pair, width), pair_columns(query_t, pair, width))
            scores = jnp.where(same_row, scores, -3e38)
            top = jnp.max(scores, axis=0, keepdims=True)
            exp_scores = jnp.exp2((scores - top) * exponent_scale)
            probs = (exp_scores * (1.0 / jnp.sum(exp_scores, axis=0, keepdims=True))).astype(BF16)
            probs_wide = probs.astype(F32)
            outs.append(pair_diagonal(dot_nn(values_t[heads], probs), width))
            dprobs = dot_nn(pair_group(values, pair, width), pair_columns(dattn_t, pair, width))
            delta = jnp.sum(probs_wide * dprobs, axis=0, keepdims=True)
            dscores = (probs_wide * (dprobs - delta) * scale).astype(BF16)
            dquery_parts.append(pair_diagonal(dot_nn(keys_t[heads], dscores), width))
            probs_parts.append(probs)
            dscore_parts.append(dscores)
        attended_groups.append(jnp.concatenate(outs, axis=0).astype(BF16))
        dquery_groups.append(flip(jnp.concatenate(dquery_parts, axis=0)))
        dkey_groups.append(
            dot_nn(jnp.concatenate(dscore_parts, axis=1), head_rows(queries, width)).astype(BF16)
        )
        dvalue_groups.append(
            dot_nn(jnp.concatenate(probs_parts, axis=1), head_rows(all_dattn[span], width)).astype(BF16)
        )
    attended = jnp.concatenate([flip(attended_t) for attended_t in attended_groups], axis=0)
    mixed_ref[...] = (rows.astype(F32) + dot_nn(attended, combine_ref[1])).astype(BF16)
    attended_t_ref[...] = jnp.concatenate(attended_groups, axis=1)
    dproj = jnp.concatenate(
        [jnp.concatenate(parts, axis=0) for parts in (dquery_groups, dkey_groups, dvalue_groups)],
        axis=1,
    )
    dproj_ref[...] = dproj
    dact = dot_nt(dproj, project_ref[1])
    mixed_grad = (cot.astype(F32) + norm_backward(dact, normed, inverse)).astype(BF16)
    for part, ref in enumerate(grad_refs):
        for group in range(groups):
            span = slice(group * GROUP_ROWS, (group + 1) * GROUP_ROWS)
            for frame in range(part_frames):
                start = ((group * count_in + part) * part_frames + frame) * GROUP_ROWS
                ref[frame, span] = mixed_grad[start : start + GROUP_ROWS]


def time_grads_kernel(
    factor, part_frames, row_count, place_ref, act_ref, dproj_ref, attended_t_ref, cot_ref, mixed_ref, *refs
):
    *ride_refs, stacked_s = refs
    count_in = len(ride_refs)
    features = act_ref.shape[1]
    groups = row_count // GROUP_ROWS
    stack_grads(
        [dot_tn(act_ref[...], dproj_ref[...]), dot_nn(attended_t_ref[...], cot_ref[...])],
        factor,
        stacked_s,
    )
    chunk = stacked_s.shape[0] // count_in
    part_rows = part_frames * row_count
    for part, ref in enumerate(ride_refs):
        for group in range(groups):
            for frame in range(part_frames):
                start = ((group * count_in + part) * part_frames + frame) * GROUP_ROWS
                for lane_group in range(features // LANES):
                    row = chunk + lane_group * part_rows + frame * row_count + group * GROUP_ROWS
                    ref[row : row + GROUP_ROWS] = mixed_ref[
                        start : start + GROUP_ROWS, lane_group * LANES : (lane_group + 1) * LANES
                    ]
        ref[:chunk] = stacked_s[
            pl.ds(pl.multiple_of((place_ref[0] ^ part) * chunk, GROUP_ROWS), chunk)
        ]


def space_backward_kernel(
    scale,
    factor,
    count_in,
    lists_ref,
    place_ref,
    *refs,
):
    returned_refs = refs[:count_in]
    (
        act_ref,
        kv_ref,
        keys_t_ref,
        query_ref,
        probs_ref,
        inverse_sum_ref,
        attended_ref,
        combine_ref,
        mixed_grad_ref,
        dquery_ref,
        dkv_ref,
        stacked_ref,
        dscores_s,
        dkv_s,
    ) = refs[count_in:]
    me = place_ref[0]
    frame_count, row_count, features = mixed_grad_ref.shape
    width = features // HEADS
    block_count = row_count // BLOCK
    rim = HREACH * BLOCK
    for distance, ref in enumerate(returned_refs):
        rows = ref.shape[1]
        span = pl.ds(pl.multiple_of((me ^ distance) * rows, GROUP_ROWS), rows)
        mixed_grad_ref[:, span] = ref[...]
    for frame in range(frame_count):
        dkv_s[frame] = jnp.zeros(dkv_s.shape[1:], F32)
        all_dattn_t = dot_nt(combine_ref[0], mixed_grad_ref[frame]).astype(BF16)
        for block in range(block_count):
            span = slice(block * BLOCK, (block + 1) * BLOCK)
            places = listed_blocks(lists_ref, frame, block)
            values = jnp.concatenate(
                [kv_ref[frame, pl.ds(place * BLOCK, BLOCK), features:] for place in places], axis=0
            )
            block_keys_t = jnp.concatenate([keys_t_ref[frame, place] for place in places], axis=1)
            dattn_t = all_dattn_t[:, span]
            dattn_wide = dattn_t.astype(F32)
            inverse_sum = inverse_sum_ref[frame, block]
            scaled_dattn = flip(dattn_wide * head_spread(inverse_sum, width))
            delta = jnp.sum(
                (dattn_wide * attended_ref[frame, :, span].astype(F32)).reshape(
                    HEADS, width, BLOCK
                ),
                axis=1,
            )
            row_scale = inverse_sum * scale
            dquery_parts = []
            for pair in range(HEADS // 2):
                heads = slice(pair * 2 * width, (pair + 1) * 2 * width)
                columns = slice(pair * 2 * BLOCK, (pair + 1) * 2 * BLOCK)
                pair_delta = jnp.concatenate(
                    [delta[2 * pair : 2 * pair + 1], delta[2 * pair + 1 : 2 * pair + 2]], axis=1
                )
                pair_scale = jnp.concatenate(
                    [row_scale[2 * pair : 2 * pair + 1], row_scale[2 * pair + 1 : 2 * pair + 2]],
                    axis=1,
                )
                dprobs = dot_nn(pair_group(values, pair, width), pair_columns(dattn_t, pair, width))
                probs = probs_ref[frame, block, :, columns].astype(F32)
                dscores = (probs * ((dprobs - pair_delta) * pair_scale)).astype(BF16)
                dscores_s[frame, block, :, columns] = dscores
                dquery_parts.append(pair_diagonal(dot_nn(block_keys_t[heads], dscores), width))
            dquery_ref[frame, span] = flip(jnp.concatenate(dquery_parts, axis=0))
            dkeys = dot_nn(dscores_s[frame, block], head_rows(query_ref[frame, span], width))
            dvalues = dot_nn(probs_ref[frame, block], head_rows(scaled_dattn, width))
            for entry, place in enumerate(places):
                rows = pl.ds(place * BLOCK, BLOCK)
                listed = slice(entry * BLOCK, (entry + 1) * BLOCK)
                dkv_s[frame, rows, :features] += dkeys[listed]
                dkv_s[frame, rows, features:] += dvalues[listed]
        dkv_ref[frame] = dkv_s[frame].astype(BF16)
    extended = dkv_ref.shape[1]
    act = act_ref[...]
    own_act = act[:, rim : rim + row_count].reshape(frame_count * row_count, features)
    stack_grads(
        [
            dot_tn(own_act, dquery_ref[...].reshape(frame_count * row_count, features)),
            dot_tn(
                act.reshape(frame_count * extended, features),
                dkv_ref[...].reshape(frame_count * extended, 2 * features),
            ),
            sum(
                dot_nn(attended_ref[frame], mixed_grad_ref[frame]) for frame in range(frame_count)
            ),
        ],
        factor,
        stacked_ref,
    )


def dact_kernel(place_ref, dquery_ref, dkv_ref, project_ref, dact_ref, near_ref, far_ref, dact_s):
    frame_count, row_count, features = dquery_ref.shape
    rim = near_ref.shape[1]
    core = place_ref[1] % 2
    for frame in range(frame_count):
        dact = dot_nt(dkv_ref[frame], project_ref[0, :, features:])
        dact_s[frame] = dact.astype(BF16)
        dact_ref[frame] = dact[rim : rim + row_count] + dot_nt(
            dquery_ref[frame], project_ref[0, :, :features]
        )
    near_ref[...] = dact_s[:, pl.ds(halo_start(core, rim, row_count, True), rim)]
    far_ref[...] = dact_s[:, pl.ds(halo_start(core, rim, row_count, False), rim)]


def field_kernel(place_ref, wave_ref, mixed_grad_ref, dact_ref, near_ref, far_ref, *refs):
    *ride_refs, field_ref, mixed_ref = refs
    frame_count, row_count, features = wave_ref.shape
    rows = row_count // len(ride_refs)
    lane_groups = features // LANES
    part_rows = frame_count * rows
    for frame in range(frame_count):
        normed, inverse = layer_norm(wave_ref[frame])
        dact = dact_ref[frame] + near_ref[frame].astype(F32) + far_ref[frame].astype(F32)
        field_ref[frame] = (
            mixed_grad_ref[frame].astype(F32) + norm_backward(dact, normed, inverse)
        ).astype(BF16)
        for distance, ref in enumerate(ride_refs):
            span = pl.ds(pl.multiple_of((place_ref[0] ^ distance) * rows, GROUP_ROWS), rows)
            for lane_group in range(lane_groups):
                start = ref.shape[0] - (lane_groups - lane_group) * part_rows + frame * rows
                mixed_ref[frame, span, lane_group * LANES : (lane_group + 1) * LANES] = ref[
                    start : start + rows
                ]


def ordered_sum(me, refs, parts_s):
    rows = parts_s.shape[1]
    for distance, ref in enumerate(refs):
        parts_s[me ^ distance] = ref[:rows]
    total = parts_s[0].astype(F32)
    for part in range(1, len(refs)):
        total = total + parts_s[part].astype(F32)
    return total.astype(BF16)


def cores_kernel(place_ref, space_ref, *refs):
    *ride_refs, kept_ref, sent_ref, parts_s, time_s = refs
    core = place_ref[1] % 2
    time_s[...] = ordered_sum(place_ref[0], ride_refs, parts_s)
    space_half, time_half = space_ref.shape[0] // 2, time_s.shape[0] // 2
    for half, ref in ((core, kept_ref), (1 - core, sent_ref)):
        ref[:space_half] = space_ref[
            pl.ds(pl.multiple_of(half * space_half, GROUP_ROWS), space_half)
        ]
        ref[space_half:] = time_s[pl.ds(pl.multiple_of(half * time_half, GROUP_ROWS), time_half)]


def split_kernel(place_ref, kept_ref, arrived_ref, *refs):
    *part_refs, time_ref, sum_s = refs
    sum_s[...] = (kept_ref[...].astype(F32) + arrived_ref[...].astype(F32)).astype(BF16)
    rows = part_refs[0].shape[0]
    for distance, ref in enumerate(part_refs):
        ref[...] = sum_s[pl.ds(pl.multiple_of((place_ref[0] ^ distance) * rows, GROUP_ROWS), rows)]
    time_ref[...] = sum_s[rows * len(part_refs) :]


def tm_sum_kernel(place_ref, *refs):
    *part_refs, total_ref, parts_s = refs
    total_ref[...] = ordered_sum(place_ref[0], part_refs, parts_s)


def space_sum_kernel(place_ref, *refs):
    *part_refs, total_ref, parts_s = refs
    count_in = len(part_refs) // 2
    rows = parts_s.shape[1]
    me = place_ref[1] // 2
    total_ref[:rows] = ordered_sum(me, part_refs[:count_in], parts_s)
    total_ref[rows:] = ordered_sum(me, part_refs[count_in:], parts_s)


def join_kernel(place_ref, *refs):
    *part_refs, joined_ref = refs
    me = place_ref[0]
    for distance, ref in enumerate(part_refs):
        rows = ref.shape[0]
        joined_ref[pl.ds(pl.multiple_of((me ^ distance) * rows, GROUP_ROWS), rows)] = ref[...]


def grads_kernel(time_count, place_ref, own_ref, other_ref, project_ref, combine_ref, halves_s):
    features = combine_ref.shape[1]
    core = place_ref[1] % 2
    halves_s[core] = own_ref[...]
    halves_s[1 - core] = other_ref[...]
    rows = halves_s.shape[1] // time_count // 2

    def place_rows(layer, row, piece):
        while piece.shape[0]:
            group, inner = divmod(row, features)
            taken = min(piece.shape[0], features - inner)
            start = group * LANES
            target, start = (
                (project_ref, start) if start < 3 * features else (combine_ref, start - 3 * features)
            )
            target[layer, inner : inner + taken, start : start + LANES] = piece[:taken].astype(F32)
            row, piece = row + taken, piece[taken:]

    for half in range(2):
        for part in range(time_count):
            start = 2 * part * rows
            place_rows(0, (half * time_count + part) * rows, halves_s[half, start : start + rows])
            place_rows(1, (2 * part + half) * rows, halves_s[half, start + rows : start + 2 * rows])


def stack_grads(grads, factor, stacked_ref):
    row = 0
    for grad in grads:
        for lane in range(0, grad.shape[1], LANES):
            stacked_ref[row : row + grad.shape[0]] = (
                grad[:, lane : lane + LANES] * factor
            ).astype(BF16)
            row += grad.shape[0]


def in_hbm(cells):
    return pltpu.with_memory_space_constraint(cells, pltpu.HBM)


def swap_far(cells, axis):
    pairs = [(i, i + 1) for i in range(1, lax.axis_size(axis) - 1, 2)]
    return lax.ppermute(cells, axis, pairs + [(j, i) for i, j in pairs])


def exchange(cells, axis, distance):
    return lax.ppermute(cells, axis, [(i, i ^ distance) for i in range(lax.axis_size(axis))])


def per_device(wave_field, cotangent, block_lists, project_weights, combine_weights):
    frame_count, row_count, features = wave_field.shape
    width = features // HEADS
    scale = 1.0 / math.sqrt(width)
    block_count = row_count // BLOCK
    list_length = block_lists.shape[-1]
    rim = HREACH * BLOCK
    extended = row_count + 2 * rim
    keys_count = list_length * BLOCK
    time_count = lax.axis_size("tm")
    all_frames = frame_count * time_count
    sent_rows = row_count // time_count
    factor = 1.0 / math.sqrt(frame_count * row_count * time_count * lax.axis_size("space"))
    space_count = lax.axis_size("space") // 2
    grad_rows = 4 * features // LANES * features
    chunk = grad_rows // time_count
    half_rows = grad_rows // 2 + chunk // 2
    ride_rows = chunk + frame_count * sent_rows * features // LANES
    tokens = all_frames * sent_rows
    places = block_count + 2 * HREACH
    smem_spec = pl.BlockSpec(memory_space=pltpu.SMEM)
    vmem_spec = pl.BlockSpec(memory_space=pltpu.VMEM)
    hbm_spec = pl.BlockSpec(memory_space=pl.ANY)

    def call(body, name, scalars, operands, outs, scratch=(), matmuls=1, in_spec=vmem_spec):
        def typed(shape):
            return (shape[:-1], shape[-1]) if not isinstance(shape[-1], int) else (shape, BF16)

        return pl.pallas_call(
            body,
            in_specs=[smem_spec] * len(scalars) + [in_spec] * len(operands),
            out_specs=[vmem_spec] * len(outs),
            out_shape=[jax.ShapeDtypeStruct(*typed(shape)) for shape in outs],
            scratch_shapes=[
                pltpu.VMEM(*typed(shape)) if isinstance(shape, tuple) else shape
                for shape in scratch
            ],
            compiler_params=pltpu.CompilerParams(vmem_limit_bytes=VMEM_BYTES),
            cost_estimate=cost(matmuls),
            name=name,
        )(*scalars, *operands)

    def over_tm(pieces):
        return [pieces[0]] + [exchange(pieces[d], "tm", d) for d in range(1, time_count)]

    def over_space(piece):
        return [piece] + [exchange(piece, "space", 2 * d) for d in range(1, space_count)]

    own = (frame_count, row_count, features)
    part = (frame_count, sent_rows, features)
    near = exchange(wave_field, "space", 1)
    far = swap_far(wave_field, "space")
    place = jnp.stack([lax.axis_index("tm"), lax.axis_index("space")]).astype(jnp.int32)
    wave, project, turned, combine, *cot_parts = call(
        prepare_kernel,
        "prepare",
        [place],
        [in_hbm(cells) for cells in (wave_field, cotangent, project_weights, combine_weights)],
        [
            own,
            (2, features, 3 * features),
            (2, 3 * features, features),
            (2, features, features),
            *[part] * time_count,
        ],
        [own, pltpu.SemaphoreType.DMA((4,))],
        matmuls=8,
        in_spec=hbm_spec,
    )
    arrived_cot = over_tm(cot_parts)
    block_lists = in_hbm(block_lists)

    outs = call(
        space_forward_kernel,
        "space_forward",
        [block_lists, place],
        [near, far, wave, project, turned, combine],
        [
            (frame_count, extended, features),
            (frame_count, extended, 2 * features),
            (frame_count, places, features, BLOCK),
            own,
            (frame_count, block_count, keys_count, HEADS * BLOCK),
            (frame_count, block_count, HEADS, BLOCK, F32),
            (frame_count, features, row_count),
            *[part] * time_count,
        ],
        [(frame_count, places, features, BLOCK), own, (frame_count, extended, features)],
        matmuls=40,
    )
    kept_space, parts = outs[:7], outs[7:]
    arrived = over_tm(parts)

    def time_body(*refs):
        time_kernel(scale, time_count, *refs)

    outs = call(
        time_body,
        "time_pair",
        [],
        [*arrived, *arrived_cot, project, turned, combine],
        [
            *[part] * time_count,
            (tokens, features),
            (tokens, 3 * features),
            (features, tokens),
            (tokens, features),
            (tokens, features),
        ],
        matmuls=36,
    )
    parts, kept_time = outs[:time_count], outs[time_count:]

    def time_grads_body(*refs):
        time_grads_kernel(factor, frame_count, sent_rows, *refs)

    rides = call(
        time_grads_body,
        "time_grads",
        [place],
        kept_time,
        [(ride_rows, LANES)] * time_count,
        [(grad_rows, LANES)],
        matmuls=6,
    )
    returned = over_tm(parts)
    rides = over_tm(rides)

    def backward_body(*refs):
        space_backward_kernel(scale, factor, time_count, *refs)

    mixed_grad, dquery, dkv, space_grads = call(
        backward_body,
        "space_backward",
        [block_lists, place],
        [*returned, *kept_space, combine],
        [own, own, (frame_count, extended, 2 * features), (grad_rows, LANES)],
        [
            (frame_count, block_count, keys_count, HEADS * BLOCK),
            (frame_count, extended, 2 * features, F32),
        ],
        matmuls=44,
    )

    kept, sent = call(
        cores_kernel,
        "add_tm_time",
        [place],
        [space_grads, *rides],
        [(half_rows, LANES)] * 2,
        [(time_count, chunk, LANES), (chunk, LANES)],
    )
    other = exchange(sent, "space", 1)
    dact, to_near, to_far = call(
        dact_kernel,
        "space_dact",
        [place],
        [dquery, dkv, project],
        [(*own, F32), (frame_count, rim, features), (frame_count, rim, features)],
        [(frame_count, extended, features)],
        matmuls=3,
    )
    *space_pieces, time_piece = call(
        split_kernel,
        "add_cores",
        [place],
        [kept, other],
        [(chunk // 2, LANES)] * (time_count + 1),
        [(half_rows, LANES)],
    )
    to_near, to_far, *space_pieces = lax.optimization_barrier((to_near, to_far, *space_pieces))
    space_pieces = over_tm(space_pieces)
    time_pieces = over_space(time_piece)
    from_near = exchange(to_near, "space", 1)
    from_far = swap_far(to_far, "space")
    (space_piece,) = call(
        tm_sum_kernel,
        "add_tm_space",
        [place],
        space_pieces,
        [(chunk // 2, LANES)],
        [(time_count, chunk // 2, LANES)],
    )
    (piece,) = call(
        space_sum_kernel,
        "add_space",
        [place],
        over_space(space_piece) + time_pieces,
        [(chunk, LANES)],
        [(space_count, chunk // 2, LANES)],
    )
    joined = over_tm([piece] * time_count)
    field_grad, mixed_field = call(
        field_kernel,
        "field_grad",
        [place],
        [wave, mixed_grad, dact, from_near, from_far, *rides],
        [own, own],
        matmuls=3,
    )
    field_grad, mixed_field, *joined = lax.optimization_barrier((field_grad, mixed_field, *joined))
    (own_half,) = call(join_kernel, "join_tm", [place], joined, [(grad_rows, LANES)])
    other_half = exchange(own_half, "space", 1)

    def grads_body(*refs):
        grads_kernel(time_count, *refs)

    project_grad, combine_grad = call(
        grads_body,
        "weight_grads",
        [place],
        [own_half, other_half],
        [(2, features, 3 * features, F32), (2, features, features, F32)],
        [(2, grad_rows, LANES)],
    )
    return (mixed_field, field_grad, project_grad, combine_grad)


def solution(mesh):
    in_specs = (P("tm", "space", None), P("tm", "space", None), P("tm", "space", None), P(), P())
    out_specs = (P("tm", "space", None), P("tm", "space", None), P(), P())
    return jax.shard_map(
        per_device, mesh=mesh, in_specs=in_specs, out_specs=out_specs, check_vma=False
    )
```

time: 108 us -> 95.8 us (0.89)
  starting transfers between devices: 43.3 us -> 35.1 us
  Pallas kernels: 41.8 us -> 38.1 us
  local copies, waits for them, and re-layouts: 1.4 us -> 0 us
  waiting for transfers between devices: 20.4 us -> 21.5 us
    ppermute x4 -> x2, starting transfers between devices: 7.36 us -> 1.33 us  [swap_far(): return lax.ppermute(cells, axis, pairs + [(j, i) for i, j in pairs])]
    pallas_call x14 -> x13, Pallas kernels: 41.8 us -> 38.1 us  [call(): pl.pallas_call(body, in_specs=[smem_spec] * len(scalars) + [in_spec] * le...]
    ppermute x26 -> x28, starting transfers between devices: 35.9 us -> 33.8 us  [exchange(): lax.ppermute(cells, axis, [(i, i ^ distance) for i in range(lax.axis_size...]
    ppermute x26 -> x28, waiting for transfers between devices: 19.4 us -> 21.5 us  [exchange(): lax.ppermute(cells, axis, [(i, i ^ distance) for i in range(lax.axis_size...]
    unnamed x1 -> x0, local copies, waits for them, and re-layouts: 1.4 us -> none
  transfers between devices with their start and end apart: 30 -> 30, of which waited for: 14 -> 15; matrix products, arithmetic and copies ran while one was open for 1% -> 0% of each run, Pallas kernels for 25% -> 26%
where the time goes in v4:
time: 95.8 us; the launch traced here: 95.5 us
  Pallas kernels  38.1 us (40%)
  starting transfers between devices  35.1 us (37%)
  waiting for transfers between devices  21.5 us (22%)
    pallas_call x13, Pallas kernels, call(): pl.pallas_call(body, in_specs=[smem_spec] * len(scalars) + [in_spec] * le...  38.1 us
    ppermute x28, starting transfers between devices, exchange(): lax.ppermute(cells, axis, [(i, i ^ distance) for i in range(lax.axis_size...  33.8 us
    ppermute x28, waiting for transfers between devices, exchange(): lax.ppermute(cells, axis, [(i, i ^ distance) for i in range(lax.axis_size...  21.5 us
  transfers between devices with their start and end apart: 30, of which 15 were waited for; matrix products, arithmetic and copies ran while one was open for 0% of the time, Pallas kernels for 26%

profile of v4, /device:TPU:0, one launch (start us, length us, event | category | flops | bytes accessed | tf_op | source)
XLA Modules:
  0.0 95.5 jit_solution(10553946545845430931)
XLA Ops:
  1.9 2.1 %prepare.1 = (bf16[2,256,256]{2,1,0:T(8,128)(2,1)S(1)}, bf16[2,256,768]{2,1,0:T(8,128)(2,1)S(1)}, bf16[2,768,256]{2,1,0:T(8,128)(2,1)S(1)}, bf16[2,256,256]{2,1,...) custom-call(s32[2]{0:T(128)S(1)} %pad_add_fusion.place_ref.refs_1_.r, ...), custom_call_target="tpu_custom_call" | custom-call | flops 2147483648 | bytes 8388608 | tf_op jit(solution)/shard_map/prepare/pallas_call | solution.py:609
  4.0 2.6 %collective-permute-start.5 = (bf16[2,64,256]{2,1,0:T(8,128)(2,1)S(1)}, bf16[2,64,256]{2,1,0:T(8,128)(2,1)S(1)}, u32[]{:S(2)}, u32[]{:S(2)}) collective-permute-start(bf16[2,64,256]{2,1,0:T(8,128)(2,1)S(1)} %get-tuple-element.75), channel_id=1, source_target_pairs={{0,8},{8,0},{16,24},{24,16},{1,9},{9,1},{17,25},{25,17},{2,10},{10... | collective-permute-start | bytes 196616 | tf_op jit(solution)/shard_map/ppermute | solution.py:578
  8.1 9.2 %space_forward.1 = (bf16[2,768,256]{2,1,0:T(8,128)(2,1)S(1)}, bf16[2,768,512]{2,1,0:T(8,128)(2,1)S(1)}, bf16[2,6,256,128]{3,2,1,0:T(8,128)(2,1)S(1)}, bf16[2,256...) custom-call(s32[2,2,4]{2,1,0:T(2,128)} %refs_0_.1, ...), custom_call_target="tpu_custom_call" | custom-call | flops 10737418240 | bytes 41943040 | tf_op jit(solution)/shard_map/space_forward/pallas_call | solution.py:609
  17.3 2.0 %collective-permute-start.2 = (bf16[2,64,256]{2,1,0:T(8,128)(2,1)S(1)}, bf16[2,64,256]{2,1,0:T(8,128)(2,1)S(1)}, u32[]{:S(2)}, u32[]{:S(2)}) collective-permute-start(bf16[2,64,256]{2,1,0:T(8,128)(2,1)S(1)} %get-tuple-element.71), channel_id=1, source_target_pairs={{0,8},{8,0},{16,24},{24,16},{1,9},{9,1},{17,25},{25,17},{2,10},{10... | collective-permute-start | bytes 196616 | tf_op jit(solution)/shard_map/ppermute | solution.py:578
  19.3 1.5 %collective-permute-start.3 = (bf16[2,64,256]{2,1,0:T(8,128)(2,1)S(1)}, bf16[2,64,256]{2,1,0:T(8,128)(2,1)S(1)}, u32[]{:S(2)}, u32[]{:S(2)}) collective-permute-start(bf16[2,64,256]{2,1,0:T(8,128)(2,1)S(1)} %get-tuple-element.72), channel_id=1, source_target_pairs={{0,16},{8,24},{16,0},{24,8},{1,17},{9,25},{17,1},{25,9},{2,18},{10... | collective-permute-start | bytes 196616 | tf_op jit(solution)/shard_map/ppermute | solution.py:578
  21.6 1.9 %collective-permute-done.3.refs_2_ = bf16[2,64,256]{2,1,0:T(8,128)(2,1)S(1)} collective-permute-done((bf16[2,64,256]{2,1,0:T(8,128)(2,1)S(1)}, bf16[2,64,256]{2,1,0:T(8,128)(2,1)S(1)}, u32[]{:S(2)}, u32[]{:S(2)}) %collective-permute-start.3) | collective-permute-done | bytes 65568 | tf_op jit(solution)/shard_map/ppermute | solution.py:578
  23.6 2.4 %collective-permute-done.4.refs_3_ = bf16[2,64,256]{2,1,0:T(8,128)(2,1)S(1)} collective-permute-done((bf16[2,64,256]{2,1,0:T(8,128)(2,1)S(1)}, bf16[2,64,256]{2,1,0:T(8,128)(2,1)S(1)}, u32[]{:S(2)}, u32[]{:S(2)}) %collective-permute-start.4) | collective-permute-done | bytes 65568 | tf_op jit(solution)/shard_map/ppermute | solution.py:578
  26.0 8.9 %time_pair.1 = (bf16[2,64,256]{2,1,0:T(8,128)(2,1)S(1)}, bf16[2,64,256]{2,1,0:T(8,128)(2,1)S(1)}, bf16[2,64,256]{2,1,0:T(8,128)(2,1)S(1)}, bf16[2,64,256]{2,1,0:...) custom-call(bf16[2,64,256]{2,1,0:T(8,128)(2,1)S(1)} %get-tuple-eleme, ...), custom_call_target="tpu_custom_call" | custom-call | flops 9663676416 | bytes 37748736 | tf_op jit(solution)/shard_map/time_pair/pallas_call | solution.py:609
  35.4 1.9 %collective-permute-start.8 = (bf16[2,64,256]{2,1,0:T(8,128)(2,1)S(1)}, bf16[2,64,256]{2,1,0:T(8,128)(2,1)S(1)}, u32[]{:S(2)}, u32[]{:S(2)}) collective-permute-start(bf16[2,64,256]{2,1,0:T(8,128)(2,1)S(1)} %get-tuple-element.79), channel_id=1, source_target_pairs={{0,8},{8,0},{16,24},{24,16},{1,9},{9,1},{17,25},{25,17},{2,10},{10... | collective-permute-start | bytes 196616 | tf_op jit(solution)/shard_map/ppermute | solution.py:578
  40.8 2.3 %collective-permute-start.13 = (bf16[768,128]{1,0:T(8,128)(2,1)S(1)}, bf16[768,128]{1,0:T(8,128)(2,1)S(1)}, u32[]{:S(2)}, u32[]{:S(2)}) collective-permute-start(bf16[768,128]{1,0:T(8,128)(2,1)S(1)} %get-tuple-element.104), channel_id=1, source_target_pairs={{0,24},{8,16},{16,8},{24,0},{1,25},{9,17},{17,9},{25,1},{2,26},{10... | collective-permute-start | bytes 589832 | tf_op jit(solution)/shard_map/ppermute | solution.py:578
  43.1 8.5 %space_backward.1 = (bf16[2,256,256]{2,1,0:T(8,128)(2,1)S(1)}, bf16[2,256,256]{2,1,0:T(8,128)(2,1)S(1)}, bf16[2,768,512]{2,1,0:T(8,128)(2,1)S(1)}, bf16[2048,128]{1,0:T(8,128)(2,1)S(1)}) custom-call(s32[2,2,4]{2,1,0:T(2,128)} %refs_0_.1, s32[2]{0:T(128)S(1)} %pad_add_fusion.place_ref.refs_1_.refs_0_, bf16[2,64,256]{2,1,0:T(8,128)(2,1)S(1)} %get-tuple-element.78.refs_2_, ...), custom_call_target="tpu_custom_call" | custom-call | flops 11811160064 | bytes 46137344 | tf_op jit(solution)/shard_map/space_backward/pallas_call | solution.py:609
  56.1 2.2 %collective-permute-start.19 = (bf16[256,128]{1,0:T(8,128)(2,1)S(1)}, bf16[256,128]{1,0:T(8,128)(2,1)S(1)}, u32[]{:S(2)}, u32[]{:S(2)}) collective-permute-start(bf16[256,128]{1,0:T(8,128)(2,1)S(1)} %get-tuple-element.118), channel_id=1, source_target_pairs={{0,24},{8,16},{16,8},{24,0},{1,25},{9,17},{17,9},{25,1},{2,26},{10... | collective-permute-start | bytes 196616 | tf_op jit(solution)/shard_map/ppermute | solution.py:578
  59.2 4.5 %collective-permute-start.23 = (bf16[256,128]{1,0:T(8,128)(2,1)S(1)}, bf16[256,128]{1,0:T(8,128)(2,1)S(1)}, u32[]{:S(2)}, u32[]{:S(2)}) collective-permute-start(bf16[256,128]{1,0:T(8,128)(2,1)S(1)} %get-tuple-element.119.refs_4_), channel_id=1, source_target_pairs={{0,2},{1,3},{2,0},{3,1},{4,6},{5,7},{6,4},{7,5},{8,10},{9,11},{10,... | collective-permute-start | bytes 196616 | tf_op jit(solution)/shard_map/ppermute | solution.py:578
  63.6 3.1 %collective-permute-start.24 = (bf16[256,128]{1,0:T(8,128)(2,1)S(1)}, bf16[256,128]{1,0:T(8,128)(2,1)S(1)}, u32[]{:S(2)}, u32[]{:S(2)}) collective-permute-start(bf16[256,128]{1,0:T(8,128)(2,1)S(1)} %get-tuple-element.119.refs_4_), channel_id=1, source_target_pairs={{0,4},{1,5},{2,6},{3,7},{4,0},{5,1},{6,2},{7,3},{8,12},{9,13},{10,... | collective-permute-start | bytes 196616 | tf_op jit(solution)/shard_map/ppermute | solution.py:578
  68.2 1.8 %collective-permute-done.23.refs_5_ = bf16[256,128]{1,0:T(8,128)(2,1)S(1)} collective-permute-done((bf16[256,128]{1,0:T(8,128)(2,1)S(1)}, bf16[256,128]{1,0:T(8,128)(2,1)S(1)}, u32[]{:S(2)}, u32[]{:S(2)}) %collective-permute-start.23) | collective-permute-done | bytes 65568 | tf_op jit(solution)/shard_map/ppermute | solution.py:578
  70.0 3.0 %collective-permute-done.24.refs_6_ = bf16[256,128]{1,0:T(8,128)(2,1)S(1)} collective-permute-done((bf16[256,128]{1,0:T(8,128)(2,1)S(1)}, bf16[256,128]{1,0:T(8,128)(2,1)S(1)}, u32[]{:S(2)}, u32[]{:S(2)}) %collective-permute-start.24) | collective-permute-done | bytes 65568 | tf_op jit(solution)/shard_map/ppermute | solution.py:578
  74.9 2.1 %collective-permute-start.22 = (bf16[256,128]{1,0:T(8,128)(2,1)S(1)}, bf16[256,128]{1,0:T(8,128)(2,1)S(1)}, u32[]{:S(2)}, u32[]{:S(2)}) collective-permute-start(bf16[256,128]{1,0:T(8,128)(2,1)S(1)} %add_tm_space.1.refs_0_), channel_id=1, source_target_pairs={{0,6},{1,7},{2,4},{3,5},{4,2},{5,3},{6,0},{7,1},{8,14},{9,15},{10,... | collective-permute-start | bytes 196616 | tf_op jit(solution)/shard_map/ppermute | solution.py:578
  77.0 3.0 %collective-permute-done.21.refs_2_ = bf16[256,128]{1,0:T(8,128)(2,1)S(1)} collective-permute-done((bf16[256,128]{1,0:T(8,128)(2,1)S(1)}, bf16[256,128]{1,0:T(8,128)(2,1)S(1)}, u32[]{:S(2)}, u32[]{:S(2)}) %collective-permute-start.21) | collective-permute-done | bytes 65568 | tf_op jit(solution)/shard_map/ppermute | solution.py:578
  80.0 1.6 %collective-permute-done.22.refs_3_ = bf16[256,128]{1,0:T(8,128)(2,1)S(1)} collective-permute-done((bf16[256,128]{1,0:T(8,128)(2,1)S(1)}, bf16[256,128]{1,0:T(8,128)(2,1)S(1)}, u32[]{:S(2)}, u32[]{:S(2)}) %collective-permute-start.22) | collective-permute-done | bytes 65568 | tf_op jit(solution)/shard_map/ppermute | solution.py:578
  83.6 2.1 %collective-permute-start.28 = (bf16[512,128]{1,0:T(8,128)(2,1)S(1)}, bf16[512,128]{1,0:T(8,128)(2,1)S(1)}, u32[]{:S(2)}, u32[]{:S(2)}) collective-permute-start(bf16[512,128]{1,0:T(8,128)(2,1)S(1)} %add_space.1.refs_0_), channel_id=1, source_target_pairs={{0,24},{8,16},{16,8},{24,0},{1,25},{9,17},{17,9},{25,1},{2,26},{10... | collective-permute-start | bytes 393224 | tf_op jit(solution)/shard_map/ppermute | solution.py:578
  85.8 1.8 %field_grad.1 = (bf16[2,256,256]{2,1,0:T(8,128)(2,1)}, bf16[2,256,256]{2,1,0:T(8,128)(2,1)}) custom-call(s32[2]{0:T(128)S(1)} %pad_add_fusion.place_ref.refs_1_.refs_0_, bf16[2,256,256]{2,1,0:T(8,128)(2,1)S(1)} %get-tuple-element.66.wave_ref, bf16[2,256,256]{2,1,0:T(8,128)(2,1)S(1)} %get-tuple-element.89.mixed_grad_ref, ...), custom_call_target="tpu_custom_call" | custom-call | flops 805306368 | bytes 3145728 | tf_op jit(solution)/shard_map/field_grad/pallas_call | solution.py:609
  88.9 2.0 %collective-permute-done.28.refs_3_ = bf16[512,128]{1,0:T(8,128)(2,1)S(1)} collective-permute-done((bf16[512,128]{1,0:T(8,128)(2,1)S(1)}, bf16[512,128]{1,0:T(8,128)(2,1)S(1)}, u32[]{:S(2)}, u32[]{:S(2)}) %collective-permute-start.28) | collective-permute-done | bytes 131104 | tf_op jit(solution)/shard_map/ppermute | solution.py:578
  91.6 1.9 %collective-permute-done.29.refs_2_ = bf16[2048,128]{1,0:T(8,128)(2,1)S(1)} collective-permute-done((bf16[2048,128]{1,0:T(8,128)(2,1)S(1)}, bf16[2048,128]{1,0:T(8,128)(2,1)S(1)}, u32[]{:S(2)}, u32[]{:S(2)}) %collective-permute-start.29) | collective-permute-done | bytes 524320 | tf_op jit(solution)/shard_map/ppermute | solution.py:578
  93.5 2.1 %weight_grads.1 = (f32[2,256,768]{2,1,0:T(8,128)}, f32[2,256,256]{2,1,0:T(8,128)}) custom-call(s32[2]{0:T(128)S(1)} %pad_add_fusion.place_ref.refs_1_.refs_0_, bf16[2048,128]{1,0:T(8,128)(2,1)S(1)} %join_tm.1.refs_1_, bf16[2048,128]{1,0:T(8,128)(2,1)S(1)} %collective-permute-done.29.refs_2_), custom_call_target="tpu_custom_call" | custom-call | flops 268435456 | bytes 1048576 | tf_op jit(solution)/shard_map/weight_grads/pallas_call | solution.py:609
  (50 shorter events, 20.3 us)
Async XLA Ops:
  0.6 7.5 %collective-permute-start = (bf16[2,256,256]{2,1,0:T(8,128)(2,1)}, bf16[2,256,256]{2,1,0:T(8,128)(2,1)S(1)}, u32[]{:S(2)}, u32[]{:S(2)}) collective-permute-start(bf16[2,256,256]{2,1,0:T(8,128)(2,1)} %wave_hbm.1), channel_id=1, source_target_pairs={{0,1},{1,0},{2,3},{3,2},{4,5},{5,4},{6,7},{7,6},{8,9},{9,8},{10,11... | collective-permute-start | bytes 786440 | tf_op jit(solution)/shard_map/ppermute | solution.py:578
  1.1 6.9 %collective-permute-start.1 = (bf16[2,256,256]{2,1,0:T(8,128)(2,1)}, bf16[2,256,256]{2,1,0:T(8,128)(2,1)S(1)}, u32[]{:S(2)}, u32[]{:S(2)}) collective-permute-start(bf16[2,256,256]{2,1,0:T(8,128)(2,1)} %wave_hbm.1), channel_id=1, source_target_pairs={{1,2},{3,4},{5,6},{2,1},{4,3},{6,5},{9,10},{11,12},{13,14},{10,9},... | collective-permute-start | bytes 786440 | tf_op jit(solution)/shard_map/ppermute | solution.py:574
  4.0 16.9 %collective-permute-start.5 = (bf16[2,64,256]{2,1,0:T(8,128)(2,1)S(1)}, bf16[2,64,256]{2,1,0:T(8,128)(2,1)S(1)}, u32[]{:S(2)}, u32[]{:S(2)}) collective-permute-start(bf16[2,64,256]{2,1,0:T(8,128)(2,1)S(1)} %get-tuple-element.75), channel_id=1, source_target_pairs={{0,8},{8,0},{16,24},{24,16},{1,9},{9,1},{17,25},{25,17},{2,10},{10... | collective-permute-start | bytes 196616 | tf_op jit(solution)/shard_map/ppermute | solution.py:578
  6.5 14.3 %collective-permute-start.6 = (bf16[2,64,256]{2,1,0:T(8,128)(2,1)S(1)}, bf16[2,64,256]{2,1,0:T(8,128)(2,1)S(1)}, u32[]{:S(2)}, u32[]{:S(2)}) collective-permute-start(bf16[2,64,256]{2,1,0:T(8,128)(2,1)S(1)} %get-tuple-element.76), channel_id=1, source_target_pairs={{0,16},{8,24},{16,0},{24,8},{1,17},{9,25},{17,1},{25,9},{2,18},{10... | collective-permute-start | bytes 196616 | tf_op jit(solution)/shard_map/ppermute | solution.py:578
  8.1 12.8 %collective-permute-start.7 = (bf16[2,64,256]{2,1,0:T(8,128)(2,1)S(1)}, bf16[2,64,256]{2,1,0:T(8,128)(2,1)S(1)}, u32[]{:S(2)}, u32[]{:S(2)}) collective-permute-start(bf16[2,64,256]{2,1,0:T(8,128)(2,1)S(1)} %get-tuple-element.77), channel_id=1, source_target_pairs={{0,24},{8,16},{16,8},{24,0},{1,25},{9,17},{17,9},{25,1},{2,26},{10... | collective-permute-start | bytes 196616 | tf_op jit(solution)/shard_map/ppermute | solution.py:578
  34.9 5.8 %collective-permute-start.10 = (bf16[2,64,256]{2,1,0:T(8,128)(2,1)S(1)}, bf16[2,64,256]{2,1,0:T(8,128)(2,1)S(1)}, u32[]{:S(2)}, u32[]{:S(2)}) collective-permute-start(bf16[2,64,256]{2,1,0:T(8,128)(2,1)S(1)} %get-tuple-element.81), channel_id=1, source_target_pairs={{0,24},{8,16},{16,8},{24,0},{1,25},{9,17},{17,9},{25,1},{2,26},{10... | collective-permute-start | bytes 196616 | tf_op jit(solution)/shard_map/ppermute | solution.py:578
  35.4 7.7 %collective-permute-start.8 = (bf16[2,64,256]{2,1,0:T(8,128)(2,1)S(1)}, bf16[2,64,256]{2,1,0:T(8,128)(2,1)S(1)}, u32[]{:S(2)}, u32[]{:S(2)}) collective-permute-start(bf16[2,64,256]{2,1,0:T(8,128)(2,1)S(1)} %get-tuple-element.79), channel_id=1, source_target_pairs={{0,8},{8,0},{16,24},{24,16},{1,9},{9,1},{17,25},{25,17},{2,10},{10... | collective-permute-start | bytes 196616 | tf_op jit(solution)/shard_map/ppermute | solution.py:578
  37.3 5.8 %collective-permute-start.9 = (bf16[2,64,256]{2,1,0:T(8,128)(2,1)S(1)}, bf16[2,64,256]{2,1,0:T(8,128)(2,1)S(1)}, u32[]{:S(2)}, u32[]{:S(2)}) collective-permute-start(bf16[2,64,256]{2,1,0:T(8,128)(2,1)S(1)} %get-tuple-element.80), channel_id=1, source_target_pairs={{0,16},{8,24},{16,0},{24,8},{1,17},{9,25},{17,1},{25,9},{2,18},{10... | collective-permute-start | bytes 196616 | tf_op jit(solution)/shard_map/ppermute | solution.py:578
  39.5 12.0 %collective-permute-start.11 = (bf16[768,128]{1,0:T(8,128)(2,1)S(1)}, bf16[768,128]{1,0:T(8,128)(2,1)S(1)}, u32[]{:S(2)}, u32[]{:S(2)}) collective-permute-start(bf16[768,128]{1,0:T(8,128)(2,1)S(1)} %get-tuple-element.102), channel_id=1, source_target_pairs={{0,8},{8,0},{16,24},{24,16},{1,9},{9,1},{17,25},{25,17},{2,10},{10... | collective-permute-start | bytes 589832 | tf_op jit(solution)/shard_map/ppermute | solution.py:578
  40.1 11.4 %collective-permute-start.12 = (bf16[768,128]{1,0:T(8,128)(2,1)S(1)}, bf16[768,128]{1,0:T(8,128)(2,1)S(1)}, u32[]{:S(2)}, u32[]{:S(2)}) collective-permute-start(bf16[768,128]{1,0:T(8,128)(2,1)S(1)} %get-tuple-element.103), channel_id=1, source_target_pairs={{0,16},{8,24},{16,0},{24,8},{1,17},{9,25},{17,1},{25,9},{2,18},{10... | collective-permute-start | bytes 589832 | tf_op jit(solution)/shard_map/ppermute | solution.py:578
  40.8 10.8 %collective-permute-start.13 = (bf16[768,128]{1,0:T(8,128)(2,1)S(1)}, bf16[768,128]{1,0:T(8,128)(2,1)S(1)}, u32[]{:S(2)}, u32[]{:S(2)}) collective-permute-start(bf16[768,128]{1,0:T(8,128)(2,1)S(1)} %get-tuple-element.104), channel_id=1, source_target_pairs={{0,24},{8,16},{16,8},{24,0},{1,25},{9,17},{17,9},{25,1},{2,26},{10... | collective-permute-start | bytes 589832 | tf_op jit(solution)/shard_map/ppermute | solution.py:578
  55.3 8.3 %collective-permute-start.18 = (bf16[256,128]{1,0:T(8,128)(2,1)S(1)}, bf16[256,128]{1,0:T(8,128)(2,1)S(1)}, u32[]{:S(2)}, u32[]{:S(2)}) collective-permute-start(bf16[256,128]{1,0:T(8,128)(2,1)S(1)} %get-tuple-element.117), channel_id=1, source_target_pairs={{0,16},{8,24},{16,0},{24,8},{1,17},{9,25},{17,1},{25,9},{2,18},{10... | collective-permute-start | bytes 196616 | tf_op jit(solution)/shard_map/ppermute | solution.py:578
  56.1 10.7 %collective-permute-start.19 = (bf16[256,128]{1,0:T(8,128)(2,1)S(1)}, bf16[256,128]{1,0:T(8,128)(2,1)S(1)}, u32[]{:S(2)}, u32[]{:S(2)}) collective-permute-start(bf16[256,128]{1,0:T(8,128)(2,1)S(1)} %get-tuple-element.118), channel_id=1, source_target_pairs={{0,24},{8,16},{16,8},{24,0},{1,25},{9,17},{17,9},{25,1},{2,26},{10... | collective-permute-start | bytes 196616 | tf_op jit(solution)/shard_map/ppermute | solution.py:578
  58.3 27.5 %collective-permute-start.15 = (bf16[2,256,256]{2,1,0:T(8,128)(2,1)S(1)}, bf16[2,256,256]{2,1,0:T(8,128)(2,1)S(1)}, u32[]{:S(2)}, u32[]{:S(2)}) collective-permute-start(bf16[2,256,256]{2,1,0:T(8,128)(2,1)S(1)} %get-tuple-element.111), channel_id=1, source_target_pairs={{0,1},{1,0},{2,3},{3,2},{4,5},{5,4},{6,7},{7,6},{8,9},{9,8},{10,11... | collective-permute-start | bytes 786440 | tf_op jit(solution)/shard_map/ppermute | solution.py:578
  58.3 27.5 %collective-permute-start.16 = (bf16[2,256,256]{2,1,0:T(8,128)(2,1)S(1)}, bf16[2,256,256]{2,1,0:T(8,128)(2,1)S(1)}, u32[]{:S(2)}, u32[]{:S(2)}) collective-permute-start(bf16[2,256,256]{2,1,0:T(8,128)(2,1)S(1)} %get-tuple-element.112), channel_id=1, source_target_pairs={{1,2},{3,4},{5,6},{2,1},{4,3},{6,5},{9,10},{11,12},{13,14},{10,9},... | collective-permute-start | bytes 786440 | tf_op jit(solution)/shard_map/ppermute | solution.py:574
  59.2 10.8 %collective-permute-start.23 = (bf16[256,128]{1,0:T(8,128)(2,1)S(1)}, bf16[256,128]{1,0:T(8,128)(2,1)S(1)}, u32[]{:S(2)}, u32[]{:S(2)}) collective-permute-start(bf16[256,128]{1,0:T(8,128)(2,1)S(1)} %get-tuple-element.119.refs_4_), channel_id=1, source_target_pairs={{0,2},{1,3},{2,0},{3,1},{4,6},{5,7},{6,4},{7,5},{8,10},{9,11},{10,... | collective-permute-start | bytes 196616 | tf_op jit(solution)/shard_map/ppermute | solution.py:578
  63.6 9.3 %collective-permute-start.24 = (bf16[256,128]{1,0:T(8,128)(2,1)S(1)}, bf16[256,128]{1,0:T(8,128)(2,1)S(1)}, u32[]{:S(2)}, u32[]{:S(2)}) collective-permute-start(bf16[256,128]{1,0:T(8,128)(2,1)S(1)} %get-tuple-element.119.refs_4_), channel_id=1, source_target_pairs={{0,4},{1,5},{2,6},{3,7},{4,0},{5,1},{6,2},{7,3},{8,12},{9,13},{10,... | collective-permute-start | bytes 196616 | tf_op jit(solution)/shard_map/ppermute | solution.py:578
  66.8 8.1 %collective-permute-start.25 = (bf16[256,128]{1,0:T(8,128)(2,1)S(1)}, bf16[256,128]{1,0:T(8,128)(2,1)S(1)}, u32[]{:S(2)}, u32[]{:S(2)}) collective-permute-start(bf16[256,128]{1,0:T(8,128)(2,1)S(1)} %get-tuple-element.119.refs_4_), channel_id=1, source_target_pairs={{0,6},{1,7},{2,4},{3,5},{4,2},{5,3},{6,0},{7,1},{8,14},{9,15},{10,... | collective-permute-start | bytes 196616 | tf_op jit(solution)/shard_map/ppermute | solution.py:578
  70.0 7.0 %collective-permute-start.20 = (bf16[256,128]{1,0:T(8,128)(2,1)S(1)}, bf16[256,128]{1,0:T(8,128)(2,1)S(1)}, u32[]{:S(2)}, u32[]{:S(2)}) collective-permute-start(bf16[256,128]{1,0:T(8,128)(2,1)S(1)} %add_tm_space.1.refs_0_), channel_id=1, source_target_pairs={{0,2},{1,3},{2,0},{3,1},{4,6},{5,7},{6,4},{7,5},{8,10},{9,11},{10,... | collective-permute-start | bytes 196616 | tf_op jit(solution)/shard_map/ppermute | solution.py:578
  73.0 7.1 %collective-permute-start.21 = (bf16[256,128]{1,0:T(8,128)(2,1)S(1)}, bf16[256,128]{1,0:T(8,128)(2,1)S(1)}, u32[]{:S(2)}, u32[]{:S(2)}) collective-permute-start(bf16[256,128]{1,0:T(8,128)(2,1)S(1)} %add_tm_space.1.refs_0_), channel_id=1, source_target_pairs={{0,4},{1,5},{2,6},{3,7},{4,0},{5,1},{6,2},{7,3},{8,12},{9,13},{10,... | collective-permute-start | bytes 196616 | tf_op jit(solution)/shard_map/ppermute | solution.py:578
  74.9 6.7 %collective-permute-start.22 = (bf16[256,128]{1,0:T(8,128)(2,1)S(1)}, bf16[256,128]{1,0:T(8,128)(2,1)S(1)}, u32[]{:S(2)}, u32[]{:S(2)}) collective-permute-start(bf16[256,128]{1,0:T(8,128)(2,1)S(1)} %add_tm_space.1.refs_0_), channel_id=1, source_target_pairs={{0,6},{1,7},{2,4},{3,5},{4,2},{5,3},{6,0},{7,1},{8,14},{9,15},{10,... | collective-permute-start | bytes 196616 | tf_op jit(solution)/shard_map/ppermute | solution.py:578
  82.2 6.4 %collective-permute-start.26 = (bf16[512,128]{1,0:T(8,128)(2,1)S(1)}, bf16[512,128]{1,0:T(8,128)(2,1)S(1)}, u32[]{:S(2)}, u32[]{:S(2)}) collective-permute-start(bf16[512,128]{1,0:T(8,128)(2,1)S(1)} %add_space.1.refs_0_), channel_id=1, source_target_pairs={{0,8},{8,0},{16,24},{24,16},{1,9},{9,1},{17,25},{25,17},{2,10},{10... | collective-permute-start | bytes 393224 | tf_op jit(solution)/shard_map/ppermute | solution.py:578
  82.9 6.0 %collective-permute-start.27 = (bf16[512,128]{1,0:T(8,128)(2,1)S(1)}, bf16[512,128]{1,0:T(8,128)(2,1)S(1)}, u32[]{:S(2)}, u32[]{:S(2)}) collective-permute-start(bf16[512,128]{1,0:T(8,128)(2,1)S(1)} %add_space.1.refs_0_), channel_id=1, source_target_pairs={{0,16},{8,24},{16,0},{24,8},{1,17},{9,25},{17,1},{25,9},{2,18},{10... | collective-permute-start | bytes 393224 | tf_op jit(solution)/shard_map/ppermute | solution.py:578
  83.6 7.3 %collective-permute-start.28 = (bf16[512,128]{1,0:T(8,128)(2,1)S(1)}, bf16[512,128]{1,0:T(8,128)(2,1)S(1)}, u32[]{:S(2)}, u32[]{:S(2)}) collective-permute-start(bf16[512,128]{1,0:T(8,128)(2,1)S(1)} %add_space.1.refs_0_), channel_id=1, source_target_pairs={{0,24},{8,16},{16,8},{24,0},{1,25},{9,17},{17,9},{25,1},{2,26},{10... | collective-permute-start | bytes 393224 | tf_op jit(solution)/shard_map/ppermute | solution.py:578
  (6 other events, 21.9 us)

commit v5 on v4

--- a/solution.py
+++ b/solution.py
@@ -106,7 +106,6 @@
 
 
 def prepare_kernel(
-    place_ref,
     wave_hbm,
     cot_hbm,
     project_hbm,
@@ -115,33 +114,27 @@
     project_ref,
     turned_ref,
     combine_ref,
-    *rest,
+    cot_ref,
+    sems,
 ):
-    *sent_refs, cot_s, sems = rest
     moves = [
         pltpu.make_async_copy(source, target, sems.at[index])
         for index, (source, target) in enumerate(
             (
-                (cot_hbm, cot_s),
                 (project_hbm, project_ref),
                 (wave_hbm, wave_ref),
                 (combine_hbm, combine_ref),
+                (cot_hbm, cot_ref),
             )
         )
     ]
     for move in moves:
         move.start()
     moves[0].wait()
-    for distance, ref in enumerate(sent_refs):
-        rows = ref.shape[1]
-        ref[...] = cot_s[
-            :, pl.ds(pl.multiple_of((place_ref[0] ^ distance) * rows, GROUP_ROWS), rows)
-        ]
-    moves[1].wait()
     for layer in range(2):
         turned_ref[layer] = flip(project_ref[layer])
-    moves[2].wait()
-    moves[3].wait()
+    for move in moves[1:]:
+        move.wait()
 
 
 def halo_start(core, rim, row_count, near):
@@ -155,6 +148,7 @@
     near_ref,
     far_ref,
     wave_ref,
+    cot_ref,
     project_ref,
     turned_ref,
     combine_ref,
@@ -218,9 +212,9 @@
             ).astype(BF16)
     for distance, ref in enumerate(sent_refs):
         rows = ref.shape[1]
-        ref[...] = mixed_s[
-            :, pl.ds(pl.multiple_of((me ^ distance) * rows, GROUP_ROWS), rows)
-        ]
+        span = pl.ds(pl.multiple_of((me ^ distance) * rows, GROUP_ROWS), rows)
+        ref[:, :, :features] = mixed_s[:, span]
+        ref[:, :, features:] = cot_ref[:, span]
 
 
 def time_kernel(
@@ -228,30 +222,30 @@
     count_in,
     *refs,
 ):
-    arrived_refs, cot_refs = refs[:count_in], refs[count_in : 2 * count_in]
-    project_ref, turned_ref, combine_ref = refs[2 * count_in : 2 * count_in + 3]
-    grad_refs = refs[2 * count_in + 3 : 3 * count_in + 3]
-    act_ref, dproj_ref, attended_t_ref, cot_ref, mixed_ref = refs[3 * count_in + 3 :]
+    arrived_refs = refs[:count_in]
+    project_ref, turned_ref, combine_ref = refs[count_in : count_in + 3]
+    grad_refs = refs[count_in + 3 : 2 * count_in + 3]
+    act_ref, dproj_ref, attended_t_ref, cot_ref, mixed_ref = refs[2 * count_in + 3 :]
     part_frames, row_count, features = grad_refs[0].shape
     width = features // HEADS
     count = part_frames * count_in * GROUP_ROWS
     groups = row_count // GROUP_ROWS
     exponent_scale = scale * math.log2(math.e)
 
-    def grouped(part_refs):
+    def grouped(lanes):
         return jnp.concatenate(
             [
-                ref[:, group * GROUP_ROWS : (group + 1) * GROUP_ROWS].reshape(
+                ref[:, group * GROUP_ROWS : (group + 1) * GROUP_ROWS, lanes].reshape(
                     part_frames * GROUP_ROWS, features
                 )
                 for group in range(groups)
-                for ref in part_refs
+                for ref in arrived_refs
             ],
             axis=0,
         )
 
-    rows = grouped(arrived_refs)
-    cot = grouped(cot_refs)
+    rows = grouped(slice(0, features))
+    cot = grouped(slice(features, 2 * features))
     cot_ref[...] = cot
     normed, inverse = layer_norm(rows)
     act = normed.astype(BF16)
@@ -509,17 +503,25 @@
 
 
 def tm_sum_kernel(place_ref, *refs):
-    *part_refs, total_ref, parts_s = refs
-    total_ref[...] = ordered_sum(place_ref[0], part_refs, parts_s)
-
-
-def space_sum_kernel(place_ref, *refs):
-    *part_refs, total_ref, parts_s = refs
-    count_in = len(part_refs) // 2
-    rows = parts_s.shape[1]
-    me = place_ref[1] // 2
-    total_ref[:rows] = ordered_sum(me, part_refs[:count_in], parts_s)
-    total_ref[rows:] = ordered_sum(me, part_refs[count_in:], parts_s)
+    *part_refs, time_ref, time_other_ref, space_out_ref, time_out_ref, parts_s = refs
+    space_out_ref[...] = ordered_sum(place_ref[0], part_refs, parts_s)
+    time_out_ref[...] = add_rounded(time_ref, time_other_ref)
+
+
+def add_rounded(left_ref, right_ref):
+    return (left_ref[...].astype(F32) + right_ref[...].astype(F32)).astype(BF16)
+
+
+def pairs_kernel(*refs):
+    out_refs = refs[2 * len(refs) // 3 :]
+    for index, ref in enumerate(out_refs):
+        ref[...] = add_rounded(refs[2 * index], refs[2 * index + 1])
+
+
+def both_kernel(space_ref, space_other_ref, time_ref, total_ref):
+    rows = space_ref.shape[0]
+    total_ref[:rows] = add_rounded(space_ref, space_other_ref)
+    total_ref[rows:] = time_ref[...]
 
 
 def join_kernel(place_ref, *refs):
@@ -623,38 +625,34 @@
     def over_tm(pieces):
         return [pieces[0]] + [exchange(pieces[d], "tm", d) for d in range(1, time_count)]
 
-    def over_space(piece):
-        return [piece] + [exchange(piece, "space", 2 * d) for d in range(1, space_count)]
-
     own = (frame_count, row_count, features)
     part = (frame_count, sent_rows, features)
     near = exchange(wave_field, "space", 1)
     far = swap_far(wave_field, "space")
     place = jnp.stack([lax.axis_index("tm"), lax.axis_index("space")]).astype(jnp.int32)
-    wave, project, turned, combine, *cot_parts = call(
+    wave, project, turned, combine, cot = call(
         prepare_kernel,
         "prepare",
-        [place],
+        [],
         [in_hbm(cells) for cells in (wave_field, cotangent, project_weights, combine_weights)],
         [
             own,
             (2, features, 3 * features),
             (2, 3 * features, features),
             (2, features, features),
-            *[part] * time_count,
+            own,
         ],
-        [own, pltpu.SemaphoreType.DMA((4,))],
+        [pltpu.SemaphoreType.DMA((4,))],
         matmuls=8,
         in_spec=hbm_spec,
     )
-    arrived_cot = over_tm(cot_parts)
     block_lists = in_hbm(block_lists)
 
     outs = call(
         space_forward_kernel,
         "space_forward",
         [block_lists, place],
-        [near, far, wave, project, turned, combine],
+        [near, far, wave, cot, project, turned, combine],
         [
             (frame_count, extended, features),
             (frame_count, extended, 2 * features),
@@ -663,7 +661,7 @@
             (frame_count, block_count, keys_count, HEADS * BLOCK),
             (frame_count, block_count, HEADS, BLOCK, F32),
             (frame_count, features, row_count),
-            *[part] * time_count,
+            *[(frame_count, sent_rows, 2 * features)] * time_count,
         ],
         [(frame_count, places, features, BLOCK), own, (frame_count, extended, features)],
         matmuls=40,
@@ -678,7 +676,7 @@
         time_body,
         "time_pair",
         [],
-        [*arrived, *arrived_cot, project, turned, combine],
+        [*arrived, project, turned, combine],
         [
             *[part] * time_count,
             (tokens, features),
@@ -749,25 +747,35 @@
         [(half_rows, LANES)],
     )
     to_near, to_far, *space_pieces = lax.optimization_barrier((to_near, to_far, *space_pieces))
+    steps = [2 << bit for bit in range((space_count - 1).bit_length())]
     space_pieces = over_tm(space_pieces)
-    time_pieces = over_space(time_piece)
+    time_other = exchange(time_piece, "space", steps[0])
+    from_far = swap_far(to_far, "space")
     from_near = exchange(to_near, "space", 1)
-    from_far = swap_far(to_far, "space")
-    (space_piece,) = call(
+    space_piece, time_piece = call(
         tm_sum_kernel,
         "add_tm_space",
         [place],
-        space_pieces,
-        [(chunk // 2, LANES)],
+        [*space_pieces, time_piece, time_other],
+        [(chunk // 2, LANES)] * 2,
         [(time_count, chunk // 2, LANES)],
     )
+    for step, time_step in zip(steps, steps[1:]):
+        space_other = exchange(space_piece, "space", step)
+        time_other = exchange(time_piece, "space", time_step)
+        space_piece, time_piece = call(
+            pairs_kernel,
+            "add_space",
+            [],
+            [space_piece, space_other, time_piece, time_other],
+            [(chunk // 2, LANES)] * 2,
+        )
     (piece,) = call(
-        space_sum_kernel,
-        "add_space",
-        [place],
-        over_space(space_piece) + time_pieces,
+        both_kernel,
+        "add_space_last",
+        [],
+        [space_piece, exchange(space_piece, "space", steps[-1]), time_piece],
         [(chunk, LANES)],
-        [(space_count, chunk // 2, LANES)],
     )
     joined = over_tm([piece] * time_count)
     field_grad, mixed_field = call(

time: 95.8 us -> 93.1 us (0.972)
  starting transfers between devices: 35.1 us -> 33.4 us
  Pallas kernels: 38.1 us -> 36.9 us
    ppermute x28 -> x23, starting transfers between devices: 33.8 us -> 32.1 us  [exchange(): lax.ppermute(cells, axis, [(i, i ^ distance) for i in range(lax.axis_size...]
    pallas_call x13 -> x14, Pallas kernels: 38.1 us -> 36.9 us  [call(): pl.pallas_call(body, in_specs=[smem_spec] * len(scalars) + [in_spec] * le...]
    ppermute x28 -> x23, waiting for transfers between devices: 21.5 us -> 21.7 us  [exchange(): lax.ppermute(cells, axis, [(i, i ^ distance) for i in range(lax.axis_size...]
  transfers between devices with their start and end apart: 30 -> 25, of which waited for: 15 -> 10; matrix products, arithmetic and copies ran while one was open for 0% -> 0% of each run, Pallas kernels for 26% -> 16%
where the time goes in v5:
time: 93.1 us; the launch traced here: 92.9 us
  Pallas kernels  36.9 us (40%)
  starting transfers between devices  33.4 us (36%)
  waiting for transfers between devices  21.7 us (23%)
    pallas_call x14, Pallas kernels, call(): pl.pallas_call(body, in_specs=[smem_spec] * len(scalars) + [in_spec] * le...  36.9 us
    ppermute x23, starting transfers between devices, exchange(): lax.ppermute(cells, axis, [(i, i ^ distance) for i in range(lax.axis_size...  32.1 us
    ppermute x23, waiting for transfers between devices, exchange(): lax.ppermute(cells, axis, [(i, i ^ distance) for i in range(lax.axis_size...  21.7 us
  transfers between devices with their start and end apart: 25, of which 10 were waited for; matrix products, arithmetic and copies ran while one was open for 0% of the time, Pallas kernels for 16%

profile of v5, /device:TPU:0, one launch (start us, length us, event | category | flops | bytes accessed | tf_op | source)
XLA Modules:
  0.0 92.9 jit_solution(4964837349342316870)
XLA Ops:
  3.4 9.2 %space_forward.1 = (bf16[2,768,256]{2,1,0:T(8,128)(2,1)S(1)}, bf16[2,768,512]{2,1,0:T(8,128)(2,1)S(1)}, bf16[2,6,256,128]{3,2,1,0:T(8,128)(2,1)S(1)}, bf16[2,256...) custom-call(s32[2,2,4]{2,1,0:T(2,128)} %refs_0_.1, ...), custom_call_target="tpu_custom_call" | custom-call | flops 10737418240 | bytes 41943040 | tf_op jit(solution)/shard_map/space_forward/pallas_call | solution.py:611
  12.6 2.6 %collective-permute-start.2 = (bf16[2,64,512]{2,1,0:T(8,128)(2,1)S(1)}, bf16[2,64,512]{2,1,0:T(8,128)(2,1)S(1)}, u32[]{:S(2)}, u32[]{:S(2)}) collective-permute-start(bf16[2,64,512]{2,1,0:T(8,128)(2,1)S(1)} %get-tuple-element.73), channel_id=1, source_target_pairs={{0,8},{8,0},{16,24},{24,16},{1,9},{9,1},{17,25},{25,17},{2,10},{10... | collective-permute-start | bytes 393224 | tf_op jit(solution)/shard_map/ppermute | solution.py:580
  15.2 1.5 %collective-permute-start.3 = (bf16[2,64,512]{2,1,0:T(8,128)(2,1)S(1)}, bf16[2,64,512]{2,1,0:T(8,128)(2,1)S(1)}, u32[]{:S(2)}, u32[]{:S(2)}) collective-permute-start(bf16[2,64,512]{2,1,0:T(8,128)(2,1)S(1)} %get-tuple-element.74), channel_id=1, source_target_pairs={{0,16},{8,24},{16,0},{24,8},{1,17},{9,25},{17,1},{25,9},{2,18},{10... | collective-permute-start | bytes 393224 | tf_op jit(solution)/shard_map/ppermute | solution.py:580
  18.1 2.0 %collective-permute-done.3.refs_2_ = bf16[2,64,512]{2,1,0:T(8,128)(2,1)S(1)} collective-permute-done((bf16[2,64,512]{2,1,0:T(8,128)(2,1)S(1)}, bf16[2,64,512]{2,1,0:T(8,128)(2,1)S(1)}, u32[]{:S(2)}, u32[]{:S(2)}) %collective-permute-start.3) | collective-permute-done | bytes 131104 | tf_op jit(solution)/shard_map/ppermute | solution.py:580
  20.2 2.4 %collective-permute-done.4.refs_3_ = bf16[2,64,512]{2,1,0:T(8,128)(2,1)S(1)} collective-permute-done((bf16[2,64,512]{2,1,0:T(8,128)(2,1)S(1)}, bf16[2,64,512]{2,1,0:T(8,128)(2,1)S(1)}, u32[]{:S(2)}, u32[]{:S(2)}) %collective-permute-start.4) | collective-permute-done | bytes 131104 | tf_op jit(solution)/shard_map/ppermute | solution.py:580
  22.6 8.9 %time_pair.1 = (bf16[2,64,256]{2,1,0:T(8,128)(2,1)S(1)}, bf16[2,64,256]{2,1,0:T(8,128)(2,1)S(1)}, bf16[2,64,256]{2,1,0:T(8,128)(2,1)S(1)}, bf16[2,64,256]{2,1,0:...) custom-call(bf16[2,64,512]{2,1,0:T(8,128)(2,1)S(1)} %get-tuple-eleme, ...), custom_call_target="tpu_custom_call" | custom-call | flops 9663676416 | bytes 37748736 | tf_op jit(solution)/shard_map/time_pair/pallas_call | solution.py:611
  32.6 2.5 %collective-permute-start.7 = (bf16[2,64,256]{2,1,0:T(8,128)(2,1)S(1)}, bf16[2,64,256]{2,1,0:T(8,128)(2,1)S(1)}, u32[]{:S(2)}, u32[]{:S(2)}) collective-permute-start(bf16[2,64,256]{2,1,0:T(8,128)(2,1)S(1)} %get-tuple-element.79), channel_id=1, source_target_pairs={{0,24},{8,16},{16,8},{24,0},{1,25},{9,17},{17,9},{25,1},{2,26},{10... | collective-permute-start | bytes 196616 | tf_op jit(solution)/shard_map/ppermute | solution.py:580
  36.6 1.5 %collective-permute-start.8 = (bf16[768,128]{1,0:T(8,128)(2,1)S(1)}, bf16[768,128]{1,0:T(8,128)(2,1)S(1)}, u32[]{:S(2)}, u32[]{:S(2)}) collective-permute-start(bf16[768,128]{1,0:T(8,128)(2,1)S(1)} %get-tuple-element.100), channel_id=1, source_target_pairs={{0,8},{8,0},{16,24},{24,16},{1,9},{9,1},{17,25},{25,17},{2,10},{10... | collective-permute-start | bytes 589832 | tf_op jit(solution)/shard_map/ppermute | solution.py:580
  38.1 1.5 %collective-permute-start.9 = (bf16[768,128]{1,0:T(8,128)(2,1)S(1)}, bf16[768,128]{1,0:T(8,128)(2,1)S(1)}, u32[]{:S(2)}, u32[]{:S(2)}) collective-permute-start(bf16[768,128]{1,0:T(8,128)(2,1)S(1)} %get-tuple-element.101), channel_id=1, source_target_pairs={{0,16},{8,24},{16,0},{24,8},{1,17},{9,25},{17,1},{25,9},{2,18},{10... | collective-permute-start | bytes 589832 | tf_op jit(solution)/shard_map/ppermute | solution.py:580
  39.7 8.5 %space_backward.1 = (bf16[2,256,256]{2,1,0:T(8,128)(2,1)S(1)}, bf16[2,256,256]{2,1,0:T(8,128)(2,1)S(1)}, bf16[2,768,512]{2,1,0:T(8,128)(2,1)S(1)}, bf16[2048,128]{1,0:T(8,128)(2,1)S(1)}) custom-call(s32[2,2,4]{2,1,0:T(2,128)} %refs_0_.1, s32[2]{0:T(128)S(1)} %pad_add_fusion.place_ref.refs_1_.refs_0_, bf16[2,64,256]{2,1,0:T(8,128)(2,1)S(1)} %get-tuple-element.76.refs_2_, ...), custom_call_target="tpu_custom_call" | custom-call | flops 11811160064 | bytes 46137344 | tf_op jit(solution)/shard_map/space_backward/pallas_call | solution.py:611
  49.4 2.3 %collective-permute-start.11 = (bf16[1280,128]{1,0:T(8,128)(2,1)S(1)}, bf16[1280,128]{1,0:T(8,128)(2,1)S(1)}, u32[]{:S(2)}, u32[]{:S(2)}) collective-permute-start(bf16[1280,128]{1,0:T(8,128)(2,1)S(1)} %get-tuple-element.104), channel_id=1, source_target_pairs={{0,1},{1,0},{2,3},{3,2},{4,5},{5,4},{6,7},{7,6},{8,9},{9,8},{10,11... | collective-permute-start | bytes 983048 | tf_op jit(solution)/shard_map/ppermute | solution.py:580
  54.6 1.5 %collective-permute-start.15 = (bf16[256,128]{1,0:T(8,128)(2,1)S(1)}, bf16[256,128]{1,0:T(8,128)(2,1)S(1)}, u32[]{:S(2)}, u32[]{:S(2)}) collective-permute-start(bf16[256,128]{1,0:T(8,128)(2,1)S(1)} %get-tuple-element.115), channel_id=1, source_target_pairs={{0,16},{8,24},{16,0},{24,8},{1,17},{9,25},{17,1},{25,9},{2,18},{10... | collective-permute-start | bytes 196616 | tf_op jit(solution)/shard_map/ppermute | solution.py:580
  57.3 5.8 %collective-permute-start.17 = (bf16[256,128]{1,0:T(8,128)(2,1)S(1)}, bf16[256,128]{1,0:T(8,128)(2,1)S(1)}, u32[]{:S(2)}, u32[]{:S(2)}) collective-permute-start(bf16[256,128]{1,0:T(8,128)(2,1)S(1)} %get-tuple-element.117.refs_4_), channel_id=1, source_target_pairs={{0,2},{1,3},{2,0},{3,1},{4,6},{5,7},{6,4},{7,5},{8,10},{9,11},{10,... | collective-permute-start | bytes 196616 | tf_op jit(solution)/shard_map/ppermute | solution.py:580
  63.8 1.5 %collective-permute-done.17.refs_5_ = bf16[256,128]{1,0:T(8,128)(2,1)S(1)} collective-permute-done((bf16[256,128]{1,0:T(8,128)(2,1)S(1)}, bf16[256,128]{1,0:T(8,128)(2,1)S(1)}, u32[]{:S(2)}, u32[]{:S(2)}) %collective-permute-start.17) | collective-permute-done | bytes 65568 | tf_op jit(solution)/shard_map/ppermute | solution.py:580
  66.0 2.1 %collective-permute-start.18 = (bf16[256,128]{1,0:T(8,128)(2,1)S(1)}, bf16[256,128]{1,0:T(8,128)(2,1)S(1)}, u32[]{:S(2)}, u32[]{:S(2)}) collective-permute-start(bf16[256,128]{1,0:T(8,128)(2,1)S(1)} %get-tuple-element.118.refs_0_), channel_id=1, source_target_pairs={{0,2},{1,3},{2,0},{3,1},{4,6},{5,7},{6,4},{7,5},{8,10},{9,11},{10,... | collective-permute-start | bytes 196616 | tf_op jit(solution)/shard_map/ppermute | solution.py:580
  68.1 1.6 %collective-permute-start.19 = (bf16[256,128]{1,0:T(8,128)(2,1)S(1)}, bf16[256,128]{1,0:T(8,128)(2,1)S(1)}, u32[]{:S(2)}, u32[]{:S(2)}) collective-permute-start(bf16[256,128]{1,0:T(8,128)(2,1)S(1)} %get-tuple-element.119.refs_2_), channel_id=1, source_target_pairs={{0,4},{1,5},{2,6},{3,7},{4,0},{5,1},{6,2},{7,3},{8,12},{9,13},{10,... | collective-permute-start | bytes 196616 | tf_op jit(solution)/shard_map/ppermute | solution.py:580
  69.6 4.6 %collective-permute-done.18.refs_1_ = bf16[256,128]{1,0:T(8,128)(2,1)S(1)} collective-permute-done((bf16[256,128]{1,0:T(8,128)(2,1)S(1)}, bf16[256,128]{1,0:T(8,128)(2,1)S(1)}, u32[]{:S(2)}, u32[]{:S(2)}) %collective-permute-start.18) | collective-permute-done | bytes 65568 | tf_op jit(solution)/shard_map/ppermute | solution.py:580
  75.5 4.1 %collective-permute-done.20.space_other_ref = bf16[256,128]{1,0:T(8,128)(2,1)S(1)} collective-permute-done((bf16[256,128]{1,0:T(8,128)(2,1)S(1)}, bf16[256,128]{1,0:T(8,128)(2,1)S(1)}, u32[]{:S(2)}, u32[]{:S(2)}) %collective-permute-start.20) | collective-permute-done | bytes 65568 | tf_op jit(solution)/shard_map/ppermute | solution.py:580
  79.6 2.0 %collective-permute-start.21 = (bf16[512,128]{1,0:T(8,128)(2,1)S(1)}, bf16[512,128]{1,0:T(8,128)(2,1)S(1)}, u32[]{:S(2)}, u32[]{:S(2)}) collective-permute-start(bf16[512,128]{1,0:T(8,128)(2,1)S(1)} %add_space_last.1.refs_0_), channel_id=1, source_target_pairs={{0,8},{8,0},{16,24},{24,16},{1,9},{9,1},{17,25},{25,17},{2,10},{10... | collective-permute-start | bytes 393224 | tf_op jit(solution)/shard_map/ppermute | solution.py:580
  83.3 1.8 %field_grad.1 = (bf16[2,256,256]{2,1,0:T(8,128)(2,1)}, bf16[2,256,256]{2,1,0:T(8,128)(2,1)}) custom-call(s32[2]{0:T(128)S(1)} %pad_add_fusion.place_ref.refs_1_.refs_0_, bf16[2,256,256]{2,1,0:T(8,128)(2,1)S(1)} %get-tuple-element.67.wave_ref, bf16[2,256,256]{2,1,0:T(8,128)(2,1)S(1)} %get-tuple-element.87.mixed_grad_ref, ...), custom_call_target="tpu_custom_call" | custom-call | flops 805306368 | bytes 3145728 | tf_op jit(solution)/shard_map/field_grad/pallas_call | solution.py:611
  85.1 1.4 %collective-permute-done.22.refs_2_ = bf16[512,128]{1,0:T(8,128)(2,1)S(1)} collective-permute-done((bf16[512,128]{1,0:T(8,128)(2,1)S(1)}, bf16[512,128]{1,0:T(8,128)(2,1)S(1)}, u32[]{:S(2)}, u32[]{:S(2)}) %collective-permute-start.22) | collective-permute-done | bytes 131104 | tf_op jit(solution)/shard_map/ppermute | solution.py:580
  86.6 1.7 %collective-permute-done.23.refs_3_ = bf16[512,128]{1,0:T(8,128)(2,1)S(1)} collective-permute-done((bf16[512,128]{1,0:T(8,128)(2,1)S(1)}, bf16[512,128]{1,0:T(8,128)(2,1)S(1)}, u32[]{:S(2)}, u32[]{:S(2)}) %collective-permute-start.23) | collective-permute-done | bytes 131104 | tf_op jit(solution)/shard_map/ppermute | solution.py:580
  88.9 1.9 %collective-permute-done.24.refs_2_ = bf16[2048,128]{1,0:T(8,128)(2,1)S(1)} collective-permute-done((bf16[2048,128]{1,0:T(8,128)(2,1)S(1)}, bf16[2048,128]{1,0:T(8,128)(2,1)S(1)}, u32[]{:S(2)}, u32[]{:S(2)}) %collective-permute-start.24) | collective-permute-done | bytes 524320 | tf_op jit(solution)/shard_map/ppermute | solution.py:580
  90.8 2.1 %weight_grads.1 = (f32[2,256,768]{2,1,0:T(8,128)}, f32[2,256,256]{2,1,0:T(8,128)}) custom-call(s32[2]{0:T(128)S(1)} %pad_add_fusion.place_ref.refs_1_.refs_0_, bf16[2048,128]{1,0:T(8,128)(2,1)S(1)} %join_tm.1.refs_1_, bf16[2048,128]{1,0:T(8,128)(2,1)S(1)} %collective-permute-done.24.refs_2_), custom_call_target="tpu_custom_call" | custom-call | flops 268435456 | bytes 1048576 | tf_op jit(solution)/shard_map/weight_grads/pallas_call | solution.py:611
  (41 shorter events, 17.1 us)
Async XLA Ops:
  0.6 2.7 %collective-permute-start = (bf16[2,256,256]{2,1,0:T(8,128)(2,1)}, bf16[2,256,256]{2,1,0:T(8,128)(2,1)S(1)}, u32[]{:S(2)}, u32[]{:S(2)}) collective-permute-start(bf16[2,256,256]{2,1,0:T(8,128)(2,1)} %wave_hbm.1), channel_id=1, source_target_pairs={{0,1},{1,0},{2,3},{3,2},{4,5},{5,4},{6,7},{7,6},{8,9},{9,8},{10,11... | collective-permute-start | bytes 786440 | tf_op jit(solution)/shard_map/ppermute | solution.py:580
  1.1 2.2 %collective-permute-start.1 = (bf16[2,256,256]{2,1,0:T(8,128)(2,1)}, bf16[2,256,256]{2,1,0:T(8,128)(2,1)S(1)}, u32[]{:S(2)}, u32[]{:S(2)}) collective-permute-start(bf16[2,256,256]{2,1,0:T(8,128)(2,1)} %wave_hbm.1), channel_id=1, source_target_pairs={{1,2},{3,4},{5,6},{2,1},{4,3},{6,5},{9,10},{11,12},{13,14},{10,9},... | collective-permute-start | bytes 786440 | tf_op jit(solution)/shard_map/ppermute | solution.py:576
  12.6 5.5 %collective-permute-start.2 = (bf16[2,64,512]{2,1,0:T(8,128)(2,1)S(1)}, bf16[2,64,512]{2,1,0:T(8,128)(2,1)S(1)}, u32[]{:S(2)}, u32[]{:S(2)}) collective-permute-start(bf16[2,64,512]{2,1,0:T(8,128)(2,1)S(1)} %get-tuple-element.73), channel_id=1, source_target_pairs={{0,8},{8,0},{16,24},{24,16},{1,9},{9,1},{17,25},{25,17},{2,10},{10... | collective-permute-start | bytes 393224 | tf_op jit(solution)/shard_map/ppermute | solution.py:580
  15.2 5.0 %collective-permute-start.3 = (bf16[2,64,512]{2,1,0:T(8,128)(2,1)S(1)}, bf16[2,64,512]{2,1,0:T(8,128)(2,1)S(1)}, u32[]{:S(2)}, u32[]{:S(2)}) collective-permute-start(bf16[2,64,512]{2,1,0:T(8,128)(2,1)S(1)} %get-tuple-element.74), channel_id=1, source_target_pairs={{0,16},{8,24},{16,0},{24,8},{1,17},{9,25},{17,1},{25,9},{2,18},{10... | collective-permute-start | bytes 393224 | tf_op jit(solution)/shard_map/ppermute | solution.py:580
  16.7 5.9 %collective-permute-start.4 = (bf16[2,64,512]{2,1,0:T(8,128)(2,1)S(1)}, bf16[2,64,512]{2,1,0:T(8,128)(2,1)S(1)}, u32[]{:S(2)}, u32[]{:S(2)}) collective-permute-start(bf16[2,64,512]{2,1,0:T(8,128)(2,1)S(1)} %get-tuple-element.75), channel_id=1, source_target_pairs={{0,24},{8,16},{16,8},{24,0},{1,25},{9,17},{17,9},{25,1},{2,26},{10... | collective-permute-start | bytes 393224 | tf_op jit(solution)/shard_map/ppermute | solution.py:580
  31.5 6.6 %collective-permute-start.5 = (bf16[2,64,256]{2,1,0:T(8,128)(2,1)S(1)}, bf16[2,64,256]{2,1,0:T(8,128)(2,1)S(1)}, u32[]{:S(2)}, u32[]{:S(2)}) collective-permute-start(bf16[2,64,256]{2,1,0:T(8,128)(2,1)S(1)} %get-tuple-element.77), channel_id=1, source_target_pairs={{0,8},{8,0},{16,24},{24,16},{1,9},{9,1},{17,25},{25,17},{2,10},{10... | collective-permute-start | bytes 196616 | tf_op jit(solution)/shard_map/ppermute | solution.py:580
  32.1 7.6 %collective-permute-start.6 = (bf16[2,64,256]{2,1,0:T(8,128)(2,1)S(1)}, bf16[2,64,256]{2,1,0:T(8,128)(2,1)S(1)}, u32[]{:S(2)}, u32[]{:S(2)}) collective-permute-start(bf16[2,64,256]{2,1,0:T(8,128)(2,1)S(1)} %get-tuple-element.78), channel_id=1, source_target_pairs={{0,16},{8,24},{16,0},{24,8},{1,17},{9,25},{17,1},{25,9},{2,18},{10... | collective-permute-start | bytes 196616 | tf_op jit(solution)/shard_map/ppermute | solution.py:580
  32.6 7.1 %collective-permute-start.7 = (bf16[2,64,256]{2,1,0:T(8,128)(2,1)S(1)}, bf16[2,64,256]{2,1,0:T(8,128)(2,1)S(1)}, u32[]{:S(2)}, u32[]{:S(2)}) collective-permute-start(bf16[2,64,256]{2,1,0:T(8,128)(2,1)S(1)} %get-tuple-element.79), channel_id=1, source_target_pairs={{0,24},{8,16},{16,8},{24,0},{1,25},{9,17},{17,9},{25,1},{2,26},{10... | collective-permute-start | bytes 196616 | tf_op jit(solution)/shard_map/ppermute | solution.py:580
  36.1 12.0 %collective-permute-start.10 = (bf16[768,128]{1,0:T(8,128)(2,1)S(1)}, bf16[768,128]{1,0:T(8,128)(2,1)S(1)}, u32[]{:S(2)}, u32[]{:S(2)}) collective-permute-start(bf16[768,128]{1,0:T(8,128)(2,1)S(1)} %get-tuple-element.102), channel_id=1, source_target_pairs={{0,24},{8,16},{16,8},{24,0},{1,25},{9,17},{17,9},{25,1},{2,26},{10... | collective-permute-start | bytes 589832 | tf_op jit(solution)/shard_map/ppermute | solution.py:580
  36.6 11.5 %collective-permute-start.8 = (bf16[768,128]{1,0:T(8,128)(2,1)S(1)}, bf16[768,128]{1,0:T(8,128)(2,1)S(1)}, u32[]{:S(2)}, u32[]{:S(2)}) collective-permute-start(bf16[768,128]{1,0:T(8,128)(2,1)S(1)} %get-tuple-element.100), channel_id=1, source_target_pairs={{0,8},{8,0},{16,24},{24,16},{1,9},{9,1},{17,25},{25,17},{2,10},{10... | collective-permute-start | bytes 589832 | tf_op jit(solution)/shard_map/ppermute | solution.py:580
  38.1 10.5 %collective-permute-start.9 = (bf16[768,128]{1,0:T(8,128)(2,1)S(1)}, bf16[768,128]{1,0:T(8,128)(2,1)S(1)}, u32[]{:S(2)}, u32[]{:S(2)}) collective-permute-start(bf16[768,128]{1,0:T(8,128)(2,1)S(1)} %get-tuple-element.101), channel_id=1, source_target_pairs={{0,16},{8,24},{16,0},{24,8},{1,17},{9,25},{17,1},{25,9},{2,18},{10... | collective-permute-start | bytes 589832 | tf_op jit(solution)/shard_map/ppermute | solution.py:580
  49.4 3.6 %collective-permute-start.11 = (bf16[1280,128]{1,0:T(8,128)(2,1)S(1)}, bf16[1280,128]{1,0:T(8,128)(2,1)S(1)}, u32[]{:S(2)}, u32[]{:S(2)}) collective-permute-start(bf16[1280,128]{1,0:T(8,128)(2,1)S(1)} %get-tuple-element.104), channel_id=1, source_target_pairs={{0,1},{1,0},{2,3},{3,2},{4,5},{5,4},{6,7},{7,6},{8,9},{9,8},{10,11... | collective-permute-start | bytes 983048 | tf_op jit(solution)/shard_map/ppermute | solution.py:580
  53.7 9.4 %collective-permute-start.14 = (bf16[256,128]{1,0:T(8,128)(2,1)S(1)}, bf16[256,128]{1,0:T(8,128)(2,1)S(1)}, u32[]{:S(2)}, u32[]{:S(2)}) collective-permute-start(bf16[256,128]{1,0:T(8,128)(2,1)S(1)} %get-tuple-element.114), channel_id=1, source_target_pairs={{0,8},{8,0},{16,24},{24,16},{1,9},{9,1},{17,25},{25,17},{2,10},{10... | collective-permute-start | bytes 196616 | tf_op jit(solution)/shard_map/ppermute | solution.py:580
  54.6 9.2 %collective-permute-start.15 = (bf16[256,128]{1,0:T(8,128)(2,1)S(1)}, bf16[256,128]{1,0:T(8,128)(2,1)S(1)}, u32[]{:S(2)}, u32[]{:S(2)}) collective-permute-start(bf16[256,128]{1,0:T(8,128)(2,1)S(1)} %get-tuple-element.115), channel_id=1, source_target_pairs={{0,16},{8,24},{16,0},{24,8},{1,17},{9,25},{17,1},{25,9},{2,18},{10... | collective-permute-start | bytes 196616 | tf_op jit(solution)/shard_map/ppermute | solution.py:580
  56.0 7.8 %collective-permute-start.16 = (bf16[256,128]{1,0:T(8,128)(2,1)S(1)}, bf16[256,128]{1,0:T(8,128)(2,1)S(1)}, u32[]{:S(2)}, u32[]{:S(2)}) collective-permute-start(bf16[256,128]{1,0:T(8,128)(2,1)S(1)} %get-tuple-element.116), channel_id=1, source_target_pairs={{0,24},{8,16},{16,8},{24,0},{1,25},{9,17},{17,9},{25,1},{2,26},{10... | collective-permute-start | bytes 196616 | tf_op jit(solution)/shard_map/ppermute | solution.py:580
  57.3 8.1 %collective-permute-start.17 = (bf16[256,128]{1,0:T(8,128)(2,1)S(1)}, bf16[256,128]{1,0:T(8,128)(2,1)S(1)}, u32[]{:S(2)}, u32[]{:S(2)}) collective-permute-start(bf16[256,128]{1,0:T(8,128)(2,1)S(1)} %get-tuple-element.117.refs_4_), channel_id=1, source_target_pairs={{0,2},{1,3},{2,0},{3,1},{4,6},{5,7},{6,4},{7,5},{8,10},{9,11},{10,... | collective-permute-start | bytes 196616 | tf_op jit(solution)/shard_map/ppermute | solution.py:580
  63.1 20.2 %collective-permute-start.12 = (bf16[2,256,256]{2,1,0:T(8,128)(2,1)S(1)}, bf16[2,256,256]{2,1,0:T(8,128)(2,1)S(1)}, u32[]{:S(2)}, u32[]{:S(2)}) collective-permute-start(bf16[2,256,256]{2,1,0:T(8,128)(2,1)S(1)} %get-tuple-element.109), channel_id=1, source_target_pairs={{0,1},{1,0},{2,3},{3,2},{4,5},{5,4},{6,7},{7,6},{8,9},{9,8},{10,11... | collective-permute-start | bytes 786440 | tf_op jit(solution)/shard_map/ppermute | solution.py:580
  63.1 20.2 %collective-permute-start.13 = (bf16[2,256,256]{2,1,0:T(8,128)(2,1)S(1)}, bf16[2,256,256]{2,1,0:T(8,128)(2,1)S(1)}, u32[]{:S(2)}, u32[]{:S(2)}) collective-permute-start(bf16[2,256,256]{2,1,0:T(8,128)(2,1)S(1)} %get-tuple-element.110), channel_id=1, source_target_pairs={{1,2},{3,4},{5,6},{2,1},{4,3},{6,5},{9,10},{11,12},{13,14},{10,9},... | collective-permute-start | bytes 786440 | tf_op jit(solution)/shard_map/ppermute | solution.py:576
  66.0 8.3 %collective-permute-start.18 = (bf16[256,128]{1,0:T(8,128)(2,1)S(1)}, bf16[256,128]{1,0:T(8,128)(2,1)S(1)}, u32[]{:S(2)}, u32[]{:S(2)}) collective-permute-start(bf16[256,128]{1,0:T(8,128)(2,1)S(1)} %get-tuple-element.118.refs_0_), channel_id=1, source_target_pairs={{0,2},{1,3},{2,0},{3,1},{4,6},{5,7},{6,4},{7,5},{8,10},{9,11},{10,... | collective-permute-start | bytes 196616 | tf_op jit(solution)/shard_map/ppermute | solution.py:580
  68.1 6.2 %collective-permute-start.19 = (bf16[256,128]{1,0:T(8,128)(2,1)S(1)}, bf16[256,128]{1,0:T(8,128)(2,1)S(1)}, u32[]{:S(2)}, u32[]{:S(2)}) collective-permute-start(bf16[256,128]{1,0:T(8,128)(2,1)S(1)} %get-tuple-element.119.refs_2_), channel_id=1, source_target_pairs={{0,4},{1,5},{2,6},{3,7},{4,0},{5,1},{6,2},{7,3},{8,12},{9,13},{10,... | collective-permute-start | bytes 196616 | tf_op jit(solution)/shard_map/ppermute | solution.py:580
  74.3 5.2 %collective-permute-start.20 = (bf16[256,128]{1,0:T(8,128)(2,1)S(1)}, bf16[256,128]{1,0:T(8,128)(2,1)S(1)}, u32[]{:S(2)}, u32[]{:S(2)}) collective-permute-start(bf16[256,128]{1,0:T(8,128)(2,1)S(1)} %get-tuple-element.120.space_ref), channel_id=1, source_target_pairs={{0,4},{1,5},{2,6},{3,7},{4,0},{5,1},{6,2},{7,3},{8,12},{9,13},{10,... | collective-permute-start | bytes 196616 | tf_op jit(solution)/shard_map/ppermute | solution.py:580
  79.6 5.5 %collective-permute-start.21 = (bf16[512,128]{1,0:T(8,128)(2,1)S(1)}, bf16[512,128]{1,0:T(8,128)(2,1)S(1)}, u32[]{:S(2)}, u32[]{:S(2)}) collective-permute-start(bf16[512,128]{1,0:T(8,128)(2,1)S(1)} %add_space_last.1.refs_0_), channel_id=1, source_target_pairs={{0,8},{8,0},{16,24},{24,16},{1,9},{9,1},{17,25},{25,17},{2,10},{10... | collective-permute-start | bytes 393224 | tf_op jit(solution)/shard_map/ppermute | solution.py:580
  81.6 5.0 %collective-permute-start.22 = (bf16[512,128]{1,0:T(8,128)(2,1)S(1)}, bf16[512,128]{1,0:T(8,128)(2,1)S(1)}, u32[]{:S(2)}, u32[]{:S(2)}) collective-permute-start(bf16[512,128]{1,0:T(8,128)(2,1)S(1)} %add_space_last.1.refs_0_), channel_id=1, source_target_pairs={{0,16},{8,24},{16,0},{24,8},{1,17},{9,25},{17,1},{25,9},{2,18},{10... | collective-permute-start | bytes 393224 | tf_op jit(solution)/shard_map/ppermute | solution.py:580
  82.4 5.9 %collective-permute-start.23 = (bf16[512,128]{1,0:T(8,128)(2,1)S(1)}, bf16[512,128]{1,0:T(8,128)(2,1)S(1)}, u32[]{:S(2)}, u32[]{:S(2)}) collective-permute-start(bf16[512,128]{1,0:T(8,128)(2,1)S(1)} %add_space_last.1.refs_0_), channel_id=1, source_target_pairs={{0,24},{8,16},{16,8},{24,0},{1,25},{9,17},{17,9},{25,1},{2,26},{10... | collective-permute-start | bytes 393224 | tf_op jit(solution)/shard_map/ppermute | solution.py:580
  (1 other events, 2.0 us)

commit v6 on v5

--- a/solution.py
+++ b/solution.py
@@ -105,7 +105,32 @@
     ]
 
 
+def halo_start(core, rim, row_count, near):
+    after = core == 0 if near else core != 0
+    return pl.multiple_of(jnp.where(after, rim + row_count, 0), BLOCK)
+
+
+def project_rows(
+    frame, start, rows, project_ref, turned_ref, act_ref, kv_ref, keys_t_ref, values_t_ref
+):
+    features = rows.shape[1]
+    normed, _ = layer_norm(rows)
+    act = normed.astype(BF16)
+    span = pl.ds(start, rows.shape[0])
+    act_ref[frame, span] = act
+    kv_ref[frame, span] = dot_nn(act, project_ref[0, :, features:]).astype(BF16)
+    keys_t = dot_nt(turned_ref[0, features : 2 * features], act).astype(BF16)
+    values_t = dot_nt(turned_ref[0, 2 * features :], act).astype(BF16)
+    for block in range(rows.shape[0] // BLOCK):
+        lanes = slice(block * BLOCK, (block + 1) * BLOCK)
+        keys_t_ref[frame, start // BLOCK + block] = keys_t[:, lanes]
+        values_t_ref[frame, start // BLOCK + block] = values_t[:, lanes]
+    return act
+
+
 def prepare_kernel(
+    place_ref,
+    near_ref,
     wave_hbm,
     cot_hbm,
     project_hbm,
@@ -115,6 +140,12 @@
     turned_ref,
     combine_ref,
     cot_ref,
+    query_ref,
+    query_t_ref,
+    act_ref,
+    kv_ref,
+    keys_t_ref,
+    values_t_ref,
     sems,
 ):
     moves = [
@@ -130,85 +161,125 @@
     ]
     for move in moves:
         move.start()
+    frame_count, row_count, features = wave_ref.shape
+    rim = near_ref.shape[1]
+    core = place_ref[1] % 2
     moves[0].wait()
-    for layer in range(2):
-        turned_ref[layer] = flip(project_ref[layer])
-    for move in moves[1:]:
-        move.wait()
-
-
-def halo_start(core, rim, row_count, near):
-    after = core == 0 if near else core != 0
-    return pl.multiple_of(jnp.where(after, rim + row_count, 0), BLOCK)
+    turned_ref[0] = flip(project_ref[0])
+    for frame in range(frame_count):
+        project_rows(
+            frame,
+            halo_start(core, rim, row_count, True),
+            near_ref[frame],
+            project_ref,
+            turned_ref,
+            act_ref,
+            kv_ref,
+            keys_t_ref,
+            values_t_ref,
+        )
+    moves[1].wait()
+    for frame in range(frame_count):
+        act = project_rows(
+            frame, rim, wave_ref[frame], project_ref, turned_ref, act_ref, kv_ref, keys_t_ref, values_t_ref
+        )
+        query_ref[frame] = dot_nn(act, project_ref[0, :, :features]).astype(BF16)
+        query_t_ref[frame] = dot_nt(turned_ref[0, :features], act).astype(BF16)
+    turned_ref[1] = flip(project_ref[1])
+    moves[2].wait()
+    moves[3].wait()
 
 
 def space_forward_kernel(
     lists_ref,
     place_ref,
-    near_ref,
     far_ref,
     wave_ref,
     cot_ref,
     project_ref,
     turned_ref,
     combine_ref,
+    query_t_ref,
+    act_in,
+    kv_in,
+    keys_t_in,
+    values_t_in,
     act_ref,
     kv_ref,
     keys_t_ref,
-    query_ref,
+    values_t_ref,
     probs_ref,
     inverse_sum_ref,
     attended_ref,
     *rest,
 ):
-    *sent_refs, values_t, mixed_s, extended_s = rest
+    del act_in, kv_in, keys_t_in, values_t_in
+    *sent_refs, mixed_s = rest
     me = place_ref[0]
     core = place_ref[1] % 2
     frame_count, row_count, features = wave_ref.shape
-    rim = near_ref.shape[1]
+    rim = far_ref.shape[1]
     width = features // HEADS
     block_count = row_count // BLOCK
     exponent_scale = math.log2(math.e) / math.sqrt(width)
     for frame in range(frame_count):
-        extended_s[frame, rim : rim + row_count] = wave_ref[frame]
-        extended_s[frame, pl.ds(halo_start(core, rim, row_count, True), rim)] = near_ref[frame]
-        extended_s[frame, pl.ds(halo_start(core, rim, row_count, False), rim)] = far_ref[frame]
-        normed, _ = layer_norm(extended_s[frame])
-        act = normed.astype(BF16)
-        act_ref[frame] = act
-        kv_ref[frame] = dot_nn(act, project_ref[0, :, features:]).astype(BF16)
-        own_act = act[rim : rim + row_count]
-        query_ref[frame] = dot_nn(own_act, project_ref[0, :, :features]).astype(BF16)
-        queries_t = dot_nt(turned_ref[0, :features], own_act).astype(BF16)
-        all_keys_t = dot_nt(turned_ref[0, features : 2 * features], act).astype(BF16)
-        all_values_t = dot_nt(turned_ref[0, 2 * features :], act).astype(BF16)
-        for place in range(block_count + 2 * HREACH):
-            keys_t_ref[frame, place] = all_keys_t[:, place * BLOCK : (place + 1) * BLOCK]
-            values_t[frame, place] = all_values_t[:, place * BLOCK : (place + 1) * BLOCK]
-        for block in range(block_count):
-            places = listed_blocks(lists_ref, frame, block)
-            keys = jnp.concatenate(
-                [kv_ref[frame, pl.ds(place * BLOCK, BLOCK), :features] for place in places], axis=0
+        project_rows(
+            frame,
+            halo_start(core, rim, row_count, False),
+            far_ref[frame],
+            project_ref,
+            turned_ref,
+            act_ref,
+            kv_ref,
+            keys_t_ref,
+            values_t_ref,
+        )
+    blocks = [(frame, block) for frame in range(frame_count) for block in range(block_count)]
+    loaded = {}
+
+    def load(index):
+        frame, block = blocks[index]
+        places = listed_blocks(lists_ref, frame, block)
+        keys = jnp.concatenate(
+            [kv_ref[frame, pl.ds(place * BLOCK, BLOCK), :features] for place in places], axis=0
+        )
+        loaded[index] = (keys, query_t_ref[frame, :, block * BLOCK : (block + 1) * BLOCK], places)
+
+    def pair_scores(step):
+        index, pair = divmod(step, HEADS // 2)
+        if index not in loaded:
+            load(index)
+        keys, query_t, _ = loaded[index]
+        return dot_nn(pair_group(keys, pair, width), pair_columns(query_t, pair, width))
+
+    steps = len(blocks) * HEADS // 2
+    scores = pair_scores(0)
+    outs = []
+    for step in range(steps):
+        following = pair_scores(step + 1) if step + 1 < steps else None
+        index, pair = divmod(step, HEADS // 2)
+        frame, block = blocks[index]
+        if pair == 0:
+            block_values_t = jnp.concatenate(
+                [values_t_ref[frame, place] for place in loaded[index][2]], axis=1
             )
-            block_values_t = jnp.concatenate([values_t[frame, place] for place in places], axis=1)
-            query_t = queries_t[:, block * BLOCK : (block + 1) * BLOCK]
             outs = []
-            for pair in range(HEADS // 2):
-                scores = dot_nn(pair_group(keys, pair, width), pair_columns(query_t, pair, width))
-                top = jnp.max(scores, axis=0, keepdims=True)
-                exp_scores = jnp.exp2((scores - top) * exponent_scale)
-                inverse_sum = 1.0 / jnp.sum(exp_scores, axis=0, keepdims=True)
-                probs = exp_scores.astype(BF16)
-                probs_ref[frame, block, :, pair * 2 * BLOCK : (pair + 1) * 2 * BLOCK] = probs
-                inverse_sum_ref[frame, block, 2 * pair : 2 * pair + 1] = inverse_sum[:, :BLOCK]
-                inverse_sum_ref[frame, block, 2 * pair + 1 : 2 * pair + 2] = inverse_sum[:, BLOCK:]
-                out = dot_nn(block_values_t[pair * 2 * width : (pair + 1) * 2 * width], probs)
-                outs.append(pair_diagonal(out * inverse_sum, width))
+        top = jnp.max(scores, axis=0, keepdims=True)
+        exp_scores = jnp.exp2((scores - top) * exponent_scale)
+        inverse_sum = 1.0 / jnp.sum(exp_scores, axis=0, keepdims=True)
+        probs = exp_scores.astype(BF16)
+        probs_ref[frame, block, :, pair * 2 * BLOCK : (pair + 1) * 2 * BLOCK] = probs
+        inverse_sum_ref[frame, block, 2 * pair : 2 * pair + 1] = inverse_sum[:, :BLOCK]
+        inverse_sum_ref[frame, block, 2 * pair + 1 : 2 * pair + 2] = inverse_sum[:, BLOCK:]
+        out = dot_nn(block_values_t[pair * 2 * width : (pair + 1) * 2 * width], probs)
+        outs.append(pair_diagonal(out * inverse_sum, width))
+        scores = following
+        if pair == HEADS // 2 - 1:
             attended_t = jnp.concatenate(outs, axis=0)
-            attended_ref[frame, :, block * BLOCK : (block + 1) * BLOCK] = attended_t.astype(BF16)
-            mixed_s[frame, block * BLOCK : (block + 1) * BLOCK] = (
-                wave_ref[frame, block * BLOCK : (block + 1) * BLOCK].astype(F32)
-                + dot_nn(flip(attended_t), combine_ref[0])
+            span = slice(block * BLOCK, (block + 1) * BLOCK)
+            attended_ref[frame, :, span] = attended_t.astype(BF16)
+            mixed_s[frame, span] = (
+                wave_ref[frame, span].astype(F32) + dot_nn(flip(attended_t), combine_ref[0])
             ).astype(BF16)
     for distance, ref in enumerate(sent_refs):
         rows = ref.shape[1]
@@ -254,43 +325,62 @@
     projected_t = dot_nt(turned_ref[1], act).astype(BF16)
     all_dattn = dot_nt(cot, combine_ref[1]).astype(BF16)
     all_dattn_t = dot_nt(combine_ref[1], cot).astype(BF16)
-    key_row = lax.broadcasted_iota(jnp.int32, (count, 2 * count), 0) % GROUP_ROWS
-    query_row = lax.broadcasted_iota(jnp.int32, (count, 2 * count), 1) % GROUP_ROWS
+    all_count = HEADS * count
+    key_row = lax.broadcasted_iota(jnp.int32, (count, all_count), 0) % GROUP_ROWS
+    query_row = lax.broadcasted_iota(jnp.int32, (count, all_count), 1) % GROUP_ROWS
     same_row = key_row == query_row
     attended_groups, dquery_groups, dkey_groups, dvalue_groups = [], [], [], []
+    pairs = range(HEADS // 2)
+
+    def products(group):
+        span = slice(group * count, (group + 1) * count)
+        return tuple(
+            jnp.concatenate(
+                [
+                    dot_nn(pair_group(left, pair, width), pair_columns(right, pair, width))
+                    for pair in pairs
+                ],
+                axis=1,
+            )
+            for left, right in (
+                (projected[span, features : 2 * features], projected_t[:features, span]),
+                (projected[span, 2 * features :], all_dattn_t[:, span]),
+            )
+        )
+
+    def by_heads(left_t, right):
+        return jnp.concatenate(
+            [
+                pair_diagonal(
+                    dot_nn(
+                        left_t[pair * 2 * width : (pair + 1) * 2 * width],
+                        right[:, pair * 2 * count : (pair + 1) * 2 * count],
+                    ),
+                    width,
+                )
+                for pair in pairs
+            ],
+            axis=0,
+        )
+
+    scores, dprobs = products(0)
     for group in range(groups):
+        following = products(group + 1) if group + 1 < groups else (None, None)
         span = slice(group * count, (group + 1) * count)
-        queries = projected[span, :features]
-        keys = projected[span, features : 2 * features]
-        values = projected[span, 2 * features :]
-        query_t = projected_t[:features, span]
-        keys_t = projected_t[features : 2 * features, span]
-        values_t = projected_t[2 * features :, span]
-        dattn_t = all_dattn_t[:, span]
-        outs, probs_parts, dscore_parts, dquery_parts = [], [], [], []
-        for pair in range(HEADS // 2):
-            heads = slice(pair * 2 * width, (pair + 1) * 2 * width)
-            scores = dot_nn(pair_group(keys, pair, width), pair_columns(query_t, pair, width))
-            scores = jnp.where(same_row, scores, -3e38)
-            top = jnp.max(scores, axis=0, keepdims=True)
-            exp_scores = jnp.exp2((scores - top) * exponent_scale)
-            probs = (exp_scores * (1.0 / jnp.sum(exp_scores, axis=0, keepdims=True))).astype(BF16)
-            probs_wide = probs.astype(F32)
-            outs.append(pair_diagonal(dot_nn(values_t[heads], probs), width))
-            dprobs = dot_nn(pair_group(values, pair, width), pair_columns(dattn_t, pair, width))
-            delta = jnp.sum(probs_wide * dprobs, axis=0, keepdims=True)
-            dscores = (probs_wide * (dprobs - delta) * scale).astype(BF16)
-            dquery_parts.append(pair_diagonal(dot_nn(keys_t[heads], dscores), width))
-            probs_parts.append(probs)
-            dscore_parts.append(dscores)
-        attended_groups.append(jnp.concatenate(outs, axis=0).astype(BF16))
-        dquery_groups.append(flip(jnp.concatenate(dquery_parts, axis=0)))
+        scores = jnp.where(same_row, scores, -3e38)
+        top = jnp.max(scores, axis=0, keepdims=True)
+        exp_scores = jnp.exp2((scores - top) * exponent_scale)
+        probs = (exp_scores * (1.0 / jnp.sum(exp_scores, axis=0, keepdims=True))).astype(BF16)
+        probs_wide = probs.astype(F32)
+        delta = jnp.sum(probs_wide * dprobs, axis=0, keepdims=True)
+        dscores = (probs_wide * (dprobs - delta) * scale).astype(BF16)
+        attended_groups.append(by_heads(projected_t[2 * features :, span], probs).astype(BF16))
+        dquery_groups.append(flip(by_heads(projected_t[features : 2 * features, span], dscores)))
         dkey_groups.append(
-            dot_nn(jnp.concatenate(dscore_parts, axis=1), head_rows(queries, width)).astype(BF16)
-        )
-        dvalue_groups.append(
-            dot_nn(jnp.concatenate(probs_parts, axis=1), head_rows(all_dattn[span], width)).astype(BF16)
-        )
+            dot_nn(dscores, head_rows(projected[span, :features], width)).astype(BF16)
+        )
+        dvalue_groups.append(dot_nn(probs, head_rows(all_dattn[span], width)).astype(BF16))
+        scores, dprobs = following
     attended = jnp.concatenate([flip(attended_t) for attended_t in attended_groups], axis=0)
     mixed_ref[...] = (rows.astype(F32) + dot_nn(attended, combine_ref[1])).astype(BF16)
     attended_t_ref[...] = jnp.concatenate(attended_groups, axis=1)
@@ -371,20 +461,56 @@
         rows = ref.shape[1]
         span = pl.ds(pl.multiple_of((me ^ distance) * rows, GROUP_ROWS), rows)
         mixed_grad_ref[:, span] = ref[...]
-    for frame in range(frame_count):
-        dkv_s[frame] = jnp.zeros(dkv_s.shape[1:], F32)
-        all_dattn_t = dot_nt(combine_ref[0], mixed_grad_ref[frame]).astype(BF16)
-        for block in range(block_count):
+    blocks = [(frame, block) for frame in range(frame_count) for block in range(block_count)]
+    all_dattn_t = [
+        dot_nt(combine_ref[0], mixed_grad_ref[frame]).astype(BF16) for frame in range(frame_count)
+    ]
+    loaded = {}
+
+    def load(index):
+        frame, block = blocks[index]
+        places = listed_blocks(lists_ref, frame, block)
+        values = jnp.concatenate(
+            [kv_ref[frame, pl.ds(place * BLOCK, BLOCK), features:] for place in places], axis=0
+        )
+        loaded[index] = (
+            values,
+            all_dattn_t[frame][:, block * BLOCK : (block + 1) * BLOCK],
+            places,
+        )
+
+    def pair_products(step):
+        index, pair = divmod(step, HEADS // 2)
+        if index not in loaded:
+            load(index)
+        values, dattn_t, _ = loaded[index]
+        return dot_nn(pair_group(values, pair, width), pair_columns(dattn_t, pair, width))
+
+    def add_listed(index, lanes, parts):
+        frame = blocks[index][0]
+        for entry, place in enumerate(loaded[index][2]):
+            rows = pl.ds(place * BLOCK, BLOCK)
+            dkv_s[frame, rows, lanes] += parts[entry * BLOCK : (entry + 1) * BLOCK]
+
+    def add_keys(index):
+        frame, block = blocks[index]
+        queries = head_rows(query_ref[frame, block * BLOCK : (block + 1) * BLOCK], width)
+        add_listed(index, slice(0, features), dot_nn(dscores_s[frame, block], queries))
+
+    dkv_s[...] = jnp.zeros(dkv_s.shape, F32)
+    steps = len(blocks) * HEADS // 2
+    dprobs = pair_products(0)
+    dquery_parts = []
+    for step in range(steps):
+        following = pair_products(step + 1) if step + 1 < steps else None
+        index, pair = divmod(step, HEADS // 2)
+        frame, block = blocks[index]
+        _, dattn_t, places = loaded[index]
+        if pair == 0:
             span = slice(block * BLOCK, (block + 1) * BLOCK)
-            places = listed_blocks(lists_ref, frame, block)
-            values = jnp.concatenate(
-                [kv_ref[frame, pl.ds(place * BLOCK, BLOCK), features:] for place in places], axis=0
-            )
             block_keys_t = jnp.concatenate([keys_t_ref[frame, place] for place in places], axis=1)
-            dattn_t = all_dattn_t[:, span]
             dattn_wide = dattn_t.astype(F32)
             inverse_sum = inverse_sum_ref[frame, block]
-            scaled_dattn = flip(dattn_wide * head_spread(inverse_sum, width))
             delta = jnp.sum(
                 (dattn_wide * attended_ref[frame, :, span].astype(F32)).reshape(
                     HEADS, width, BLOCK
@@ -393,30 +519,30 @@
             )
             row_scale = inverse_sum * scale
             dquery_parts = []
-            for pair in range(HEADS // 2):
-                heads = slice(pair * 2 * width, (pair + 1) * 2 * width)
-                columns = slice(pair * 2 * BLOCK, (pair + 1) * 2 * BLOCK)
-                pair_delta = jnp.concatenate(
-                    [delta[2 * pair : 2 * pair + 1], delta[2 * pair + 1 : 2 * pair + 2]], axis=1
-                )
-                pair_scale = jnp.concatenate(
-                    [row_scale[2 * pair : 2 * pair + 1], row_scale[2 * pair + 1 : 2 * pair + 2]],
-                    axis=1,
-                )
-                dprobs = dot_nn(pair_group(values, pair, width), pair_columns(dattn_t, pair, width))
-                probs = probs_ref[frame, block, :, columns].astype(F32)
-                dscores = (probs * ((dprobs - pair_delta) * pair_scale)).astype(BF16)
-                dscores_s[frame, block, :, columns] = dscores
-                dquery_parts.append(pair_diagonal(dot_nn(block_keys_t[heads], dscores), width))
+        if pair == 1:
+            scaled_dattn = flip(dattn_wide * head_spread(inverse_sum, width))
+            add_listed(
+                index,
+                slice(features, 2 * features),
+                dot_nn(probs_ref[frame, block], head_rows(scaled_dattn, width)),
+            )
+        if pair == 2 and index:
+            add_keys(index - 1)
+        heads = slice(pair * 2 * width, (pair + 1) * 2 * width)
+        columns = slice(pair * 2 * BLOCK, (pair + 1) * 2 * BLOCK)
+        pair_delta, pair_scale = (
+            jnp.concatenate([rows[2 * pair : 2 * pair + 1], rows[2 * pair + 1 : 2 * pair + 2]], axis=1)
+            for rows in (delta, row_scale)
+        )
+        probs = probs_ref[frame, block, :, columns].astype(F32)
+        dscores = (probs * ((dprobs - pair_delta) * pair_scale)).astype(BF16)
+        dscores_s[frame, block, :, columns] = dscores
+        dquery_parts.append(pair_diagonal(dot_nn(block_keys_t[heads], dscores), width))
+        dprobs = following
+        if pair == HEADS // 2 - 1:
             dquery_ref[frame, span] = flip(jnp.concatenate(dquery_parts, axis=0))
-            dkeys = dot_nn(dscores_s[frame, block], head_rows(query_ref[frame, span], width))
-            dvalues = dot_nn(probs_ref[frame, block], head_rows(scaled_dattn, width))
-            for entry, place in enumerate(places):
-                rows = pl.ds(place * BLOCK, BLOCK)
-                listed = slice(entry * BLOCK, (entry + 1) * BLOCK)
-                dkv_s[frame, rows, :features] += dkeys[listed]
-                dkv_s[frame, rows, features:] += dvalues[listed]
-        dkv_ref[frame] = dkv_s[frame].astype(BF16)
+    add_keys(len(blocks) - 1)
+    dkv_ref[...] = dkv_s[...].astype(BF16)
     extended = dkv_ref.shape[1]
     act = act_ref[...]
     own_act = act[:, rim : rim + row_count].reshape(frame_count * row_count, features)
@@ -518,43 +644,54 @@
         ref[...] = add_rounded(refs[2 * index], refs[2 * index + 1])
 
 
-def both_kernel(space_ref, space_other_ref, time_ref, total_ref):
-    rows = space_ref.shape[0]
-    total_ref[:rows] = add_rounded(space_ref, space_other_ref)
-    total_ref[rows:] = time_ref[...]
-
-
 def join_kernel(place_ref, *refs):
     *part_refs, joined_ref = refs
-    me = place_ref[0]
-    for distance, ref in enumerate(part_refs):
-        rows = ref.shape[0]
-        joined_ref[pl.ds(pl.multiple_of((me ^ distance) * rows, GROUP_ROWS), rows)] = ref[...]
-
-
-def grads_kernel(time_count, place_ref, own_ref, other_ref, project_ref, combine_ref, halves_s):
-    features = combine_ref.shape[1]
+    count_in = len(part_refs) // 2
+    rows = part_refs[0].shape[0]
+    for layer in range(2):
+        for distance in range(count_in):
+            start = (2 * (place_ref[0] ^ distance) + layer) * rows
+            joined_ref[pl.ds(pl.multiple_of(start, GROUP_ROWS), rows)] = part_refs[
+                layer * count_in + distance
+            ][...]
+
+
+def grads_kernel(time_count, own, place_ref, half_ref, *refs):
+    project_hbm, combine_hbm, wide_s, sems = refs[-4:]
+    features = combine_hbm.shape[1]
     core = place_ref[1] % 2
-    halves_s[core] = own_ref[...]
-    halves_s[1 - core] = other_ref[...]
-    rows = halves_s.shape[1] // time_count // 2
-
-    def place_rows(layer, row, piece):
-        while piece.shape[0]:
-            group, inner = divmod(row, features)
-            taken = min(piece.shape[0], features - inner)
-            start = group * LANES
-            target, start = (
-                (project_ref, start) if start < 3 * features else (combine_ref, start - 3 * features)
-            )
-            target[layer, inner : inner + taken, start : start + LANES] = piece[:taken].astype(F32)
-            row, piece = row + taken, piece[taken:]
+    rows = half_ref.shape[0] // time_count // 2
+    wide_s[...] = half_ref[...].astype(F32).reshape(wide_s.shape)
+
+    def write(half):
+        moves = []
+        for part in range(time_count):
+            for layer, row in ((0, (half * time_count + part) * rows), (1, (2 * part + half) * rows)):
+                group, inner = divmod(row, features)
+                start = group * LANES
+                target, start = (
+                    (project_hbm, start)
+                    if start < 3 * features
+                    else (combine_hbm, start - 3 * features)
+                )
+                piece = 2 * part + layer
+                moves.append(
+                    pltpu.make_async_copy(
+                        wide_s.at[piece],
+                        target.at[layer, pl.ds(inner, rows), pl.ds(start, LANES)],
+                        sems.at[piece],
+                    )
+                )
+        for move in moves:
+            move.start()
+        for move in moves:
+            move.wait()
 
     for half in range(2):
-        for part in range(time_count):
-            start = 2 * part * rows
-            place_rows(0, (half * time_count + part) * rows, halves_s[half, start : start + rows])
-            place_rows(1, (2 * part + half) * rows, halves_s[half, start + rows : start + 2 * rows])
+
+        @pl.when((core if own else 1 - core) == half)
+        def _():
+            write(half)
 
 
 def stack_grads(grads, factor, stacked_ref):
@@ -604,14 +741,18 @@
     vmem_spec = pl.BlockSpec(memory_space=pltpu.VMEM)
     hbm_spec = pl.BlockSpec(memory_space=pl.ANY)
 
-    def call(body, name, scalars, operands, outs, scratch=(), matmuls=1, in_spec=vmem_spec):
+    def call(
+        body, name, scalars, operands, outs, scratch=(), matmuls=1, hbm=(), aliases=None, out_spec=None
+    ):
         def typed(shape):
             return (shape[:-1], shape[-1]) if not isinstance(shape[-1], int) else (shape, BF16)
 
         return pl.pallas_call(
             body,
-            in_specs=[smem_spec] * len(scalars) + [in_spec] * len(operands),
-            out_specs=[vmem_spec] * len(outs),
+            in_specs=[smem_spec] * len(scalars)
+            + [vmem_spec] * len(operands)
+            + [hbm_spec] * len(hbm),
+            out_specs=[out_spec or vmem_spec] * len(outs),
             out_shape=[jax.ShapeDtypeStruct(*typed(shape)) for shape in outs],
             scratch_shapes=[
                 pltpu.VMEM(*typed(shape)) if isinstance(shape, tuple) else shape
@@ -619,8 +760,9 @@
             ],
             compiler_params=pltpu.CompilerParams(vmem_limit_bytes=VMEM_BYTES),
             cost_estimate=cost(matmuls),
+            input_output_aliases=aliases or {},
             name=name,
-        )(*scalars, *operands)
+        )(*scalars, *operands, *hbm)
 
     def over_tm(pieces):
         return [pieces[0]] + [exchange(pieces[d], "tm", d) for d in range(1, time_count)]
@@ -630,43 +772,49 @@
     near = exchange(wave_field, "space", 1)
     far = swap_far(wave_field, "space")
     place = jnp.stack([lax.axis_index("tm"), lax.axis_index("space")]).astype(jnp.int32)
-    wave, project, turned, combine, cot = call(
+    extended_shapes = [
+        (frame_count, extended, features),
+        (frame_count, extended, 2 * features),
+        (frame_count, places, features, BLOCK),
+        (frame_count, places, features, BLOCK),
+    ]
+    wave, project, turned, combine, cot, queries, queries_t, *projected = call(
         prepare_kernel,
         "prepare",
-        [],
-        [in_hbm(cells) for cells in (wave_field, cotangent, project_weights, combine_weights)],
+        [place],
+        [near],
         [
             own,
             (2, features, 3 * features),
             (2, 3 * features, features),
             (2, features, features),
             own,
+            own,
+            (frame_count, features, row_count),
+            *extended_shapes,
         ],
         [pltpu.SemaphoreType.DMA((4,))],
-        matmuls=8,
-        in_spec=hbm_spec,
+        matmuls=12,
+        hbm=[in_hbm(cells) for cells in (wave_field, cotangent, project_weights, combine_weights)],
     )
     block_lists = in_hbm(block_lists)
-
-    outs = call(
+    act, keys_values, keys_t, _, probs, inverse_sum, attended, *parts = call(
         space_forward_kernel,
         "space_forward",
         [block_lists, place],
-        [near, far, wave, cot, project, turned, combine],
+        [far, wave, cot, project, turned, combine, queries_t, *projected],
         [
-            (frame_count, extended, features),
-            (frame_count, extended, 2 * features),
-            (frame_count, places, features, BLOCK),
-            own,
+            *extended_shapes,
             (frame_count, block_count, keys_count, HEADS * BLOCK),
             (frame_count, block_count, HEADS, BLOCK, F32),
             (frame_count, features, row_count),
             *[(frame_count, sent_rows, 2 * features)] * time_count,
         ],
-        [(frame_count, places, features, BLOCK), own, (frame_count, extended, features)],
+        [own],
         matmuls=40,
-    )
-    kept_space, parts = outs[:7], outs[7:]
+        aliases={9 + index: index for index in range(4)},
+    )
+    kept_space = [act, keys_values, keys_t, queries, probs, inverse_sum, attended]
     arrived = over_tm(parts)
 
     def time_body(*refs):
@@ -746,12 +894,13 @@
         [(chunk // 2, LANES)] * (time_count + 1),
         [(half_rows, LANES)],
     )
-    to_near, to_far, *space_pieces = lax.optimization_barrier((to_near, to_far, *space_pieces))
     steps = [2 << bit for bit in range((space_count - 1).bit_length())]
-    space_pieces = over_tm(space_pieces)
-    time_other = exchange(time_piece, "space", steps[0])
     from_far = swap_far(to_far, "space")
     from_near = exchange(to_near, "space", 1)
+    from_near, from_far, *space_pieces = lax.optimization_barrier(
+        (from_near, from_far, *over_tm(space_pieces))
+    )
+    time_other = exchange(time_piece, "space", steps[0])
     space_piece, time_piece = call(
         tm_sum_kernel,
         "add_tm_space",
@@ -770,14 +919,13 @@
             [space_piece, space_other, time_piece, time_other],
             [(chunk // 2, LANES)] * 2,
         )
-    (piece,) = call(
-        both_kernel,
-        "add_space_last",
-        [],
-        [space_piece, exchange(space_piece, "space", steps[-1]), time_piece],
-        [(chunk, LANES)],
-    )
-    joined = over_tm([piece] * time_count)
+    space_other = exchange(space_piece, "space", steps[-1])
+    time_joined = over_tm([time_piece] * time_count)
+    (space_piece,) = call(
+        pairs_kernel, "add_space_last", [], [space_piece, space_other], [(chunk // 2, LANES)]
+    )
+    joined = over_tm([space_piece] * time_count) + time_joined
+
     field_grad, mixed_field = call(
         field_kernel,
         "field_grad",
@@ -790,17 +938,27 @@
     (own_half,) = call(join_kernel, "join_tm", [place], joined, [(grad_rows, LANES)])
     other_half = exchange(own_half, "space", 1)
 
-    def grads_body(*refs):
-        grads_kernel(time_count, *refs)
-
-    project_grad, combine_grad = call(
-        grads_body,
-        "weight_grads",
-        [place],
-        [own_half, other_half],
-        [(2, features, 3 * features, F32), (2, features, features, F32)],
-        [(2, grad_rows, LANES)],
-    )
+    grads = ()
+    for half in (own_half, other_half):
+
+        def grads_body(*refs, mine=half is own_half):
+            grads_kernel(time_count, mine, *refs)
+
+        grads = call(
+            grads_body,
+            "weight_grads",
+            [place],
+            [half],
+            [(2, features, 3 * features, F32), (2, features, features, F32)],
+            [
+                (2 * time_count, grad_rows // time_count // 2, LANES, F32),
+                pltpu.SemaphoreType.DMA((2 * time_count,)),
+            ],
+            hbm=grads,
+            aliases={2: 0, 3: 1} if grads else None,
+            out_spec=pl.BlockSpec(memory_space=pltpu.HBM),
+        )
+    project_grad, combine_grad = grads
     return (mixed_field, field_grad, project_grad, combine_grad)
 
 

time: 93.1 us -> 83.3 us (0.89)
  Pallas kernels: 36.9 us -> 28.9 us
  waiting for transfers between devices: 21.7 us -> 17.6 us
  starting transfers between devices: 33.4 us -> 35.6 us
    pallas_call x14 -> x15, Pallas kernels: 36.9 us -> 28.9 us  [call(): pl.pallas_call(body, in_specs=[smem_spec] * len(scalars) + [vmem_spec] *...]
    ppermute x23 -> x26, waiting for transfers between devices: 21.7 us -> 17.6 us  [exchange(): lax.ppermute(cells, axis, [(i, i ^ distance) for i in range(lax.axis_size...]
    ppermute x23 -> x26, starting transfers between devices: 32.1 us -> 34.3 us  [exchange(): lax.ppermute(cells, axis, [(i, i ^ distance) for i in range(lax.axis_size...]
  transfers between devices with their start and end apart: 25 -> 28, of which waited for: 10 -> 12; matrix products, arithmetic and copies ran while one was open for 0% -> 0% of each run, Pallas kernels for 16% -> 19%
where the time goes in v6:
time: 83.3 us; the launch traced here: 83.1 us
  starting transfers between devices  35.6 us (43%)
  Pallas kernels  28.9 us (35%)
  waiting for transfers between devices  17.6 us (21%)
  between operations  0.97 us (1%)
    ppermute x26, starting transfers between devices, exchange(): lax.ppermute(cells, axis, [(i, i ^ distance) for i in range(lax.axis_size...  34.3 us
    pallas_call x15, Pallas kernels, call(): pl.pallas_call(body, in_specs=[smem_spec] * len(scalars) + [vmem_spec] *...  28.9 us
    ppermute x26, waiting for transfers between devices, exchange(): lax.ppermute(cells, axis, [(i, i ^ distance) for i in range(lax.axis_size...  17.6 us
  transfers between devices with their start and end apart: 28, of which 12 were waited for; matrix products, arithmetic and copies ran while one was open for 0% of the time, Pallas kernels for 19%

profile of v6, /device:TPU:0, one launch (start us, length us, event | category | flops | bytes accessed | tf_op | source)
XLA Modules:
  0.0 83.1 jit_solution(10583890680087341936)
XLA Ops:
  2.5 3.1 %prepare.1 = (bf16[2,256,256]{2,1,0:T(8,128)(2,1)S(1)}, bf16[2,256,768]{2,1,0:T(8,128)(2,1)S(1)}, bf16[2,768,256]{2,1,0:T(8,128)(2,1)S(1)}, bf16[2,256,256]{2,1,...) custom-call(s32[2]{0:T(128)S(1)} %pad_add_fusion.place_ref.refs_1_.r, ...), custom_call_target="tpu_custom_call" | custom-call | flops 3221225472 | bytes 12582912 | tf_op jit(solution)/shard_map/prepare/pallas_call | solution.py:750
  5.7 5.6 %space_forward.1 = (bf16[2,768,256]{2,1,0:T(8,128)(2,1)S(1)}, bf16[2,768,512]{2,1,0:T(8,128)(2,1)S(1)}, bf16[2,6,256,128]{3,2,1,0:T(8,128)(2,1)S(1)}, bf16[2,6,2...) custom-call(s32[2,2,4]{2,1,0:T(2,128)} %refs_0_.1, ...), custom_call_target="tpu_custom_call", output_to_operand_aliasing={{0}: (9, {}), {1}: (10, {}), {2}: (11, {}), {3}: (12, {})} | custom-call | flops 10737418240 | bytes 41943040 | tf_op jit(solution)/shard_map/space_forward/pallas_call | solution.py:750
  11.3 2.9 %collective-permute-start.2 = (bf16[2,64,512]{2,1,0:T(8,128)(2,1)S(1)}, bf16[2,64,512]{2,1,0:T(8,128)(2,1)S(1)}, u32[]{:S(2)}, u32[]{:S(2)}) collective-permute-start(bf16[2,64,512]{2,1,0:T(8,128)(2,1)S(1)} %get-tuple-element.89), channel_id=1, source_target_pairs={{0,8},{8,0},{16,24},{24,16},{1,9},{9,1},{17,25},{25,17},{2,10},{10... | collective-permute-start | bytes 393224 | tf_op jit(solution)/shard_map/ppermute | solution.py:717
  14.3 1.5 %collective-permute-start.3 = (bf16[2,64,512]{2,1,0:T(8,128)(2,1)S(1)}, bf16[2,64,512]{2,1,0:T(8,128)(2,1)S(1)}, u32[]{:S(2)}, u32[]{:S(2)}) collective-permute-start(bf16[2,64,512]{2,1,0:T(8,128)(2,1)S(1)} %get-tuple-element.90), channel_id=1, source_target_pairs={{0,16},{8,24},{16,0},{24,8},{1,17},{9,25},{17,1},{25,9},{2,18},{10... | collective-permute-start | bytes 393224 | tf_op jit(solution)/shard_map/ppermute | solution.py:717
  15.8 1.4 %collective-permute-done.2.refs_1_ = bf16[2,64,512]{2,1,0:T(8,128)(2,1)S(1)} collective-permute-done((bf16[2,64,512]{2,1,0:T(8,128)(2,1)S(1)}, bf16[2,64,512]{2,1,0:T(8,128)(2,1)S(1)}, u32[]{:S(2)}, u32[]{:S(2)}) %collective-permute-start.2) | collective-permute-done | bytes 131104 | tf_op jit(solution)/shard_map/ppermute | solution.py:717
  17.2 2.0 %collective-permute-done.3.refs_2_ = bf16[2,64,512]{2,1,0:T(8,128)(2,1)S(1)} collective-permute-done((bf16[2,64,512]{2,1,0:T(8,128)(2,1)S(1)}, bf16[2,64,512]{2,1,0:T(8,128)(2,1)S(1)}, u32[]{:S(2)}, u32[]{:S(2)}) %collective-permute-start.3) | collective-permute-done | bytes 131104 | tf_op jit(solution)/shard_map/ppermute | solution.py:717
  19.2 3.8 %collective-permute-done.4.refs_3_ = bf16[2,64,512]{2,1,0:T(8,128)(2,1)S(1)} collective-permute-done((bf16[2,64,512]{2,1,0:T(8,128)(2,1)S(1)}, bf16[2,64,512]{2,1,0:T(8,128)(2,1)S(1)}, u32[]{:S(2)}, u32[]{:S(2)}) %collective-permute-start.4) | collective-permute-done | bytes 131104 | tf_op jit(solution)/shard_map/ppermute | solution.py:717
  23.0 3.6 %time_pair.1 = (bf16[2,64,256]{2,1,0:T(8,128)(2,1)S(1)}, bf16[2,64,256]{2,1,0:T(8,128)(2,1)S(1)}, bf16[2,64,256]{2,1,0:T(8,128)(2,1)S(1)}, bf16[2,64,256]{2,1,0:...) custom-call(bf16[2,64,512]{2,1,0:T(8,128)(2,1)S(1)} %get-tuple-eleme, ...), custom_call_target="tpu_custom_call" | custom-call | flops 9663676416 | bytes 37748736 | tf_op jit(solution)/shard_map/time_pair/pallas_call | solution.py:750
  26.8 3.4 %collective-permute-start.7 = (bf16[2,64,256]{2,1,0:T(8,128)(2,1)S(1)}, bf16[2,64,256]{2,1,0:T(8,128)(2,1)S(1)}, u32[]{:S(2)}, u32[]{:S(2)}) collective-permute-start(bf16[2,64,256]{2,1,0:T(8,128)(2,1)S(1)} %get-tuple-element.95), channel_id=1, source_target_pairs={{0,24},{8,16},{16,8},{24,0},{1,25},{9,17},{17,9},{25,1},{2,26},{10... | collective-permute-start | bytes 196616 | tf_op jit(solution)/shard_map/ppermute | solution.py:717
  31.9 2.9 %collective-permute-start.12 = (bf16[768,128]{1,0:T(8,128)(2,1)S(1)}, bf16[768,128]{1,0:T(8,128)(2,1)S(1)}, u32[]{:S(2)}, u32[]{:S(2)}) collective-permute-start(bf16[768,128]{1,0:T(8,128)(2,1)S(1)} %get-tuple-element.118), channel_id=1, source_target_pairs={{0,24},{8,16},{16,8},{24,0},{1,25},{9,17},{17,9},{25,1},{2,26},{10... | collective-permute-start | bytes 589832 | tf_op jit(solution)/shard_map/ppermute | solution.py:717
  34.8 6.4 %space_backward.1 = (bf16[2,256,256]{2,1,0:T(8,128)(2,1)S(1)}, bf16[2,256,256]{2,1,0:T(8,128)(2,1)S(1)}, bf16[2,768,512]{2,1,0:T(8,128)(2,1)S(1)}, bf16[2048,128]{1,0:T(8,128)(2,1)S(1)}) custom-call(s32[2,2,4]{2,1,0:T(2,128)} %refs_0_.1, s32[2]{0:T(128)S(1)} %pad_add_fusion.place_ref.refs_1_.refs_0_, bf16[2,64,256]{2,1,0:T(8,128)(2,1)S(1)} %get-tuple-element.92.refs_2_, ...), custom_call_target="tpu_custom_call" | custom-call | flops 11811160064 | bytes 46137344 | tf_op jit(solution)/shard_map/space_backward/pallas_call | solution.py:750
  41.2 1.8 %collective-permute-done.11.refs_2_ = bf16[768,128]{1,0:T(8,128)(2,1)S(1)} collective-permute-done((bf16[768,128]{1,0:T(8,128)(2,1)S(1)}, bf16[768,128]{1,0:T(8,128)(2,1)S(1)}, u32[]{:S(2)}, u32[]{:S(2)}) %collective-permute-start.11) | collective-permute-done | bytes 196640 | tf_op jit(solution)/shard_map/ppermute | solution.py:717
  47.0 1.4 %collective-permute-start.14 = (bf16[256,128]{1,0:T(8,128)(2,1)S(1)}, bf16[256,128]{1,0:T(8,128)(2,1)S(1)}, u32[]{:S(2)}, u32[]{:S(2)}) collective-permute-start(bf16[256,128]{1,0:T(8,128)(2,1)S(1)} %get-tuple-element.122), channel_id=1, source_target_pairs={{0,8},{8,0},{16,24},{24,16},{1,9},{9,1},{17,25},{25,17},{2,10},{10... | collective-permute-start | bytes 196616 | tf_op jit(solution)/shard_map/ppermute | solution.py:717
  50.6 5.0 %collective-permute-start.17 = (bf16[256,128]{1,0:T(8,128)(2,1)S(1)}, bf16[256,128]{1,0:T(8,128)(2,1)S(1)}, u32[]{:S(2)}, u32[]{:S(2)}) collective-permute-start(bf16[256,128]{1,0:T(8,128)(2,1)S(1)} %get-tuple-element.133.refs_4_), channel_id=1, source_target_pairs={{0,2},{1,3},{2,0},{3,1},{4,6},{5,7},{6,4},{7,5},{8,10},{9,11},{10,... | collective-permute-start | bytes 196616 | tf_op jit(solution)/shard_map/ppermute | solution.py:717
  55.6 2.6 %collective-permute-done.17.refs_5_ = bf16[256,128]{1,0:T(8,128)(2,1)S(1)} collective-permute-done((bf16[256,128]{1,0:T(8,128)(2,1)S(1)}, bf16[256,128]{1,0:T(8,128)(2,1)S(1)}, u32[]{:S(2)}, u32[]{:S(2)}) %collective-permute-start.17) | collective-permute-done | bytes 65568 | tf_op jit(solution)/shard_map/ppermute | solution.py:717
  58.8 2.3 %collective-permute-start.18 = (bf16[256,128]{1,0:T(8,128)(2,1)S(1)}, bf16[256,128]{1,0:T(8,128)(2,1)S(1)}, u32[]{:S(2)}, u32[]{:S(2)}) collective-permute-start(bf16[256,128]{1,0:T(8,128)(2,1)S(1)} %get-tuple-element.134.refs_0_), channel_id=1, source_target_pairs={{0,2},{1,3},{2,0},{3,1},{4,6},{5,7},{6,4},{7,5},{8,10},{9,11},{10,... | collective-permute-start | bytes 196616 | tf_op jit(solution)/shard_map/ppermute | solution.py:717
  61.1 2.1 %collective-permute-start.19 = (bf16[256,128]{1,0:T(8,128)(2,1)S(1)}, bf16[256,128]{1,0:T(8,128)(2,1)S(1)}, u32[]{:S(2)}, u32[]{:S(2)}) collective-permute-start(bf16[256,128]{1,0:T(8,128)(2,1)S(1)} %get-tuple-element.135.refs_2_), channel_id=1, source_target_pairs={{0,4},{1,5},{2,6},{3,7},{4,0},{5,1},{6,2},{7,3},{8,12},{9,13},{10,... | collective-permute-start | bytes 196616 | tf_op jit(solution)/shard_map/ppermute | solution.py:717
  63.3 3.5 %collective-permute-done.19.refs_3_ = bf16[256,128]{1,0:T(8,128)(2,1)S(1)} collective-permute-done((bf16[256,128]{1,0:T(8,128)(2,1)S(1)}, bf16[256,128]{1,0:T(8,128)(2,1)S(1)}, u32[]{:S(2)}, u32[]{:S(2)}) %collective-permute-start.19) | collective-permute-done | bytes 65568 | tf_op jit(solution)/shard_map/ppermute | solution.py:717
  66.9 1.6 %collective-permute-start.20 = (bf16[256,128]{1,0:T(8,128)(2,1)S(1)}, bf16[256,128]{1,0:T(8,128)(2,1)S(1)}, u32[]{:S(2)}, u32[]{:S(2)}) collective-permute-start(bf16[256,128]{1,0:T(8,128)(2,1)S(1)} %get-tuple-element.136.refs_0_), channel_id=1, source_target_pairs={{0,4},{1,5},{2,6},{3,7},{4,0},{5,1},{6,2},{7,3},{8,12},{9,13},{10,... | collective-permute-start | bytes 196616 | tf_op jit(solution)/shard_map/ppermute | solution.py:717
  68.5 1.7 %collective-permute-start.26 = (bf16[256,128]{1,0:T(8,128)(2,1)S(1)}, bf16[256,128]{1,0:T(8,128)(2,1)S(1)}, u32[]{:S(2)}, u32[]{:S(2)}) collective-permute-start(bf16[256,128]{1,0:T(8,128)(2,1)S(1)} %get-tuple-element.144.refs_4_), channel_id=1, source_target_pairs={{0,24},{8,16},{16,8},{24,0},{1,25},{9,17},{17,9},{25,1},{2,26},{10... | collective-permute-start | bytes 196616 | tf_op jit(solution)/shard_map/ppermute | solution.py:717
  72.2 1.7 %collective-permute-start.23 = (bf16[256,128]{1,0:T(8,128)(2,1)S(1)}, bf16[256,128]{1,0:T(8,128)(2,1)S(1)}, u32[]{:S(2)}, u32[]{:S(2)}) collective-permute-start(bf16[256,128]{1,0:T(8,128)(2,1)S(1)} %add_space_last.1.refs_0_), channel_id=1, source_target_pairs={{0,24},{8,16},{16,8},{24,0},{1,25},{9,17},{17,9},{25,1},{2,26},{10... | collective-permute-start | bytes 196616 | tf_op jit(solution)/shard_map/ppermute | solution.py:717
  75.8 1.8 %field_grad.1 = (bf16[2,256,256]{2,1,0:T(8,128)(2,1)}, bf16[2,256,256]{2,1,0:T(8,128)(2,1)}) custom-call(s32[2]{0:T(128)S(1)} %pad_add_fusion.place_ref.refs_1_.refs_0_, bf16[2,256,256]{2,1,0:T(8,128)(2,1)S(1)} %get-tuple-element.78.wave_ref, bf16[2,256,256]{2,1,0:T(8,128)(2,1)S(1)} %get-tuple-element.103.mixed_grad_ref, ...), custom_call_target="tpu_custom_call" | custom-call | flops 805306368 | bytes 3145728 | tf_op jit(solution)/shard_map/field_grad/pallas_call | solution.py:750
  79.4 1.6 %weight_grads.2 = (f32[2,256,768]{2,1,0:T(8,128)}, f32[2,256,256]{2,1,0:T(8,128)}) custom-call(s32[2]{0:T(128)S(1)} %pad_add_fusion.place_ref.refs_1_.refs_0_, bf16[2048,128]{1,0:T(8,128)(2,1)S(1)} %join_tm.1.refs_1_), custom_call_target="tpu_custom_call" | custom-call | flops 268435456 | bytes 1048576 | tf_op jit(solution)/shard_map/weight_grads/pallas_call | solution.py:750
  81.3 1.6 %weight_grads.3 = (f32[2,256,768]{2,1,0:T(8,128)}, f32[2,256,256]{2,1,0:T(8,128)}) custom-call(s32[2]{0:T(128)S(1)} %pad_add_fusion.place_ref.refs_1_.refs_0_, bf16[2048,128]{1,0:T(8,128)(2,1)S(1)} %collective-permute-done.27.refs_1_, f32[2,256,768]{2,1,0:T(8,128)} %get-tuple-element.148.refs_2_, ...), custom_call_target="tpu_custom_call", output_to_operand_aliasing={{0}: (2, {}), {1}: (3, {})} | custom-call | flops 268435456 | bytes 1048576 | tf_op jit(solution)/shard_map/weight_grads/pallas_call | solution.py:750
  (48 shorter events, 16.9 us)
Async XLA Ops:
  1.1 4.5 %collective-permute-start.1 = (bf16[2,256,256]{2,1,0:T(8,128)(2,1)}, bf16[2,256,256]{2,1,0:T(8,128)(2,1)S(1)}, u32[]{:S(2)}, u32[]{:S(2)}) collective-permute-start(bf16[2,256,256]{2,1,0:T(8,128)(2,1)} %wave_hbm.1), channel_id=1, source_target_pairs={{1,2},{3,4},{5,6},{2,1},{4,3},{6,5},{9,10},{11,12},{13,14},{10,9},... | collective-permute-start | bytes 786440 | tf_op jit(solution)/shard_map/ppermute | solution.py:713
  11.3 5.9 %collective-permute-start.2 = (bf16[2,64,512]{2,1,0:T(8,128)(2,1)S(1)}, bf16[2,64,512]{2,1,0:T(8,128)(2,1)S(1)}, u32[]{:S(2)}, u32[]{:S(2)}) collective-permute-start(bf16[2,64,512]{2,1,0:T(8,128)(2,1)S(1)} %get-tuple-element.89), channel_id=1, source_target_pairs={{0,8},{8,0},{16,24},{24,16},{1,9},{9,1},{17,25},{25,17},{2,10},{10... | collective-permute-start | bytes 393224 | tf_op jit(solution)/shard_map/ppermute | solution.py:717
  14.3 5.0 %collective-permute-start.3 = (bf16[2,64,512]{2,1,0:T(8,128)(2,1)S(1)}, bf16[2,64,512]{2,1,0:T(8,128)(2,1)S(1)}, u32[]{:S(2)}, u32[]{:S(2)}) collective-permute-start(bf16[2,64,512]{2,1,0:T(8,128)(2,1)S(1)} %get-tuple-element.90), channel_id=1, source_target_pairs={{0,16},{8,24},{16,0},{24,8},{1,17},{9,25},{17,1},{25,9},{2,18},{10... | collective-permute-start | bytes 393224 | tf_op jit(solution)/shard_map/ppermute | solution.py:717
  15.8 7.2 %collective-permute-start.4 = (bf16[2,64,512]{2,1,0:T(8,128)(2,1)S(1)}, bf16[2,64,512]{2,1,0:T(8,128)(2,1)S(1)}, u32[]{:S(2)}, u32[]{:S(2)}) collective-permute-start(bf16[2,64,512]{2,1,0:T(8,128)(2,1)S(1)} %get-tuple-element.91), channel_id=1, source_target_pairs={{0,24},{8,16},{16,8},{24,0},{1,25},{9,17},{17,9},{25,1},{2,26},{10... | collective-permute-start | bytes 393224 | tf_op jit(solution)/shard_map/ppermute | solution.py:717
  26.6 5.2 %collective-permute-start.5 = (bf16[2,64,256]{2,1,0:T(8,128)(2,1)S(1)}, bf16[2,64,256]{2,1,0:T(8,128)(2,1)S(1)}, u32[]{:S(2)}, u32[]{:S(2)}) collective-permute-start(bf16[2,64,256]{2,1,0:T(8,128)(2,1)S(1)} %get-tuple-element.93), channel_id=1, source_target_pairs={{0,8},{8,0},{16,24},{24,16},{1,9},{9,1},{17,25},{25,17},{2,10},{10... | collective-permute-start | bytes 196616 | tf_op jit(solution)/shard_map/ppermute | solution.py:717
  26.8 8.0 %collective-permute-start.6 = (bf16[2,64,256]{2,1,0:T(8,128)(2,1)S(1)}, bf16[2,64,256]{2,1,0:T(8,128)(2,1)S(1)}, u32[]{:S(2)}, u32[]{:S(2)}) collective-permute-start(bf16[2,64,256]{2,1,0:T(8,128)(2,1)S(1)} %get-tuple-element.94), channel_id=1, source_target_pairs={{0,16},{8,24},{16,0},{24,8},{1,17},{9,25},{17,1},{25,9},{2,18},{10... | collective-permute-start | bytes 196616 | tf_op jit(solution)/shard_map/ppermute | solution.py:717
  26.8 8.0 %collective-permute-start.7 = (bf16[2,64,256]{2,1,0:T(8,128)(2,1)S(1)}, bf16[2,64,256]{2,1,0:T(8,128)(2,1)S(1)}, u32[]{:S(2)}, u32[]{:S(2)}) collective-permute-start(bf16[2,64,256]{2,1,0:T(8,128)(2,1)S(1)} %get-tuple-element.95), channel_id=1, source_target_pairs={{0,24},{8,16},{16,8},{24,0},{1,25},{9,17},{17,9},{25,1},{2,26},{10... | collective-permute-start | bytes 196616 | tf_op jit(solution)/shard_map/ppermute | solution.py:717
  31.2 10.0 %collective-permute-start.10 = (bf16[768,128]{1,0:T(8,128)(2,1)S(1)}, bf16[768,128]{1,0:T(8,128)(2,1)S(1)}, u32[]{:S(2)}, u32[]{:S(2)}) collective-permute-start(bf16[768,128]{1,0:T(8,128)(2,1)S(1)} %get-tuple-element.116), channel_id=1, source_target_pairs={{0,8},{8,0},{16,24},{24,16},{1,9},{9,1},{17,25},{25,17},{2,10},{10... | collective-permute-start | bytes 589832 | tf_op jit(solution)/shard_map/ppermute | solution.py:717
  31.4 11.5 %collective-permute-start.11 = (bf16[768,128]{1,0:T(8,128)(2,1)S(1)}, bf16[768,128]{1,0:T(8,128)(2,1)S(1)}, u32[]{:S(2)}, u32[]{:S(2)}) collective-permute-start(bf16[768,128]{1,0:T(8,128)(2,1)S(1)} %get-tuple-element.117), channel_id=1, source_target_pairs={{0,16},{8,24},{16,0},{24,8},{1,17},{9,25},{17,1},{25,9},{2,18},{10... | collective-permute-start | bytes 589832 | tf_op jit(solution)/shard_map/ppermute | solution.py:717
  31.9 11.1 %collective-permute-start.12 = (bf16[768,128]{1,0:T(8,128)(2,1)S(1)}, bf16[768,128]{1,0:T(8,128)(2,1)S(1)}, u32[]{:S(2)}, u32[]{:S(2)}) collective-permute-start(bf16[768,128]{1,0:T(8,128)(2,1)S(1)} %get-tuple-element.118), channel_id=1, source_target_pairs={{0,24},{8,16},{16,8},{24,0},{1,25},{9,17},{17,9},{25,1},{2,26},{10... | collective-permute-start | bytes 589832 | tf_op jit(solution)/shard_map/ppermute | solution.py:717
  45.1 5.5 %collective-permute-start.8 = (bf16[2,256,256]{2,1,0:T(8,128)(2,1)S(1)}, bf16[2,256,256]{2,1,0:T(8,128)(2,1)S(1)}, u32[]{:S(2)}, u32[]{:S(2)}) collective-permute-start(bf16[2,256,256]{2,1,0:T(8,128)(2,1)S(1)} %get-tuple-element.107), channel_id=1, source_target_pairs={{0,1},{1,0},{2,3},{3,2},{4,5},{5,4},{6,7},{7,6},{8,9},{9,8},{10,11... | collective-permute-start | bytes 786440 | tf_op jit(solution)/shard_map/ppermute | solution.py:717
  45.6 9.9 %collective-permute-start.9 = (bf16[2,256,256]{2,1,0:T(8,128)(2,1)S(1)}, bf16[2,256,256]{2,1,0:T(8,128)(2,1)S(1)}, u32[]{:S(2)}, u32[]{:S(2)}) collective-permute-start(bf16[2,256,256]{2,1,0:T(8,128)(2,1)S(1)} %get-tuple-element.108), channel_id=1, source_target_pairs={{1,2},{3,4},{5,6},{2,1},{4,3},{6,5},{9,10},{11,12},{13,14},{10,9},... | collective-permute-start | bytes 786440 | tf_op jit(solution)/shard_map/ppermute | solution.py:713
  47.0 8.5 %collective-permute-start.14 = (bf16[256,128]{1,0:T(8,128)(2,1)S(1)}, bf16[256,128]{1,0:T(8,128)(2,1)S(1)}, u32[]{:S(2)}, u32[]{:S(2)}) collective-permute-start(bf16[256,128]{1,0:T(8,128)(2,1)S(1)} %get-tuple-element.122), channel_id=1, source_target_pairs={{0,8},{8,0},{16,24},{24,16},{1,9},{9,1},{17,25},{25,17},{2,10},{10... | collective-permute-start | bytes 196616 | tf_op jit(solution)/shard_map/ppermute | solution.py:717
  48.4 7.2 %collective-permute-start.15 = (bf16[256,128]{1,0:T(8,128)(2,1)S(1)}, bf16[256,128]{1,0:T(8,128)(2,1)S(1)}, u32[]{:S(2)}, u32[]{:S(2)}) collective-permute-start(bf16[256,128]{1,0:T(8,128)(2,1)S(1)} %get-tuple-element.123), channel_id=1, source_target_pairs={{0,16},{8,24},{16,0},{24,8},{1,17},{9,25},{17,1},{25,9},{2,18},{10... | collective-permute-start | bytes 196616 | tf_op jit(solution)/shard_map/ppermute | solution.py:717
  49.4 6.2 %collective-permute-start.16 = (bf16[256,128]{1,0:T(8,128)(2,1)S(1)}, bf16[256,128]{1,0:T(8,128)(2,1)S(1)}, u32[]{:S(2)}, u32[]{:S(2)}) collective-permute-start(bf16[256,128]{1,0:T(8,128)(2,1)S(1)} %get-tuple-element.124), channel_id=1, source_target_pairs={{0,24},{8,16},{16,8},{24,0},{1,25},{9,17},{17,9},{25,1},{2,26},{10... | collective-permute-start | bytes 196616 | tf_op jit(solution)/shard_map/ppermute | solution.py:717
  50.6 7.6 %collective-permute-start.17 = (bf16[256,128]{1,0:T(8,128)(2,1)S(1)}, bf16[256,128]{1,0:T(8,128)(2,1)S(1)}, u32[]{:S(2)}, u32[]{:S(2)}) collective-permute-start(bf16[256,128]{1,0:T(8,128)(2,1)S(1)} %get-tuple-element.133.refs_4_), channel_id=1, source_target_pairs={{0,2},{1,3},{2,0},{3,1},{4,6},{5,7},{6,4},{7,5},{8,10},{9,11},{10,... | collective-permute-start | bytes 196616 | tf_op jit(solution)/shard_map/ppermute | solution.py:717
  58.8 4.5 %collective-permute-start.18 = (bf16[256,128]{1,0:T(8,128)(2,1)S(1)}, bf16[256,128]{1,0:T(8,128)(2,1)S(1)}, u32[]{:S(2)}, u32[]{:S(2)}) collective-permute-start(bf16[256,128]{1,0:T(8,128)(2,1)S(1)} %get-tuple-element.134.refs_0_), channel_id=1, source_target_pairs={{0,2},{1,3},{2,0},{3,1},{4,6},{5,7},{6,4},{7,5},{8,10},{9,11},{10,... | collective-permute-start | bytes 196616 | tf_op jit(solution)/shard_map/ppermute | solution.py:717
  61.1 5.8 %collective-permute-start.19 = (bf16[256,128]{1,0:T(8,128)(2,1)S(1)}, bf16[256,128]{1,0:T(8,128)(2,1)S(1)}, u32[]{:S(2)}, u32[]{:S(2)}) collective-permute-start(bf16[256,128]{1,0:T(8,128)(2,1)S(1)} %get-tuple-element.135.refs_2_), channel_id=1, source_target_pairs={{0,4},{1,5},{2,6},{3,7},{4,0},{5,1},{6,2},{7,3},{8,12},{9,13},{10,... | collective-permute-start | bytes 196616 | tf_op jit(solution)/shard_map/ppermute | solution.py:717
  66.9 5.3 %collective-permute-start.20 = (bf16[256,128]{1,0:T(8,128)(2,1)S(1)}, bf16[256,128]{1,0:T(8,128)(2,1)S(1)}, u32[]{:S(2)}, u32[]{:S(2)}) collective-permute-start(bf16[256,128]{1,0:T(8,128)(2,1)S(1)} %get-tuple-element.136.refs_0_), channel_id=1, source_target_pairs={{0,4},{1,5},{2,6},{3,7},{4,0},{5,1},{6,2},{7,3},{8,12},{9,13},{10,... | collective-permute-start | bytes 196616 | tf_op jit(solution)/shard_map/ppermute | solution.py:717
  68.5 6.0 %collective-permute-start.26 = (bf16[256,128]{1,0:T(8,128)(2,1)S(1)}, bf16[256,128]{1,0:T(8,128)(2,1)S(1)}, u32[]{:S(2)}, u32[]{:S(2)}) collective-permute-start(bf16[256,128]{1,0:T(8,128)(2,1)S(1)} %get-tuple-element.144.refs_4_), channel_id=1, source_target_pairs={{0,24},{8,16},{16,8},{24,0},{1,25},{9,17},{17,9},{25,1},{2,26},{10... | collective-permute-start | bytes 196616 | tf_op jit(solution)/shard_map/ppermute | solution.py:717
  70.2 7.4 %collective-permute-start.25 = (bf16[256,128]{1,0:T(8,128)(2,1)S(1)}, bf16[256,128]{1,0:T(8,128)(2,1)S(1)}, u32[]{:S(2)}, u32[]{:S(2)}) collective-permute-start(bf16[256,128]{1,0:T(8,128)(2,1)S(1)} %get-tuple-element.144.refs_4_), channel_id=1, source_target_pairs={{0,16},{8,24},{16,0},{24,8},{1,17},{9,25},{17,1},{25,9},{2,18},{10... | collective-permute-start | bytes 196616 | tf_op jit(solution)/shard_map/ppermute | solution.py:717
  70.7 6.9 %collective-permute-start.24 = (bf16[256,128]{1,0:T(8,128)(2,1)S(1)}, bf16[256,128]{1,0:T(8,128)(2,1)S(1)}, u32[]{:S(2)}, u32[]{:S(2)}) collective-permute-start(bf16[256,128]{1,0:T(8,128)(2,1)S(1)} %get-tuple-element.144.refs_4_), channel_id=1, source_target_pairs={{0,8},{8,0},{16,24},{24,16},{1,9},{9,1},{17,25},{25,17},{2,10},{10... | collective-permute-start | bytes 196616 | tf_op jit(solution)/shard_map/ppermute | solution.py:717
  72.2 5.3 %collective-permute-start.23 = (bf16[256,128]{1,0:T(8,128)(2,1)S(1)}, bf16[256,128]{1,0:T(8,128)(2,1)S(1)}, u32[]{:S(2)}, u32[]{:S(2)}) collective-permute-start(bf16[256,128]{1,0:T(8,128)(2,1)S(1)} %add_space_last.1.refs_0_), channel_id=1, source_target_pairs={{0,24},{8,16},{16,8},{24,0},{1,25},{9,17},{17,9},{25,1},{2,26},{10... | collective-permute-start | bytes 196616 | tf_op jit(solution)/shard_map/ppermute | solution.py:717
  74.5 4.3 %collective-permute-start.21 = (bf16[256,128]{1,0:T(8,128)(2,1)S(1)}, bf16[256,128]{1,0:T(8,128)(2,1)S(1)}, u32[]{:S(2)}, u32[]{:S(2)}) collective-permute-start(bf16[256,128]{1,0:T(8,128)(2,1)S(1)} %add_space_last.1.refs_0_), channel_id=1, source_target_pairs={{0,8},{8,0},{16,24},{24,16},{1,9},{9,1},{17,25},{25,17},{2,10},{10... | collective-permute-start | bytes 196616 | tf_op jit(solution)/shard_map/ppermute | solution.py:717
  (4 other events, 10.8 us)

commit v7 on v6

--- a/solution.py
+++ b/solution.py
@@ -448,9 +448,11 @@
         mixed_grad_ref,
         dquery_ref,
         dkv_ref,
-        stacked_ref,
+        kept_ref,
+        sent_ref,
         dscores_s,
         dkv_s,
+        stacked_s,
     ) = refs[count_in:]
     me = place_ref[0]
     frame_count, row_count, features = mixed_grad_ref.shape
@@ -558,8 +560,9 @@
             ),
         ],
         factor,
-        stacked_ref,
-    )
+        stacked_s,
+    )
+    halve(place_ref[1] % 2, stacked_s, kept_ref, sent_ref)
 
 
 def dact_kernel(place_ref, dquery_ref, dkv_ref, project_ref, dact_ref, near_ref, far_ref, dact_s):
@@ -607,25 +610,24 @@
     return total.astype(BF16)
 
 
-def cores_kernel(place_ref, space_ref, *refs):
+def halve(core, whole_s, kept_ref, sent_ref):
+    half = kept_ref.shape[0]
+    kept_ref[...] = whole_s[pl.ds(pl.multiple_of(core * half, GROUP_ROWS), half)]
+    sent_ref[...] = whole_s[pl.ds(pl.multiple_of((1 - core) * half, GROUP_ROWS), half)]
+
+
+def cores_kernel(place_ref, *refs):
     *ride_refs, kept_ref, sent_ref, parts_s, time_s = refs
-    core = place_ref[1] % 2
     time_s[...] = ordered_sum(place_ref[0], ride_refs, parts_s)
-    space_half, time_half = space_ref.shape[0] // 2, time_s.shape[0] // 2
-    for half, ref in ((core, kept_ref), (1 - core, sent_ref)):
-        ref[:space_half] = space_ref[
-            pl.ds(pl.multiple_of(half * space_half, GROUP_ROWS), space_half)
-        ]
-        ref[space_half:] = time_s[pl.ds(pl.multiple_of(half * time_half, GROUP_ROWS), time_half)]
+    halve(place_ref[1] % 2, time_s, kept_ref, sent_ref)
 
 
 def split_kernel(place_ref, kept_ref, arrived_ref, *refs):
-    *part_refs, time_ref, sum_s = refs
-    sum_s[...] = (kept_ref[...].astype(F32) + arrived_ref[...].astype(F32)).astype(BF16)
+    *part_refs, sum_s = refs
+    sum_s[...] = add_rounded(kept_ref, arrived_ref)
     rows = part_refs[0].shape[0]
     for distance, ref in enumerate(part_refs):
         ref[...] = sum_s[pl.ds(pl.multiple_of((place_ref[0] ^ distance) * rows, GROUP_ROWS), rows)]
-    time_ref[...] = sum_s[rows * len(part_refs) :]
 
 
 def tm_sum_kernel(place_ref, *refs):
@@ -644,16 +646,19 @@
         ref[...] = add_rounded(refs[2 * index], refs[2 * index + 1])
 
 
+def both_kernel(space_ref, space_other_ref, time_ref, total_ref):
+    rows = space_ref.shape[0]
+    total_ref[:rows] = add_rounded(space_ref, space_other_ref)
+    total_ref[rows:] = time_ref[...]
+
+
 def join_kernel(place_ref, *refs):
     *part_refs, joined_ref = refs
-    count_in = len(part_refs) // 2
-    rows = part_refs[0].shape[0]
-    for layer in range(2):
-        for distance in range(count_in):
-            start = (2 * (place_ref[0] ^ distance) + layer) * rows
-            joined_ref[pl.ds(pl.multiple_of(start, GROUP_ROWS), rows)] = part_refs[
-                layer * count_in + distance
-            ][...]
+    for distance, ref in enumerate(part_refs):
+        rows = ref.shape[0]
+        joined_ref[pl.ds(pl.multiple_of((place_ref[0] ^ distance) * rows, GROUP_ROWS), rows)] = ref[
+            ...
+        ]
 
 
 def grads_kernel(time_count, own, place_ref, half_ref, *refs):
@@ -733,7 +738,6 @@
     space_count = lax.axis_size("space") // 2
     grad_rows = 4 * features // LANES * features
     chunk = grad_rows // time_count
-    half_rows = grad_rows // 2 + chunk // 2
     ride_rows = chunk + frame_count * sent_rows * features // LANES
     tokens = all_frames * sent_rows
     places = block_count + 2 * HREACH
@@ -851,32 +855,63 @@
     )
     returned = over_tm(parts)
     rides = over_tm(rides)
+    returned[1], rides[0] = lax.optimization_barrier((returned[1], rides[0]))
 
     def backward_body(*refs):
         space_backward_kernel(scale, factor, time_count, *refs)
 
-    mixed_grad, dquery, dkv, space_grads = call(
+    mixed_grad, dquery, dkv, space_kept, space_sent = call(
         backward_body,
         "space_backward",
         [block_lists, place],
         [*returned, *kept_space, combine],
-        [own, own, (frame_count, extended, 2 * features), (grad_rows, LANES)],
+        [own, own, (frame_count, extended, 2 * features), *[(grad_rows // 2, LANES)] * 2],
         [
             (frame_count, block_count, keys_count, HEADS * BLOCK),
             (frame_count, extended, 2 * features, F32),
+            (grad_rows, LANES),
         ],
         matmuls=44,
     )
 
-    kept, sent = call(
+    def add_pair(name, piece, other):
+        (total,) = call(pairs_kernel, name, [], [piece, other], [(chunk // 2, LANES)])
+        return total
+
+    space_other = exchange(space_sent, "space", 1)
+    time_kept, time_sent = call(
         cores_kernel,
         "add_tm_time",
         [place],
-        [space_grads, *rides],
-        [(half_rows, LANES)] * 2,
+        rides,
+        [(chunk // 2, LANES)] * 2,
         [(time_count, chunk, LANES), (chunk, LANES)],
-    )
-    other = exchange(sent, "space", 1)
+        matmuls=24,
+    )
+    time_other = exchange(time_sent, "space", 1)
+    space_other, time_kept = lax.optimization_barrier((space_other, time_kept))
+    space_pieces = call(
+        split_kernel,
+        "add_cores",
+        [place],
+        [space_kept, space_other],
+        [(chunk // 2, LANES)] * time_count,
+        [(grad_rows // 2, LANES)],
+    )
+    space_pieces = over_tm(space_pieces)
+    time_piece = add_pair("add_cores_time", time_kept, time_other)
+    steps = [2 << bit for bit in range((space_count - 1).bit_length())]
+    time_other = exchange(time_piece, "space", steps[0])
+    space_piece, time_piece = call(
+        tm_sum_kernel,
+        "add_tm_space",
+        [place],
+        [*space_pieces, time_piece, time_other],
+        [(chunk // 2, LANES)] * 2,
+        [(time_count, chunk // 2, LANES)],
+    )
+
+    space_piece, dquery = lax.optimization_barrier((space_piece, dquery))
     dact, to_near, to_far = call(
         dact_kernel,
         "space_dact",
@@ -886,45 +921,26 @@
         [(frame_count, extended, features)],
         matmuls=3,
     )
-    *space_pieces, time_piece = call(
-        split_kernel,
-        "add_cores",
-        [place],
-        [kept, other],
-        [(chunk // 2, LANES)] * (time_count + 1),
-        [(half_rows, LANES)],
-    )
-    steps = [2 << bit for bit in range((space_count - 1).bit_length())]
-    from_far = swap_far(to_far, "space")
-    from_near = exchange(to_near, "space", 1)
-    from_near, from_far, *space_pieces = lax.optimization_barrier(
-        (from_near, from_far, *over_tm(space_pieces))
-    )
-    time_other = exchange(time_piece, "space", steps[0])
-    space_piece, time_piece = call(
-        tm_sum_kernel,
-        "add_tm_space",
-        [place],
-        [*space_pieces, time_piece, time_other],
-        [(chunk // 2, LANES)] * 2,
-        [(time_count, chunk // 2, LANES)],
-    )
     for step, time_step in zip(steps, steps[1:]):
         space_other = exchange(space_piece, "space", step)
         time_other = exchange(time_piece, "space", time_step)
-        space_piece, time_piece = call(
-            pairs_kernel,
-            "add_space",
-            [],
-            [space_piece, space_other, time_piece, time_other],
-            [(chunk // 2, LANES)] * 2,
-        )
+        space_other, to_near, to_far = lax.optimization_barrier((space_other, to_near, to_far))
+        space_piece = add_pair("add_space", space_piece, space_other)
+        space_piece, time_other = lax.optimization_barrier((space_piece, time_other))
+        time_piece = add_pair("add_space_time", time_piece, time_other)
     space_other = exchange(space_piece, "space", steps[-1])
-    time_joined = over_tm([time_piece] * time_count)
-    (space_piece,) = call(
-        pairs_kernel, "add_space_last", [], [space_piece, space_other], [(chunk // 2, LANES)]
-    )
-    joined = over_tm([space_piece] * time_count) + time_joined
+    time_piece, to_near, to_far = lax.optimization_barrier((time_piece, to_near, to_far))
+    from_far = swap_far(to_far, "space")
+    from_near = exchange(to_near, "space", 1)
+    (piece,) = call(
+        both_kernel,
+        "add_space_last",
+        [],
+        [space_piece, space_other, time_piece],
+        [(chunk, LANES)],
+        matmuls=64,
+    )
+    joined = over_tm([piece] * time_count)
 
     field_grad, mixed_field = call(
         field_kernel,

time: 83.3 us -> 81.2 us (0.975)
  starting transfers between devices: 35.6 us -> 28.3 us
  waiting for transfers between devices: 17.6 us -> 22.7 us
    ppermute x26 -> x24, starting transfers between devices: 34.3 us -> 27 us  [exchange(): lax.ppermute(cells, axis, [(i, i ^ distance) for i in range(lax.axis_size...]
    ppermute x26 -> x24, waiting for transfers between devices: 17.6 us -> 22.7 us  [exchange(): lax.ppermute(cells, axis, [(i, i ^ distance) for i in range(lax.axis_size...]
    pallas_call x15 -> x17, Pallas kernels: 28.9 us -> 28.9 us  [call(): pl.pallas_call(body, in_specs=[smem_spec] * len(scalars) + [vmem_spec] *...]
  transfers between devices with their start and end apart: 28 -> 26, of which waited for: 12 -> 13; matrix products, arithmetic and copies ran while one was open for 0% -> 0% of each run, Pallas kernels for 19% -> 21%
where the time goes in v7:
time: 81.2 us; the launch traced here: 81 us
  Pallas kernels  28.9 us (36%)
  starting transfers between devices  28.3 us (35%)
  waiting for transfers between devices  22.7 us (28%)
  between operations  0.97 us (1%)
    pallas_call x17, Pallas kernels, call(): pl.pallas_call(body, in_specs=[smem_spec] * len(scalars) + [vmem_spec] *...  28.9 us
    ppermute x24, starting transfers between devices, exchange(): lax.ppermute(cells, axis, [(i, i ^ distance) for i in range(lax.axis_size...  27 us
    ppermute x24, waiting for transfers between devices, exchange(): lax.ppermute(cells, axis, [(i, i ^ distance) for i in range(lax.axis_size...  22.7 us
  transfers between devices with their start and end apart: 26, of which 13 were waited for; matrix products, arithmetic and copies ran while one was open for 0% of the time, Pallas kernels for 21%

profile of v7, /device:TPU:0, one launch (start us, length us, event | category | flops | bytes accessed | tf_op | source)
XLA Modules:
  0.0 81.0 jit_solution(12792418819016546769)
XLA Ops:
  2.5 3.1 %prepare.1 = (bf16[2,256,256]{2,1,0:T(8,128)(2,1)S(1)}, bf16[2,256,768]{2,1,0:T(8,128)(2,1)S(1)}, bf16[2,768,256]{2,1,0:T(8,128)(2,1)S(1)}, bf16[2,256,256]{2,1,...) custom-call(s32[2]{0:T(128)S(1)} %pad_add_fusion.place_ref.refs_0_.r, ...), custom_call_target="tpu_custom_call" | custom-call | flops 3221225472 | bytes 12582912 | tf_op jit(solution)/shard_map/prepare/pallas_call | solution.py:754
  5.7 5.6 %space_forward.1 = (bf16[2,768,256]{2,1,0:T(8,128)(2,1)S(1)}, bf16[2,768,512]{2,1,0:T(8,128)(2,1)S(1)}, bf16[2,6,256,128]{3,2,1,0:T(8,128)(2,1)S(1)}, bf16[2,6,2...) custom-call(s32[2,2,4]{2,1,0:T(2,128)} %refs_0_.1, ...), custom_call_target="tpu_custom_call", output_to_operand_aliasing={{0}: (9, {}), {1}: (10, {}), {2}: (11, {}), {3}: (12, {})} | custom-call | flops 10737418240 | bytes 41943040 | tf_op jit(solution)/shard_map/space_forward/pallas_call | solution.py:754
  11.3 2.9 %collective-permute-start.2 = (bf16[2,64,512]{2,1,0:T(8,128)(2,1)S(1)}, bf16[2,64,512]{2,1,0:T(8,128)(2,1)S(1)}, u32[]{:S(2)}, u32[]{:S(2)}) collective-permute-start(bf16[2,64,512]{2,1,0:T(8,128)(2,1)S(1)} %get-tuple-element.91), channel_id=1, source_target_pairs={{0,8},{8,0},{16,24},{24,16},{1,9},{9,1},{17,25},{25,17},{2,10},{10... | collective-permute-start | bytes 393224 | tf_op jit(solution)/shard_map/ppermute | solution.py:722
  14.3 1.5 %collective-permute-start.3 = (bf16[2,64,512]{2,1,0:T(8,128)(2,1)S(1)}, bf16[2,64,512]{2,1,0:T(8,128)(2,1)S(1)}, u32[]{:S(2)}, u32[]{:S(2)}) collective-permute-start(bf16[2,64,512]{2,1,0:T(8,128)(2,1)S(1)} %get-tuple-element.92), channel_id=1, source_target_pairs={{0,16},{8,24},{16,0},{24,8},{1,17},{9,25},{17,1},{25,9},{2,18},{10... | collective-permute-start | bytes 393224 | tf_op jit(solution)/shard_map/ppermute | solution.py:722
  15.8 1.4 %collective-permute-done.2.refs_1_ = bf16[2,64,512]{2,1,0:T(8,128)(2,1)S(1)} collective-permute-done((bf16[2,64,512]{2,1,0:T(8,128)(2,1)S(1)}, bf16[2,64,512]{2,1,0:T(8,128)(2,1)S(1)}, u32[]{:S(2)}, u32[]{:S(2)}) %collective-permute-start.2) | collective-permute-done | bytes 131104 | tf_op jit(solution)/shard_map/ppermute | solution.py:722
  17.2 2.0 %collective-permute-done.3.refs_2_ = bf16[2,64,512]{2,1,0:T(8,128)(2,1)S(1)} collective-permute-done((bf16[2,64,512]{2,1,0:T(8,128)(2,1)S(1)}, bf16[2,64,512]{2,1,0:T(8,128)(2,1)S(1)}, u32[]{:S(2)}, u32[]{:S(2)}) %collective-permute-start.3) | collective-permute-done | bytes 131104 | tf_op jit(solution)/shard_map/ppermute | solution.py:722
  19.2 3.8 %collective-permute-done.4.refs_3_ = bf16[2,64,512]{2,1,0:T(8,128)(2,1)S(1)} collective-permute-done((bf16[2,64,512]{2,1,0:T(8,128)(2,1)S(1)}, bf16[2,64,512]{2,1,0:T(8,128)(2,1)S(1)}, u32[]{:S(2)}, u32[]{:S(2)}) %collective-permute-start.4) | collective-permute-done | bytes 131104 | tf_op jit(solution)/shard_map/ppermute | solution.py:722
  23.0 3.6 %time_pair.1 = (bf16[2,64,256]{2,1,0:T(8,128)(2,1)S(1)}, bf16[2,64,256]{2,1,0:T(8,128)(2,1)S(1)}, bf16[2,64,256]{2,1,0:T(8,128)(2,1)S(1)}, bf16[2,64,256]{2,1,0:...) custom-call(bf16[2,64,512]{2,1,0:T(8,128)(2,1)S(1)} %get-tuple-eleme, ...), custom_call_target="tpu_custom_call" | custom-call | flops 9663676416 | bytes 37748736 | tf_op jit(solution)/shard_map/time_pair/pallas_call | solution.py:754
  26.8 3.3 %collective-permute-start.7 = (bf16[2,64,256]{2,1,0:T(8,128)(2,1)S(1)}, bf16[2,64,256]{2,1,0:T(8,128)(2,1)S(1)}, u32[]{:S(2)}, u32[]{:S(2)}) collective-permute-start(bf16[2,64,256]{2,1,0:T(8,128)(2,1)S(1)} %get-tuple-element.104), channel_id=1, source_target_pairs={{0,24},{8,16},{16,8},{24,0},{1,25},{9,17},{17,9},{25,1},{2,26},{10... | collective-permute-start | bytes 196616 | tf_op jit(solution)/shard_map/ppermute | solution.py:722
  31.9 2.9 %collective-permute-start.11 = (bf16[768,128]{1,0:T(8,128)(2,1)S(1)}, bf16[768,128]{1,0:T(8,128)(2,1)S(1)}, u32[]{:S(2)}, u32[]{:S(2)}) collective-permute-start(bf16[768,128]{1,0:T(8,128)(2,1)S(1)} %get-tuple-element.118), channel_id=1, source_target_pairs={{0,24},{8,16},{16,8},{24,0},{1,25},{9,17},{17,9},{25,1},{2,26},{10... | collective-permute-start | bytes 589832 | tf_op jit(solution)/shard_map/ppermute | solution.py:722
  34.8 6.5 %space_backward.1 = (bf16[2,256,256]{2,1,0:T(8,128)(2,1)S(1)}, bf16[2,256,256]{2,1,0:T(8,128)(2,1)S(1)}, bf16[2,768,512]{2,1,0:T(8,128)(2,1)S(1)}, bf16[1024,128]{1,0:T(8,128)(2,1)S(1)}, bf16[1024,128]{1,0:T(8,128)(2,1)S(1)}) custom-call(s32[2,2,4]{2,1,0:T(2,128)} %refs_0_.1, s32[2]{0:T(128)S(1)} %pad_add_fusion.place_ref.refs_0_.refs_1_, ...), custom_call_target="tpu_custom_call" | custom-call | flops 11811160064 | bytes 46137344 | tf_op jit(solution)/shard_map/space_backward/pallas_call | solution.py:754
  41.4 1.6 %collective-permute-done.10.refs_2_ = bf16[768,128]{1,0:T(8,128)(2,1)S(1)} collective-permute-done((bf16[768,128]{1,0:T(8,128)(2,1)S(1)}, bf16[768,128]{1,0:T(8,128)(2,1)S(1)}, u32[]{:S(2)}, u32[]{:S(2)}) %collective-permute-start.10) | collective-permute-done | bytes 196640 | tf_op jit(solution)/shard_map/ppermute | solution.py:722
  44.4 1.3 %collective-permute-start.12 = (bf16[256,128]{1,0:T(8,128)(2,1)S(1)}, bf16[256,128]{1,0:T(8,128)(2,1)S(1)}, u32[]{:S(2)}, u32[]{:S(2)}) collective-permute-start(bf16[256,128]{1,0:T(8,128)(2,1)S(1)} %get-tuple-element.122), channel_id=1, source_target_pairs={{0,8},{8,0},{16,24},{24,16},{1,9},{9,1},{17,25},{25,17},{2,10},{10... | collective-permute-start | bytes 196616 | tf_op jit(solution)/shard_map/ppermute | solution.py:722
  48.0 3.8 %collective-permute-start.16 = (bf16[256,128]{1,0:T(8,128)(2,1)S(1)}, bf16[256,128]{1,0:T(8,128)(2,1)S(1)}, u32[]{:S(2)}, u32[]{:S(2)}) collective-permute-start(bf16[256,128]{1,0:T(8,128)(2,1)S(1)} %add_cores_time.1.refs_4_), channel_id=1, source_target_pairs={{0,2},{1,3},{2,0},{3,1},{4,6},{5,7},{6,4},{7,5},{8,10},{9,11},{10,... | collective-permute-start | bytes 196616 | tf_op jit(solution)/shard_map/ppermute | solution.py:722
  52.1 2.0 %collective-permute-done.16.refs_5_ = bf16[256,128]{1,0:T(8,128)(2,1)S(1)} collective-permute-done((bf16[256,128]{1,0:T(8,128)(2,1)S(1)}, bf16[256,128]{1,0:T(8,128)(2,1)S(1)}, u32[]{:S(2)}, u32[]{:S(2)}) %collective-permute-start.16) | collective-permute-done | bytes 65568 | tf_op jit(solution)/shard_map/ppermute | solution.py:722
  54.7 2.1 %collective-permute-start.17 = (bf16[256,128]{1,0:T(8,128)(2,1)S(1)}, bf16[256,128]{1,0:T(8,128)(2,1)S(1)}, u32[]{:S(2)}, u32[]{:S(2)}) collective-permute-start(bf16[256,128]{1,0:T(8,128)(2,1)S(1)} %get-tuple-element.133.refs_0_), channel_id=1, source_target_pairs={{0,2},{1,3},{2,0},{3,1},{4,6},{5,7},{6,4},{7,5},{8,10},{9,11},{10,... | collective-permute-start | bytes 196616 | tf_op jit(solution)/shard_map/ppermute | solution.py:722
  57.9 1.3 %space_dact.1 = (f32[2,256,256]{2,1,0:T(8,128)S(1)}, bf16[2,256,256]{2,1,0:T(8,128)(2,1)S(1)}, bf16[2,256,256]{2,1,0:T(8,128)(2,1)S(1)}) custom-call(s32[2]{0:T(128)S(1)} %pad_add_fusion.place_ref.refs_0_.refs_1_, bf16[2,256,256]{2,1,0:T(8,128)(2,1)S(1)} %get-tuple-element.129.dquery_ref, bf16[2,768,512]{2,1,0:T(8,128)(2,1)S(1)} %get-tuple-element.130.dkv_ref, ...), custom_call_target="tpu_custom_call" | custom-call | flops 805306368 | bytes 3145728 | tf_op jit(solution)/shard_map/space_dact/pallas_call | solution.py:754
  59.7 3.0 %collective-permute-done.18.refs_1_ = bf16[256,128]{1,0:T(8,128)(2,1)S(1)} collective-permute-done((bf16[256,128]{1,0:T(8,128)(2,1)S(1)}, bf16[256,128]{1,0:T(8,128)(2,1)S(1)}, u32[]{:S(2)}, u32[]{:S(2)}) %collective-permute-start.18) | collective-permute-done | bytes 65568 | tf_op jit(solution)/shard_map/ppermute | solution.py:722
  63.9 4.3 %collective-permute-done.21.space_other_ref = bf16[256,128]{1,0:T(8,128)(2,1)S(1)} collective-permute-done((bf16[256,128]{1,0:T(8,128)(2,1)S(1)}, bf16[256,128]{1,0:T(8,128)(2,1)S(1)}, u32[]{:S(2)}, u32[]{:S(2)}) %collective-permute-start.21) | collective-permute-done | bytes 65568 | tf_op jit(solution)/shard_map/ppermute | solution.py:722
  68.2 1.7 %collective-permute-start.24 = (bf16[512,128]{1,0:T(8,128)(2,1)S(1)}, bf16[512,128]{1,0:T(8,128)(2,1)S(1)}, u32[]{:S(2)}, u32[]{:S(2)}) collective-permute-start(bf16[512,128]{1,0:T(8,128)(2,1)S(1)} %add_space_last.1.refs_0_), channel_id=1, source_target_pairs={{0,24},{8,16},{16,8},{24,0},{1,25},{9,17},{17,9},{25,1},{2,26},{10... | collective-permute-start | bytes 393224 | tf_op jit(solution)/shard_map/ppermute | solution.py:722
  71.7 1.8 %field_grad.1 = (bf16[2,256,256]{2,1,0:T(8,128)(2,1)}, bf16[2,256,256]{2,1,0:T(8,128)(2,1)}) custom-call(s32[2]{0:T(128)S(1)} %pad_add_fusion.place_ref.refs_0_.refs_1_, bf16[2,256,256]{2,1,0:T(8,128)(2,1)S(1)} %get-tuple-element.80.wave_ref, bf16[2,256,256]{2,1,0:T(8,128)(2,1)S(1)} %get-tuple-element.112.mixed_grad_ref, ...), custom_call_target="tpu_custom_call" | custom-call | flops 805306368 | bytes 3145728 | tf_op jit(solution)/shard_map/field_grad/pallas_call | solution.py:754
  73.5 1.9 %collective-permute-done.24.refs_3_ = bf16[512,128]{1,0:T(8,128)(2,1)S(1)} collective-permute-done((bf16[512,128]{1,0:T(8,128)(2,1)S(1)}, bf16[512,128]{1,0:T(8,128)(2,1)S(1)}, u32[]{:S(2)}, u32[]{:S(2)}) %collective-permute-start.24) | collective-permute-done | bytes 131104 | tf_op jit(solution)/shard_map/ppermute | solution.py:722
  77.3 1.6 %weight_grads.2 = (f32[2,256,768]{2,1,0:T(8,128)}, f32[2,256,256]{2,1,0:T(8,128)}) custom-call(s32[2]{0:T(128)S(1)} %pad_add_fusion.place_ref.refs_0_.refs_1_, bf16[2048,128]{1,0:T(8,128)(2,1)S(1)} %join_tm.1.refs_1_), custom_call_target="tpu_custom_call" | custom-call | flops 268435456 | bytes 1048576 | tf_op jit(solution)/shard_map/weight_grads/pallas_call | solution.py:754
  79.2 1.6 %weight_grads.3 = (f32[2,256,768]{2,1,0:T(8,128)}, f32[2,256,256]{2,1,0:T(8,128)}) custom-call(s32[2]{0:T(128)S(1)} %pad_add_fusion.place_ref.refs_0_.refs_1_, bf16[2048,128]{1,0:T(8,128)(2,1)S(1)} %collective-permute-done.25.refs_1_, f32[2,256,768]{2,1,0:T(8,128)} %get-tuple-element.152.refs_2_, ...), custom_call_target="tpu_custom_call", output_to_operand_aliasing={{0}: (2, {}), {1}: (3, {})} | custom-call | flops 268435456 | bytes 1048576 | tf_op jit(solution)/shard_map/weight_grads/pallas_call | solution.py:754
  (46 shorter events, 15.3 us)
Async XLA Ops:
  1.1 4.5 %collective-permute-start.1 = (bf16[2,256,256]{2,1,0:T(8,128)(2,1)}, bf16[2,256,256]{2,1,0:T(8,128)(2,1)S(1)}, u32[]{:S(2)}, u32[]{:S(2)}) collective-permute-start(bf16[2,256,256]{2,1,0:T(8,128)(2,1)} %wave_hbm.1), channel_id=1, source_target_pairs={{1,2},{3,4},{5,6},{2,1},{4,3},{6,5},{9,10},{11,12},{13,14},{10,9},... | collective-permute-start | bytes 786440 | tf_op jit(solution)/shard_map/ppermute | solution.py:718
  11.3 5.9 %collective-permute-start.2 = (bf16[2,64,512]{2,1,0:T(8,128)(2,1)S(1)}, bf16[2,64,512]{2,1,0:T(8,128)(2,1)S(1)}, u32[]{:S(2)}, u32[]{:S(2)}) collective-permute-start(bf16[2,64,512]{2,1,0:T(8,128)(2,1)S(1)} %get-tuple-element.91), channel_id=1, source_target_pairs={{0,8},{8,0},{16,24},{24,16},{1,9},{9,1},{17,25},{25,17},{2,10},{10... | collective-permute-start | bytes 393224 | tf_op jit(solution)/shard_map/ppermute | solution.py:722
  14.3 5.0 %collective-permute-start.3 = (bf16[2,64,512]{2,1,0:T(8,128)(2,1)S(1)}, bf16[2,64,512]{2,1,0:T(8,128)(2,1)S(1)}, u32[]{:S(2)}, u32[]{:S(2)}) collective-permute-start(bf16[2,64,512]{2,1,0:T(8,128)(2,1)S(1)} %get-tuple-element.92), channel_id=1, source_target_pairs={{0,16},{8,24},{16,0},{24,8},{1,17},{9,25},{17,1},{25,9},{2,18},{10... | collective-permute-start | bytes 393224 | tf_op jit(solution)/shard_map/ppermute | solution.py:722
  15.8 7.2 %collective-permute-start.4 = (bf16[2,64,512]{2,1,0:T(8,128)(2,1)S(1)}, bf16[2,64,512]{2,1,0:T(8,128)(2,1)S(1)}, u32[]{:S(2)}, u32[]{:S(2)}) collective-permute-start(bf16[2,64,512]{2,1,0:T(8,128)(2,1)S(1)} %get-tuple-element.93), channel_id=1, source_target_pairs={{0,24},{8,16},{16,8},{24,0},{1,25},{9,17},{17,9},{25,1},{2,26},{10... | collective-permute-start | bytes 393224 | tf_op jit(solution)/shard_map/ppermute | solution.py:722
  26.6 5.2 %collective-permute-start.5 = (bf16[2,64,256]{2,1,0:T(8,128)(2,1)S(1)}, bf16[2,64,256]{2,1,0:T(8,128)(2,1)S(1)}, u32[]{:S(2)}, u32[]{:S(2)}) collective-permute-start(bf16[2,64,256]{2,1,0:T(8,128)(2,1)S(1)} %get-tuple-element.95), channel_id=1, source_target_pairs={{0,8},{8,0},{16,24},{24,16},{1,9},{9,1},{17,25},{25,17},{2,10},{10... | collective-permute-start | bytes 196616 | tf_op jit(solution)/shard_map/ppermute | solution.py:722
  26.8 8.0 %collective-permute-start.6 = (bf16[2,64,256]{2,1,0:T(8,128)(2,1)S(1)}, bf16[2,64,256]{2,1,0:T(8,128)(2,1)S(1)}, u32[]{:S(2)}, u32[]{:S(2)}) collective-permute-start(bf16[2,64,256]{2,1,0:T(8,128)(2,1)S(1)} %get-tuple-element.103), channel_id=1, source_target_pairs={{0,16},{8,24},{16,0},{24,8},{1,17},{9,25},{17,1},{25,9},{2,18},{10... | collective-permute-start | bytes 196616 | tf_op jit(solution)/shard_map/ppermute | solution.py:722
  26.8 8.0 %collective-permute-start.7 = (bf16[2,64,256]{2,1,0:T(8,128)(2,1)S(1)}, bf16[2,64,256]{2,1,0:T(8,128)(2,1)S(1)}, u32[]{:S(2)}, u32[]{:S(2)}) collective-permute-start(bf16[2,64,256]{2,1,0:T(8,128)(2,1)S(1)} %get-tuple-element.104), channel_id=1, source_target_pairs={{0,24},{8,16},{16,8},{24,0},{1,25},{9,17},{17,9},{25,1},{2,26},{10... | collective-permute-start | bytes 196616 | tf_op jit(solution)/shard_map/ppermute | solution.py:722
  31.2 10.1 %collective-permute-start.9 = (bf16[768,128]{1,0:T(8,128)(2,1)S(1)}, bf16[768,128]{1,0:T(8,128)(2,1)S(1)}, u32[]{:S(2)}, u32[]{:S(2)}) collective-permute-start(bf16[768,128]{1,0:T(8,128)(2,1)S(1)} %get-tuple-element.116), channel_id=1, source_target_pairs={{0,8},{8,0},{16,24},{24,16},{1,9},{9,1},{17,25},{25,17},{2,10},{10... | collective-permute-start | bytes 589832 | tf_op jit(solution)/shard_map/ppermute | solution.py:722
  31.4 11.5 %collective-permute-start.10 = (bf16[768,128]{1,0:T(8,128)(2,1)S(1)}, bf16[768,128]{1,0:T(8,128)(2,1)S(1)}, u32[]{:S(2)}, u32[]{:S(2)}) collective-permute-start(bf16[768,128]{1,0:T(8,128)(2,1)S(1)} %get-tuple-element.117), channel_id=1, source_target_pairs={{0,16},{8,24},{16,0},{24,8},{1,17},{9,25},{17,1},{25,9},{2,18},{10... | collective-permute-start | bytes 589832 | tf_op jit(solution)/shard_map/ppermute | solution.py:722
  31.9 11.1 %collective-permute-start.11 = (bf16[768,128]{1,0:T(8,128)(2,1)S(1)}, bf16[768,128]{1,0:T(8,128)(2,1)S(1)}, u32[]{:S(2)}, u32[]{:S(2)}) collective-permute-start(bf16[768,128]{1,0:T(8,128)(2,1)S(1)} %get-tuple-element.118), channel_id=1, source_target_pairs={{0,24},{8,16},{16,8},{24,0},{1,25},{9,17},{17,9},{25,1},{2,26},{10... | collective-permute-start | bytes 589832 | tf_op jit(solution)/shard_map/ppermute | solution.py:722
  41.3 2.5 %collective-permute-start.8 = (bf16[1024,128]{1,0:T(8,128)(2,1)S(1)}, bf16[1024,128]{1,0:T(8,128)(2,1)S(1)}, u32[]{:S(2)}, u32[]{:S(2)}) collective-permute-start(bf16[1024,128]{1,0:T(8,128)(2,1)S(1)} %get-tuple-element.114), channel_id=1, source_target_pairs={{0,1},{1,0},{2,3},{3,2},{4,5},{5,4},{6,7},{7,6},{8,9},{9,8},{10,11... | collective-permute-start | bytes 786440 | tf_op jit(solution)/shard_map/ppermute | solution.py:722
  43.7 4.3 %collective-permute-start.15 = (bf16[256,128]{1,0:T(8,128)(2,1)S(1)}, bf16[256,128]{1,0:T(8,128)(2,1)S(1)}, u32[]{:S(2)}, u32[]{:S(2)}) collective-permute-start(bf16[256,128]{1,0:T(8,128)(2,1)S(1)} %get-tuple-element.126), channel_id=1, source_target_pairs={{0,1},{1,0},{2,3},{3,2},{4,5},{5,4},{6,7},{7,6},{8,9},{9,8},{10,11... | collective-permute-start | bytes 196616 | tf_op jit(solution)/shard_map/ppermute | solution.py:722
  44.4 7.4 %collective-permute-start.12 = (bf16[256,128]{1,0:T(8,128)(2,1)S(1)}, bf16[256,128]{1,0:T(8,128)(2,1)S(1)}, u32[]{:S(2)}, u32[]{:S(2)}) collective-permute-start(bf16[256,128]{1,0:T(8,128)(2,1)S(1)} %get-tuple-element.122), channel_id=1, source_target_pairs={{0,8},{8,0},{16,24},{24,16},{1,9},{9,1},{17,25},{25,17},{2,10},{10... | collective-permute-start | bytes 196616 | tf_op jit(solution)/shard_map/ppermute | solution.py:722
  45.8 6.0 %collective-permute-start.13 = (bf16[256,128]{1,0:T(8,128)(2,1)S(1)}, bf16[256,128]{1,0:T(8,128)(2,1)S(1)}, u32[]{:S(2)}, u32[]{:S(2)}) collective-permute-start(bf16[256,128]{1,0:T(8,128)(2,1)S(1)} %get-tuple-element.123), channel_id=1, source_target_pairs={{0,16},{8,24},{16,0},{24,8},{1,17},{9,25},{17,1},{25,9},{2,18},{10... | collective-permute-start | bytes 196616 | tf_op jit(solution)/shard_map/ppermute | solution.py:722
  46.9 5.2 %collective-permute-start.14 = (bf16[256,128]{1,0:T(8,128)(2,1)S(1)}, bf16[256,128]{1,0:T(8,128)(2,1)S(1)}, u32[]{:S(2)}, u32[]{:S(2)}) collective-permute-start(bf16[256,128]{1,0:T(8,128)(2,1)S(1)} %get-tuple-element.124), channel_id=1, source_target_pairs={{0,24},{8,16},{16,8},{24,0},{1,25},{9,17},{17,9},{25,1},{2,26},{10... | collective-permute-start | bytes 196616 | tf_op jit(solution)/shard_map/ppermute | solution.py:722
  48.0 6.0 %collective-permute-start.16 = (bf16[256,128]{1,0:T(8,128)(2,1)S(1)}, bf16[256,128]{1,0:T(8,128)(2,1)S(1)}, u32[]{:S(2)}, u32[]{:S(2)}) collective-permute-start(bf16[256,128]{1,0:T(8,128)(2,1)S(1)} %add_cores_time.1.refs_4_), channel_id=1, source_target_pairs={{0,2},{1,3},{2,0},{3,1},{4,6},{5,7},{6,4},{7,5},{8,10},{9,11},{10,... | collective-permute-start | bytes 196616 | tf_op jit(solution)/shard_map/ppermute | solution.py:722
  54.7 5.0 %collective-permute-start.17 = (bf16[256,128]{1,0:T(8,128)(2,1)S(1)}, bf16[256,128]{1,0:T(8,128)(2,1)S(1)}, u32[]{:S(2)}, u32[]{:S(2)}) collective-permute-start(bf16[256,128]{1,0:T(8,128)(2,1)S(1)} %get-tuple-element.133.refs_0_), channel_id=1, source_target_pairs={{0,2},{1,3},{2,0},{3,1},{4,6},{5,7},{6,4},{7,5},{8,10},{9,11},{10,... | collective-permute-start | bytes 196616 | tf_op jit(solution)/shard_map/ppermute | solution.py:722
  56.8 5.9 %collective-permute-start.18 = (bf16[256,128]{1,0:T(8,128)(2,1)S(1)}, bf16[256,128]{1,0:T(8,128)(2,1)S(1)}, u32[]{:S(2)}, u32[]{:S(2)}) collective-permute-start(bf16[256,128]{1,0:T(8,128)(2,1)S(1)} %get-tuple-element.132.refs_0_), channel_id=1, source_target_pairs={{0,4},{1,5},{2,6},{3,7},{4,0},{5,1},{6,2},{7,3},{8,12},{9,13},{10,... | collective-permute-start | bytes 196616 | tf_op jit(solution)/shard_map/ppermute | solution.py:722
  62.6 5.5 %collective-permute-start.21 = (bf16[256,128]{1,0:T(8,128)(2,1)S(1)}, bf16[256,128]{1,0:T(8,128)(2,1)S(1)}, u32[]{:S(2)}, u32[]{:S(2)}) collective-permute-start(bf16[256,128]{1,0:T(8,128)(2,1)S(1)} %add_space.1.space_ref), channel_id=1, source_target_pairs={{0,4},{1,5},{2,6},{3,7},{4,0},{5,1},{6,2},{7,3},{8,12},{9,13},{10,... | collective-permute-start | bytes 196616 | tf_op jit(solution)/shard_map/ppermute | solution.py:722
  63.1 8.6 %collective-permute-start.19 = (bf16[2,256,256]{2,1,0:T(8,128)(2,1)S(1)}, bf16[2,256,256]{2,1,0:T(8,128)(2,1)S(1)}, u32[]{:S(2)}, u32[]{:S(2)}) collective-permute-start(bf16[2,256,256]{2,1,0:T(8,128)(2,1)S(1)} %get-tuple-element.140), channel_id=1, source_target_pairs={{0,1},{1,0},{2,3},{3,2},{4,5},{5,4},{6,7},{7,6},{8,9},{9,8},{10,11... | collective-permute-start | bytes 786440 | tf_op jit(solution)/shard_map/ppermute | solution.py:722
  63.2 8.5 %collective-permute-start.20 = (bf16[2,256,256]{2,1,0:T(8,128)(2,1)S(1)}, bf16[2,256,256]{2,1,0:T(8,128)(2,1)S(1)}, u32[]{:S(2)}, u32[]{:S(2)}) collective-permute-start(bf16[2,256,256]{2,1,0:T(8,128)(2,1)S(1)} %get-tuple-element.141), channel_id=1, source_target_pairs={{1,2},{3,4},{5,6},{2,1},{4,3},{6,5},{9,10},{11,12},{13,14},{10,9},... | collective-permute-start | bytes 786440 | tf_op jit(solution)/shard_map/ppermute | solution.py:718
  68.2 7.2 %collective-permute-start.24 = (bf16[512,128]{1,0:T(8,128)(2,1)S(1)}, bf16[512,128]{1,0:T(8,128)(2,1)S(1)}, u32[]{:S(2)}, u32[]{:S(2)}) collective-permute-start(bf16[512,128]{1,0:T(8,128)(2,1)S(1)} %add_space_last.1.refs_0_), channel_id=1, source_target_pairs={{0,24},{8,16},{16,8},{24,0},{1,25},{9,17},{17,9},{25,1},{2,26},{10... | collective-permute-start | bytes 393224 | tf_op jit(solution)/shard_map/ppermute | solution.py:722
  69.9 6.7 %collective-permute-start.23 = (bf16[512,128]{1,0:T(8,128)(2,1)S(1)}, bf16[512,128]{1,0:T(8,128)(2,1)S(1)}, u32[]{:S(2)}, u32[]{:S(2)}) collective-permute-start(bf16[512,128]{1,0:T(8,128)(2,1)S(1)} %add_space_last.1.refs_0_), channel_id=1, source_target_pairs={{0,16},{8,24},{16,0},{24,8},{1,17},{9,25},{17,1},{25,9},{2,18},{10... | collective-permute-start | bytes 393224 | tf_op jit(solution)/shard_map/ppermute | solution.py:722
  70.6 6.0 %collective-permute-start.22 = (bf16[512,128]{1,0:T(8,128)(2,1)S(1)}, bf16[512,128]{1,0:T(8,128)(2,1)S(1)}, u32[]{:S(2)}, u32[]{:S(2)}) collective-permute-start(bf16[512,128]{1,0:T(8,128)(2,1)S(1)} %add_space_last.1.refs_0_), channel_id=1, source_target_pairs={{0,8},{8,0},{16,24},{24,16},{1,9},{9,1},{17,25},{25,17},{2,10},{10... | collective-permute-start | bytes 393224 | tf_op jit(solution)/shard_map/ppermute | solution.py:722
  (2 other events, 3.9 us)

commit v8 on v7

--- a/solution.py
+++ b/solution.py
@@ -191,6 +191,8 @@
 
 
 def space_forward_kernel(
+    frame,
+    sent_rows,
     lists_ref,
     place_ref,
     far_ref,
@@ -200,68 +202,55 @@
     turned_ref,
     combine_ref,
     query_t_ref,
-    act_in,
-    kv_in,
-    keys_t_in,
-    values_t_in,
-    act_ref,
-    kv_ref,
-    keys_t_ref,
-    values_t_ref,
-    probs_ref,
-    inverse_sum_ref,
-    attended_ref,
     *rest,
 ):
-    del act_in, kv_in, keys_t_in, values_t_in
-    *sent_refs, mixed_s = rest
     me = place_ref[0]
     core = place_ref[1] % 2
-    frame_count, row_count, features = wave_ref.shape
+    _, row_count, features = wave_ref.shape
+    mixed_s = rest[-1]
+    refs = rest[-8 - row_count // sent_rows : -1]
+    act_ref, kv_ref, keys_t_ref, values_t_ref, probs_ref, inverse_sum_ref, attended_ref = refs[:7]
+    sent_refs = refs[7:]
     rim = far_ref.shape[1]
     width = features // HEADS
     block_count = row_count // BLOCK
     exponent_scale = math.log2(math.e) / math.sqrt(width)
-    for frame in range(frame_count):
-        project_rows(
-            frame,
-            halo_start(core, rim, row_count, False),
-            far_ref[frame],
-            project_ref,
-            turned_ref,
-            act_ref,
-            kv_ref,
-            keys_t_ref,
-            values_t_ref,
-        )
-    blocks = [(frame, block) for frame in range(frame_count) for block in range(block_count)]
+    project_rows(
+        frame,
+        halo_start(core, rim, row_count, False),
+        far_ref[0],
+        project_ref,
+        turned_ref,
+        act_ref,
+        kv_ref,
+        keys_t_ref,
+        values_t_ref,
+    )
     loaded = {}
 
-    def load(index):
-        frame, block = blocks[index]
+    def load(block):
         places = listed_blocks(lists_ref, frame, block)
         keys = jnp.concatenate(
             [kv_ref[frame, pl.ds(place * BLOCK, BLOCK), :features] for place in places], axis=0
         )
-        loaded[index] = (keys, query_t_ref[frame, :, block * BLOCK : (block + 1) * BLOCK], places)
+        loaded[block] = (keys, query_t_ref[frame, :, block * BLOCK : (block + 1) * BLOCK], places)
 
     def pair_scores(step):
-        index, pair = divmod(step, HEADS // 2)
-        if index not in loaded:
-            load(index)
-        keys, query_t, _ = loaded[index]
+        block, pair = divmod(step, HEADS // 2)
+        if block not in loaded:
+            load(block)
+        keys, query_t, _ = loaded[block]
         return dot_nn(pair_group(keys, pair, width), pair_columns(query_t, pair, width))
 
-    steps = len(blocks) * HEADS // 2
+    steps = block_count * HEADS // 2
     scores = pair_scores(0)
     outs = []
     for step in range(steps):
         following = pair_scores(step + 1) if step + 1 < steps else None
-        index, pair = divmod(step, HEADS // 2)
-        frame, block = blocks[index]
+        block, pair = divmod(step, HEADS // 2)
         if pair == 0:
             block_values_t = jnp.concatenate(
-                [values_t_ref[frame, place] for place in loaded[index][2]], axis=1
+                [values_t_ref[frame, place] for place in loaded[block][2]], axis=1
             )
             outs = []
         top = jnp.max(scores, axis=0, keepdims=True)
@@ -278,14 +267,13 @@
             attended_t = jnp.concatenate(outs, axis=0)
             span = slice(block * BLOCK, (block + 1) * BLOCK)
             attended_ref[frame, :, span] = attended_t.astype(BF16)
-            mixed_s[frame, span] = (
+            mixed_s[span] = (
                 wave_ref[frame, span].astype(F32) + dot_nn(flip(attended_t), combine_ref[0])
             ).astype(BF16)
     for distance, ref in enumerate(sent_refs):
-        rows = ref.shape[1]
-        span = pl.ds(pl.multiple_of((me ^ distance) * rows, GROUP_ROWS), rows)
-        ref[:, :, :features] = mixed_s[:, span]
-        ref[:, :, features:] = cot_ref[:, span]
+        span = pl.ds(pl.multiple_of((me ^ distance) * sent_rows, GROUP_ROWS), sent_rows)
+        ref[frame, :, :features] = mixed_s[span]
+        ref[frame, :, features:] = cot_ref[frame, span]
 
 
 def time_kernel(
@@ -652,21 +640,13 @@
     total_ref[rows:] = time_ref[...]
 
 
-def join_kernel(place_ref, *refs):
-    *part_refs, joined_ref = refs
-    for distance, ref in enumerate(part_refs):
-        rows = ref.shape[0]
-        joined_ref[pl.ds(pl.multiple_of((place_ref[0] ^ distance) * rows, GROUP_ROWS), rows)] = ref[
-            ...
-        ]
-
-
-def grads_kernel(time_count, own, place_ref, half_ref, *refs):
+def grads_kernel(time_count, own, place_ref, *refs):
     project_hbm, combine_hbm, wide_s, sems = refs[-4:]
     features = combine_hbm.shape[1]
     core = place_ref[1] % 2
-    rows = half_ref.shape[0] // time_count // 2
-    wide_s[...] = half_ref[...].astype(F32).reshape(wide_s.shape)
+    rows = wide_s.shape[1] // 2
+    for distance, ref in enumerate(refs[:time_count]):
+        wide_s[place_ref[0] ^ distance] = ref[...].astype(F32)
 
     def write(half):
         moves = []
@@ -682,7 +662,7 @@
                 piece = 2 * part + layer
                 moves.append(
                     pltpu.make_async_copy(
-                        wide_s.at[piece],
+                        wide_s.at[part, pl.ds(layer * rows, rows)],
                         target.at[layer, pl.ds(inner, rows), pl.ds(start, LANES)],
                         sems.at[piece],
                     )
@@ -774,7 +754,7 @@
     own = (frame_count, row_count, features)
     part = (frame_count, sent_rows, features)
     near = exchange(wave_field, "space", 1)
-    far = swap_far(wave_field, "space")
+    fars = [swap_far(wave_field[frame : frame + 1], "space") for frame in range(frame_count)]
     place = jnp.stack([lax.axis_index("tm"), lax.axis_index("space")]).astype(jnp.int32)
     extended_shapes = [
         (frame_count, extended, features),
@@ -802,22 +782,29 @@
         hbm=[in_hbm(cells) for cells in (wave_field, cotangent, project_weights, combine_weights)],
     )
     block_lists = in_hbm(block_lists)
-    act, keys_values, keys_t, _, probs, inverse_sum, attended, *parts = call(
-        space_forward_kernel,
-        "space_forward",
-        [block_lists, place],
-        [far, wave, cot, project, turned, combine, queries_t, *projected],
-        [
-            *extended_shapes,
-            (frame_count, block_count, keys_count, HEADS * BLOCK),
-            (frame_count, block_count, HEADS, BLOCK, F32),
-            (frame_count, features, row_count),
-            *[(frame_count, sent_rows, 2 * features)] * time_count,
-        ],
-        [own],
-        matmuls=40,
-        aliases={9 + index: index for index in range(4)},
-    )
+    space_outs = projected
+    for frame, far in enumerate(fars):
+
+        def forward_body(*refs, frame=frame):
+            space_forward_kernel(frame, sent_rows, *refs)
+
+        space_outs = call(
+            forward_body,
+            "space_forward",
+            [block_lists, place],
+            [far, wave, cot, project, turned, combine, queries_t, *space_outs],
+            [
+                *extended_shapes,
+                (frame_count, block_count, keys_count, HEADS * BLOCK),
+                (frame_count, block_count, HEADS, BLOCK, F32),
+                (frame_count, features, row_count),
+                *[(frame_count, sent_rows, 2 * features)] * time_count,
+            ],
+            [(row_count, features)],
+            matmuls=20,
+            aliases={9 + index: index for index in range(len(space_outs))},
+        )
+    act, keys_values, keys_t, _, probs, inverse_sum, attended, *parts = space_outs
     kept_space = [act, keys_values, keys_t, queries, probs, inverse_sum, attended]
     arrived = over_tm(parts)
 
@@ -921,14 +908,15 @@
         [(frame_count, extended, features)],
         matmuls=3,
     )
+    sent_piece = space_piece
     for step, time_step in zip(steps, steps[1:]):
-        space_other = exchange(space_piece, "space", step)
+        space_other = exchange(sent_piece, "space", step)
         time_other = exchange(time_piece, "space", time_step)
         space_other, to_near, to_far = lax.optimization_barrier((space_other, to_near, to_far))
-        space_piece = add_pair("add_space", space_piece, space_other)
-        space_piece, time_other = lax.optimization_barrier((space_piece, time_other))
+        sent_piece = add_pair("add_space", space_piece, space_other)
+        space_piece, time_other = lax.optimization_barrier((sent_piece, time_other))
         time_piece = add_pair("add_space_time", time_piece, time_other)
-    space_other = exchange(space_piece, "space", steps[-1])
+    space_other = exchange(sent_piece, "space", steps[-1])
     time_piece, to_near, to_far = lax.optimization_barrier((time_piece, to_near, to_far))
     from_far = swap_far(to_far, "space")
     from_near = exchange(to_near, "space", 1)
@@ -942,6 +930,9 @@
     )
     joined = over_tm([piece] * time_count)
 
+    others = exchange(piece, "space", 1)
+    from_near, others = lax.optimization_barrier((from_near, others))
+
     field_grad, mixed_field = call(
         field_kernel,
         "field_grad",
@@ -951,27 +942,26 @@
         matmuls=3,
     )
     field_grad, mixed_field, *joined = lax.optimization_barrier((field_grad, mixed_field, *joined))
-    (own_half,) = call(join_kernel, "join_tm", [place], joined, [(grad_rows, LANES)])
-    other_half = exchange(own_half, "space", 1)
+    others = [others] + [exchange(part, "space", 1) for part in joined[1:]]
 
     grads = ()
-    for half in (own_half, other_half):
-
-        def grads_body(*refs, mine=half is own_half):
+    for half in (joined, others):
+
+        def grads_body(*refs, mine=half is joined):
             grads_kernel(time_count, mine, *refs)
 
         grads = call(
             grads_body,
             "weight_grads",
             [place],
-            [half],
+            half,
             [(2, features, 3 * features, F32), (2, features, features, F32)],
             [
-                (2 * time_count, grad_rows // time_count // 2, LANES, F32),
+                (time_count, chunk, LANES, F32),
                 pltpu.SemaphoreType.DMA((2 * time_count,)),
             ],
             hbm=grads,
-            aliases={2: 0, 3: 1} if grads else None,
+            aliases={1 + time_count: 0, 2 + time_count: 1} if grads else None,
             out_spec=pl.BlockSpec(memory_space=pltpu.HBM),
         )
     project_grad, combine_grad = grads

time: 81.2 us -> 83.2 us (1.025)
  starting transfers between devices: 28.3 us -> 35.3 us
  waiting for transfers between devices: 22.7 us -> 15.9 us
  local copies, waits for them, and re-layouts: 0 us -> 0.98 us
    ppermute x24 -> x27, waiting for transfers between devices: 22.7 us -> 15.9 us  [exchange(): lax.ppermute(cells, axis, [(i, i ^ distance) for i in range(lax.axis_size...]
    ppermute x24 -> x27, starting transfers between devices: 27 us -> 33.3 us  [exchange(): lax.ppermute(cells, axis, [(i, i ^ distance) for i in range(lax.axis_size...]
    slice x0 -> x1, local copies, waits for them, and re-layouts: none -> 0.98 us  [per_device(): wave_field[frame:frame + 1]]
    ppermute x2 -> x3, starting transfers between devices: 1.34 us -> 2.02 us  [swap_far(): return lax.ppermute(cells, axis, pairs + [(j, i) for i, j in pairs])]
  transfers between devices with their start and end apart: 26 -> 30, of which waited for: 13 -> 10; matrix products, arithmetic and copies ran while one was open for 0% -> 1% of each run, Pallas kernels for 21% -> 24%
where the time goes in v8:
time: 83.2 us; the launch traced here: 82.9 us
  starting transfers between devices  35.3 us (42%)
  Pallas kernels  29.6 us (36%)
  waiting for transfers between devices  15.9 us (19%)
  between operations  0.99 us (1%)
  local copies, waits for them, and re-layouts  0.98 us (1%)
    ppermute x27, starting transfers between devices, exchange(): lax.ppermute(cells, axis, [(i, i ^ distance) for i in range(lax.axis_size...  33.3 us
    pallas_call x17, Pallas kernels, call(): pl.pallas_call(body, in_specs=[smem_spec] * len(scalars) + [vmem_spec] *...  29.6 us
    ppermute x27, waiting for transfers between devices, exchange(): lax.ppermute(cells, axis, [(i, i ^ distance) for i in range(lax.axis_size...  15.9 us
    ppermute x3, starting transfers between devices, swap_far(): return lax.ppermute(cells, axis, pairs + [(j, i) for i, j in pairs])  2.02 us
  transfers between devices with their start and end apart: 30, of which 10 were waited for; matrix products, arithmetic and copies ran while one was open for 1% of the time, Pallas kernels for 24%

profile of v8, /device:TPU:0, one launch (start us, length us, event | category | flops | bytes accessed | tf_op | source)
XLA Modules:
  0.0 82.9 jit_solution(5779170863187955968)
XLA Ops:
  3.6 3.1 %prepare.1 = (bf16[2,256,256]{2,1,0:T(8,128)(2,1)S(1)}, bf16[2,256,768]{2,1,0:T(8,128)(2,1)S(1)}, bf16[2,768,256]{2,1,0:T(8,128)(2,1)S(1)}, bf16[2,256,256]{2,1,...) custom-call(s32[2]{0:T(128)S(1)} %pad_add_fusion.place_ref.refs_1_.r, ...), custom_call_target="tpu_custom_call" | custom-call | flops 3221225472 | bytes 12582912 | tf_op jit(solution)/shard_map/prepare/pallas_call | solution.py:734
  6.7 3.5 %space_forward.2 = (bf16[2,768,256]{2,1,0:T(8,128)(2,1)S(1)}, bf16[2,768,512]{2,1,0:T(8,128)(2,1)S(1)}, bf16[2,6,256,128]{3,2,1,0:T(8,128)(2,1)S(1)}, bf16[2,6,2...) custom-call(s32[2,2,4]{2,1,0:T(2,128)} %refs_0_.5, ...), custom_call_target="tpu_custom_call", output_to_operand_aliasing={{0}: (9, {}), {1}: (10, {}), {2}: (11, {}), {3}: (12, {})} | custom-call | flops 5368709120 | bytes 20971520 | tf_op jit(solution)/shard_map/space_forward/pallas_call | solution.py:734
  10.2 3.5 %space_forward.3 = (bf16[2,768,256]{2,1,0:T(8,128)(2,1)S(1)}, bf16[2,768,512]{2,1,0:T(8,128)(2,1)S(1)}, bf16[2,6,256,128]{3,2,1,0:T(8,128)(2,1)S(1)}, bf16[2,6,2...) custom-call(s32[2,2,4]{2,1,0:T(2,128)} %refs_0_.5, ...), custom_call_target="tpu_custom_call", output_to_operand_aliasing={{0}: (9, {}), {1}: (10, {}), {2}: (11, {}), {3}: (12, {}), ... | custom-call | flops 5368709120 | bytes 20971520 | tf_op jit(solution)/shard_map/space_forward/pallas_call | solution.py:734
  13.7 2.6 %collective-permute-start.3 = (bf16[2,64,512]{2,1,0:T(8,128)(2,1)S(1)}, bf16[2,64,512]{2,1,0:T(8,128)(2,1)S(1)}, u32[]{:S(2)}, u32[]{:S(2)}) collective-permute-start(bf16[2,64,512]{2,1,0:T(8,128)(2,1)S(1)} %get-tuple-element.115), channel_id=1, source_target_pairs={{0,8},{8,0},{16,24},{24,16},{1,9},{9,1},{17,25},{25,17},{2,10},{10... | collective-permute-start | bytes 393224 | tf_op jit(solution)/shard_map/ppermute | solution.py:702
  16.3 1.6 %collective-permute-start.4 = (bf16[2,64,512]{2,1,0:T(8,128)(2,1)S(1)}, bf16[2,64,512]{2,1,0:T(8,128)(2,1)S(1)}, u32[]{:S(2)}, u32[]{:S(2)}) collective-permute-start(bf16[2,64,512]{2,1,0:T(8,128)(2,1)S(1)} %get-tuple-element.116), channel_id=1, source_target_pairs={{0,16},{8,24},{16,0},{24,8},{1,17},{9,25},{17,1},{25,9},{2,18},{10... | collective-permute-start | bytes 393224 | tf_op jit(solution)/shard_map/ppermute | solution.py:702
  19.2 2.0 %collective-permute-done.4.refs_2_ = bf16[2,64,512]{2,1,0:T(8,128)(2,1)S(1)} collective-permute-done((bf16[2,64,512]{2,1,0:T(8,128)(2,1)S(1)}, bf16[2,64,512]{2,1,0:T(8,128)(2,1)S(1)}, u32[]{:S(2)}, u32[]{:S(2)}) %collective-permute-start.4) | collective-permute-done | bytes 131104 | tf_op jit(solution)/shard_map/ppermute | solution.py:702
  21.2 3.1 %collective-permute-done.5.refs_3_ = bf16[2,64,512]{2,1,0:T(8,128)(2,1)S(1)} collective-permute-done((bf16[2,64,512]{2,1,0:T(8,128)(2,1)S(1)}, bf16[2,64,512]{2,1,0:T(8,128)(2,1)S(1)}, u32[]{:S(2)}, u32[]{:S(2)}) %collective-permute-start.5) | collective-permute-done | bytes 131104 | tf_op jit(solution)/shard_map/ppermute | solution.py:702
  24.4 3.6 %time_pair.1 = (bf16[2,64,256]{2,1,0:T(8,128)(2,1)S(1)}, bf16[2,64,256]{2,1,0:T(8,128)(2,1)S(1)}, bf16[2,64,256]{2,1,0:T(8,128)(2,1)S(1)}, bf16[2,64,256]{2,1,0:...) custom-call(bf16[2,64,512]{2,1,0:T(8,128)(2,1)S(1)} %get-tuple-eleme, ...), custom_call_target="tpu_custom_call" | custom-call | flops 9663676416 | bytes 37748736 | tf_op jit(solution)/shard_map/time_pair/pallas_call | solution.py:734
  28.8 2.7 %collective-permute-start.8 = (bf16[2,64,256]{2,1,0:T(8,128)(2,1)S(1)}, bf16[2,64,256]{2,1,0:T(8,128)(2,1)S(1)}, u32[]{:S(2)}, u32[]{:S(2)}) collective-permute-start(bf16[2,64,256]{2,1,0:T(8,128)(2,1)S(1)} %get-tuple-element.128), channel_id=1, source_target_pairs={{0,24},{8,16},{16,8},{24,0},{1,25},{9,17},{17,9},{25,1},{2,26},{10... | collective-permute-start | bytes 196616 | tf_op jit(solution)/shard_map/ppermute | solution.py:702
  33.4 2.7 %collective-permute-start.12 = (bf16[768,128]{1,0:T(8,128)(2,1)S(1)}, bf16[768,128]{1,0:T(8,128)(2,1)S(1)}, u32[]{:S(2)}, u32[]{:S(2)}) collective-permute-start(bf16[768,128]{1,0:T(8,128)(2,1)S(1)} %get-tuple-element.142), channel_id=1, source_target_pairs={{0,24},{8,16},{16,8},{24,0},{1,25},{9,17},{17,9},{25,1},{2,26},{10... | collective-permute-start | bytes 589832 | tf_op jit(solution)/shard_map/ppermute | solution.py:702
  36.1 6.5 %space_backward.1 = (bf16[2,256,256]{2,1,0:T(8,128)(2,1)S(1)}, bf16[2,256,256]{2,1,0:T(8,128)(2,1)S(1)}, bf16[2,768,512]{2,1,0:T(8,128)(2,1)S(1)}, bf16[1024,128]{1,0:T(8,128)(2,1)S(1)}, bf16[1024,128]{1,0:T(8,128)(2,1)S(1)}) custom-call(s32[2,2,4]{2,1,0:T(2,128)} %refs_0_.5, s32[2]{0:T(128)S(1)} %pad_add_fusion.place_ref.refs_1_.refs_0_, ...), custom_call_target="tpu_custom_call" | custom-call | flops 11811160064 | bytes 46137344 | tf_op jit(solution)/shard_map/space_backward/pallas_call | solution.py:734
  46.0 2.1 %collective-permute-start.13 = (bf16[256,128]{1,0:T(8,128)(2,1)S(1)}, bf16[256,128]{1,0:T(8,128)(2,1)S(1)}, u32[]{:S(2)}, u32[]{:S(2)}) collective-permute-start(bf16[256,128]{1,0:T(8,128)(2,1)S(1)} %get-tuple-element.146), channel_id=1, source_target_pairs={{0,8},{8,0},{16,24},{24,16},{1,9},{9,1},{17,25},{25,17},{2,10},{10... | collective-permute-start | bytes 196616 | tf_op jit(solution)/shard_map/ppermute | solution.py:702
  49.7 5.4 %collective-permute-start.17 = (bf16[256,128]{1,0:T(8,128)(2,1)S(1)}, bf16[256,128]{1,0:T(8,128)(2,1)S(1)}, u32[]{:S(2)}, u32[]{:S(2)}) collective-permute-start(bf16[256,128]{1,0:T(8,128)(2,1)S(1)} %add_cores_time.1.refs_4_), channel_id=1, source_target_pairs={{0,2},{1,3},{2,0},{3,1},{4,6},{5,7},{6,4},{7,5},{8,10},{9,11},{10,... | collective-permute-start | bytes 196616 | tf_op jit(solution)/shard_map/ppermute | solution.py:702
  55.1 2.2 %collective-permute-done.17.refs_5_ = bf16[256,128]{1,0:T(8,128)(2,1)S(1)} collective-permute-done((bf16[256,128]{1,0:T(8,128)(2,1)S(1)}, bf16[256,128]{1,0:T(8,128)(2,1)S(1)}, u32[]{:S(2)}, u32[]{:S(2)}) %collective-permute-start.17) | collective-permute-done | bytes 65568 | tf_op jit(solution)/shard_map/ppermute | solution.py:702
  58.0 2.1 %collective-permute-start.18 = (bf16[256,128]{1,0:T(8,128)(2,1)S(1)}, bf16[256,128]{1,0:T(8,128)(2,1)S(1)}, u32[]{:S(2)}, u32[]{:S(2)}) collective-permute-start(bf16[256,128]{1,0:T(8,128)(2,1)S(1)} %get-tuple-element.157.refs_0_), channel_id=1, source_target_pairs={{0,2},{1,3},{2,0},{3,1},{4,6},{5,7},{6,4},{7,5},{8,10},{9,11},{10,... | collective-permute-start | bytes 196616 | tf_op jit(solution)/shard_map/ppermute | solution.py:702
  63.0 2.5 %collective-permute-start.21 = (bf16[256,128]{1,0:T(8,128)(2,1)S(1)}, bf16[256,128]{1,0:T(8,128)(2,1)S(1)}, u32[]{:S(2)}, u32[]{:S(2)}) collective-permute-start(bf16[256,128]{1,0:T(8,128)(2,1)S(1)} %add_space.1.space_ref), channel_id=1, source_target_pairs={{0,4},{1,5},{2,6},{3,7},{4,0},{5,1},{6,2},{7,3},{8,12},{9,13},{10,... | collective-permute-start | bytes 196616 | tf_op jit(solution)/shard_map/ppermute | solution.py:702
  65.4 1.6 %collective-permute-done.19.refs_1_ = bf16[256,128]{1,0:T(8,128)(2,1)S(1)} collective-permute-done((bf16[256,128]{1,0:T(8,128)(2,1)S(1)}, bf16[256,128]{1,0:T(8,128)(2,1)S(1)}, u32[]{:S(2)}, u32[]{:S(2)}) %collective-permute-start.19) | collective-permute-done | bytes 65568 | tf_op jit(solution)/shard_map/ppermute | solution.py:702
  68.2 1.5 %collective-permute-start.22 = (bf16[512,128]{1,0:T(8,128)(2,1)S(1)}, bf16[512,128]{1,0:T(8,128)(2,1)S(1)}, u32[]{:S(2)}, u32[]{:S(2)}) collective-permute-start(bf16[512,128]{1,0:T(8,128)(2,1)S(1)} %add_space_last.1.refs_1_), channel_id=1, source_target_pairs={{0,1},{1,0},{2,3},{3,2},{4,5},{5,4},{6,7},{7,6},{8,9},{9,8},{10,11... | collective-permute-start | bytes 393224 | tf_op jit(solution)/shard_map/ppermute | solution.py:702
  69.7 1.9 %collective-permute-start.26 = (bf16[512,128]{1,0:T(8,128)(2,1)S(1)}, bf16[512,128]{1,0:T(8,128)(2,1)S(1)}, u32[]{:S(2)}, u32[]{:S(2)}) collective-permute-start(bf16[512,128]{1,0:T(8,128)(2,1)S(1)} %add_space_last.1.refs_1_), channel_id=1, source_target_pairs={{0,24},{8,16},{16,8},{24,0},{1,25},{9,17},{17,9},{25,1},{2,26},{10... | collective-permute-start | bytes 393224 | tf_op jit(solution)/shard_map/ppermute | solution.py:702
  73.2 1.8 %field_grad.1 = (bf16[2,256,256]{2,1,0:T(8,128)(2,1)}, bf16[2,256,256]{2,1,0:T(8,128)(2,1)}) custom-call(s32[2]{0:T(128)S(1)} %pad_add_fusion.place_ref.refs_1_.refs_0_, bf16[2,256,256]{2,1,0:T(8,128)(2,1)S(1)} %get-tuple-element.93.refs_3_.wave_ref, bf16[2,256,256]{2,1,0:T(8,128)(2,1)S(1)} %get-tuple-element.136.mixed_grad_ref, ...), custom_call_target="tpu_custom_call" | custom-call | flops 805306368 | bytes 3145728 | tf_op jit(solution)/shard_map/field_grad/pallas_call | solution.py:734
  75.0 2.0 %collective-permute-done.26.refs_4_ = bf16[512,128]{1,0:T(8,128)(2,1)S(1)} collective-permute-done((bf16[512,128]{1,0:T(8,128)(2,1)S(1)}, bf16[512,128]{1,0:T(8,128)(2,1)S(1)}, u32[]{:S(2)}, u32[]{:S(2)}) %collective-permute-start.26) | collective-permute-done | bytes 131104 | tf_op jit(solution)/shard_map/ppermute | solution.py:702
  76.9 1.9 %collective-permute-done.25.refs_3_ = bf16[512,128]{1,0:T(8,128)(2,1)S(1)} collective-permute-done((bf16[512,128]{1,0:T(8,128)(2,1)S(1)}, bf16[512,128]{1,0:T(8,128)(2,1)S(1)}, u32[]{:S(2)}, u32[]{:S(2)}) %collective-permute-start.25) | collective-permute-done | bytes 131104 | tf_op jit(solution)/shard_map/ppermute | solution.py:702
  79.4 1.6 %weight_grads.2 = (f32[2,256,768]{2,1,0:T(8,128)}, f32[2,256,256]{2,1,0:T(8,128)}) custom-call(s32[2]{0:T(128)S(1)} %pad_add_fusion.place_ref.refs_1_.refs_0_, bf16[512,128]{1,0:T(8,128)(2,1)S(1)} %add_space_last.1.refs_1_, bf16[512,128]{1,0:T(8,128)(2,1)S(1)} %collective-permute-done.24.refs_2_, bf16[512,128]{1,0:T(8,128)(2,1)S(1)} %collective-permute-done.25.refs_3_, ...), custom_call_target="tpu_custom_call" | custom-call | flops 268435456 | bytes 1048576 | tf_op jit(solution)/shard_map/weight_grads/pallas_call | solution.py:734
  81.1 1.7 %weight_grads.3 = (f32[2,256,768]{2,1,0:T(8,128)}, f32[2,256,256]{2,1,0:T(8,128)}) custom-call(s32[2]{0:T(128)S(1)} %pad_add_fusion.place_ref.refs_1_.refs_0_, bf16[512,128]{1,0:T(8,128)(2,1)S(1)} %collective-permute-done.22.refs_1_, bf16[512,128]{1,0:T(8,128)(2,1)S(1)} %collective-permute-done.27.refs_2_, ...), custom_call_target="tpu_custom_call", output_to_operand_aliasing={{0}: (5, {}), {1}: (6, {})} | custom-call | flops 268435456 | bytes 1048576 | tf_op jit(solution)/shard_map/weight_grads/pallas_call | solution.py:734
  (55 shorter events, 18.8 us)
Async XLA Ops:
  2.1 4.6 %collective-permute-start.2 = (bf16[1,256,256]{2,1,0:T(8,128)(2,1)S(1)}, bf16[1,256,256]{2,1,0:T(8,128)(2,1)S(1)}, u32[]{:S(2)}, u32[]{:S(2)}) collective-permute-start(bf16[1,256,256]{2,1,0:T(8,128)(2,1)S(1)} %get-tuple-element.182), channel_id=1, source_target_pairs={{1,2},{3,4},{5,6},{2,1},{4,3},{6,5},{9,10},{11,12},{13,14},{10,9},... | collective-permute-start | bytes 393224 | tf_op jit(solution)/shard_map/ppermute | solution.py:698
  2.8 7.4 %collective-permute-start.1 = (bf16[1,256,256]{2,1,0:T(8,128)(2,1)S(1)}, bf16[1,256,256]{2,1,0:T(8,128)(2,1)S(1)}, u32[]{:S(2)}, u32[]{:S(2)}) collective-permute-start(bf16[1,256,256]{2,1,0:T(8,128)(2,1)S(1)} %get-tuple-element.183), channel_id=1, source_target_pairs={{1,2},{3,4},{5,6},{2,1},{4,3},{6,5},{9,10},{11,12},{13,14},{10,9},... | collective-permute-start | bytes 393224 | tf_op jit(solution)/shard_map/ppermute | solution.py:698
  13.7 5.5 %collective-permute-start.3 = (bf16[2,64,512]{2,1,0:T(8,128)(2,1)S(1)}, bf16[2,64,512]{2,1,0:T(8,128)(2,1)S(1)}, u32[]{:S(2)}, u32[]{:S(2)}) collective-permute-start(bf16[2,64,512]{2,1,0:T(8,128)(2,1)S(1)} %get-tuple-element.115), channel_id=1, source_target_pairs={{0,8},{8,0},{16,24},{24,16},{1,9},{9,1},{17,25},{25,17},{2,10},{10... | collective-permute-start | bytes 393224 | tf_op jit(solution)/shard_map/ppermute | solution.py:702
  16.3 5.0 %collective-permute-start.4 = (bf16[2,64,512]{2,1,0:T(8,128)(2,1)S(1)}, bf16[2,64,512]{2,1,0:T(8,128)(2,1)S(1)}, u32[]{:S(2)}, u32[]{:S(2)}) collective-permute-start(bf16[2,64,512]{2,1,0:T(8,128)(2,1)S(1)} %get-tuple-element.116), channel_id=1, source_target_pairs={{0,16},{8,24},{16,0},{24,8},{1,17},{9,25},{17,1},{25,9},{2,18},{10... | collective-permute-start | bytes 393224 | tf_op jit(solution)/shard_map/ppermute | solution.py:702
  17.8 6.6 %collective-permute-start.5 = (bf16[2,64,512]{2,1,0:T(8,128)(2,1)S(1)}, bf16[2,64,512]{2,1,0:T(8,128)(2,1)S(1)}, u32[]{:S(2)}, u32[]{:S(2)}) collective-permute-start(bf16[2,64,512]{2,1,0:T(8,128)(2,1)S(1)} %get-tuple-element.117), channel_id=1, source_target_pairs={{0,24},{8,16},{16,8},{24,0},{1,25},{9,17},{17,9},{25,1},{2,26},{10... | collective-permute-start | bytes 393224 | tf_op jit(solution)/shard_map/ppermute | solution.py:702
  28.0 5.5 %collective-permute-start.6 = (bf16[2,64,256]{2,1,0:T(8,128)(2,1)S(1)}, bf16[2,64,256]{2,1,0:T(8,128)(2,1)S(1)}, u32[]{:S(2)}, u32[]{:S(2)}) collective-permute-start(bf16[2,64,256]{2,1,0:T(8,128)(2,1)S(1)} %get-tuple-element.119), channel_id=1, source_target_pairs={{0,8},{8,0},{16,24},{24,16},{1,9},{9,1},{17,25},{25,17},{2,10},{10... | collective-permute-start | bytes 196616 | tf_op jit(solution)/shard_map/ppermute | solution.py:702
  28.1 8.1 %collective-permute-start.7 = (bf16[2,64,256]{2,1,0:T(8,128)(2,1)S(1)}, bf16[2,64,256]{2,1,0:T(8,128)(2,1)S(1)}, u32[]{:S(2)}, u32[]{:S(2)}) collective-permute-start(bf16[2,64,256]{2,1,0:T(8,128)(2,1)S(1)} %get-tuple-element.127), channel_id=1, source_target_pairs={{0,16},{8,24},{16,0},{24,8},{1,17},{9,25},{17,1},{25,9},{2,18},{10... | collective-permute-start | bytes 196616 | tf_op jit(solution)/shard_map/ppermute | solution.py:702
  28.8 7.3 %collective-permute-start.8 = (bf16[2,64,256]{2,1,0:T(8,128)(2,1)S(1)}, bf16[2,64,256]{2,1,0:T(8,128)(2,1)S(1)}, u32[]{:S(2)}, u32[]{:S(2)}) collective-permute-start(bf16[2,64,256]{2,1,0:T(8,128)(2,1)S(1)} %get-tuple-element.128), channel_id=1, source_target_pairs={{0,24},{8,16},{16,8},{24,0},{1,25},{9,17},{17,9},{25,1},{2,26},{10... | collective-permute-start | bytes 196616 | tf_op jit(solution)/shard_map/ppermute | solution.py:702
  32.6 10.8 %collective-permute-start.10 = (bf16[768,128]{1,0:T(8,128)(2,1)S(1)}, bf16[768,128]{1,0:T(8,128)(2,1)S(1)}, u32[]{:S(2)}, u32[]{:S(2)}) collective-permute-start(bf16[768,128]{1,0:T(8,128)(2,1)S(1)} %get-tuple-element.140), channel_id=1, source_target_pairs={{0,8},{8,0},{16,24},{24,16},{1,9},{9,1},{17,25},{25,17},{2,10},{10... | collective-permute-start | bytes 589832 | tf_op jit(solution)/shard_map/ppermute | solution.py:702
  32.7 10.6 %collective-permute-start.11 = (bf16[768,128]{1,0:T(8,128)(2,1)S(1)}, bf16[768,128]{1,0:T(8,128)(2,1)S(1)}, u32[]{:S(2)}, u32[]{:S(2)}) collective-permute-start(bf16[768,128]{1,0:T(8,128)(2,1)S(1)} %get-tuple-element.141), channel_id=1, source_target_pairs={{0,16},{8,24},{16,0},{24,8},{1,17},{9,25},{17,1},{25,9},{2,18},{10... | collective-permute-start | bytes 589832 | tf_op jit(solution)/shard_map/ppermute | solution.py:702
  33.4 10.7 %collective-permute-start.12 = (bf16[768,128]{1,0:T(8,128)(2,1)S(1)}, bf16[768,128]{1,0:T(8,128)(2,1)S(1)}, u32[]{:S(2)}, u32[]{:S(2)}) collective-permute-start(bf16[768,128]{1,0:T(8,128)(2,1)S(1)} %get-tuple-element.142), channel_id=1, source_target_pairs={{0,24},{8,16},{16,8},{24,0},{1,25},{9,17},{17,9},{25,1},{2,26},{10... | collective-permute-start | bytes 589832 | tf_op jit(solution)/shard_map/ppermute | solution.py:702
  44.8 4.8 %collective-permute-start.16 = (bf16[256,128]{1,0:T(8,128)(2,1)S(1)}, bf16[256,128]{1,0:T(8,128)(2,1)S(1)}, u32[]{:S(2)}, u32[]{:S(2)}) collective-permute-start(bf16[256,128]{1,0:T(8,128)(2,1)S(1)} %get-tuple-element.150), channel_id=1, source_target_pairs={{0,1},{1,0},{2,3},{3,2},{4,5},{5,4},{6,7},{7,6},{8,9},{9,8},{10,11... | collective-permute-start | bytes 196616 | tf_op jit(solution)/shard_map/ppermute | solution.py:702
  46.0 9.1 %collective-permute-start.13 = (bf16[256,128]{1,0:T(8,128)(2,1)S(1)}, bf16[256,128]{1,0:T(8,128)(2,1)S(1)}, u32[]{:S(2)}, u32[]{:S(2)}) collective-permute-start(bf16[256,128]{1,0:T(8,128)(2,1)S(1)} %get-tuple-element.146), channel_id=1, source_target_pairs={{0,8},{8,0},{16,24},{24,16},{1,9},{9,1},{17,25},{25,17},{2,10},{10... | collective-permute-start | bytes 196616 | tf_op jit(solution)/shard_map/ppermute | solution.py:702
  48.1 7.0 %collective-permute-start.14 = (bf16[256,128]{1,0:T(8,128)(2,1)S(1)}, bf16[256,128]{1,0:T(8,128)(2,1)S(1)}, u32[]{:S(2)}, u32[]{:S(2)}) collective-permute-start(bf16[256,128]{1,0:T(8,128)(2,1)S(1)} %get-tuple-element.147), channel_id=1, source_target_pairs={{0,16},{8,24},{16,0},{24,8},{1,17},{9,25},{17,1},{25,9},{2,18},{10... | collective-permute-start | bytes 196616 | tf_op jit(solution)/shard_map/ppermute | solution.py:702
  48.7 6.4 %collective-permute-start.15 = (bf16[256,128]{1,0:T(8,128)(2,1)S(1)}, bf16[256,128]{1,0:T(8,128)(2,1)S(1)}, u32[]{:S(2)}, u32[]{:S(2)}) collective-permute-start(bf16[256,128]{1,0:T(8,128)(2,1)S(1)} %get-tuple-element.148), channel_id=1, source_target_pairs={{0,24},{8,16},{16,8},{24,0},{1,25},{9,17},{17,9},{25,1},{2,26},{10... | collective-permute-start | bytes 196616 | tf_op jit(solution)/shard_map/ppermute | solution.py:702
  49.7 7.7 %collective-permute-start.17 = (bf16[256,128]{1,0:T(8,128)(2,1)S(1)}, bf16[256,128]{1,0:T(8,128)(2,1)S(1)}, u32[]{:S(2)}, u32[]{:S(2)}) collective-permute-start(bf16[256,128]{1,0:T(8,128)(2,1)S(1)} %add_cores_time.1.refs_4_), channel_id=1, source_target_pairs={{0,2},{1,3},{2,0},{3,1},{4,6},{5,7},{6,4},{7,5},{8,10},{9,11},{10,... | collective-permute-start | bytes 196616 | tf_op jit(solution)/shard_map/ppermute | solution.py:702
  58.0 5.0 %collective-permute-start.18 = (bf16[256,128]{1,0:T(8,128)(2,1)S(1)}, bf16[256,128]{1,0:T(8,128)(2,1)S(1)}, u32[]{:S(2)}, u32[]{:S(2)}) collective-permute-start(bf16[256,128]{1,0:T(8,128)(2,1)S(1)} %get-tuple-element.157.refs_0_), channel_id=1, source_target_pairs={{0,2},{1,3},{2,0},{3,1},{4,6},{5,7},{6,4},{7,5},{8,10},{9,11},{10,... | collective-permute-start | bytes 196616 | tf_op jit(solution)/shard_map/ppermute | solution.py:702
  60.1 7.0 %collective-permute-start.19 = (bf16[256,128]{1,0:T(8,128)(2,1)S(1)}, bf16[256,128]{1,0:T(8,128)(2,1)S(1)}, u32[]{:S(2)}, u32[]{:S(2)}) collective-permute-start(bf16[256,128]{1,0:T(8,128)(2,1)S(1)} %get-tuple-element.156.refs_0_), channel_id=1, source_target_pairs={{0,4},{1,5},{2,6},{3,7},{4,0},{5,1},{6,2},{7,3},{8,12},{9,13},{10,... | collective-permute-start | bytes 196616 | tf_op jit(solution)/shard_map/ppermute | solution.py:702
  63.0 5.2 %collective-permute-start.21 = (bf16[256,128]{1,0:T(8,128)(2,1)S(1)}, bf16[256,128]{1,0:T(8,128)(2,1)S(1)}, u32[]{:S(2)}, u32[]{:S(2)}) collective-permute-start(bf16[256,128]{1,0:T(8,128)(2,1)S(1)} %add_space.1.space_ref), channel_id=1, source_target_pairs={{0,4},{1,5},{2,6},{3,7},{4,0},{5,1},{6,2},{7,3},{8,12},{9,13},{10,... | collective-permute-start | bytes 196616 | tf_op jit(solution)/shard_map/ppermute | solution.py:702
  67.1 6.1 %collective-permute-start.20 = (bf16[2,256,256]{2,1,0:T(8,128)(2,1)S(1)}, bf16[2,256,256]{2,1,0:T(8,128)(2,1)S(1)}, u32[]{:S(2)}, u32[]{:S(2)}) collective-permute-start(bf16[2,256,256]{2,1,0:T(8,128)(2,1)S(1)} %get-tuple-element.164), channel_id=1, source_target_pairs={{0,1},{1,0},{2,3},{3,2},{4,5},{5,4},{6,7},{7,6},{8,9},{9,8},{10,11... | collective-permute-start | bytes 786440 | tf_op jit(solution)/shard_map/ppermute | solution.py:702
  67.2 6.0 %collective-permute-start.23 = (bf16[2,256,256]{2,1,0:T(8,128)(2,1)S(1)}, bf16[2,256,256]{2,1,0:T(8,128)(2,1)S(1)}, u32[]{:S(2)}, u32[]{:S(2)}) collective-permute-start(bf16[2,256,256]{2,1,0:T(8,128)(2,1)S(1)} %get-tuple-element.168), channel_id=1, source_target_pairs={{1,2},{3,4},{5,6},{2,1},{4,3},{6,5},{9,10},{11,12},{13,14},{10,9},... | collective-permute-start | bytes 786440 | tf_op jit(solution)/shard_map/ppermute | solution.py:698
  69.7 7.3 %collective-permute-start.26 = (bf16[512,128]{1,0:T(8,128)(2,1)S(1)}, bf16[512,128]{1,0:T(8,128)(2,1)S(1)}, u32[]{:S(2)}, u32[]{:S(2)}) collective-permute-start(bf16[512,128]{1,0:T(8,128)(2,1)S(1)} %add_space_last.1.refs_1_), channel_id=1, source_target_pairs={{0,24},{8,16},{16,8},{24,0},{1,25},{9,17},{17,9},{25,1},{2,26},{10... | collective-permute-start | bytes 393224 | tf_op jit(solution)/shard_map/ppermute | solution.py:702
  71.5 7.3 %collective-permute-start.25 = (bf16[512,128]{1,0:T(8,128)(2,1)S(1)}, bf16[512,128]{1,0:T(8,128)(2,1)S(1)}, u32[]{:S(2)}, u32[]{:S(2)}) collective-permute-start(bf16[512,128]{1,0:T(8,128)(2,1)S(1)} %add_space_last.1.refs_1_), channel_id=1, source_target_pairs={{0,16},{8,24},{16,0},{24,8},{1,17},{9,25},{17,1},{25,9},{2,18},{10... | collective-permute-start | bytes 393224 | tf_op jit(solution)/shard_map/ppermute | solution.py:702
  72.1 6.8 %collective-permute-start.24 = (bf16[512,128]{1,0:T(8,128)(2,1)S(1)}, bf16[512,128]{1,0:T(8,128)(2,1)S(1)}, u32[]{:S(2)}, u32[]{:S(2)}) collective-permute-start(bf16[512,128]{1,0:T(8,128)(2,1)S(1)} %add_space_last.1.refs_1_), channel_id=1, source_target_pairs={{0,8},{8,0},{16,24},{24,16},{1,9},{9,1},{17,25},{25,17},{2,10},{10... | collective-permute-start | bytes 393224 | tf_op jit(solution)/shard_map/ppermute | solution.py:702
  (6 other events, 15.5 us)

commit v9 on v7

--- a/solution.py
+++ b/solution.py
@@ -429,7 +429,6 @@
 
 def space_backward_kernel(
     scale,
-    factor,
     count_in,
     lists_ref,
     place_ref,
@@ -444,15 +443,17 @@
         probs_ref,
         inverse_sum_ref,
         attended_ref,
+        project_ref,
         combine_ref,
         mixed_grad_ref,
         dquery_ref,
         dkv_ref,
-        kept_ref,
-        sent_ref,
+        dact_ref,
+        near_ref,
+        far_ref,
         dscores_s,
         dkv_s,
-        stacked_s,
+        dact_s,
     ) = refs[count_in:]
     me = place_ref[0]
     frame_count, row_count, features = mixed_grad_ref.shape
@@ -545,7 +546,32 @@
             dquery_ref[frame, span] = flip(jnp.concatenate(dquery_parts, axis=0))
     add_keys(len(blocks) - 1)
     dkv_ref[...] = dkv_s[...].astype(BF16)
+    core = place_ref[1] % 2
+    for frame in range(frame_count):
+        dact = dot_nt(dkv_ref[frame], project_ref[0, :, features:])
+        dact_s[frame] = dact.astype(BF16)
+        dact_ref[frame] = dact[rim : rim + row_count] + dot_nt(
+            dquery_ref[frame], project_ref[0, :, :features]
+        )
+    near_ref[...] = dact_s[:, pl.ds(halo_start(core, rim, row_count, True), rim)]
+    far_ref[...] = dact_s[:, pl.ds(halo_start(core, rim, row_count, False), rim)]
+
+
+def space_grads_kernel(
+    factor,
+    place_ref,
+    act_ref,
+    dquery_ref,
+    dkv_ref,
+    attended_ref,
+    mixed_grad_ref,
+    kept_ref,
+    sent_ref,
+    stacked_s,
+):
+    frame_count, row_count, features = mixed_grad_ref.shape
     extended = dkv_ref.shape[1]
+    rim = (extended - row_count) // 2
     act = act_ref[...]
     own_act = act[:, rim : rim + row_count].reshape(frame_count * row_count, features)
     stack_grads(
@@ -563,20 +589,6 @@
         stacked_s,
     )
     halve(place_ref[1] % 2, stacked_s, kept_ref, sent_ref)
-
-
-def dact_kernel(place_ref, dquery_ref, dkv_ref, project_ref, dact_ref, near_ref, far_ref, dact_s):
-    frame_count, row_count, features = dquery_ref.shape
-    rim = near_ref.shape[1]
-    core = place_ref[1] % 2
-    for frame in range(frame_count):
-        dact = dot_nt(dkv_ref[frame], project_ref[0, :, features:])
-        dact_s[frame] = dact.astype(BF16)
-        dact_ref[frame] = dact[rim : rim + row_count] + dot_nt(
-            dquery_ref[frame], project_ref[0, :, :features]
-        )
-    near_ref[...] = dact_s[:, pl.ds(halo_start(core, rim, row_count, True), rim)]
-    far_ref[...] = dact_s[:, pl.ds(halo_start(core, rim, row_count, False), rim)]
 
 
 def field_kernel(place_ref, wave_ref, mixed_grad_ref, dact_ref, near_ref, far_ref, *refs):
@@ -646,19 +658,16 @@
         ref[...] = add_rounded(refs[2 * index], refs[2 * index + 1])
 
 
-def both_kernel(space_ref, space_other_ref, time_ref, total_ref):
-    rows = space_ref.shape[0]
-    total_ref[:rows] = add_rounded(space_ref, space_other_ref)
-    total_ref[rows:] = time_ref[...]
-
-
 def join_kernel(place_ref, *refs):
     *part_refs, joined_ref = refs
-    for distance, ref in enumerate(part_refs):
-        rows = ref.shape[0]
-        joined_ref[pl.ds(pl.multiple_of((place_ref[0] ^ distance) * rows, GROUP_ROWS), rows)] = ref[
-            ...
-        ]
+    count_in = len(part_refs) // 2
+    rows = part_refs[0].shape[0]
+    for layer in range(2):
+        for distance in range(count_in):
+            start = (2 * (place_ref[0] ^ distance) + layer) * rows
+            joined_ref[pl.ds(pl.multiple_of(start, GROUP_ROWS), rows)] = part_refs[
+                layer * count_in + distance
+            ][...]
 
 
 def grads_kernel(time_count, own, place_ref, half_ref, *refs):
@@ -858,20 +867,41 @@
     returned[1], rides[0] = lax.optimization_barrier((returned[1], rides[0]))
 
     def backward_body(*refs):
-        space_backward_kernel(scale, factor, time_count, *refs)
-
-    mixed_grad, dquery, dkv, space_kept, space_sent = call(
+        space_backward_kernel(scale, time_count, *refs)
+
+    mixed_grad, dquery, dkv, dact, to_near, to_far = call(
         backward_body,
         "space_backward",
         [block_lists, place],
-        [*returned, *kept_space, combine],
-        [own, own, (frame_count, extended, 2 * features), *[(grad_rows // 2, LANES)] * 2],
+        [*returned, *kept_space, project, combine],
+        [
+            own,
+            own,
+            (frame_count, extended, 2 * features),
+            (*own, F32),
+            *[(frame_count, rim, features)] * 2,
+        ],
         [
             (frame_count, block_count, keys_count, HEADS * BLOCK),
             (frame_count, extended, 2 * features, F32),
-            (grad_rows, LANES),
+            (frame_count, extended, features),
         ],
         matmuls=44,
+    )
+    from_far = swap_far(to_far, "space")
+    from_near = exchange(to_near, "space", 1)
+
+    def space_grads_body(*refs):
+        space_grads_kernel(factor, *refs)
+
+    space_kept, space_sent = call(
+        space_grads_body,
+        "space_grads",
+        [place],
+        [act, dquery, dkv, attended, mixed_grad],
+        [(grad_rows // 2, LANES)] * 2,
+        [(grad_rows, LANES)],
+        matmuls=8,
     )
 
     def add_pair(name, piece, other):
@@ -901,6 +931,9 @@
     space_pieces = over_tm(space_pieces)
     time_piece = add_pair("add_cores_time", time_kept, time_other)
     steps = [2 << bit for bit in range((space_count - 1).bit_length())]
+    from_near, from_far, *space_pieces = lax.optimization_barrier(
+        (from_near, from_far, *space_pieces)
+    )
     time_other = exchange(time_piece, "space", steps[0])
     space_piece, time_piece = call(
         tm_sum_kernel,
@@ -910,37 +943,17 @@
         [(chunk // 2, LANES)] * 2,
         [(time_count, chunk // 2, LANES)],
     )
-
-    space_piece, dquery = lax.optimization_barrier((space_piece, dquery))
-    dact, to_near, to_far = call(
-        dact_kernel,
-        "space_dact",
-        [place],
-        [dquery, dkv, project],
-        [(*own, F32), (frame_count, rim, features), (frame_count, rim, features)],
-        [(frame_count, extended, features)],
-        matmuls=3,
-    )
+    sent_piece = space_piece
     for step, time_step in zip(steps, steps[1:]):
-        space_other = exchange(space_piece, "space", step)
+        space_other = exchange(sent_piece, "space", step)
         time_other = exchange(time_piece, "space", time_step)
-        space_other, to_near, to_far = lax.optimization_barrier((space_other, to_near, to_far))
-        space_piece = add_pair("add_space", space_piece, space_other)
-        space_piece, time_other = lax.optimization_barrier((space_piece, time_other))
+        sent_piece = add_pair("add_space", space_piece, space_other)
+        space_piece, time_other = lax.optimization_barrier((sent_piece, time_other))
         time_piece = add_pair("add_space_time", time_piece, time_other)
-    space_other = exchange(space_piece, "space", steps[-1])
-    time_piece, to_near, to_far = lax.optimization_barrier((time_piece, to_near, to_far))
-    from_far = swap_far(to_far, "space")
-    from_near = exchange(to_near, "space", 1)
-    (piece,) = call(
-        both_kernel,
-        "add_space_last",
-        [],
-        [space_piece, space_other, time_piece],
-        [(chunk, LANES)],
-        matmuls=64,
-    )
-    joined = over_tm([piece] * time_count)
+    space_other = exchange(sent_piece, "space", steps[-1])
+    time_joined = over_tm([time_piece] * time_count)
+    space_piece = add_pair("add_space_last", space_piece, space_other)
+    joined = over_tm([space_piece] * time_count) + time_joined
 
     field_grad, mixed_field = call(
         field_kernel,

time: 81.2 us -> 82.9 us (1.021)
  starting transfers between devices: 28.3 us -> 36.2 us
  waiting for transfers between devices: 22.7 us -> 16.4 us
    ppermute x24 -> x27, starting transfers between devices: 27 us -> 34.9 us  [exchange(): lax.ppermute(cells, axis, [(i, i ^ distance) for i in range(lax.axis_size...]
    ppermute x24 -> x27, waiting for transfers between devices: 22.7 us -> 16.4 us  [exchange(): lax.ppermute(cells, axis, [(i, i ^ distance) for i in range(lax.axis_size...]
  transfers between devices with their start and end apart: 26 -> 29, of which waited for: 13 -> 13; matrix products, arithmetic and copies ran while one was open for 0% -> 0% of each run, Pallas kernels for 21% -> 21%
where the time goes in v9:
time: 82.9 us; the launch traced here: 82.7 us
  starting transfers between devices  36.2 us (44%)
  Pallas kernels  29.1 us (35%)
  waiting for transfers between devices  16.4 us (20%)
  between operations  0.97 us (1%)
    ppermute x27, starting transfers between devices, exchange(): lax.ppermute(cells, axis, [(i, i ^ distance) for i in range(lax.axis_size...  34.9 us
    pallas_call x17, Pallas kernels, call(): pl.pallas_call(body, in_specs=[smem_spec] * len(scalars) + [vmem_spec] *...  29.1 us
    ppermute x27, waiting for transfers between devices, exchange(): lax.ppermute(cells, axis, [(i, i ^ distance) for i in range(lax.axis_size...  16.4 us
  transfers between devices with their start and end apart: 29, of which 13 were waited for; matrix products, arithmetic and copies ran while one was open for 0% of the time, Pallas kernels for 21%

profile of v9, /device:TPU:0, one launch (start us, length us, event | category | flops | bytes accessed | tf_op | source)
XLA Modules:
  0.0 82.7 jit_solution(14815197662438267369)
XLA Ops:
  2.5 3.1 %prepare.1 = (bf16[2,256,256]{2,1,0:T(8,128)(2,1)S(1)}, bf16[2,256,768]{2,1,0:T(8,128)(2,1)S(1)}, bf16[2,768,256]{2,1,0:T(8,128)(2,1)S(1)}, bf16[2,256,256]{2,1,...) custom-call(s32[2]{0:T(128)S(1)} %pad_add_fusion.place_ref.refs_0_.r, ...), custom_call_target="tpu_custom_call" | custom-call | flops 3221225472 | bytes 12582912 | tf_op jit(solution)/shard_map/prepare/pallas_call | solution.py:763
  5.7 5.6 %space_forward.1 = (bf16[2,768,256]{2,1,0:T(8,128)(2,1)S(1)}, bf16[2,768,512]{2,1,0:T(8,128)(2,1)S(1)}, bf16[2,6,256,128]{3,2,1,0:T(8,128)(2,1)S(1)}, bf16[2,6,2...) custom-call(s32[2,2,4]{2,1,0:T(2,128)} %refs_0_.1, ...), custom_call_target="tpu_custom_call", output_to_operand_aliasing={{0}: (9, {}), {1}: (10, {}), {2}: (11, {}), {3}: (12, {})} | custom-call | flops 10737418240 | bytes 41943040 | tf_op jit(solution)/shard_map/space_forward/pallas_call | solution.py:763
  11.3 2.9 %collective-permute-start.2 = (bf16[2,64,512]{2,1,0:T(8,128)(2,1)S(1)}, bf16[2,64,512]{2,1,0:T(8,128)(2,1)S(1)}, u32[]{:S(2)}, u32[]{:S(2)}) collective-permute-start(bf16[2,64,512]{2,1,0:T(8,128)(2,1)S(1)} %get-tuple-element.93), channel_id=1, source_target_pairs={{0,8},{8,0},{16,24},{24,16},{1,9},{9,1},{17,25},{25,17},{2,10},{10... | collective-permute-start | bytes 393224 | tf_op jit(solution)/shard_map/ppermute | solution.py:731
  14.3 1.5 %collective-permute-start.3 = (bf16[2,64,512]{2,1,0:T(8,128)(2,1)S(1)}, bf16[2,64,512]{2,1,0:T(8,128)(2,1)S(1)}, u32[]{:S(2)}, u32[]{:S(2)}) collective-permute-start(bf16[2,64,512]{2,1,0:T(8,128)(2,1)S(1)} %get-tuple-element.94), channel_id=1, source_target_pairs={{0,16},{8,24},{16,0},{24,8},{1,17},{9,25},{17,1},{25,9},{2,18},{10... | collective-permute-start | bytes 393224 | tf_op jit(solution)/shard_map/ppermute | solution.py:731
  15.8 1.4 %collective-permute-done.2.refs_1_ = bf16[2,64,512]{2,1,0:T(8,128)(2,1)S(1)} collective-permute-done((bf16[2,64,512]{2,1,0:T(8,128)(2,1)S(1)}, bf16[2,64,512]{2,1,0:T(8,128)(2,1)S(1)}, u32[]{:S(2)}, u32[]{:S(2)}) %collective-permute-start.2) | collective-permute-done | bytes 131104 | tf_op jit(solution)/shard_map/ppermute | solution.py:731
  17.2 2.0 %collective-permute-done.3.refs_2_ = bf16[2,64,512]{2,1,0:T(8,128)(2,1)S(1)} collective-permute-done((bf16[2,64,512]{2,1,0:T(8,128)(2,1)S(1)}, bf16[2,64,512]{2,1,0:T(8,128)(2,1)S(1)}, u32[]{:S(2)}, u32[]{:S(2)}) %collective-permute-start.3) | collective-permute-done | bytes 131104 | tf_op jit(solution)/shard_map/ppermute | solution.py:731
  19.2 3.8 %collective-permute-done.4.refs_3_ = bf16[2,64,512]{2,1,0:T(8,128)(2,1)S(1)} collective-permute-done((bf16[2,64,512]{2,1,0:T(8,128)(2,1)S(1)}, bf16[2,64,512]{2,1,0:T(8,128)(2,1)S(1)}, u32[]{:S(2)}, u32[]{:S(2)}) %collective-permute-start.4) | collective-permute-done | bytes 131104 | tf_op jit(solution)/shard_map/ppermute | solution.py:731
  23.0 3.6 %time_pair.1 = (bf16[2,64,256]{2,1,0:T(8,128)(2,1)S(1)}, bf16[2,64,256]{2,1,0:T(8,128)(2,1)S(1)}, bf16[2,64,256]{2,1,0:T(8,128)(2,1)S(1)}, bf16[2,64,256]{2,1,0:...) custom-call(bf16[2,64,512]{2,1,0:T(8,128)(2,1)S(1)} %get-tuple-eleme, ...), custom_call_target="tpu_custom_call" | custom-call | flops 9663676416 | bytes 37748736 | tf_op jit(solution)/shard_map/time_pair/pallas_call | solution.py:763
  26.8 3.4 %collective-permute-start.7 = (bf16[2,64,256]{2,1,0:T(8,128)(2,1)S(1)}, bf16[2,64,256]{2,1,0:T(8,128)(2,1)S(1)}, u32[]{:S(2)}, u32[]{:S(2)}) collective-permute-start(bf16[2,64,256]{2,1,0:T(8,128)(2,1)S(1)} %get-tuple-element.106), channel_id=1, source_target_pairs={{0,24},{8,16},{16,8},{24,0},{1,25},{9,17},{17,9},{25,1},{2,26},{10... | collective-permute-start | bytes 196616 | tf_op jit(solution)/shard_map/ppermute | solution.py:731
  31.9 2.9 %collective-permute-start.13 = (bf16[768,128]{1,0:T(8,128)(2,1)S(1)}, bf16[768,128]{1,0:T(8,128)(2,1)S(1)}, u32[]{:S(2)}, u32[]{:S(2)}) collective-permute-start(bf16[768,128]{1,0:T(8,128)(2,1)S(1)} %get-tuple-element.125), channel_id=1, source_target_pairs={{0,24},{8,16},{16,8},{24,0},{1,25},{9,17},{17,9},{25,1},{2,26},{10... | collective-permute-start | bytes 589832 | tf_op jit(solution)/shard_map/ppermute | solution.py:731
  34.8 6.6 %space_backward.1 = (bf16[2,256,256]{2,1,0:T(8,128)(2,1)S(1)}, bf16[2,256,256]{2,1,0:T(8,128)(2,1)S(1)}, bf16[2,768,512]{2,1,0:T(8,128)(2,1)S(1)}, f32[2,256,256...) custom-call(s32[2,2,4]{2,1,0:T(2,128)} %refs_0_.1, ...), custom_call_target="tpu_custom_call" | custom-call | flops 11811160064 | bytes 46137344 | tf_op jit(solution)/shard_map/space_backward/pallas_call | solution.py:763
  42.2 1.4 %space_grads.1 = (bf16[1024,128]{1,0:T(8,128)(2,1)S(1)}, bf16[1024,128]{1,0:T(8,128)(2,1)S(1)}) custom-call(s32[2]{0:T(128)S(1)} %pad_add_fusion.place_ref.refs_0_.refs_1_, bf16[2,768,256]{2,1,0:T(8,128)(2,1)S(1)} %get-tuple-element.107.refs_6_.refs_1_, bf16[2,256,256]{2,1,0:T(8,128)(2,1)S(1)} %get-tuple-element.118.refs_2_, ...), custom_call_target="tpu_custom_call" | custom-call | flops 2147483648 | bytes 8388608 | tf_op jit(solution)/shard_map/space_grads/pallas_call | solution.py:763
  43.6 5.6 %collective-permute-start.10 = (bf16[1024,128]{1,0:T(8,128)(2,1)S(1)}, bf16[1024,128]{1,0:T(8,128)(2,1)S(1)}, u32[]{:S(2)}, u32[]{:S(2)}) collective-permute-start(bf16[1024,128]{1,0:T(8,128)(2,1)S(1)} %get-tuple-element.121), channel_id=1, source_target_pairs={{0,1},{1,0},{2,3},{3,2},{4,5},{5,4},{6,7},{7,6},{8,9},{9,8},{10,11... | collective-permute-start | bytes 786440 | tf_op jit(solution)/shard_map/ppermute | solution.py:731
  53.2 1.4 %collective-permute-start.16 = (bf16[256,128]{1,0:T(8,128)(2,1)S(1)}, bf16[256,128]{1,0:T(8,128)(2,1)S(1)}, u32[]{:S(2)}, u32[]{:S(2)}) collective-permute-start(bf16[256,128]{1,0:T(8,128)(2,1)S(1)} %get-tuple-element.131), channel_id=1, source_target_pairs={{0,24},{8,16},{16,8},{24,0},{1,25},{9,17},{17,9},{25,1},{2,26},{10... | collective-permute-start | bytes 196616 | tf_op jit(solution)/shard_map/ppermute | solution.py:731
  54.7 1.6 %collective-permute-start.18 = (bf16[256,128]{1,0:T(8,128)(2,1)S(1)}, bf16[256,128]{1,0:T(8,128)(2,1)S(1)}, u32[]{:S(2)}, u32[]{:S(2)}) collective-permute-start(bf16[256,128]{1,0:T(8,128)(2,1)S(1)} %add_cores_time.1.refs_4_), channel_id=1, source_target_pairs={{0,2},{1,3},{2,0},{3,1},{4,6},{5,7},{6,4},{7,5},{8,10},{9,11},{10,... | collective-permute-start | bytes 196616 | tf_op jit(solution)/shard_map/ppermute | solution.py:731
  59.6 1.6 %collective-permute-start.19 = (bf16[256,128]{1,0:T(8,128)(2,1)S(1)}, bf16[256,128]{1,0:T(8,128)(2,1)S(1)}, u32[]{:S(2)}, u32[]{:S(2)}) collective-permute-start(bf16[256,128]{1,0:T(8,128)(2,1)S(1)} %get-tuple-element.142.refs_0_), channel_id=1, source_target_pairs={{0,2},{1,3},{2,0},{3,1},{4,6},{5,7},{6,4},{7,5},{8,10},{9,11},{10,... | collective-permute-start | bytes 196616 | tf_op jit(solution)/shard_map/ppermute | solution.py:731
  61.2 1.8 %collective-permute-start.20 = (bf16[256,128]{1,0:T(8,128)(2,1)S(1)}, bf16[256,128]{1,0:T(8,128)(2,1)S(1)}, u32[]{:S(2)}, u32[]{:S(2)}) collective-permute-start(bf16[256,128]{1,0:T(8,128)(2,1)S(1)} %get-tuple-element.143.refs_0_), channel_id=1, source_target_pairs={{0,4},{1,5},{2,6},{3,7},{4,0},{5,1},{6,2},{7,3},{8,12},{9,13},{10,... | collective-permute-start | bytes 196616 | tf_op jit(solution)/shard_map/ppermute | solution.py:731
  63.0 1.6 %collective-permute-done.19.refs_1_ = bf16[256,128]{1,0:T(8,128)(2,1)S(1)} collective-permute-done((bf16[256,128]{1,0:T(8,128)(2,1)S(1)}, bf16[256,128]{1,0:T(8,128)(2,1)S(1)}, u32[]{:S(2)}, u32[]{:S(2)}) %collective-permute-start.19) | collective-permute-done | bytes 65568 | tf_op jit(solution)/shard_map/ppermute | solution.py:731
  65.8 1.9 %collective-permute-done.20.refs_1_ = bf16[256,128]{1,0:T(8,128)(2,1)S(1)} collective-permute-done((bf16[256,128]{1,0:T(8,128)(2,1)S(1)}, bf16[256,128]{1,0:T(8,128)(2,1)S(1)}, u32[]{:S(2)}, u32[]{:S(2)}) %collective-permute-start.20) | collective-permute-done | bytes 65568 | tf_op jit(solution)/shard_map/ppermute | solution.py:731
  67.7 1.7 %collective-permute-start.27 = (bf16[256,128]{1,0:T(8,128)(2,1)S(1)}, bf16[256,128]{1,0:T(8,128)(2,1)S(1)}, u32[]{:S(2)}, u32[]{:S(2)}) collective-permute-start(bf16[256,128]{1,0:T(8,128)(2,1)S(1)} %add_space_time.1.refs_4_), channel_id=1, source_target_pairs={{0,24},{8,16},{16,8},{24,0},{1,25},{9,17},{17,9},{25,1},{2,26},{10... | collective-permute-start | bytes 196616 | tf_op jit(solution)/shard_map/ppermute | solution.py:731
  71.3 1.7 %collective-permute-start.24 = (bf16[256,128]{1,0:T(8,128)(2,1)S(1)}, bf16[256,128]{1,0:T(8,128)(2,1)S(1)}, u32[]{:S(2)}, u32[]{:S(2)}) collective-permute-start(bf16[256,128]{1,0:T(8,128)(2,1)S(1)} %add_space_last.1.refs_0_), channel_id=1, source_target_pairs={{0,24},{8,16},{16,8},{24,0},{1,25},{9,17},{17,9},{25,1},{2,26},{10... | collective-permute-start | bytes 196616 | tf_op jit(solution)/shard_map/ppermute | solution.py:731
  74.9 1.8 %field_grad.1 = (bf16[2,256,256]{2,1,0:T(8,128)(2,1)}, bf16[2,256,256]{2,1,0:T(8,128)(2,1)}) custom-call(s32[2]{0:T(128)S(1)} %pad_add_fusion.place_ref.refs_0_.refs_1_, bf16[2,256,256]{2,1,0:T(8,128)(2,1)S(1)} %get-tuple-element.82.wave_ref, bf16[2,256,256]{2,1,0:T(8,128)(2,1)S(1)} %get-tuple-element.114.refs_5_.mixed_grad_ref, ...), custom_call_target="tpu_custom_call" | custom-call | flops 805306368 | bytes 3145728 | tf_op jit(solution)/shard_map/field_grad/pallas_call | solution.py:763
  79.0 1.6 %weight_grads.2 = (f32[2,256,768]{2,1,0:T(8,128)}, f32[2,256,256]{2,1,0:T(8,128)}) custom-call(s32[2]{0:T(128)S(1)} %pad_add_fusion.place_ref.refs_0_.refs_1_, bf16[2048,128]{1,0:T(8,128)(2,1)S(1)} %join_tm.1.refs_1_), custom_call_target="tpu_custom_call" | custom-call | flops 268435456 | bytes 1048576 | tf_op jit(solution)/shard_map/weight_grads/pallas_call | solution.py:763
  80.9 1.6 %weight_grads.3 = (f32[2,256,768]{2,1,0:T(8,128)}, f32[2,256,256]{2,1,0:T(8,128)}) custom-call(s32[2]{0:T(128)S(1)} %pad_add_fusion.place_ref.refs_0_.refs_1_, bf16[2048,128]{1,0:T(8,128)(2,1)S(1)} %collective-permute-done.28.refs_1_, f32[2,256,768]{2,1,0:T(8,128)} %get-tuple-element.156.refs_2_, ...), custom_call_target="tpu_custom_call", output_to_operand_aliasing={{0}: (2, {}), {1}: (3, {})} | custom-call | flops 268435456 | bytes 1048576 | tf_op jit(solution)/shard_map/weight_grads/pallas_call | solution.py:763
  (52 shorter events, 19.4 us)
Async XLA Ops:
  1.1 4.5 %collective-permute-start.1 = (bf16[2,256,256]{2,1,0:T(8,128)(2,1)}, bf16[2,256,256]{2,1,0:T(8,128)(2,1)S(1)}, u32[]{:S(2)}, u32[]{:S(2)}) collective-permute-start(bf16[2,256,256]{2,1,0:T(8,128)(2,1)} %wave_hbm.1), channel_id=1, source_target_pairs={{1,2},{3,4},{5,6},{2,1},{4,3},{6,5},{9,10},{11,12},{13,14},{10,9},... | collective-permute-start | bytes 786440 | tf_op jit(solution)/shard_map/ppermute | solution.py:727
  11.3 5.9 %collective-permute-start.2 = (bf16[2,64,512]{2,1,0:T(8,128)(2,1)S(1)}, bf16[2,64,512]{2,1,0:T(8,128)(2,1)S(1)}, u32[]{:S(2)}, u32[]{:S(2)}) collective-permute-start(bf16[2,64,512]{2,1,0:T(8,128)(2,1)S(1)} %get-tuple-element.93), channel_id=1, source_target_pairs={{0,8},{8,0},{16,24},{24,16},{1,9},{9,1},{17,25},{25,17},{2,10},{10... | collective-permute-start | bytes 393224 | tf_op jit(solution)/shard_map/ppermute | solution.py:731
  14.3 5.0 %collective-permute-start.3 = (bf16[2,64,512]{2,1,0:T(8,128)(2,1)S(1)}, bf16[2,64,512]{2,1,0:T(8,128)(2,1)S(1)}, u32[]{:S(2)}, u32[]{:S(2)}) collective-permute-start(bf16[2,64,512]{2,1,0:T(8,128)(2,1)S(1)} %get-tuple-element.94), channel_id=1, source_target_pairs={{0,16},{8,24},{16,0},{24,8},{1,17},{9,25},{17,1},{25,9},{2,18},{10... | collective-permute-start | bytes 393224 | tf_op jit(solution)/shard_map/ppermute | solution.py:731
  15.8 7.2 %collective-permute-start.4 = (bf16[2,64,512]{2,1,0:T(8,128)(2,1)S(1)}, bf16[2,64,512]{2,1,0:T(8,128)(2,1)S(1)}, u32[]{:S(2)}, u32[]{:S(2)}) collective-permute-start(bf16[2,64,512]{2,1,0:T(8,128)(2,1)S(1)} %get-tuple-element.95), channel_id=1, source_target_pairs={{0,24},{8,16},{16,8},{24,0},{1,25},{9,17},{17,9},{25,1},{2,26},{10... | collective-permute-start | bytes 393224 | tf_op jit(solution)/shard_map/ppermute | solution.py:731
  26.6 5.2 %collective-permute-start.5 = (bf16[2,64,256]{2,1,0:T(8,128)(2,1)S(1)}, bf16[2,64,256]{2,1,0:T(8,128)(2,1)S(1)}, u32[]{:S(2)}, u32[]{:S(2)}) collective-permute-start(bf16[2,64,256]{2,1,0:T(8,128)(2,1)S(1)} %get-tuple-element.97), channel_id=1, source_target_pairs={{0,8},{8,0},{16,24},{24,16},{1,9},{9,1},{17,25},{25,17},{2,10},{10... | collective-permute-start | bytes 196616 | tf_op jit(solution)/shard_map/ppermute | solution.py:731
  26.8 8.0 %collective-permute-start.6 = (bf16[2,64,256]{2,1,0:T(8,128)(2,1)S(1)}, bf16[2,64,256]{2,1,0:T(8,128)(2,1)S(1)}, u32[]{:S(2)}, u32[]{:S(2)}) collective-permute-start(bf16[2,64,256]{2,1,0:T(8,128)(2,1)S(1)} %get-tuple-element.105), channel_id=1, source_target_pairs={{0,16},{8,24},{16,0},{24,8},{1,17},{9,25},{17,1},{25,9},{2,18},{10... | collective-permute-start | bytes 196616 | tf_op jit(solution)/shard_map/ppermute | solution.py:731
  26.8 8.0 %collective-permute-start.7 = (bf16[2,64,256]{2,1,0:T(8,128)(2,1)S(1)}, bf16[2,64,256]{2,1,0:T(8,128)(2,1)S(1)}, u32[]{:S(2)}, u32[]{:S(2)}) collective-permute-start(bf16[2,64,256]{2,1,0:T(8,128)(2,1)S(1)} %get-tuple-element.106), channel_id=1, source_target_pairs={{0,24},{8,16},{16,8},{24,0},{1,25},{9,17},{17,9},{25,1},{2,26},{10... | collective-permute-start | bytes 196616 | tf_op jit(solution)/shard_map/ppermute | solution.py:731
  31.2 12.3 %collective-permute-start.11 = (bf16[768,128]{1,0:T(8,128)(2,1)S(1)}, bf16[768,128]{1,0:T(8,128)(2,1)S(1)}, u32[]{:S(2)}, u32[]{:S(2)}) collective-permute-start(bf16[768,128]{1,0:T(8,128)(2,1)S(1)} %get-tuple-element.123), channel_id=1, source_target_pairs={{0,8},{8,0},{16,24},{24,16},{1,9},{9,1},{17,25},{25,17},{2,10},{10... | collective-permute-start | bytes 589832 | tf_op jit(solution)/shard_map/ppermute | solution.py:731
  31.4 17.8 %collective-permute-start.12 = (bf16[768,128]{1,0:T(8,128)(2,1)S(1)}, bf16[768,128]{1,0:T(8,128)(2,1)S(1)}, u32[]{:S(2)}, u32[]{:S(2)}) collective-permute-start(bf16[768,128]{1,0:T(8,128)(2,1)S(1)} %get-tuple-element.124), channel_id=1, source_target_pairs={{0,16},{8,24},{16,0},{24,8},{1,17},{9,25},{17,1},{25,9},{2,18},{10... | collective-permute-start | bytes 589832 | tf_op jit(solution)/shard_map/ppermute | solution.py:731
  31.9 17.3 %collective-permute-start.13 = (bf16[768,128]{1,0:T(8,128)(2,1)S(1)}, bf16[768,128]{1,0:T(8,128)(2,1)S(1)}, u32[]{:S(2)}, u32[]{:S(2)}) collective-permute-start(bf16[768,128]{1,0:T(8,128)(2,1)S(1)} %get-tuple-element.125), channel_id=1, source_target_pairs={{0,24},{8,16},{16,8},{24,0},{1,25},{9,17},{17,9},{25,1},{2,26},{10... | collective-permute-start | bytes 589832 | tf_op jit(solution)/shard_map/ppermute | solution.py:731
  41.4 13.2 %collective-permute-start.8 = (bf16[2,256,256]{2,1,0:T(8,128)(2,1)S(1)}, bf16[2,256,256]{2,1,0:T(8,128)(2,1)S(1)}, u32[]{:S(2)}, u32[]{:S(2)}) collective-permute-start(bf16[2,256,256]{2,1,0:T(8,128)(2,1)S(1)} %get-tuple-element.116), channel_id=1, source_target_pairs={{0,1},{1,0},{2,3},{3,2},{4,5},{5,4},{6,7},{7,6},{8,9},{9,8},{10,11... | collective-permute-start | bytes 786440 | tf_op jit(solution)/shard_map/ppermute | solution.py:731
  41.5 14.8 %collective-permute-start.9 = (bf16[2,256,256]{2,1,0:T(8,128)(2,1)S(1)}, bf16[2,256,256]{2,1,0:T(8,128)(2,1)S(1)}, u32[]{:S(2)}, u32[]{:S(2)}) collective-permute-start(bf16[2,256,256]{2,1,0:T(8,128)(2,1)S(1)} %get-tuple-element.117), channel_id=1, source_target_pairs={{1,2},{3,4},{5,6},{2,1},{4,3},{6,5},{9,10},{11,12},{13,14},{10,9},... | collective-permute-start | bytes 786440 | tf_op jit(solution)/shard_map/ppermute | solution.py:727
  43.6 6.8 %collective-permute-start.10 = (bf16[1024,128]{1,0:T(8,128)(2,1)S(1)}, bf16[1024,128]{1,0:T(8,128)(2,1)S(1)}, u32[]{:S(2)}, u32[]{:S(2)}) collective-permute-start(bf16[1024,128]{1,0:T(8,128)(2,1)S(1)} %get-tuple-element.121), channel_id=1, source_target_pairs={{0,1},{1,0},{2,3},{3,2},{4,5},{5,4},{6,7},{7,6},{8,9},{9,8},{10,11... | collective-permute-start | bytes 786440 | tf_op jit(solution)/shard_map/ppermute | solution.py:731
  51.0 5.3 %collective-permute-start.14 = (bf16[256,128]{1,0:T(8,128)(2,1)S(1)}, bf16[256,128]{1,0:T(8,128)(2,1)S(1)}, u32[]{:S(2)}, u32[]{:S(2)}) collective-permute-start(bf16[256,128]{1,0:T(8,128)(2,1)S(1)} %get-tuple-element.129), channel_id=1, source_target_pairs={{0,8},{8,0},{16,24},{24,16},{1,9},{9,1},{17,25},{25,17},{2,10},{10... | collective-permute-start | bytes 196616 | tf_op jit(solution)/shard_map/ppermute | solution.py:731
  52.4 5.0 %collective-permute-start.15 = (bf16[256,128]{1,0:T(8,128)(2,1)S(1)}, bf16[256,128]{1,0:T(8,128)(2,1)S(1)}, u32[]{:S(2)}, u32[]{:S(2)}) collective-permute-start(bf16[256,128]{1,0:T(8,128)(2,1)S(1)} %get-tuple-element.130), channel_id=1, source_target_pairs={{0,16},{8,24},{16,0},{24,8},{1,17},{9,25},{17,1},{25,9},{2,18},{10... | collective-permute-start | bytes 196616 | tf_op jit(solution)/shard_map/ppermute | solution.py:731
  53.2 5.2 %collective-permute-start.16 = (bf16[256,128]{1,0:T(8,128)(2,1)S(1)}, bf16[256,128]{1,0:T(8,128)(2,1)S(1)}, u32[]{:S(2)}, u32[]{:S(2)}) collective-permute-start(bf16[256,128]{1,0:T(8,128)(2,1)S(1)} %get-tuple-element.131), channel_id=1, source_target_pairs={{0,24},{8,16},{16,8},{24,0},{1,25},{9,17},{17,9},{25,1},{2,26},{10... | collective-permute-start | bytes 196616 | tf_op jit(solution)/shard_map/ppermute | solution.py:731
  54.7 4.3 %collective-permute-start.18 = (bf16[256,128]{1,0:T(8,128)(2,1)S(1)}, bf16[256,128]{1,0:T(8,128)(2,1)S(1)}, u32[]{:S(2)}, u32[]{:S(2)}) collective-permute-start(bf16[256,128]{1,0:T(8,128)(2,1)S(1)} %add_cores_time.1.refs_4_), channel_id=1, source_target_pairs={{0,2},{1,3},{2,0},{3,1},{4,6},{5,7},{6,4},{7,5},{8,10},{9,11},{10,... | collective-permute-start | bytes 196616 | tf_op jit(solution)/shard_map/ppermute | solution.py:731
  59.6 5.0 %collective-permute-start.19 = (bf16[256,128]{1,0:T(8,128)(2,1)S(1)}, bf16[256,128]{1,0:T(8,128)(2,1)S(1)}, u32[]{:S(2)}, u32[]{:S(2)}) collective-permute-start(bf16[256,128]{1,0:T(8,128)(2,1)S(1)} %get-tuple-element.142.refs_0_), channel_id=1, source_target_pairs={{0,2},{1,3},{2,0},{3,1},{4,6},{5,7},{6,4},{7,5},{8,10},{9,11},{10,... | collective-permute-start | bytes 196616 | tf_op jit(solution)/shard_map/ppermute | solution.py:731
  61.2 6.5 %collective-permute-start.20 = (bf16[256,128]{1,0:T(8,128)(2,1)S(1)}, bf16[256,128]{1,0:T(8,128)(2,1)S(1)}, u32[]{:S(2)}, u32[]{:S(2)}) collective-permute-start(bf16[256,128]{1,0:T(8,128)(2,1)S(1)} %get-tuple-element.143.refs_0_), channel_id=1, source_target_pairs={{0,4},{1,5},{2,6},{3,7},{4,0},{5,1},{6,2},{7,3},{8,12},{9,13},{10,... | collective-permute-start | bytes 196616 | tf_op jit(solution)/shard_map/ppermute | solution.py:731
  64.6 6.6 %collective-permute-start.21 = (bf16[256,128]{1,0:T(8,128)(2,1)S(1)}, bf16[256,128]{1,0:T(8,128)(2,1)S(1)}, u32[]{:S(2)}, u32[]{:S(2)}) collective-permute-start(bf16[256,128]{1,0:T(8,128)(2,1)S(1)} %add_space.1.refs_0_), channel_id=1, source_target_pairs={{0,4},{1,5},{2,6},{3,7},{4,0},{5,1},{6,2},{7,3},{8,12},{9,13},{10,... | collective-permute-start | bytes 196616 | tf_op jit(solution)/shard_map/ppermute | solution.py:731
  67.7 6.4 %collective-permute-start.27 = (bf16[256,128]{1,0:T(8,128)(2,1)S(1)}, bf16[256,128]{1,0:T(8,128)(2,1)S(1)}, u32[]{:S(2)}, u32[]{:S(2)}) collective-permute-start(bf16[256,128]{1,0:T(8,128)(2,1)S(1)} %add_space_time.1.refs_4_), channel_id=1, source_target_pairs={{0,24},{8,16},{16,8},{24,0},{1,25},{9,17},{17,9},{25,1},{2,26},{10... | collective-permute-start | bytes 196616 | tf_op jit(solution)/shard_map/ppermute | solution.py:731
  69.4 7.2 %collective-permute-start.26 = (bf16[256,128]{1,0:T(8,128)(2,1)S(1)}, bf16[256,128]{1,0:T(8,128)(2,1)S(1)}, u32[]{:S(2)}, u32[]{:S(2)}) collective-permute-start(bf16[256,128]{1,0:T(8,128)(2,1)S(1)} %add_space_time.1.refs_4_), channel_id=1, source_target_pairs={{0,16},{8,24},{16,0},{24,8},{1,17},{9,25},{17,1},{25,9},{2,18},{10... | collective-permute-start | bytes 196616 | tf_op jit(solution)/shard_map/ppermute | solution.py:731
  70.5 6.1 %collective-permute-start.25 = (bf16[256,128]{1,0:T(8,128)(2,1)S(1)}, bf16[256,128]{1,0:T(8,128)(2,1)S(1)}, u32[]{:S(2)}, u32[]{:S(2)}) collective-permute-start(bf16[256,128]{1,0:T(8,128)(2,1)S(1)} %add_space_time.1.refs_4_), channel_id=1, source_target_pairs={{0,8},{8,0},{16,24},{24,16},{1,9},{9,1},{17,25},{25,17},{2,10},{10... | collective-permute-start | bytes 196616 | tf_op jit(solution)/shard_map/ppermute | solution.py:731
  71.3 5.3 %collective-permute-start.24 = (bf16[256,128]{1,0:T(8,128)(2,1)S(1)}, bf16[256,128]{1,0:T(8,128)(2,1)S(1)}, u32[]{:S(2)}, u32[]{:S(2)}) collective-permute-start(bf16[256,128]{1,0:T(8,128)(2,1)S(1)} %add_space_last.1.refs_0_), channel_id=1, source_target_pairs={{0,24},{8,16},{16,8},{24,0},{1,25},{9,17},{17,9},{25,1},{2,26},{10... | collective-permute-start | bytes 196616 | tf_op jit(solution)/shard_map/ppermute | solution.py:731
  (5 other events, 15.7 us)

commit v10 on v7

--- a/solution.py
+++ b/solution.py
@@ -646,19 +646,16 @@
         ref[...] = add_rounded(refs[2 * index], refs[2 * index + 1])
 
 
-def both_kernel(space_ref, space_other_ref, time_ref, total_ref):
-    rows = space_ref.shape[0]
-    total_ref[:rows] = add_rounded(space_ref, space_other_ref)
-    total_ref[rows:] = time_ref[...]
-
-
 def join_kernel(place_ref, *refs):
     *part_refs, joined_ref = refs
-    for distance, ref in enumerate(part_refs):
-        rows = ref.shape[0]
-        joined_ref[pl.ds(pl.multiple_of((place_ref[0] ^ distance) * rows, GROUP_ROWS), rows)] = ref[
-            ...
-        ]
+    count_in = len(part_refs) // 2
+    rows = part_refs[0].shape[0]
+    for layer in range(2):
+        for distance in range(count_in):
+            start = (2 * (place_ref[0] ^ distance) + layer) * rows
+            joined_ref[pl.ds(pl.multiple_of(start, GROUP_ROWS), rows)] = part_refs[
+                layer * count_in + distance
+            ][...]
 
 
 def grads_kernel(time_count, own, place_ref, half_ref, *refs):
@@ -879,6 +876,16 @@
         return total
 
     space_other = exchange(space_sent, "space", 1)
+    dact, to_near, to_far = call(
+        dact_kernel,
+        "space_dact",
+        [place],
+        [dquery, dkv, project],
+        [(*own, F32), (frame_count, rim, features), (frame_count, rim, features)],
+        [(frame_count, extended, features)],
+        matmuls=3,
+    )
+    rides[0], to_near, to_far = lax.optimization_barrier((rides[0], to_near, to_far))
     time_kept, time_sent = call(
         cores_kernel,
         "add_tm_time",
@@ -898,7 +905,10 @@
         [(chunk // 2, LANES)] * time_count,
         [(grad_rows // 2, LANES)],
     )
+    to_near, to_far, *space_pieces = lax.optimization_barrier((to_near, to_far, *space_pieces))
     space_pieces = over_tm(space_pieces)
+    from_far = swap_far(to_far, "space")
+    from_near = exchange(to_near, "space", 1)
     time_piece = add_pair("add_cores_time", time_kept, time_other)
     steps = [2 << bit for bit in range((space_count - 1).bit_length())]
     time_other = exchange(time_piece, "space", steps[0])
@@ -911,36 +921,17 @@
         [(time_count, chunk // 2, LANES)],
     )
 
-    space_piece, dquery = lax.optimization_barrier((space_piece, dquery))
-    dact, to_near, to_far = call(
-        dact_kernel,
-        "space_dact",
-        [place],
-        [dquery, dkv, project],
-        [(*own, F32), (frame_count, rim, features), (frame_count, rim, features)],
-        [(frame_count, extended, features)],
-        matmuls=3,
-    )
+    sent_piece = space_piece
     for step, time_step in zip(steps, steps[1:]):
-        space_other = exchange(space_piece, "space", step)
+        space_other = exchange(sent_piece, "space", step)
         time_other = exchange(time_piece, "space", time_step)
-        space_other, to_near, to_far = lax.optimization_barrier((space_other, to_near, to_far))
-        space_piece = add_pair("add_space", space_piece, space_other)
-        space_piece, time_other = lax.optimization_barrier((space_piece, time_other))
+        sent_piece = add_pair("add_space", space_piece, space_other)
+        space_piece, time_other = lax.optimization_barrier((sent_piece, time_other))
         time_piece = add_pair("add_space_time", time_piece, time_other)
-    space_other = exchange(space_piece, "space", steps[-1])
-    time_piece, to_near, to_far = lax.optimization_barrier((time_piece, to_near, to_far))
-    from_far = swap_far(to_far, "space")
-    from_near = exchange(to_near, "space", 1)
-    (piece,) = call(
-        both_kernel,
-        "add_space_last",
-        [],
-        [space_piece, space_other, time_piece],
-        [(chunk, LANES)],
-        matmuls=64,
-    )
-    joined = over_tm([piece] * time_count)
+    space_other = exchange(sent_piece, "space", steps[-1])
+    time_joined = over_tm([time_piece] * time_count)
+    space_piece = add_pair("add_space_last", space_piece, space_other)
+    joined = over_tm([space_piece] * time_count) + time_joined
 
     field_grad, mixed_field = call(
         field_kernel,

time: 81.2 us -> 81.6 us (level)
  starting transfers between devices: 28.3 us -> 33.7 us
  waiting for transfers between devices: 22.7 us -> 17.7 us
    ppermute x24 -> x27, starting transfers between devices: 27 us -> 32.3 us  [exchange(): lax.ppermute(cells, axis, [(i, i ^ distance) for i in range(lax.axis_size...]
    ppermute x24 -> x27, waiting for transfers between devices: 22.7 us -> 17.7 us  [exchange(): lax.ppermute(cells, axis, [(i, i ^ distance) for i in range(lax.axis_size...]
  transfers between devices with their start and end apart: 26 -> 29, of which waited for: 13 -> 12; matrix products, arithmetic and copies ran while one was open for 0% -> 0% of each run, Pallas kernels for 21% -> 21%
where the time goes in v10:
time: 81.6 us; the launch traced here: 81.4 us
  starting transfers between devices  33.7 us (41%)
  Pallas kernels  28.9 us (35%)
  waiting for transfers between devices  17.7 us (22%)
  between operations  0.98 us (1%)
    ppermute x27, starting transfers between devices, exchange(): lax.ppermute(cells, axis, [(i, i ^ distance) for i in range(lax.axis_size...  32.3 us
    pallas_call x17, Pallas kernels, call(): pl.pallas_call(body, in_specs=[smem_spec] * len(scalars) + [vmem_spec] *...  28.9 us
    ppermute x27, waiting for transfers between devices, exchange(): lax.ppermute(cells, axis, [(i, i ^ distance) for i in range(lax.axis_size...  17.7 us
  transfers between devices with their start and end apart: 29, of which 12 were waited for; matrix products, arithmetic and copies ran while one was open for 0% of the time, Pallas kernels for 21%

profile of v10, /device:TPU:0, one launch (start us, length us, event | category | flops | bytes accessed | tf_op | source)
XLA Modules:
  0.0 81.4 jit_solution(2995777499811767723)
XLA Ops:
  2.5 3.1 %prepare.1 = (bf16[2,256,256]{2,1,0:T(8,128)(2,1)S(1)}, bf16[2,256,768]{2,1,0:T(8,128)(2,1)S(1)}, bf16[2,768,256]{2,1,0:T(8,128)(2,1)S(1)}, bf16[2,256,256]{2,1,...) custom-call(s32[2]{0:T(128)S(1)} %pad_add_fusion.place_ref.refs_0_.r, ...), custom_call_target="tpu_custom_call" | custom-call | flops 3221225472 | bytes 12582912 | tf_op jit(solution)/shard_map/prepare/pallas_call | solution.py:751
  5.7 5.6 %space_forward.1 = (bf16[2,768,256]{2,1,0:T(8,128)(2,1)S(1)}, bf16[2,768,512]{2,1,0:T(8,128)(2,1)S(1)}, bf16[2,6,256,128]{3,2,1,0:T(8,128)(2,1)S(1)}, bf16[2,6,2...) custom-call(s32[2,2,4]{2,1,0:T(2,128)} %refs_0_.1, ...), custom_call_target="tpu_custom_call", output_to_operand_aliasing={{0}: (9, {}), {1}: (10, {}), {2}: (11, {}), {3}: (12, {})} | custom-call | flops 10737418240 | bytes 41943040 | tf_op jit(solution)/shard_map/space_forward/pallas_call | solution.py:751
  11.3 2.9 %collective-permute-start.2 = (bf16[2,64,512]{2,1,0:T(8,128)(2,1)S(1)}, bf16[2,64,512]{2,1,0:T(8,128)(2,1)S(1)}, u32[]{:S(2)}, u32[]{:S(2)}) collective-permute-start(bf16[2,64,512]{2,1,0:T(8,128)(2,1)S(1)} %get-tuple-element.96), channel_id=1, source_target_pairs={{0,8},{8,0},{16,24},{24,16},{1,9},{9,1},{17,25},{25,17},{2,10},{10... | collective-permute-start | bytes 393224 | tf_op jit(solution)/shard_map/ppermute | solution.py:719
  14.3 1.5 %collective-permute-start.3 = (bf16[2,64,512]{2,1,0:T(8,128)(2,1)S(1)}, bf16[2,64,512]{2,1,0:T(8,128)(2,1)S(1)}, u32[]{:S(2)}, u32[]{:S(2)}) collective-permute-start(bf16[2,64,512]{2,1,0:T(8,128)(2,1)S(1)} %get-tuple-element.97), channel_id=1, source_target_pairs={{0,16},{8,24},{16,0},{24,8},{1,17},{9,25},{17,1},{25,9},{2,18},{10... | collective-permute-start | bytes 393224 | tf_op jit(solution)/shard_map/ppermute | solution.py:719
  15.8 1.4 %collective-permute-done.2.refs_1_ = bf16[2,64,512]{2,1,0:T(8,128)(2,1)S(1)} collective-permute-done((bf16[2,64,512]{2,1,0:T(8,128)(2,1)S(1)}, bf16[2,64,512]{2,1,0:T(8,128)(2,1)S(1)}, u32[]{:S(2)}, u32[]{:S(2)}) %collective-permute-start.2) | collective-permute-done | bytes 131104 | tf_op jit(solution)/shard_map/ppermute | solution.py:719
  17.2 2.0 %collective-permute-done.3.refs_2_ = bf16[2,64,512]{2,1,0:T(8,128)(2,1)S(1)} collective-permute-done((bf16[2,64,512]{2,1,0:T(8,128)(2,1)S(1)}, bf16[2,64,512]{2,1,0:T(8,128)(2,1)S(1)}, u32[]{:S(2)}, u32[]{:S(2)}) %collective-permute-start.3) | collective-permute-done | bytes 131104 | tf_op jit(solution)/shard_map/ppermute | solution.py:719
  19.2 3.8 %collective-permute-done.4.refs_3_ = bf16[2,64,512]{2,1,0:T(8,128)(2,1)S(1)} collective-permute-done((bf16[2,64,512]{2,1,0:T(8,128)(2,1)S(1)}, bf16[2,64,512]{2,1,0:T(8,128)(2,1)S(1)}, u32[]{:S(2)}, u32[]{:S(2)}) %collective-permute-start.4) | collective-permute-done | bytes 131104 | tf_op jit(solution)/shard_map/ppermute | solution.py:719
  23.0 3.6 %time_pair.1 = (bf16[2,64,256]{2,1,0:T(8,128)(2,1)S(1)}, bf16[2,64,256]{2,1,0:T(8,128)(2,1)S(1)}, bf16[2,64,256]{2,1,0:T(8,128)(2,1)S(1)}, bf16[2,64,256]{2,1,0:...) custom-call(bf16[2,64,512]{2,1,0:T(8,128)(2,1)S(1)} %get-tuple-eleme, ...), custom_call_target="tpu_custom_call" | custom-call | flops 9663676416 | bytes 37748736 | tf_op jit(solution)/shard_map/time_pair/pallas_call | solution.py:751
  26.8 3.3 %collective-permute-start.7 = (bf16[2,64,256]{2,1,0:T(8,128)(2,1)S(1)}, bf16[2,64,256]{2,1,0:T(8,128)(2,1)S(1)}, u32[]{:S(2)}, u32[]{:S(2)}) collective-permute-start(bf16[2,64,256]{2,1,0:T(8,128)(2,1)S(1)} %get-tuple-element.109), channel_id=1, source_target_pairs={{0,24},{8,16},{16,8},{24,0},{1,25},{9,17},{17,9},{25,1},{2,26},{10... | collective-permute-start | bytes 196616 | tf_op jit(solution)/shard_map/ppermute | solution.py:719
  31.9 2.9 %collective-permute-start.11 = (bf16[768,128]{1,0:T(8,128)(2,1)S(1)}, bf16[768,128]{1,0:T(8,128)(2,1)S(1)}, u32[]{:S(2)}, u32[]{:S(2)}) collective-permute-start(bf16[768,128]{1,0:T(8,128)(2,1)S(1)} %get-tuple-element.131), channel_id=1, source_target_pairs={{0,24},{8,16},{16,8},{24,0},{1,25},{9,17},{17,9},{25,1},{2,26},{10... | collective-permute-start | bytes 589832 | tf_op jit(solution)/shard_map/ppermute | solution.py:719
  34.8 6.5 %space_backward.1 = (bf16[2,256,256]{2,1,0:T(8,128)(2,1)S(1)}, bf16[2,256,256]{2,1,0:T(8,128)(2,1)S(1)}, bf16[2,768,512]{2,1,0:T(8,128)(2,1)S(1)}, bf16[1024,128]{1,0:T(8,128)(2,1)S(1)}, bf16[1024,128]{1,0:T(8,128)(2,1)S(1)}) custom-call(s32[2,2,4]{2,1,0:T(2,128)} %refs_0_.1, s32[2]{0:T(128)S(1)} %pad_add_fusion.place_ref.refs_0_.refs_1_, ...), custom_call_target="tpu_custom_call" | custom-call | flops 11811160064 | bytes 46137344 | tf_op jit(solution)/shard_map/space_backward/pallas_call | solution.py:751
  41.3 1.3 %space_dact.1 = (f32[2,256,256]{2,1,0:T(8,128)S(1)}, bf16[2,256,256]{2,1,0:T(8,128)(2,1)S(1)}, bf16[2,256,256]{2,1,0:T(8,128)(2,1)S(1)}) custom-call(s32[2]{0:T(128)S(1)} %pad_add_fusion.place_ref.refs_0_.refs_1_, bf16[2,256,256]{2,1,0:T(8,128)(2,1)S(1)} %get-tuple-element.118.dquery_ref, bf16[2,768,512]{2,1,0:T(8,128)(2,1)S(1)} %get-tuple-element.119.dkv_ref, ...), custom_call_target="tpu_custom_call" | custom-call | flops 805306368 | bytes 3145728 | tf_op jit(solution)/shard_map/space_dact/pallas_call | solution.py:751
  46.9 1.5 %collective-permute-start.16 = (bf16[256,128]{1,0:T(8,128)(2,1)S(1)}, bf16[256,128]{1,0:T(8,128)(2,1)S(1)}, u32[]{:S(2)}, u32[]{:S(2)}) collective-permute-start(bf16[256,128]{1,0:T(8,128)(2,1)S(1)} %get-tuple-element.145), channel_id=1, source_target_pairs={{0,24},{8,16},{16,8},{24,0},{1,25},{9,17},{17,9},{25,1},{2,26},{10... | collective-permute-start | bytes 196616 | tf_op jit(solution)/shard_map/ppermute | solution.py:719
  48.5 4.2 %collective-permute-start.18 = (bf16[256,128]{1,0:T(8,128)(2,1)S(1)}, bf16[256,128]{1,0:T(8,128)(2,1)S(1)}, u32[]{:S(2)}, u32[]{:S(2)}) collective-permute-start(bf16[256,128]{1,0:T(8,128)(2,1)S(1)} %add_cores_time.1.refs_4_), channel_id=1, source_target_pairs={{0,2},{1,3},{2,0},{3,1},{4,6},{5,7},{6,4},{7,5},{8,10},{9,11},{10,... | collective-permute-start | bytes 196616 | tf_op jit(solution)/shard_map/ppermute | solution.py:719
  53.4 1.5 %collective-permute-done.18.refs_5_ = bf16[256,128]{1,0:T(8,128)(2,1)S(1)} collective-permute-done((bf16[256,128]{1,0:T(8,128)(2,1)S(1)}, bf16[256,128]{1,0:T(8,128)(2,1)S(1)}, u32[]{:S(2)}, u32[]{:S(2)}) %collective-permute-start.18) | collective-permute-done | bytes 65568 | tf_op jit(solution)/shard_map/ppermute | solution.py:719
  55.6 2.1 %collective-permute-start.19 = (bf16[256,128]{1,0:T(8,128)(2,1)S(1)}, bf16[256,128]{1,0:T(8,128)(2,1)S(1)}, u32[]{:S(2)}, u32[]{:S(2)}) collective-permute-start(bf16[256,128]{1,0:T(8,128)(2,1)S(1)} %get-tuple-element.148.refs_0_), channel_id=1, source_target_pairs={{0,2},{1,3},{2,0},{3,1},{4,6},{5,7},{6,4},{7,5},{8,10},{9,11},{10,... | collective-permute-start | bytes 196616 | tf_op jit(solution)/shard_map/ppermute | solution.py:719
  57.7 1.6 %collective-permute-start.20 = (bf16[256,128]{1,0:T(8,128)(2,1)S(1)}, bf16[256,128]{1,0:T(8,128)(2,1)S(1)}, u32[]{:S(2)}, u32[]{:S(2)}) collective-permute-start(bf16[256,128]{1,0:T(8,128)(2,1)S(1)} %get-tuple-element.149.refs_0_), channel_id=1, source_target_pairs={{0,4},{1,5},{2,6},{3,7},{4,0},{5,1},{6,2},{7,3},{8,12},{9,13},{10,... | collective-permute-start | bytes 196616 | tf_op jit(solution)/shard_map/ppermute | solution.py:719
  59.2 4.7 %collective-permute-done.19.refs_1_ = bf16[256,128]{1,0:T(8,128)(2,1)S(1)} collective-permute-done((bf16[256,128]{1,0:T(8,128)(2,1)S(1)}, bf16[256,128]{1,0:T(8,128)(2,1)S(1)}, u32[]{:S(2)}, u32[]{:S(2)}) %collective-permute-start.19) | collective-permute-done | bytes 65568 | tf_op jit(solution)/shard_map/ppermute | solution.py:719
  64.9 1.7 %collective-permute-start.27 = (bf16[256,128]{1,0:T(8,128)(2,1)S(1)}, bf16[256,128]{1,0:T(8,128)(2,1)S(1)}, u32[]{:S(2)}, u32[]{:S(2)}) collective-permute-start(bf16[256,128]{1,0:T(8,128)(2,1)S(1)} %add_space_time.1.refs_4_), channel_id=1, source_target_pairs={{0,24},{8,16},{16,8},{24,0},{1,25},{9,17},{17,9},{25,1},{2,26},{10... | collective-permute-start | bytes 196616 | tf_op jit(solution)/shard_map/ppermute | solution.py:719
  67.5 1.6 %collective-permute-done.21.refs_1_ = bf16[256,128]{1,0:T(8,128)(2,1)S(1)} collective-permute-done((bf16[256,128]{1,0:T(8,128)(2,1)S(1)}, bf16[256,128]{1,0:T(8,128)(2,1)S(1)}, u32[]{:S(2)}, u32[]{:S(2)}) %collective-permute-start.21) | collective-permute-done | bytes 65568 | tf_op jit(solution)/shard_map/ppermute | solution.py:719
  70.4 1.8 %collective-permute-start.24 = (bf16[256,128]{1,0:T(8,128)(2,1)S(1)}, bf16[256,128]{1,0:T(8,128)(2,1)S(1)}, u32[]{:S(2)}, u32[]{:S(2)}) collective-permute-start(bf16[256,128]{1,0:T(8,128)(2,1)S(1)} %add_space_last.1.refs_0_), channel_id=1, source_target_pairs={{0,24},{8,16},{16,8},{24,0},{1,25},{9,17},{17,9},{25,1},{2,26},{10... | collective-permute-start | bytes 196616 | tf_op jit(solution)/shard_map/ppermute | solution.py:719
  74.0 1.8 %field_grad.1 = (bf16[2,256,256]{2,1,0:T(8,128)(2,1)}, bf16[2,256,256]{2,1,0:T(8,128)(2,1)}) custom-call(s32[2]{0:T(128)S(1)} %pad_add_fusion.place_ref.refs_0_.refs_1_, bf16[2,256,256]{2,1,0:T(8,128)(2,1)S(1)} %get-tuple-element.85.wave_ref, bf16[2,256,256]{2,1,0:T(8,128)(2,1)S(1)} %get-tuple-element.117.mixed_grad_ref, ...), custom_call_target="tpu_custom_call" | custom-call | flops 805306368 | bytes 3145728 | tf_op jit(solution)/shard_map/field_grad/pallas_call | solution.py:751
  77.7 1.6 %weight_grads.2 = (f32[2,256,768]{2,1,0:T(8,128)}, f32[2,256,256]{2,1,0:T(8,128)}) custom-call(s32[2]{0:T(128)S(1)} %pad_add_fusion.place_ref.refs_0_.refs_1_, bf16[2048,128]{1,0:T(8,128)(2,1)S(1)} %join_tm.1.refs_1_), custom_call_target="tpu_custom_call" | custom-call | flops 268435456 | bytes 1048576 | tf_op jit(solution)/shard_map/weight_grads/pallas_call | solution.py:751
  79.6 1.6 %weight_grads.3 = (f32[2,256,768]{2,1,0:T(8,128)}, f32[2,256,256]{2,1,0:T(8,128)}) custom-call(s32[2]{0:T(128)S(1)} %pad_add_fusion.place_ref.refs_0_.refs_1_, bf16[2048,128]{1,0:T(8,128)(2,1)S(1)} %collective-permute-done.28.refs_1_, f32[2,256,768]{2,1,0:T(8,128)} %get-tuple-element.162.refs_2_, ...), custom_call_target="tpu_custom_call", output_to_operand_aliasing={{0}: (2, {}), {1}: (3, {})} | custom-call | flops 268435456 | bytes 1048576 | tf_op jit(solution)/shard_map/weight_grads/pallas_call | solution.py:751
  (52 shorter events, 16.5 us)
Async XLA Ops:
  1.1 4.5 %collective-permute-start.1 = (bf16[2,256,256]{2,1,0:T(8,128)(2,1)}, bf16[2,256,256]{2,1,0:T(8,128)(2,1)S(1)}, u32[]{:S(2)}, u32[]{:S(2)}) collective-permute-start(bf16[2,256,256]{2,1,0:T(8,128)(2,1)} %wave_hbm.1), channel_id=1, source_target_pairs={{1,2},{3,4},{5,6},{2,1},{4,3},{6,5},{9,10},{11,12},{13,14},{10,9},... | collective-permute-start | bytes 786440 | tf_op jit(solution)/shard_map/ppermute | solution.py:715
  11.3 5.9 %collective-permute-start.2 = (bf16[2,64,512]{2,1,0:T(8,128)(2,1)S(1)}, bf16[2,64,512]{2,1,0:T(8,128)(2,1)S(1)}, u32[]{:S(2)}, u32[]{:S(2)}) collective-permute-start(bf16[2,64,512]{2,1,0:T(8,128)(2,1)S(1)} %get-tuple-element.96), channel_id=1, source_target_pairs={{0,8},{8,0},{16,24},{24,16},{1,9},{9,1},{17,25},{25,17},{2,10},{10... | collective-permute-start | bytes 393224 | tf_op jit(solution)/shard_map/ppermute | solution.py:719
  14.3 5.0 %collective-permute-start.3 = (bf16[2,64,512]{2,1,0:T(8,128)(2,1)S(1)}, bf16[2,64,512]{2,1,0:T(8,128)(2,1)S(1)}, u32[]{:S(2)}, u32[]{:S(2)}) collective-permute-start(bf16[2,64,512]{2,1,0:T(8,128)(2,1)S(1)} %get-tuple-element.97), channel_id=1, source_target_pairs={{0,16},{8,24},{16,0},{24,8},{1,17},{9,25},{17,1},{25,9},{2,18},{10... | collective-permute-start | bytes 393224 | tf_op jit(solution)/shard_map/ppermute | solution.py:719
  15.8 7.2 %collective-permute-start.4 = (bf16[2,64,512]{2,1,0:T(8,128)(2,1)S(1)}, bf16[2,64,512]{2,1,0:T(8,128)(2,1)S(1)}, u32[]{:S(2)}, u32[]{:S(2)}) collective-permute-start(bf16[2,64,512]{2,1,0:T(8,128)(2,1)S(1)} %get-tuple-element.98), channel_id=1, source_target_pairs={{0,24},{8,16},{16,8},{24,0},{1,25},{9,17},{17,9},{25,1},{2,26},{10... | collective-permute-start | bytes 393224 | tf_op jit(solution)/shard_map/ppermute | solution.py:719
  26.6 5.2 %collective-permute-start.5 = (bf16[2,64,256]{2,1,0:T(8,128)(2,1)S(1)}, bf16[2,64,256]{2,1,0:T(8,128)(2,1)S(1)}, u32[]{:S(2)}, u32[]{:S(2)}) collective-permute-start(bf16[2,64,256]{2,1,0:T(8,128)(2,1)S(1)} %get-tuple-element.100), channel_id=1, source_target_pairs={{0,8},{8,0},{16,24},{24,16},{1,9},{9,1},{17,25},{25,17},{2,10},{10... | collective-permute-start | bytes 196616 | tf_op jit(solution)/shard_map/ppermute | solution.py:719
  26.8 8.0 %collective-permute-start.6 = (bf16[2,64,256]{2,1,0:T(8,128)(2,1)S(1)}, bf16[2,64,256]{2,1,0:T(8,128)(2,1)S(1)}, u32[]{:S(2)}, u32[]{:S(2)}) collective-permute-start(bf16[2,64,256]{2,1,0:T(8,128)(2,1)S(1)} %get-tuple-element.108), channel_id=1, source_target_pairs={{0,16},{8,24},{16,0},{24,8},{1,17},{9,25},{17,1},{25,9},{2,18},{10... | collective-permute-start | bytes 196616 | tf_op jit(solution)/shard_map/ppermute | solution.py:719
  26.8 8.0 %collective-permute-start.7 = (bf16[2,64,256]{2,1,0:T(8,128)(2,1)S(1)}, bf16[2,64,256]{2,1,0:T(8,128)(2,1)S(1)}, u32[]{:S(2)}, u32[]{:S(2)}) collective-permute-start(bf16[2,64,256]{2,1,0:T(8,128)(2,1)S(1)} %get-tuple-element.109), channel_id=1, source_target_pairs={{0,24},{8,16},{16,8},{24,0},{1,25},{9,17},{17,9},{25,1},{2,26},{10... | collective-permute-start | bytes 196616 | tf_op jit(solution)/shard_map/ppermute | solution.py:719
  31.2 11.5 %collective-permute-start.9 = (bf16[768,128]{1,0:T(8,128)(2,1)S(1)}, bf16[768,128]{1,0:T(8,128)(2,1)S(1)}, u32[]{:S(2)}, u32[]{:S(2)}) collective-permute-start(bf16[768,128]{1,0:T(8,128)(2,1)S(1)} %get-tuple-element.129), channel_id=1, source_target_pairs={{0,8},{8,0},{16,24},{24,16},{1,9},{9,1},{17,25},{25,17},{2,10},{10... | collective-permute-start | bytes 589832 | tf_op jit(solution)/shard_map/ppermute | solution.py:719
  31.4 11.5 %collective-permute-start.10 = (bf16[768,128]{1,0:T(8,128)(2,1)S(1)}, bf16[768,128]{1,0:T(8,128)(2,1)S(1)}, u32[]{:S(2)}, u32[]{:S(2)}) collective-permute-start(bf16[768,128]{1,0:T(8,128)(2,1)S(1)} %get-tuple-element.130), channel_id=1, source_target_pairs={{0,16},{8,24},{16,0},{24,8},{1,17},{9,25},{17,1},{25,9},{2,18},{10... | collective-permute-start | bytes 589832 | tf_op jit(solution)/shard_map/ppermute | solution.py:719
  31.9 11.1 %collective-permute-start.11 = (bf16[768,128]{1,0:T(8,128)(2,1)S(1)}, bf16[768,128]{1,0:T(8,128)(2,1)S(1)}, u32[]{:S(2)}, u32[]{:S(2)}) collective-permute-start(bf16[768,128]{1,0:T(8,128)(2,1)S(1)} %get-tuple-element.131), channel_id=1, source_target_pairs={{0,24},{8,16},{16,8},{24,0},{1,25},{9,17},{17,9},{25,1},{2,26},{10... | collective-permute-start | bytes 589832 | tf_op jit(solution)/shard_map/ppermute | solution.py:719
  43.7 4.8 %collective-permute-start.17 = (bf16[256,128]{1,0:T(8,128)(2,1)S(1)}, bf16[256,128]{1,0:T(8,128)(2,1)S(1)}, u32[]{:S(2)}, u32[]{:S(2)}) collective-permute-start(bf16[256,128]{1,0:T(8,128)(2,1)S(1)} %get-tuple-element.147), channel_id=1, source_target_pairs={{0,1},{1,0},{2,3},{3,2},{4,5},{5,4},{6,7},{7,6},{8,9},{9,8},{10,11... | collective-permute-start | bytes 196616 | tf_op jit(solution)/shard_map/ppermute | solution.py:719
  44.9 7.8 %collective-permute-start.14 = (bf16[256,128]{1,0:T(8,128)(2,1)S(1)}, bf16[256,128]{1,0:T(8,128)(2,1)S(1)}, u32[]{:S(2)}, u32[]{:S(2)}) collective-permute-start(bf16[256,128]{1,0:T(8,128)(2,1)S(1)} %get-tuple-element.143), channel_id=1, source_target_pairs={{0,8},{8,0},{16,24},{24,16},{1,9},{9,1},{17,25},{25,17},{2,10},{10... | collective-permute-start | bytes 196616 | tf_op jit(solution)/shard_map/ppermute | solution.py:719
  45.8 7.6 %collective-permute-start.15 = (bf16[256,128]{1,0:T(8,128)(2,1)S(1)}, bf16[256,128]{1,0:T(8,128)(2,1)S(1)}, u32[]{:S(2)}, u32[]{:S(2)}) collective-permute-start(bf16[256,128]{1,0:T(8,128)(2,1)S(1)} %get-tuple-element.144), channel_id=1, source_target_pairs={{0,16},{8,24},{16,0},{24,8},{1,17},{9,25},{17,1},{25,9},{2,18},{10... | collective-permute-start | bytes 196616 | tf_op jit(solution)/shard_map/ppermute | solution.py:719
  46.9 6.5 %collective-permute-start.16 = (bf16[256,128]{1,0:T(8,128)(2,1)S(1)}, bf16[256,128]{1,0:T(8,128)(2,1)S(1)}, u32[]{:S(2)}, u32[]{:S(2)}) collective-permute-start(bf16[256,128]{1,0:T(8,128)(2,1)S(1)} %get-tuple-element.145), channel_id=1, source_target_pairs={{0,24},{8,16},{16,8},{24,0},{1,25},{9,17},{17,9},{25,1},{2,26},{10... | collective-permute-start | bytes 196616 | tf_op jit(solution)/shard_map/ppermute | solution.py:719
  48.5 6.5 %collective-permute-start.18 = (bf16[256,128]{1,0:T(8,128)(2,1)S(1)}, bf16[256,128]{1,0:T(8,128)(2,1)S(1)}, u32[]{:S(2)}, u32[]{:S(2)}) collective-permute-start(bf16[256,128]{1,0:T(8,128)(2,1)S(1)} %add_cores_time.1.refs_4_), channel_id=1, source_target_pairs={{0,2},{1,3},{2,0},{3,1},{4,6},{5,7},{6,4},{7,5},{8,10},{9,11},{10,... | collective-permute-start | bytes 196616 | tf_op jit(solution)/shard_map/ppermute | solution.py:719
  52.7 19.5 %collective-permute-start.12 = (bf16[2,256,256]{2,1,0:T(8,128)(2,1)S(1)}, bf16[2,256,256]{2,1,0:T(8,128)(2,1)S(1)}, u32[]{:S(2)}, u32[]{:S(2)}) collective-permute-start(bf16[2,256,256]{2,1,0:T(8,128)(2,1)S(1)} %get-tuple-element.138), channel_id=1, source_target_pairs={{0,1},{1,0},{2,3},{3,2},{4,5},{5,4},{6,7},{7,6},{8,9},{9,8},{10,11... | collective-permute-start | bytes 786440 | tf_op jit(solution)/shard_map/ppermute | solution.py:719
  52.7 20.0 %collective-permute-start.13 = (bf16[2,256,256]{2,1,0:T(8,128)(2,1)S(1)}, bf16[2,256,256]{2,1,0:T(8,128)(2,1)S(1)}, u32[]{:S(2)}, u32[]{:S(2)}) collective-permute-start(bf16[2,256,256]{2,1,0:T(8,128)(2,1)S(1)} %get-tuple-element.139), channel_id=1, source_target_pairs={{1,2},{3,4},{5,6},{2,1},{4,3},{6,5},{9,10},{11,12},{13,14},{10,9},... | collective-permute-start | bytes 786440 | tf_op jit(solution)/shard_map/ppermute | solution.py:715
  55.6 8.3 %collective-permute-start.19 = (bf16[256,128]{1,0:T(8,128)(2,1)S(1)}, bf16[256,128]{1,0:T(8,128)(2,1)S(1)}, u32[]{:S(2)}, u32[]{:S(2)}) collective-permute-start(bf16[256,128]{1,0:T(8,128)(2,1)S(1)} %get-tuple-element.148.refs_0_), channel_id=1, source_target_pairs={{0,2},{1,3},{2,0},{3,1},{4,6},{5,7},{6,4},{7,5},{8,10},{9,11},{10,... | collective-permute-start | bytes 196616 | tf_op jit(solution)/shard_map/ppermute | solution.py:719
  57.7 7.2 %collective-permute-start.20 = (bf16[256,128]{1,0:T(8,128)(2,1)S(1)}, bf16[256,128]{1,0:T(8,128)(2,1)S(1)}, u32[]{:S(2)}, u32[]{:S(2)}) collective-permute-start(bf16[256,128]{1,0:T(8,128)(2,1)S(1)} %get-tuple-element.149.refs_0_), channel_id=1, source_target_pairs={{0,4},{1,5},{2,6},{3,7},{4,0},{5,1},{6,2},{7,3},{8,12},{9,13},{10,... | collective-permute-start | bytes 196616 | tf_op jit(solution)/shard_map/ppermute | solution.py:719
  63.9 5.2 %collective-permute-start.21 = (bf16[256,128]{1,0:T(8,128)(2,1)S(1)}, bf16[256,128]{1,0:T(8,128)(2,1)S(1)}, u32[]{:S(2)}, u32[]{:S(2)}) collective-permute-start(bf16[256,128]{1,0:T(8,128)(2,1)S(1)} %add_space.1.refs_0_), channel_id=1, source_target_pairs={{0,4},{1,5},{2,6},{3,7},{4,0},{5,1},{6,2},{7,3},{8,12},{9,13},{10,... | collective-permute-start | bytes 196616 | tf_op jit(solution)/shard_map/ppermute | solution.py:719
  64.9 5.6 %collective-permute-start.27 = (bf16[256,128]{1,0:T(8,128)(2,1)S(1)}, bf16[256,128]{1,0:T(8,128)(2,1)S(1)}, u32[]{:S(2)}, u32[]{:S(2)}) collective-permute-start(bf16[256,128]{1,0:T(8,128)(2,1)S(1)} %add_space_time.1.refs_4_), channel_id=1, source_target_pairs={{0,24},{8,16},{16,8},{24,0},{1,25},{9,17},{17,9},{25,1},{2,26},{10... | collective-permute-start | bytes 196616 | tf_op jit(solution)/shard_map/ppermute | solution.py:719
  66.5 9.2 %collective-permute-start.26 = (bf16[256,128]{1,0:T(8,128)(2,1)S(1)}, bf16[256,128]{1,0:T(8,128)(2,1)S(1)}, u32[]{:S(2)}, u32[]{:S(2)}) collective-permute-start(bf16[256,128]{1,0:T(8,128)(2,1)S(1)} %add_space_time.1.refs_4_), channel_id=1, source_target_pairs={{0,16},{8,24},{16,0},{24,8},{1,17},{9,25},{17,1},{25,9},{2,18},{10... | collective-permute-start | bytes 196616 | tf_op jit(solution)/shard_map/ppermute | solution.py:719
  69.1 6.6 %collective-permute-start.25 = (bf16[256,128]{1,0:T(8,128)(2,1)S(1)}, bf16[256,128]{1,0:T(8,128)(2,1)S(1)}, u32[]{:S(2)}, u32[]{:S(2)}) collective-permute-start(bf16[256,128]{1,0:T(8,128)(2,1)S(1)} %add_space_time.1.refs_4_), channel_id=1, source_target_pairs={{0,8},{8,0},{16,24},{24,16},{1,9},{9,1},{17,25},{25,17},{2,10},{10... | collective-permute-start | bytes 196616 | tf_op jit(solution)/shard_map/ppermute | solution.py:719
  70.4 5.3 %collective-permute-start.24 = (bf16[256,128]{1,0:T(8,128)(2,1)S(1)}, bf16[256,128]{1,0:T(8,128)(2,1)S(1)}, u32[]{:S(2)}, u32[]{:S(2)}) collective-permute-start(bf16[256,128]{1,0:T(8,128)(2,1)S(1)} %add_space_last.1.refs_0_), channel_id=1, source_target_pairs={{0,24},{8,16},{16,8},{24,0},{1,25},{9,17},{17,9},{25,1},{2,26},{10... | collective-permute-start | bytes 196616 | tf_op jit(solution)/shard_map/ppermute | solution.py:719
  (5 other events, 14.0 us)

commit v11 on v7

--- a/solution.py
+++ b/solution.py
@@ -422,9 +422,10 @@
                     ref[row : row + GROUP_ROWS] = mixed_ref[
                         start : start + GROUP_ROWS, lane_group * LANES : (lane_group + 1) * LANES
                     ]
-        ref[:chunk] = stacked_s[
-            pl.ds(pl.multiple_of((place_ref[0] ^ part) * chunk, GROUP_ROWS), chunk)
-        ]
+        half = chunk // 2
+        for core in range(2):
+            start = pl.multiple_of((core * count_in + (place_ref[0] ^ part)) * half, GROUP_ROWS)
+            ref[core * half : (core + 1) * half] = stacked_s[pl.ds(start, half)]
 
 
 def space_backward_kernel(
@@ -666,25 +667,27 @@
     features = combine_hbm.shape[1]
     core = place_ref[1] % 2
     rows = half_ref.shape[0] // time_count // 2
-    wide_s[...] = half_ref[...].astype(F32).reshape(wide_s.shape)
+    for part in range(time_count):
+        group, inner = divmod(part * rows, features)
+        for layer in range(2):
+            wide_s[layer, inner : inner + rows, group * LANES : (group + 1) * LANES] = half_ref[
+                (2 * part + layer) * rows : (2 * part + layer + 1) * rows
+            ].astype(F32)
 
     def write(half):
         moves = []
-        for part in range(time_count):
-            for layer, row in ((0, (half * time_count + part) * rows), (1, (2 * part + half) * rows)):
-                group, inner = divmod(row, features)
-                start = group * LANES
-                target, start = (
-                    (project_hbm, start)
-                    if start < 3 * features
-                    else (combine_hbm, start - 3 * features)
-                )
-                piece = 2 * part + layer
+        for layer in range(2):
+            if half:
+                pieces = [
+                    (slice(0, features), project_hbm.at[layer, :, 2 * features :]),
+                    (slice(features, 2 * features), combine_hbm.at[layer]),
+                ]
+            else:
+                pieces = [(slice(0, 2 * features), project_hbm.at[layer, :, : 2 * features])]
+            for lanes, target in pieces:
                 moves.append(
                     pltpu.make_async_copy(
-                        wide_s.at[piece],
-                        target.at[layer, pl.ds(inner, rows), pl.ds(start, LANES)],
-                        sems.at[piece],
+                        wide_s.at[layer, :, lanes], target, sems.at[len(moves)]
                     )
                 )
         for move in moves:
@@ -773,8 +776,8 @@
 
     own = (frame_count, row_count, features)
     part = (frame_count, sent_rows, features)
+    far = swap_far(wave_field, "space")
     near = exchange(wave_field, "space", 1)
-    far = swap_far(wave_field, "space")
     place = jnp.stack([lax.axis_index("tm"), lax.axis_index("space")]).astype(jnp.int32)
     extended_shapes = [
         (frame_count, extended, features),
@@ -921,14 +924,15 @@
         [(frame_count, extended, features)],
         matmuls=3,
     )
+    sent_piece = space_piece
     for step, time_step in zip(steps, steps[1:]):
-        space_other = exchange(space_piece, "space", step)
+        space_other = exchange(sent_piece, "space", step)
         time_other = exchange(time_piece, "space", time_step)
         space_other, to_near, to_far = lax.optimization_barrier((space_other, to_near, to_far))
-        space_piece = add_pair("add_space", space_piece, space_other)
-        space_piece, time_other = lax.optimization_barrier((space_piece, time_other))
+        sent_piece = add_pair("add_space", space_piece, space_other)
+        space_piece, time_other = lax.optimization_barrier((sent_piece, time_other))
         time_piece = add_pair("add_space_time", time_piece, time_other)
-    space_other = exchange(space_piece, "space", steps[-1])
+    space_other = exchange(sent_piece, "space", steps[-1])
     time_piece, to_near, to_far = lax.optimization_barrier((time_piece, to_near, to_far))
     from_far = swap_far(to_far, "space")
     from_near = exchange(to_near, "space", 1)
@@ -967,8 +971,8 @@
             [half],
             [(2, features, 3 * features, F32), (2, features, features, F32)],
             [
-                (2 * time_count, grad_rows // time_count // 2, LANES, F32),
-                pltpu.SemaphoreType.DMA((2 * time_count,)),
+                (2, features, 2 * features, F32),
+                pltpu.SemaphoreType.DMA((4,)),
             ],
             hbm=grads,
             aliases={2: 0, 3: 1} if grads else None,

time: 81.2 us -> 79.6 us (0.980)
  waiting for transfers between devices: 22.7 us -> 19 us
  starting transfers between devices: 28.3 us -> 30.4 us
    ppermute x24, waiting for transfers between devices: 22.7 us -> 19 us  [exchange(): lax.ppermute(cells, axis, [(i, i ^ distance) for i in range(lax.axis_size...]
    ppermute x24, starting transfers between devices: 27 us -> 29.1 us  [exchange(): lax.ppermute(cells, axis, [(i, i ^ distance) for i in range(lax.axis_size...]
where the time goes in v11:
time: 79.6 us; the launch traced here: 79.4 us
  starting transfers between devices  30.4 us (38%)
  Pallas kernels  29 us (36%)
  waiting for transfers between devices  19 us (24%)
  between operations  0.96 us (1%)
    ppermute x24, starting transfers between devices, exchange(): lax.ppermute(cells, axis, [(i, i ^ distance) for i in range(lax.axis_size...  29.1 us
    pallas_call x17, Pallas kernels, call(): pl.pallas_call(body, in_specs=[smem_spec] * len(scalars) + [vmem_spec] *...  29 us
    ppermute x24, waiting for transfers between devices, exchange(): lax.ppermute(cells, axis, [(i, i ^ distance) for i in range(lax.axis_size...  19 us
  transfers between devices with their start and end apart: 26, of which 13 were waited for; matrix products, arithmetic and copies ran while one was open for 0% of the time, Pallas kernels for 21%

profile of v11, /device:TPU:0, one launch (start us, length us, event | category | flops | bytes accessed | tf_op | source)
XLA Modules:
  0.0 79.4 jit_solution(4141336207470370506)
XLA Ops:
  2.5 3.1 %prepare.1 = (bf16[2,256,256]{2,1,0:T(8,128)(2,1)S(1)}, bf16[2,256,768]{2,1,0:T(8,128)(2,1)S(1)}, bf16[2,768,256]{2,1,0:T(8,128)(2,1)S(1)}, bf16[2,256,256]{2,1,...) custom-call(s32[2]{0:T(128)S(1)} %pad_add_fusion.place_ref.refs_0_.r, ...), custom_call_target="tpu_custom_call" | custom-call | flops 3221225472 | bytes 12582912 | tf_op jit(solution)/shard_map/prepare/pallas_call | solution.py:757
  5.7 5.6 %space_forward.1 = (bf16[2,768,256]{2,1,0:T(8,128)(2,1)S(1)}, bf16[2,768,512]{2,1,0:T(8,128)(2,1)S(1)}, bf16[2,6,256,128]{3,2,1,0:T(8,128)(2,1)S(1)}, bf16[2,6,2...) custom-call(s32[2,2,4]{2,1,0:T(2,128)} %refs_0_.1, ...), custom_call_target="tpu_custom_call", output_to_operand_aliasing={{0}: (9, {}), {1}: (10, {}), {2}: (11, {}), {3}: (12, {})} | custom-call | flops 10737418240 | bytes 41943040 | tf_op jit(solution)/shard_map/space_forward/pallas_call | solution.py:757
  11.3 2.9 %collective-permute-start.2 = (bf16[2,64,512]{2,1,0:T(8,128)(2,1)S(1)}, bf16[2,64,512]{2,1,0:T(8,128)(2,1)S(1)}, u32[]{:S(2)}, u32[]{:S(2)}) collective-permute-start(bf16[2,64,512]{2,1,0:T(8,128)(2,1)S(1)} %get-tuple-element.91), channel_id=1, source_target_pairs={{0,8},{8,0},{16,24},{24,16},{1,9},{9,1},{17,25},{25,17},{2,10},{10... | collective-permute-start | bytes 393224 | tf_op jit(solution)/shard_map/ppermute | solution.py:725
  14.3 1.5 %collective-permute-start.3 = (bf16[2,64,512]{2,1,0:T(8,128)(2,1)S(1)}, bf16[2,64,512]{2,1,0:T(8,128)(2,1)S(1)}, u32[]{:S(2)}, u32[]{:S(2)}) collective-permute-start(bf16[2,64,512]{2,1,0:T(8,128)(2,1)S(1)} %get-tuple-element.92), channel_id=1, source_target_pairs={{0,16},{8,24},{16,0},{24,8},{1,17},{9,25},{17,1},{25,9},{2,18},{10... | collective-permute-start | bytes 393224 | tf_op jit(solution)/shard_map/ppermute | solution.py:725
  15.8 1.4 %collective-permute-done.2.refs_1_ = bf16[2,64,512]{2,1,0:T(8,128)(2,1)S(1)} collective-permute-done((bf16[2,64,512]{2,1,0:T(8,128)(2,1)S(1)}, bf16[2,64,512]{2,1,0:T(8,128)(2,1)S(1)}, u32[]{:S(2)}, u32[]{:S(2)}) %collective-permute-start.2) | collective-permute-done | bytes 131104 | tf_op jit(solution)/shard_map/ppermute | solution.py:725
  17.2 2.0 %collective-permute-done.3.refs_2_ = bf16[2,64,512]{2,1,0:T(8,128)(2,1)S(1)} collective-permute-done((bf16[2,64,512]{2,1,0:T(8,128)(2,1)S(1)}, bf16[2,64,512]{2,1,0:T(8,128)(2,1)S(1)}, u32[]{:S(2)}, u32[]{:S(2)}) %collective-permute-start.3) | collective-permute-done | bytes 131104 | tf_op jit(solution)/shard_map/ppermute | solution.py:725
  19.2 3.8 %collective-permute-done.4.refs_3_ = bf16[2,64,512]{2,1,0:T(8,128)(2,1)S(1)} collective-permute-done((bf16[2,64,512]{2,1,0:T(8,128)(2,1)S(1)}, bf16[2,64,512]{2,1,0:T(8,128)(2,1)S(1)}, u32[]{:S(2)}, u32[]{:S(2)}) %collective-permute-start.4) | collective-permute-done | bytes 131104 | tf_op jit(solution)/shard_map/ppermute | solution.py:725
  23.0 3.6 %time_pair.1 = (bf16[2,64,256]{2,1,0:T(8,128)(2,1)S(1)}, bf16[2,64,256]{2,1,0:T(8,128)(2,1)S(1)}, bf16[2,64,256]{2,1,0:T(8,128)(2,1)S(1)}, bf16[2,64,256]{2,1,0:...) custom-call(bf16[2,64,512]{2,1,0:T(8,128)(2,1)S(1)} %get-tuple-eleme, ...), custom_call_target="tpu_custom_call" | custom-call | flops 9663676416 | bytes 37748736 | tf_op jit(solution)/shard_map/time_pair/pallas_call | solution.py:757
  26.8 3.3 %collective-permute-start.7 = (bf16[2,64,256]{2,1,0:T(8,128)(2,1)S(1)}, bf16[2,64,256]{2,1,0:T(8,128)(2,1)S(1)}, u32[]{:S(2)}, u32[]{:S(2)}) collective-permute-start(bf16[2,64,256]{2,1,0:T(8,128)(2,1)S(1)} %get-tuple-element.104), channel_id=1, source_target_pairs={{0,24},{8,16},{16,8},{24,0},{1,25},{9,17},{17,9},{25,1},{2,26},{10... | collective-permute-start | bytes 196616 | tf_op jit(solution)/shard_map/ppermute | solution.py:725
  31.9 2.9 %collective-permute-start.11 = (bf16[768,128]{1,0:T(8,128)(2,1)S(1)}, bf16[768,128]{1,0:T(8,128)(2,1)S(1)}, u32[]{:S(2)}, u32[]{:S(2)}) collective-permute-start(bf16[768,128]{1,0:T(8,128)(2,1)S(1)} %get-tuple-element.118), channel_id=1, source_target_pairs={{0,24},{8,16},{16,8},{24,0},{1,25},{9,17},{17,9},{25,1},{2,26},{10... | collective-permute-start | bytes 589832 | tf_op jit(solution)/shard_map/ppermute | solution.py:725
  34.8 6.5 %space_backward.1 = (bf16[2,256,256]{2,1,0:T(8,128)(2,1)S(1)}, bf16[2,256,256]{2,1,0:T(8,128)(2,1)S(1)}, bf16[2,768,512]{2,1,0:T(8,128)(2,1)S(1)}, bf16[1024,128]{1,0:T(8,128)(2,1)S(1)}, bf16[1024,128]{1,0:T(8,128)(2,1)S(1)}) custom-call(s32[2,2,4]{2,1,0:T(2,128)} %refs_0_.1, s32[2]{0:T(128)S(1)} %pad_add_fusion.place_ref.refs_0_.refs_1_, ...), custom_call_target="tpu_custom_call" | custom-call | flops 11811160064 | bytes 46137344 | tf_op jit(solution)/shard_map/space_backward/pallas_call | solution.py:757
  41.4 1.6 %collective-permute-done.10.refs_2_ = bf16[768,128]{1,0:T(8,128)(2,1)S(1)} collective-permute-done((bf16[768,128]{1,0:T(8,128)(2,1)S(1)}, bf16[768,128]{1,0:T(8,128)(2,1)S(1)}, u32[]{:S(2)}, u32[]{:S(2)}) %collective-permute-start.10) | collective-permute-done | bytes 196640 | tf_op jit(solution)/shard_map/ppermute | solution.py:725
  44.4 1.3 %collective-permute-start.12 = (bf16[256,128]{1,0:T(8,128)(2,1)S(1)}, bf16[256,128]{1,0:T(8,128)(2,1)S(1)}, u32[]{:S(2)}, u32[]{:S(2)}) collective-permute-start(bf16[256,128]{1,0:T(8,128)(2,1)S(1)} %get-tuple-element.122), channel_id=1, source_target_pairs={{0,8},{8,0},{16,24},{24,16},{1,9},{9,1},{17,25},{25,17},{2,10},{10... | collective-permute-start | bytes 196616 | tf_op jit(solution)/shard_map/ppermute | solution.py:725
  48.0 3.8 %collective-permute-start.16 = (bf16[256,128]{1,0:T(8,128)(2,1)S(1)}, bf16[256,128]{1,0:T(8,128)(2,1)S(1)}, u32[]{:S(2)}, u32[]{:S(2)}) collective-permute-start(bf16[256,128]{1,0:T(8,128)(2,1)S(1)} %add_cores_time.1.refs_4_), channel_id=1, source_target_pairs={{0,2},{1,3},{2,0},{3,1},{4,6},{5,7},{6,4},{7,5},{8,10},{9,11},{10,... | collective-permute-start | bytes 196616 | tf_op jit(solution)/shard_map/ppermute | solution.py:725
  52.1 2.0 %collective-permute-done.16.refs_5_ = bf16[256,128]{1,0:T(8,128)(2,1)S(1)} collective-permute-done((bf16[256,128]{1,0:T(8,128)(2,1)S(1)}, bf16[256,128]{1,0:T(8,128)(2,1)S(1)}, u32[]{:S(2)}, u32[]{:S(2)}) %collective-permute-start.16) | collective-permute-done | bytes 65568 | tf_op jit(solution)/shard_map/ppermute | solution.py:725
  54.7 2.1 %collective-permute-start.17 = (bf16[256,128]{1,0:T(8,128)(2,1)S(1)}, bf16[256,128]{1,0:T(8,128)(2,1)S(1)}, u32[]{:S(2)}, u32[]{:S(2)}) collective-permute-start(bf16[256,128]{1,0:T(8,128)(2,1)S(1)} %get-tuple-element.133.refs_0_), channel_id=1, source_target_pairs={{0,2},{1,3},{2,0},{3,1},{4,6},{5,7},{6,4},{7,5},{8,10},{9,11},{10,... | collective-permute-start | bytes 196616 | tf_op jit(solution)/shard_map/ppermute | solution.py:725
  59.7 2.5 %collective-permute-start.21 = (bf16[256,128]{1,0:T(8,128)(2,1)S(1)}, bf16[256,128]{1,0:T(8,128)(2,1)S(1)}, u32[]{:S(2)}, u32[]{:S(2)}) collective-permute-start(bf16[256,128]{1,0:T(8,128)(2,1)S(1)} %add_space.1.space_ref), channel_id=1, source_target_pairs={{0,4},{1,5},{2,6},{3,7},{4,0},{5,1},{6,2},{7,3},{8,12},{9,13},{10,... | collective-permute-start | bytes 196616 | tf_op jit(solution)/shard_map/ppermute | solution.py:725
  62.1 1.9 %collective-permute-done.18.refs_1_ = bf16[256,128]{1,0:T(8,128)(2,1)S(1)} collective-permute-done((bf16[256,128]{1,0:T(8,128)(2,1)S(1)}, bf16[256,128]{1,0:T(8,128)(2,1)S(1)}, u32[]{:S(2)}, u32[]{:S(2)}) %collective-permute-start.18) | collective-permute-done | bytes 65568 | tf_op jit(solution)/shard_map/ppermute | solution.py:725
  64.9 1.7 %collective-permute-start.24 = (bf16[512,128]{1,0:T(8,128)(2,1)S(1)}, bf16[512,128]{1,0:T(8,128)(2,1)S(1)}, u32[]{:S(2)}, u32[]{:S(2)}) collective-permute-start(bf16[512,128]{1,0:T(8,128)(2,1)S(1)} %add_space_last.1.refs_0_), channel_id=1, source_target_pairs={{0,24},{8,16},{16,8},{24,0},{1,25},{9,17},{17,9},{25,1},{2,26},{10... | collective-permute-start | bytes 393224 | tf_op jit(solution)/shard_map/ppermute | solution.py:725
  68.5 1.8 %field_grad.1 = (bf16[2,256,256]{2,1,0:T(8,128)(2,1)}, bf16[2,256,256]{2,1,0:T(8,128)(2,1)}) custom-call(s32[2]{0:T(128)S(1)} %pad_add_fusion.place_ref.refs_0_.refs_1_, bf16[2,256,256]{2,1,0:T(8,128)(2,1)S(1)} %get-tuple-element.80.wave_ref, bf16[2,256,256]{2,1,0:T(8,128)(2,1)S(1)} %get-tuple-element.112.mixed_grad_ref, ...), custom_call_target="tpu_custom_call" | custom-call | flops 805306368 | bytes 3145728 | tf_op jit(solution)/shard_map/field_grad/pallas_call | solution.py:757
  70.3 1.5 %collective-permute-done.24.refs_3_ = bf16[512,128]{1,0:T(8,128)(2,1)S(1)} collective-permute-done((bf16[512,128]{1,0:T(8,128)(2,1)S(1)}, bf16[512,128]{1,0:T(8,128)(2,1)S(1)}, u32[]{:S(2)}, u32[]{:S(2)}) %collective-permute-start.24) | collective-permute-done | bytes 131104 | tf_op jit(solution)/shard_map/ppermute | solution.py:725
  71.7 3.3 %collective-permute-done.23.refs_2_ = bf16[512,128]{1,0:T(8,128)(2,1)S(1)} collective-permute-done((bf16[512,128]{1,0:T(8,128)(2,1)S(1)}, bf16[512,128]{1,0:T(8,128)(2,1)S(1)}, u32[]{:S(2)}, u32[]{:S(2)}) %collective-permute-start.23) | collective-permute-done | bytes 131104 | tf_op jit(solution)/shard_map/ppermute | solution.py:725
  75.8 1.7 %weight_grads.2 = (f32[2,256,768]{2,1,0:T(8,128)}, f32[2,256,256]{2,1,0:T(8,128)}) custom-call(s32[2]{0:T(128)S(1)} %pad_add_fusion.place_ref.refs_0_.refs_1_, bf16[2048,128]{1,0:T(8,128)(2,1)S(1)} %join_tm.1.refs_1_), custom_call_target="tpu_custom_call" | custom-call | flops 268435456 | bytes 1048576 | tf_op jit(solution)/shard_map/weight_grads/pallas_call | solution.py:757
  77.6 1.7 %weight_grads.3 = (f32[2,256,768]{2,1,0:T(8,128)}, f32[2,256,256]{2,1,0:T(8,128)}) custom-call(s32[2]{0:T(128)S(1)} %pad_add_fusion.place_ref.refs_0_.refs_1_, bf16[2048,128]{1,0:T(8,128)(2,1)S(1)} %collective-permute-done.25.refs_1_, f32[2,256,768]{2,1,0:T(8,128)} %get-tuple-element.152.refs_2_, ...), custom_call_target="tpu_custom_call", output_to_operand_aliasing={{0}: (2, {}), {1}: (3, {})} | custom-call | flops 268435456 | bytes 1048576 | tf_op jit(solution)/shard_map/weight_grads/pallas_call | solution.py:757
  (46 shorter events, 15.0 us)
Async XLA Ops:
  1.1 4.5 %collective-permute-start.1 = (bf16[2,256,256]{2,1,0:T(8,128)(2,1)}, bf16[2,256,256]{2,1,0:T(8,128)(2,1)S(1)}, u32[]{:S(2)}, u32[]{:S(2)}) collective-permute-start(bf16[2,256,256]{2,1,0:T(8,128)(2,1)} %wave_hbm.1), channel_id=1, source_target_pairs={{1,2},{3,4},{5,6},{2,1},{4,3},{6,5},{9,10},{11,12},{13,14},{10,9},... | collective-permute-start | bytes 786440 | tf_op jit(solution)/shard_map/ppermute | solution.py:721
  11.3 5.9 %collective-permute-start.2 = (bf16[2,64,512]{2,1,0:T(8,128)(2,1)S(1)}, bf16[2,64,512]{2,1,0:T(8,128)(2,1)S(1)}, u32[]{:S(2)}, u32[]{:S(2)}) collective-permute-start(bf16[2,64,512]{2,1,0:T(8,128)(2,1)S(1)} %get-tuple-element.91), channel_id=1, source_target_pairs={{0,8},{8,0},{16,24},{24,16},{1,9},{9,1},{17,25},{25,17},{2,10},{10... | collective-permute-start | bytes 393224 | tf_op jit(solution)/shard_map/ppermute | solution.py:725
  14.3 5.0 %collective-permute-start.3 = (bf16[2,64,512]{2,1,0:T(8,128)(2,1)S(1)}, bf16[2,64,512]{2,1,0:T(8,128)(2,1)S(1)}, u32[]{:S(2)}, u32[]{:S(2)}) collective-permute-start(bf16[2,64,512]{2,1,0:T(8,128)(2,1)S(1)} %get-tuple-element.92), channel_id=1, source_target_pairs={{0,16},{8,24},{16,0},{24,8},{1,17},{9,25},{17,1},{25,9},{2,18},{10... | collective-permute-start | bytes 393224 | tf_op jit(solution)/shard_map/ppermute | solution.py:725
  15.8 7.2 %collective-permute-start.4 = (bf16[2,64,512]{2,1,0:T(8,128)(2,1)S(1)}, bf16[2,64,512]{2,1,0:T(8,128)(2,1)S(1)}, u32[]{:S(2)}, u32[]{:S(2)}) collective-permute-start(bf16[2,64,512]{2,1,0:T(8,128)(2,1)S(1)} %get-tuple-element.93), channel_id=1, source_target_pairs={{0,24},{8,16},{16,8},{24,0},{1,25},{9,17},{17,9},{25,1},{2,26},{10... | collective-permute-start | bytes 393224 | tf_op jit(solution)/shard_map/ppermute | solution.py:725
  26.6 5.2 %collective-permute-start.5 = (bf16[2,64,256]{2,1,0:T(8,128)(2,1)S(1)}, bf16[2,64,256]{2,1,0:T(8,128)(2,1)S(1)}, u32[]{:S(2)}, u32[]{:S(2)}) collective-permute-start(bf16[2,64,256]{2,1,0:T(8,128)(2,1)S(1)} %get-tuple-element.95), channel_id=1, source_target_pairs={{0,8},{8,0},{16,24},{24,16},{1,9},{9,1},{17,25},{25,17},{2,10},{10... | collective-permute-start | bytes 196616 | tf_op jit(solution)/shard_map/ppermute | solution.py:725
  26.8 8.0 %collective-permute-start.6 = (bf16[2,64,256]{2,1,0:T(8,128)(2,1)S(1)}, bf16[2,64,256]{2,1,0:T(8,128)(2,1)S(1)}, u32[]{:S(2)}, u32[]{:S(2)}) collective-permute-start(bf16[2,64,256]{2,1,0:T(8,128)(2,1)S(1)} %get-tuple-element.103), channel_id=1, source_target_pairs={{0,16},{8,24},{16,0},{24,8},{1,17},{9,25},{17,1},{25,9},{2,18},{10... | collective-permute-start | bytes 196616 | tf_op jit(solution)/shard_map/ppermute | solution.py:725
  26.8 8.0 %collective-permute-start.7 = (bf16[2,64,256]{2,1,0:T(8,128)(2,1)S(1)}, bf16[2,64,256]{2,1,0:T(8,128)(2,1)S(1)}, u32[]{:S(2)}, u32[]{:S(2)}) collective-permute-start(bf16[2,64,256]{2,1,0:T(8,128)(2,1)S(1)} %get-tuple-element.104), channel_id=1, source_target_pairs={{0,24},{8,16},{16,8},{24,0},{1,25},{9,17},{17,9},{25,1},{2,26},{10... | collective-permute-start | bytes 196616 | tf_op jit(solution)/shard_map/ppermute | solution.py:725
  31.2 10.1 %collective-permute-start.9 = (bf16[768,128]{1,0:T(8,128)(2,1)S(1)}, bf16[768,128]{1,0:T(8,128)(2,1)S(1)}, u32[]{:S(2)}, u32[]{:S(2)}) collective-permute-start(bf16[768,128]{1,0:T(8,128)(2,1)S(1)} %get-tuple-element.116), channel_id=1, source_target_pairs={{0,8},{8,0},{16,24},{24,16},{1,9},{9,1},{17,25},{25,17},{2,10},{10... | collective-permute-start | bytes 589832 | tf_op jit(solution)/shard_map/ppermute | solution.py:725
  31.4 11.5 %collective-permute-start.10 = (bf16[768,128]{1,0:T(8,128)(2,1)S(1)}, bf16[768,128]{1,0:T(8,128)(2,1)S(1)}, u32[]{:S(2)}, u32[]{:S(2)}) collective-permute-start(bf16[768,128]{1,0:T(8,128)(2,1)S(1)} %get-tuple-element.117), channel_id=1, source_target_pairs={{0,16},{8,24},{16,0},{24,8},{1,17},{9,25},{17,1},{25,9},{2,18},{10... | collective-permute-start | bytes 589832 | tf_op jit(solution)/shard_map/ppermute | solution.py:725
  31.9 11.1 %collective-permute-start.11 = (bf16[768,128]{1,0:T(8,128)(2,1)S(1)}, bf16[768,128]{1,0:T(8,128)(2,1)S(1)}, u32[]{:S(2)}, u32[]{:S(2)}) collective-permute-start(bf16[768,128]{1,0:T(8,128)(2,1)S(1)} %get-tuple-element.118), channel_id=1, source_target_pairs={{0,24},{8,16},{16,8},{24,0},{1,25},{9,17},{17,9},{25,1},{2,26},{10... | collective-permute-start | bytes 589832 | tf_op jit(solution)/shard_map/ppermute | solution.py:725
  41.3 2.5 %collective-permute-start.8 = (bf16[1024,128]{1,0:T(8,128)(2,1)S(1)}, bf16[1024,128]{1,0:T(8,128)(2,1)S(1)}, u32[]{:S(2)}, u32[]{:S(2)}) collective-permute-start(bf16[1024,128]{1,0:T(8,128)(2,1)S(1)} %get-tuple-element.114), channel_id=1, source_target_pairs={{0,1},{1,0},{2,3},{3,2},{4,5},{5,4},{6,7},{7,6},{8,9},{9,8},{10,11... | collective-permute-start | bytes 786440 | tf_op jit(solution)/shard_map/ppermute | solution.py:725
  43.7 4.3 %collective-permute-start.15 = (bf16[256,128]{1,0:T(8,128)(2,1)S(1)}, bf16[256,128]{1,0:T(8,128)(2,1)S(1)}, u32[]{:S(2)}, u32[]{:S(2)}) collective-permute-start(bf16[256,128]{1,0:T(8,128)(2,1)S(1)} %get-tuple-element.126), channel_id=1, source_target_pairs={{0,1},{1,0},{2,3},{3,2},{4,5},{5,4},{6,7},{7,6},{8,9},{9,8},{10,11... | collective-permute-start | bytes 196616 | tf_op jit(solution)/shard_map/ppermute | solution.py:725
  44.4 7.4 %collective-permute-start.12 = (bf16[256,128]{1,0:T(8,128)(2,1)S(1)}, bf16[256,128]{1,0:T(8,128)(2,1)S(1)}, u32[]{:S(2)}, u32[]{:S(2)}) collective-permute-start(bf16[256,128]{1,0:T(8,128)(2,1)S(1)} %get-tuple-element.122), channel_id=1, source_target_pairs={{0,8},{8,0},{16,24},{24,16},{1,9},{9,1},{17,25},{25,17},{2,10},{10... | collective-permute-start | bytes 196616 | tf_op jit(solution)/shard_map/ppermute | solution.py:725
  45.8 6.0 %collective-permute-start.13 = (bf16[256,128]{1,0:T(8,128)(2,1)S(1)}, bf16[256,128]{1,0:T(8,128)(2,1)S(1)}, u32[]{:S(2)}, u32[]{:S(2)}) collective-permute-start(bf16[256,128]{1,0:T(8,128)(2,1)S(1)} %get-tuple-element.123), channel_id=1, source_target_pairs={{0,16},{8,24},{16,0},{24,8},{1,17},{9,25},{17,1},{25,9},{2,18},{10... | collective-permute-start | bytes 196616 | tf_op jit(solution)/shard_map/ppermute | solution.py:725
  46.9 5.2 %collective-permute-start.14 = (bf16[256,128]{1,0:T(8,128)(2,1)S(1)}, bf16[256,128]{1,0:T(8,128)(2,1)S(1)}, u32[]{:S(2)}, u32[]{:S(2)}) collective-permute-start(bf16[256,128]{1,0:T(8,128)(2,1)S(1)} %get-tuple-element.124), channel_id=1, source_target_pairs={{0,24},{8,16},{16,8},{24,0},{1,25},{9,17},{17,9},{25,1},{2,26},{10... | collective-permute-start | bytes 196616 | tf_op jit(solution)/shard_map/ppermute | solution.py:725
  48.0 6.0 %collective-permute-start.16 = (bf16[256,128]{1,0:T(8,128)(2,1)S(1)}, bf16[256,128]{1,0:T(8,128)(2,1)S(1)}, u32[]{:S(2)}, u32[]{:S(2)}) collective-permute-start(bf16[256,128]{1,0:T(8,128)(2,1)S(1)} %add_cores_time.1.refs_4_), channel_id=1, source_target_pairs={{0,2},{1,3},{2,0},{3,1},{4,6},{5,7},{6,4},{7,5},{8,10},{9,11},{10,... | collective-permute-start | bytes 196616 | tf_op jit(solution)/shard_map/ppermute | solution.py:725
  54.7 5.0 %collective-permute-start.17 = (bf16[256,128]{1,0:T(8,128)(2,1)S(1)}, bf16[256,128]{1,0:T(8,128)(2,1)S(1)}, u32[]{:S(2)}, u32[]{:S(2)}) collective-permute-start(bf16[256,128]{1,0:T(8,128)(2,1)S(1)} %get-tuple-element.133.refs_0_), channel_id=1, source_target_pairs={{0,2},{1,3},{2,0},{3,1},{4,6},{5,7},{6,4},{7,5},{8,10},{9,11},{10,... | collective-permute-start | bytes 196616 | tf_op jit(solution)/shard_map/ppermute | solution.py:725
  56.8 7.2 %collective-permute-start.18 = (bf16[256,128]{1,0:T(8,128)(2,1)S(1)}, bf16[256,128]{1,0:T(8,128)(2,1)S(1)}, u32[]{:S(2)}, u32[]{:S(2)}) collective-permute-start(bf16[256,128]{1,0:T(8,128)(2,1)S(1)} %get-tuple-element.132.refs_0_), channel_id=1, source_target_pairs={{0,4},{1,5},{2,6},{3,7},{4,0},{5,1},{6,2},{7,3},{8,12},{9,13},{10,... | collective-permute-start | bytes 196616 | tf_op jit(solution)/shard_map/ppermute | solution.py:725
  59.7 5.2 %collective-permute-start.21 = (bf16[256,128]{1,0:T(8,128)(2,1)S(1)}, bf16[256,128]{1,0:T(8,128)(2,1)S(1)}, u32[]{:S(2)}, u32[]{:S(2)}) collective-permute-start(bf16[256,128]{1,0:T(8,128)(2,1)S(1)} %add_space.1.space_ref), channel_id=1, source_target_pairs={{0,4},{1,5},{2,6},{3,7},{4,0},{5,1},{6,2},{7,3},{8,12},{9,13},{10,... | collective-permute-start | bytes 196616 | tf_op jit(solution)/shard_map/ppermute | solution.py:725
  64.0 4.4 %collective-permute-start.19 = (bf16[2,256,256]{2,1,0:T(8,128)(2,1)S(1)}, bf16[2,256,256]{2,1,0:T(8,128)(2,1)S(1)}, u32[]{:S(2)}, u32[]{:S(2)}) collective-permute-start(bf16[2,256,256]{2,1,0:T(8,128)(2,1)S(1)} %get-tuple-element.140), channel_id=1, source_target_pairs={{0,1},{1,0},{2,3},{3,2},{4,5},{5,4},{6,7},{7,6},{8,9},{9,8},{10,11... | collective-permute-start | bytes 786440 | tf_op jit(solution)/shard_map/ppermute | solution.py:725
  64.1 4.4 %collective-permute-start.20 = (bf16[2,256,256]{2,1,0:T(8,128)(2,1)S(1)}, bf16[2,256,256]{2,1,0:T(8,128)(2,1)S(1)}, u32[]{:S(2)}, u32[]{:S(2)}) collective-permute-start(bf16[2,256,256]{2,1,0:T(8,128)(2,1)S(1)} %get-tuple-element.141), channel_id=1, source_target_pairs={{1,2},{3,4},{5,6},{2,1},{4,3},{6,5},{9,10},{11,12},{13,14},{10,9},... | collective-permute-start | bytes 786440 | tf_op jit(solution)/shard_map/ppermute | solution.py:721
  64.9 6.8 %collective-permute-start.24 = (bf16[512,128]{1,0:T(8,128)(2,1)S(1)}, bf16[512,128]{1,0:T(8,128)(2,1)S(1)}, u32[]{:S(2)}, u32[]{:S(2)}) collective-permute-start(bf16[512,128]{1,0:T(8,128)(2,1)S(1)} %add_space_last.1.refs_0_), channel_id=1, source_target_pairs={{0,24},{8,16},{16,8},{24,0},{1,25},{9,17},{17,9},{25,1},{2,26},{10... | collective-permute-start | bytes 393224 | tf_op jit(solution)/shard_map/ppermute | solution.py:725
  66.6 8.4 %collective-permute-start.23 = (bf16[512,128]{1,0:T(8,128)(2,1)S(1)}, bf16[512,128]{1,0:T(8,128)(2,1)S(1)}, u32[]{:S(2)}, u32[]{:S(2)}) collective-permute-start(bf16[512,128]{1,0:T(8,128)(2,1)S(1)} %add_space_last.1.refs_0_), channel_id=1, source_target_pairs={{0,16},{8,24},{16,0},{24,8},{1,17},{9,25},{17,1},{25,9},{2,18},{10... | collective-permute-start | bytes 393224 | tf_op jit(solution)/shard_map/ppermute | solution.py:725
  67.3 7.7 %collective-permute-start.22 = (bf16[512,128]{1,0:T(8,128)(2,1)S(1)}, bf16[512,128]{1,0:T(8,128)(2,1)S(1)}, u32[]{:S(2)}, u32[]{:S(2)}) collective-permute-start(bf16[512,128]{1,0:T(8,128)(2,1)S(1)} %add_space_last.1.refs_0_), channel_id=1, source_target_pairs={{0,8},{8,0},{16,24},{24,16},{1,9},{9,1},{17,25},{25,17},{2,10},{10... | collective-permute-start | bytes 393224 | tf_op jit(solution)/shard_map/ppermute | solution.py:725
  (2 other events, 3.9 us)

commit v12 on v11

--- a/solution.py
+++ b/solution.py
@@ -253,10 +253,10 @@
         return dot_nn(pair_group(keys, pair, width), pair_columns(query_t, pair, width))
 
     steps = len(blocks) * HEADS // 2
-    scores = pair_scores(0)
+    scores, ahead = pair_scores(0), pair_scores(1)
     outs = []
     for step in range(steps):
-        following = pair_scores(step + 1) if step + 1 < steps else None
+        following = pair_scores(step + 2) if step + 2 < steps else None
         index, pair = divmod(step, HEADS // 2)
         frame, block = blocks[index]
         if pair == 0:
@@ -273,7 +273,7 @@
         inverse_sum_ref[frame, block, 2 * pair + 1 : 2 * pair + 2] = inverse_sum[:, BLOCK:]
         out = dot_nn(block_values_t[pair * 2 * width : (pair + 1) * 2 * width], probs)
         outs.append(pair_diagonal(out * inverse_sum, width))
-        scores = following
+        scores, ahead = ahead, following
         if pair == HEADS // 2 - 1:
             attended_t = jnp.concatenate(outs, axis=0)
             span = slice(block * BLOCK, (block + 1) * BLOCK)
@@ -502,10 +502,10 @@
 
     dkv_s[...] = jnp.zeros(dkv_s.shape, F32)
     steps = len(blocks) * HEADS // 2
-    dprobs = pair_products(0)
+    dprobs, ahead = pair_products(0), pair_products(1)
     dquery_parts = []
     for step in range(steps):
-        following = pair_products(step + 1) if step + 1 < steps else None
+        following = pair_products(step + 2) if step + 2 < steps else None
         index, pair = divmod(step, HEADS // 2)
         frame, block = blocks[index]
         _, dattn_t, places = loaded[index]
@@ -541,7 +541,7 @@
         dscores = (probs * ((dprobs - pair_delta) * pair_scale)).astype(BF16)
         dscores_s[frame, block, :, columns] = dscores
         dquery_parts.append(pair_diagonal(dot_nn(block_keys_t[heads], dscores), width))
-        dprobs = following
+        dprobs, ahead = ahead, following
         if pair == HEADS // 2 - 1:
             dquery_ref[frame, span] = flip(jnp.concatenate(dquery_parts, axis=0))
     add_keys(len(blocks) - 1)

time: 79.6 us -> 79.2 us (level)
  transfers between devices with their start and end apart: 26 -> 26, of which waited for: 13 -> 13; matrix products, arithmetic and copies ran while one was open for 0% -> 0% of each run, Pallas kernels for 21% -> 22%
where the time goes in v12:
time: 79.2 us; the launch traced here: 79 us
  starting transfers between devices  30.6 us (39%)
  Pallas kernels  28.7 us (36%)
  waiting for transfers between devices  18.6 us (23%)
  between operations  0.96 us (1%)
    ppermute x24, starting transfers between devices, exchange(): lax.ppermute(cells, axis, [(i, i ^ distance) for i in range(lax.axis_size...  29.3 us
    pallas_call x17, Pallas kernels, call(): pl.pallas_call(body, in_specs=[smem_spec] * len(scalars) + [vmem_spec] *...  28.7 us
    ppermute x24, waiting for transfers between devices, exchange(): lax.ppermute(cells, axis, [(i, i ^ distance) for i in range(lax.axis_size...  18.6 us
  transfers between devices with their start and end apart: 26, of which 13 were waited for; matrix products, arithmetic and copies ran while one was open for 0% of the time, Pallas kernels for 22%

profile of v12, /device:TPU:0, one launch (start us, length us, event | category | flops | bytes accessed | tf_op | source)
XLA Modules:
  0.0 79.0 jit_solution(7533359108038915210)
XLA Ops:
  2.5 3.1 %prepare.1 = (bf16[2,256,256]{2,1,0:T(8,128)(2,1)S(1)}, bf16[2,256,768]{2,1,0:T(8,128)(2,1)S(1)}, bf16[2,768,256]{2,1,0:T(8,128)(2,1)S(1)}, bf16[2,256,256]{2,1,...) custom-call(s32[2]{0:T(128)S(1)} %pad_add_fusion.place_ref.refs_0_.r, ...), custom_call_target="tpu_custom_call" | custom-call | flops 3221225472 | bytes 12582912 | tf_op jit(solution)/shard_map/prepare/pallas_call | solution.py:757
  5.7 5.2 %space_forward.1 = (bf16[2,768,256]{2,1,0:T(8,128)(2,1)S(1)}, bf16[2,768,512]{2,1,0:T(8,128)(2,1)S(1)}, bf16[2,6,256,128]{3,2,1,0:T(8,128)(2,1)S(1)}, bf16[2,6,2...) custom-call(s32[2,2,4]{2,1,0:T(2,128)} %refs_0_.1, ...), custom_call_target="tpu_custom_call", output_to_operand_aliasing={{0}: (9, {}), {1}: (10, {}), {2}: (11, {}), {3}: (12, {})} | custom-call | flops 10737418240 | bytes 41943040 | tf_op jit(solution)/shard_map/space_forward/pallas_call | solution.py:757
  10.9 2.9 %collective-permute-start.2 = (bf16[2,64,512]{2,1,0:T(8,128)(2,1)S(1)}, bf16[2,64,512]{2,1,0:T(8,128)(2,1)S(1)}, u32[]{:S(2)}, u32[]{:S(2)}) collective-permute-start(bf16[2,64,512]{2,1,0:T(8,128)(2,1)S(1)} %get-tuple-element.91), channel_id=1, source_target_pairs={{0,8},{8,0},{16,24},{24,16},{1,9},{9,1},{17,25},{25,17},{2,10},{10... | collective-permute-start | bytes 393224 | tf_op jit(solution)/shard_map/ppermute | solution.py:725
  13.9 1.5 %collective-permute-start.3 = (bf16[2,64,512]{2,1,0:T(8,128)(2,1)S(1)}, bf16[2,64,512]{2,1,0:T(8,128)(2,1)S(1)}, u32[]{:S(2)}, u32[]{:S(2)}) collective-permute-start(bf16[2,64,512]{2,1,0:T(8,128)(2,1)S(1)} %get-tuple-element.92), channel_id=1, source_target_pairs={{0,16},{8,24},{16,0},{24,8},{1,17},{9,25},{17,1},{25,9},{2,18},{10... | collective-permute-start | bytes 393224 | tf_op jit(solution)/shard_map/ppermute | solution.py:725
  15.4 1.4 %collective-permute-done.2.refs_1_ = bf16[2,64,512]{2,1,0:T(8,128)(2,1)S(1)} collective-permute-done((bf16[2,64,512]{2,1,0:T(8,128)(2,1)S(1)}, bf16[2,64,512]{2,1,0:T(8,128)(2,1)S(1)}, u32[]{:S(2)}, u32[]{:S(2)}) %collective-permute-start.2) | collective-permute-done | bytes 131104 | tf_op jit(solution)/shard_map/ppermute | solution.py:725
  16.8 2.0 %collective-permute-done.3.refs_2_ = bf16[2,64,512]{2,1,0:T(8,128)(2,1)S(1)} collective-permute-done((bf16[2,64,512]{2,1,0:T(8,128)(2,1)S(1)}, bf16[2,64,512]{2,1,0:T(8,128)(2,1)S(1)}, u32[]{:S(2)}, u32[]{:S(2)}) %collective-permute-start.3) | collective-permute-done | bytes 131104 | tf_op jit(solution)/shard_map/ppermute | solution.py:725
  18.8 3.8 %collective-permute-done.4.refs_3_ = bf16[2,64,512]{2,1,0:T(8,128)(2,1)S(1)} collective-permute-done((bf16[2,64,512]{2,1,0:T(8,128)(2,1)S(1)}, bf16[2,64,512]{2,1,0:T(8,128)(2,1)S(1)}, u32[]{:S(2)}, u32[]{:S(2)}) %collective-permute-start.4) | collective-permute-done | bytes 131104 | tf_op jit(solution)/shard_map/ppermute | solution.py:725
  22.6 3.6 %time_pair.1 = (bf16[2,64,256]{2,1,0:T(8,128)(2,1)S(1)}, bf16[2,64,256]{2,1,0:T(8,128)(2,1)S(1)}, bf16[2,64,256]{2,1,0:T(8,128)(2,1)S(1)}, bf16[2,64,256]{2,1,0:...) custom-call(bf16[2,64,512]{2,1,0:T(8,128)(2,1)S(1)} %get-tuple-eleme, ...), custom_call_target="tpu_custom_call" | custom-call | flops 9663676416 | bytes 37748736 | tf_op jit(solution)/shard_map/time_pair/pallas_call | solution.py:757
  26.4 3.4 %collective-permute-start.7 = (bf16[2,64,256]{2,1,0:T(8,128)(2,1)S(1)}, bf16[2,64,256]{2,1,0:T(8,128)(2,1)S(1)}, u32[]{:S(2)}, u32[]{:S(2)}) collective-permute-start(bf16[2,64,256]{2,1,0:T(8,128)(2,1)S(1)} %get-tuple-element.104), channel_id=1, source_target_pairs={{0,24},{8,16},{16,8},{24,0},{1,25},{9,17},{17,9},{25,1},{2,26},{10... | collective-permute-start | bytes 196616 | tf_op jit(solution)/shard_map/ppermute | solution.py:725
  31.4 2.9 %collective-permute-start.11 = (bf16[768,128]{1,0:T(8,128)(2,1)S(1)}, bf16[768,128]{1,0:T(8,128)(2,1)S(1)}, u32[]{:S(2)}, u32[]{:S(2)}) collective-permute-start(bf16[768,128]{1,0:T(8,128)(2,1)S(1)} %get-tuple-element.118), channel_id=1, source_target_pairs={{0,24},{8,16},{16,8},{24,0},{1,25},{9,17},{17,9},{25,1},{2,26},{10... | collective-permute-start | bytes 589832 | tf_op jit(solution)/shard_map/ppermute | solution.py:725
  34.4 6.7 %space_backward.1 = (bf16[2,256,256]{2,1,0:T(8,128)(2,1)S(1)}, bf16[2,256,256]{2,1,0:T(8,128)(2,1)S(1)}, bf16[2,768,512]{2,1,0:T(8,128)(2,1)S(1)}, bf16[1024,128]{1,0:T(8,128)(2,1)S(1)}, bf16[1024,128]{1,0:T(8,128)(2,1)S(1)}) custom-call(s32[2,2,4]{2,1,0:T(2,128)} %refs_0_.1, s32[2]{0:T(128)S(1)} %pad_add_fusion.place_ref.refs_0_.refs_1_, ...), custom_call_target="tpu_custom_call" | custom-call | flops 11811160064 | bytes 46137344 | tf_op jit(solution)/shard_map/space_backward/pallas_call | solution.py:757
  41.1 1.4 %collective-permute-done.10.refs_2_ = bf16[768,128]{1,0:T(8,128)(2,1)S(1)} collective-permute-done((bf16[768,128]{1,0:T(8,128)(2,1)S(1)}, bf16[768,128]{1,0:T(8,128)(2,1)S(1)}, u32[]{:S(2)}, u32[]{:S(2)}) %collective-permute-start.10) | collective-permute-done | bytes 196640 | tf_op jit(solution)/shard_map/ppermute | solution.py:725
  44.0 1.4 %collective-permute-start.12 = (bf16[256,128]{1,0:T(8,128)(2,1)S(1)}, bf16[256,128]{1,0:T(8,128)(2,1)S(1)}, u32[]{:S(2)}, u32[]{:S(2)}) collective-permute-start(bf16[256,128]{1,0:T(8,128)(2,1)S(1)} %get-tuple-element.122), channel_id=1, source_target_pairs={{0,8},{8,0},{16,24},{24,16},{1,9},{9,1},{17,25},{25,17},{2,10},{10... | collective-permute-start | bytes 196616 | tf_op jit(solution)/shard_map/ppermute | solution.py:725
  47.6 3.8 %collective-permute-start.16 = (bf16[256,128]{1,0:T(8,128)(2,1)S(1)}, bf16[256,128]{1,0:T(8,128)(2,1)S(1)}, u32[]{:S(2)}, u32[]{:S(2)}) collective-permute-start(bf16[256,128]{1,0:T(8,128)(2,1)S(1)} %add_cores_time.1.refs_4_), channel_id=1, source_target_pairs={{0,2},{1,3},{2,0},{3,1},{4,6},{5,7},{6,4},{7,5},{8,10},{9,11},{10,... | collective-permute-start | bytes 196616 | tf_op jit(solution)/shard_map/ppermute | solution.py:725
  51.7 1.9 %collective-permute-done.16.refs_5_ = bf16[256,128]{1,0:T(8,128)(2,1)S(1)} collective-permute-done((bf16[256,128]{1,0:T(8,128)(2,1)S(1)}, bf16[256,128]{1,0:T(8,128)(2,1)S(1)}, u32[]{:S(2)}, u32[]{:S(2)}) %collective-permute-start.16) | collective-permute-done | bytes 65568 | tf_op jit(solution)/shard_map/ppermute | solution.py:725
  54.3 2.1 %collective-permute-start.17 = (bf16[256,128]{1,0:T(8,128)(2,1)S(1)}, bf16[256,128]{1,0:T(8,128)(2,1)S(1)}, u32[]{:S(2)}, u32[]{:S(2)}) collective-permute-start(bf16[256,128]{1,0:T(8,128)(2,1)S(1)} %get-tuple-element.133.refs_0_), channel_id=1, source_target_pairs={{0,2},{1,3},{2,0},{3,1},{4,6},{5,7},{6,4},{7,5},{8,10},{9,11},{10,... | collective-permute-start | bytes 196616 | tf_op jit(solution)/shard_map/ppermute | solution.py:725
  59.3 2.5 %collective-permute-start.21 = (bf16[256,128]{1,0:T(8,128)(2,1)S(1)}, bf16[256,128]{1,0:T(8,128)(2,1)S(1)}, u32[]{:S(2)}, u32[]{:S(2)}) collective-permute-start(bf16[256,128]{1,0:T(8,128)(2,1)S(1)} %add_space.1.space_ref), channel_id=1, source_target_pairs={{0,4},{1,5},{2,6},{3,7},{4,0},{5,1},{6,2},{7,3},{8,12},{9,13},{10,... | collective-permute-start | bytes 196616 | tf_op jit(solution)/shard_map/ppermute | solution.py:725
  61.7 1.7 %collective-permute-done.18.refs_1_ = bf16[256,128]{1,0:T(8,128)(2,1)S(1)} collective-permute-done((bf16[256,128]{1,0:T(8,128)(2,1)S(1)}, bf16[256,128]{1,0:T(8,128)(2,1)S(1)}, u32[]{:S(2)}, u32[]{:S(2)}) %collective-permute-start.18) | collective-permute-done | bytes 65568 | tf_op jit(solution)/shard_map/ppermute | solution.py:725
  64.5 1.7 %collective-permute-start.24 = (bf16[512,128]{1,0:T(8,128)(2,1)S(1)}, bf16[512,128]{1,0:T(8,128)(2,1)S(1)}, u32[]{:S(2)}, u32[]{:S(2)}) collective-permute-start(bf16[512,128]{1,0:T(8,128)(2,1)S(1)} %add_space_last.1.refs_0_), channel_id=1, source_target_pairs={{0,24},{8,16},{16,8},{24,0},{1,25},{9,17},{17,9},{25,1},{2,26},{10... | collective-permute-start | bytes 393224 | tf_op jit(solution)/shard_map/ppermute | solution.py:725
  68.1 1.8 %field_grad.1 = (bf16[2,256,256]{2,1,0:T(8,128)(2,1)}, bf16[2,256,256]{2,1,0:T(8,128)(2,1)}) custom-call(s32[2]{0:T(128)S(1)} %pad_add_fusion.place_ref.refs_0_.refs_1_, bf16[2,256,256]{2,1,0:T(8,128)(2,1)S(1)} %get-tuple-element.80.wave_ref, bf16[2,256,256]{2,1,0:T(8,128)(2,1)S(1)} %get-tuple-element.112.mixed_grad_ref, ...), custom_call_target="tpu_custom_call" | custom-call | flops 805306368 | bytes 3145728 | tf_op jit(solution)/shard_map/field_grad/pallas_call | solution.py:757
  69.8 1.7 %collective-permute-done.24.refs_3_ = bf16[512,128]{1,0:T(8,128)(2,1)S(1)} collective-permute-done((bf16[512,128]{1,0:T(8,128)(2,1)S(1)}, bf16[512,128]{1,0:T(8,128)(2,1)S(1)}, u32[]{:S(2)}, u32[]{:S(2)}) %collective-permute-start.24) | collective-permute-done | bytes 131104 | tf_op jit(solution)/shard_map/ppermute | solution.py:725
  71.6 3.0 %collective-permute-done.23.refs_2_ = bf16[512,128]{1,0:T(8,128)(2,1)S(1)} collective-permute-done((bf16[512,128]{1,0:T(8,128)(2,1)S(1)}, bf16[512,128]{1,0:T(8,128)(2,1)S(1)}, u32[]{:S(2)}, u32[]{:S(2)}) %collective-permute-start.23) | collective-permute-done | bytes 131104 | tf_op jit(solution)/shard_map/ppermute | solution.py:725
  75.4 1.7 %weight_grads.2 = (f32[2,256,768]{2,1,0:T(8,128)}, f32[2,256,256]{2,1,0:T(8,128)}) custom-call(s32[2]{0:T(128)S(1)} %pad_add_fusion.place_ref.refs_0_.refs_1_, bf16[2048,128]{1,0:T(8,128)(2,1)S(1)} %join_tm.1.refs_1_), custom_call_target="tpu_custom_call" | custom-call | flops 268435456 | bytes 1048576 | tf_op jit(solution)/shard_map/weight_grads/pallas_call | solution.py:757
  77.2 1.7 %weight_grads.3 = (f32[2,256,768]{2,1,0:T(8,128)}, f32[2,256,256]{2,1,0:T(8,128)}) custom-call(s32[2]{0:T(128)S(1)} %pad_add_fusion.place_ref.refs_0_.refs_1_, bf16[2048,128]{1,0:T(8,128)(2,1)S(1)} %collective-permute-done.25.refs_1_, f32[2,256,768]{2,1,0:T(8,128)} %get-tuple-element.152.refs_2_, ...), custom_call_target="tpu_custom_call", output_to_operand_aliasing={{0}: (2, {}), {1}: (3, {})} | custom-call | flops 268435456 | bytes 1048576 | tf_op jit(solution)/shard_map/weight_grads/pallas_call | solution.py:757
  (46 shorter events, 15.1 us)
Async XLA Ops:
  1.1 4.5 %collective-permute-start.1 = (bf16[2,256,256]{2,1,0:T(8,128)(2,1)}, bf16[2,256,256]{2,1,0:T(8,128)(2,1)S(1)}, u32[]{:S(2)}, u32[]{:S(2)}) collective-permute-start(bf16[2,256,256]{2,1,0:T(8,128)(2,1)} %wave_hbm.1), channel_id=1, source_target_pairs={{1,2},{3,4},{5,6},{2,1},{4,3},{6,5},{9,10},{11,12},{13,14},{10,9},... | collective-permute-start | bytes 786440 | tf_op jit(solution)/shard_map/ppermute | solution.py:721
  10.9 5.9 %collective-permute-start.2 = (bf16[2,64,512]{2,1,0:T(8,128)(2,1)S(1)}, bf16[2,64,512]{2,1,0:T(8,128)(2,1)S(1)}, u32[]{:S(2)}, u32[]{:S(2)}) collective-permute-start(bf16[2,64,512]{2,1,0:T(8,128)(2,1)S(1)} %get-tuple-element.91), channel_id=1, source_target_pairs={{0,8},{8,0},{16,24},{24,16},{1,9},{9,1},{17,25},{25,17},{2,10},{10... | collective-permute-start | bytes 393224 | tf_op jit(solution)/shard_map/ppermute | solution.py:725
  13.9 5.0 %collective-permute-start.3 = (bf16[2,64,512]{2,1,0:T(8,128)(2,1)S(1)}, bf16[2,64,512]{2,1,0:T(8,128)(2,1)S(1)}, u32[]{:S(2)}, u32[]{:S(2)}) collective-permute-start(bf16[2,64,512]{2,1,0:T(8,128)(2,1)S(1)} %get-tuple-element.92), channel_id=1, source_target_pairs={{0,16},{8,24},{16,0},{24,8},{1,17},{9,25},{17,1},{25,9},{2,18},{10... | collective-permute-start | bytes 393224 | tf_op jit(solution)/shard_map/ppermute | solution.py:725
  15.4 7.2 %collective-permute-start.4 = (bf16[2,64,512]{2,1,0:T(8,128)(2,1)S(1)}, bf16[2,64,512]{2,1,0:T(8,128)(2,1)S(1)}, u32[]{:S(2)}, u32[]{:S(2)}) collective-permute-start(bf16[2,64,512]{2,1,0:T(8,128)(2,1)S(1)} %get-tuple-element.93), channel_id=1, source_target_pairs={{0,24},{8,16},{16,8},{24,0},{1,25},{9,17},{17,9},{25,1},{2,26},{10... | collective-permute-start | bytes 393224 | tf_op jit(solution)/shard_map/ppermute | solution.py:725
  26.2 5.2 %collective-permute-start.5 = (bf16[2,64,256]{2,1,0:T(8,128)(2,1)S(1)}, bf16[2,64,256]{2,1,0:T(8,128)(2,1)S(1)}, u32[]{:S(2)}, u32[]{:S(2)}) collective-permute-start(bf16[2,64,256]{2,1,0:T(8,128)(2,1)S(1)} %get-tuple-element.95), channel_id=1, source_target_pairs={{0,8},{8,0},{16,24},{24,16},{1,9},{9,1},{17,25},{25,17},{2,10},{10... | collective-permute-start | bytes 196616 | tf_op jit(solution)/shard_map/ppermute | solution.py:725
  26.4 8.0 %collective-permute-start.6 = (bf16[2,64,256]{2,1,0:T(8,128)(2,1)S(1)}, bf16[2,64,256]{2,1,0:T(8,128)(2,1)S(1)}, u32[]{:S(2)}, u32[]{:S(2)}) collective-permute-start(bf16[2,64,256]{2,1,0:T(8,128)(2,1)S(1)} %get-tuple-element.103), channel_id=1, source_target_pairs={{0,16},{8,24},{16,0},{24,8},{1,17},{9,25},{17,1},{25,9},{2,18},{10... | collective-permute-start | bytes 196616 | tf_op jit(solution)/shard_map/ppermute | solution.py:725
  26.4 8.0 %collective-permute-start.7 = (bf16[2,64,256]{2,1,0:T(8,128)(2,1)S(1)}, bf16[2,64,256]{2,1,0:T(8,128)(2,1)S(1)}, u32[]{:S(2)}, u32[]{:S(2)}) collective-permute-start(bf16[2,64,256]{2,1,0:T(8,128)(2,1)S(1)} %get-tuple-element.104), channel_id=1, source_target_pairs={{0,24},{8,16},{16,8},{24,0},{1,25},{9,17},{17,9},{25,1},{2,26},{10... | collective-permute-start | bytes 196616 | tf_op jit(solution)/shard_map/ppermute | solution.py:725
  30.8 10.3 %collective-permute-start.9 = (bf16[768,128]{1,0:T(8,128)(2,1)S(1)}, bf16[768,128]{1,0:T(8,128)(2,1)S(1)}, u32[]{:S(2)}, u32[]{:S(2)}) collective-permute-start(bf16[768,128]{1,0:T(8,128)(2,1)S(1)} %get-tuple-element.116), channel_id=1, source_target_pairs={{0,8},{8,0},{16,24},{24,16},{1,9},{9,1},{17,25},{25,17},{2,10},{10... | collective-permute-start | bytes 589832 | tf_op jit(solution)/shard_map/ppermute | solution.py:725
  31.0 11.6 %collective-permute-start.10 = (bf16[768,128]{1,0:T(8,128)(2,1)S(1)}, bf16[768,128]{1,0:T(8,128)(2,1)S(1)}, u32[]{:S(2)}, u32[]{:S(2)}) collective-permute-start(bf16[768,128]{1,0:T(8,128)(2,1)S(1)} %get-tuple-element.117), channel_id=1, source_target_pairs={{0,16},{8,24},{16,0},{24,8},{1,17},{9,25},{17,1},{25,9},{2,18},{10... | collective-permute-start | bytes 589832 | tf_op jit(solution)/shard_map/ppermute | solution.py:725
  31.4 11.1 %collective-permute-start.11 = (bf16[768,128]{1,0:T(8,128)(2,1)S(1)}, bf16[768,128]{1,0:T(8,128)(2,1)S(1)}, u32[]{:S(2)}, u32[]{:S(2)}) collective-permute-start(bf16[768,128]{1,0:T(8,128)(2,1)S(1)} %get-tuple-element.118), channel_id=1, source_target_pairs={{0,24},{8,16},{16,8},{24,0},{1,25},{9,17},{17,9},{25,1},{2,26},{10... | collective-permute-start | bytes 589832 | tf_op jit(solution)/shard_map/ppermute | solution.py:725
  41.0 2.3 %collective-permute-start.8 = (bf16[1024,128]{1,0:T(8,128)(2,1)S(1)}, bf16[1024,128]{1,0:T(8,128)(2,1)S(1)}, u32[]{:S(2)}, u32[]{:S(2)}) collective-permute-start(bf16[1024,128]{1,0:T(8,128)(2,1)S(1)} %get-tuple-element.114), channel_id=1, source_target_pairs={{0,1},{1,0},{2,3},{3,2},{4,5},{5,4},{6,7},{7,6},{8,9},{9,8},{10,11... | collective-permute-start | bytes 786440 | tf_op jit(solution)/shard_map/ppermute | solution.py:725
  43.3 4.3 %collective-permute-start.15 = (bf16[256,128]{1,0:T(8,128)(2,1)S(1)}, bf16[256,128]{1,0:T(8,128)(2,1)S(1)}, u32[]{:S(2)}, u32[]{:S(2)}) collective-permute-start(bf16[256,128]{1,0:T(8,128)(2,1)S(1)} %get-tuple-element.126), channel_id=1, source_target_pairs={{0,1},{1,0},{2,3},{3,2},{4,5},{5,4},{6,7},{7,6},{8,9},{9,8},{10,11... | collective-permute-start | bytes 196616 | tf_op jit(solution)/shard_map/ppermute | solution.py:725
  44.0 7.4 %collective-permute-start.12 = (bf16[256,128]{1,0:T(8,128)(2,1)S(1)}, bf16[256,128]{1,0:T(8,128)(2,1)S(1)}, u32[]{:S(2)}, u32[]{:S(2)}) collective-permute-start(bf16[256,128]{1,0:T(8,128)(2,1)S(1)} %get-tuple-element.122), channel_id=1, source_target_pairs={{0,8},{8,0},{16,24},{24,16},{1,9},{9,1},{17,25},{25,17},{2,10},{10... | collective-permute-start | bytes 196616 | tf_op jit(solution)/shard_map/ppermute | solution.py:725
  45.4 6.0 %collective-permute-start.13 = (bf16[256,128]{1,0:T(8,128)(2,1)S(1)}, bf16[256,128]{1,0:T(8,128)(2,1)S(1)}, u32[]{:S(2)}, u32[]{:S(2)}) collective-permute-start(bf16[256,128]{1,0:T(8,128)(2,1)S(1)} %get-tuple-element.123), channel_id=1, source_target_pairs={{0,16},{8,24},{16,0},{24,8},{1,17},{9,25},{17,1},{25,9},{2,18},{10... | collective-permute-start | bytes 196616 | tf_op jit(solution)/shard_map/ppermute | solution.py:725
  46.6 5.2 %collective-permute-start.14 = (bf16[256,128]{1,0:T(8,128)(2,1)S(1)}, bf16[256,128]{1,0:T(8,128)(2,1)S(1)}, u32[]{:S(2)}, u32[]{:S(2)}) collective-permute-start(bf16[256,128]{1,0:T(8,128)(2,1)S(1)} %get-tuple-element.124), channel_id=1, source_target_pairs={{0,24},{8,16},{16,8},{24,0},{1,25},{9,17},{17,9},{25,1},{2,26},{10... | collective-permute-start | bytes 196616 | tf_op jit(solution)/shard_map/ppermute | solution.py:725
  47.6 6.0 %collective-permute-start.16 = (bf16[256,128]{1,0:T(8,128)(2,1)S(1)}, bf16[256,128]{1,0:T(8,128)(2,1)S(1)}, u32[]{:S(2)}, u32[]{:S(2)}) collective-permute-start(bf16[256,128]{1,0:T(8,128)(2,1)S(1)} %add_cores_time.1.refs_4_), channel_id=1, source_target_pairs={{0,2},{1,3},{2,0},{3,1},{4,6},{5,7},{6,4},{7,5},{8,10},{9,11},{10,... | collective-permute-start | bytes 196616 | tf_op jit(solution)/shard_map/ppermute | solution.py:725
  54.3 5.0 %collective-permute-start.17 = (bf16[256,128]{1,0:T(8,128)(2,1)S(1)}, bf16[256,128]{1,0:T(8,128)(2,1)S(1)}, u32[]{:S(2)}, u32[]{:S(2)}) collective-permute-start(bf16[256,128]{1,0:T(8,128)(2,1)S(1)} %get-tuple-element.133.refs_0_), channel_id=1, source_target_pairs={{0,2},{1,3},{2,0},{3,1},{4,6},{5,7},{6,4},{7,5},{8,10},{9,11},{10,... | collective-permute-start | bytes 196616 | tf_op jit(solution)/shard_map/ppermute | solution.py:725
  56.4 7.0 %collective-permute-start.18 = (bf16[256,128]{1,0:T(8,128)(2,1)S(1)}, bf16[256,128]{1,0:T(8,128)(2,1)S(1)}, u32[]{:S(2)}, u32[]{:S(2)}) collective-permute-start(bf16[256,128]{1,0:T(8,128)(2,1)S(1)} %get-tuple-element.132.refs_0_), channel_id=1, source_target_pairs={{0,4},{1,5},{2,6},{3,7},{4,0},{5,1},{6,2},{7,3},{8,12},{9,13},{10,... | collective-permute-start | bytes 196616 | tf_op jit(solution)/shard_map/ppermute | solution.py:725
  59.3 5.2 %collective-permute-start.21 = (bf16[256,128]{1,0:T(8,128)(2,1)S(1)}, bf16[256,128]{1,0:T(8,128)(2,1)S(1)}, u32[]{:S(2)}, u32[]{:S(2)}) collective-permute-start(bf16[256,128]{1,0:T(8,128)(2,1)S(1)} %add_space.1.space_ref), channel_id=1, source_target_pairs={{0,4},{1,5},{2,6},{3,7},{4,0},{5,1},{6,2},{7,3},{8,12},{9,13},{10,... | collective-permute-start | bytes 196616 | tf_op jit(solution)/shard_map/ppermute | solution.py:725
  63.4 4.7 %collective-permute-start.19 = (bf16[2,256,256]{2,1,0:T(8,128)(2,1)S(1)}, bf16[2,256,256]{2,1,0:T(8,128)(2,1)S(1)}, u32[]{:S(2)}, u32[]{:S(2)}) collective-permute-start(bf16[2,256,256]{2,1,0:T(8,128)(2,1)S(1)} %get-tuple-element.140), channel_id=1, source_target_pairs={{0,1},{1,0},{2,3},{3,2},{4,5},{5,4},{6,7},{7,6},{8,9},{9,8},{10,11... | collective-permute-start | bytes 786440 | tf_op jit(solution)/shard_map/ppermute | solution.py:725
  63.5 4.6 %collective-permute-start.20 = (bf16[2,256,256]{2,1,0:T(8,128)(2,1)S(1)}, bf16[2,256,256]{2,1,0:T(8,128)(2,1)S(1)}, u32[]{:S(2)}, u32[]{:S(2)}) collective-permute-start(bf16[2,256,256]{2,1,0:T(8,128)(2,1)S(1)} %get-tuple-element.141), channel_id=1, source_target_pairs={{1,2},{3,4},{5,6},{2,1},{4,3},{6,5},{9,10},{11,12},{13,14},{10,9},... | collective-permute-start | bytes 786440 | tf_op jit(solution)/shard_map/ppermute | solution.py:721
  64.5 7.1 %collective-permute-start.24 = (bf16[512,128]{1,0:T(8,128)(2,1)S(1)}, bf16[512,128]{1,0:T(8,128)(2,1)S(1)}, u32[]{:S(2)}, u32[]{:S(2)}) collective-permute-start(bf16[512,128]{1,0:T(8,128)(2,1)S(1)} %add_space_last.1.refs_0_), channel_id=1, source_target_pairs={{0,24},{8,16},{16,8},{24,0},{1,25},{9,17},{17,9},{25,1},{2,26},{10... | collective-permute-start | bytes 393224 | tf_op jit(solution)/shard_map/ppermute | solution.py:725
  66.2 8.4 %collective-permute-start.23 = (bf16[512,128]{1,0:T(8,128)(2,1)S(1)}, bf16[512,128]{1,0:T(8,128)(2,1)S(1)}, u32[]{:S(2)}, u32[]{:S(2)}) collective-permute-start(bf16[512,128]{1,0:T(8,128)(2,1)S(1)} %add_space_last.1.refs_0_), channel_id=1, source_target_pairs={{0,16},{8,24},{16,0},{24,8},{1,17},{9,25},{17,1},{25,9},{2,18},{10... | collective-permute-start | bytes 393224 | tf_op jit(solution)/shard_map/ppermute | solution.py:725
  66.9 7.7 %collective-permute-start.22 = (bf16[512,128]{1,0:T(8,128)(2,1)S(1)}, bf16[512,128]{1,0:T(8,128)(2,1)S(1)}, u32[]{:S(2)}, u32[]{:S(2)}) collective-permute-start(bf16[512,128]{1,0:T(8,128)(2,1)S(1)} %add_space_last.1.refs_0_), channel_id=1, source_target_pairs={{0,8},{8,0},{16,24},{24,16},{1,9},{9,1},{17,25},{25,17},{2,10},{10... | collective-permute-start | bytes 393224 | tf_op jit(solution)/shard_map/ppermute | solution.py:725
  (2 other events, 3.9 us)
